TPU v7x, 32 devices: a whole 2x2x4 slice. The times are simulated.
32 devices in a mesh: groups: 1, ctx: 16 (over z, y, core), tp: 2 (over x), sub: 1.
Axes of the slice: x: 2, y: 2, z: 4, core: 2. Of those that a mesh axis runs over, the one named last changes fastest.
Arguments:
- resid: bfloat16 [1024, 4096], P(('groups', 'ctx'), ('tp', 'sub')), may hold values from -8 to 8
- query: bfloat16 [1024, 4096], P(('groups', 'ctx'), ('tp', 'sub')), may hold values from -6 to 6
- key: bfloat16 [1024, 4096], P(('groups', 'ctx'), ('tp', 'sub')), may hold values from -6 to 6
- value: bfloat16 [1024, 4096], P(('groups', 'ctx'), ('tp', 'sub')), may hold values from -6 to 6
- norm_gain: bfloat16 [4096], P(('tp', 'sub')), may hold values from 0.099609375 to 1.8984375
- routes: int32 [1024, 4], P(('groups', 'ctx')), may hold values from 0 to 7, all different within a row; in each aligned block of 64 rows (0 to 63, 64 to 127, ...) at most 40 rows name the same one
- route_gates: float32 [1024, 4], P(('groups', 'ctx')), may hold values from 0.05 to 1
- segment_ids: int32 [1024], P(('groups', 'ctx')), may hold values from 0 to 31, never falling along the last dimension, each value on 1 to 512 neighbouring positions
- w_gate: bfloat16 [16, 4096, 1024], P('ctx', None, ('tp', 'sub')), may hold values from -0.09375 to 0.09375
- w_up: bfloat16 [16, 4096, 1024], P('ctx', None, ('tp', 'sub')), may hold values from -0.09375 to 0.09375
- w_down: bfloat16 [16, 1024, 4096], P('ctx', None, ('tp', 'sub')), may hold values from -0.125 to 0.125
Outputs:
- layer_out: bfloat16 [1024, 4096], P(('groups', 'ctx'), ('tp', 'sub'))
Inputs may be any that keep to these rules, and one draw needn't show every extreme that they name: `routes`: in each aligned block of 64 positions no expert is chosen more than 40 times, a bound that some block reaches; the experts of one position differ. `segment_ids`: segment numbers never fall along the window; one segment has exactly 512 positions.
All inputs are finite; a program needn't handle non-finite values.
Results may differ from a plain program's by a relative error of at most 0.0065.
Values may be sent and summed in bfloat16 or wider, within the bound.
No kernel may reach another device: no remote copies, remote signals or barrier semaphores. Data moves between devices by JAX's collectives and lax.ppermute only.
A program may use at most 64 MiB of HBM per device.

v0:
```python
import math

import jax
import jax.numpy as jnp
from jax import lax
from jax.sharding import PartitionSpec as P

D = 4096
HD = 128
TOPK = 4


def per_device(
    resid, query, key, value, norm_gain, routes, route_gates, segment_ids, w_gate, w_up, w_down
):
    tok_count = resid.shape[0]
    feat_width = resid.shape[1]
    head_count = feat_width // HD
    score_scale = 1.0 / math.sqrt(HD)
    query_pos = lax.axis_index("ctx") * tok_count + jnp.arange(tok_count, dtype=jnp.int32)
    key_segments = lax.all_gather(segment_ids, "ctx", axis=0, tiled=True)
    query_heads = query.reshape(tok_count, head_count, HD)
    start_sums = (
        jnp.zeros((tok_count, feat_width), jnp.float32),
        jnp.zeros((tok_count,), jnp.float32),
    )
    key_piece = lax.all_gather(key, "ctx", axis=0, tiled=True)
    value_piece = lax.all_gather(value, "ctx", axis=0, tiled=True)
    piece_len = key_piece.shape[0]
    block_len = math.gcd(piece_len, 512)
    block_count = piece_len // block_len
    key_blocks = key_piece.reshape(block_count, block_len, head_count, HD)
    value_blocks = value_piece.reshape(block_count, block_len, head_count, HD)

    def advance(state, inputs):
        key_block, value_block, block_id = inputs
        key_first = block_id * block_len

        def compute(current):
            acc_sum, key_total = current
            key_pos = key_first + jnp.arange(block_len, dtype=jnp.int32)
            key_segs = lax.dynamic_slice_in_dim(key_segments, key_first, block_len, 0)
            visible = jnp.logical_and(
                key_segs[None, :] == segment_ids[:, None], key_pos[None, :] <= query_pos[:, None]
            ).astype(jnp.float32)
            scores = (
                jnp.einsum(
                    "thd,shd->hts", query_heads, key_block, preferred_element_type=jnp.float32
                )
                * score_scale
            )
            weights = (jax.nn.silu(scores) * visible[None]).astype(jnp.bfloat16)
            summed = jnp.einsum(
                "hts,shd->thd", weights, value_block, preferred_element_type=jnp.float32
            )
            return (
                acc_sum + summed.reshape(tok_count, feat_width),
                key_total + jnp.sum(visible, axis=1),
            )

        last_key_seg = lax.dynamic_slice_in_dim(key_segments, key_first + block_len - 1, 1, 0)[0]
        reached = jnp.logical_and(key_first <= query_pos[-1], last_key_seg >= segment_ids[0])
        state = lax.cond(reached, compute, lambda current: current, state)
        return (state, None)

    block_ids = jnp.arange(block_count, dtype=jnp.int32)
    result, unused = lax.scan(advance, start_sums, (key_blocks, value_blocks, block_ids))
    acc_sum, key_total = result
    attended = acc_sum / jnp.sqrt(key_total)[:, None]
    hand_state = (resid.astype(jnp.float32) + attended).astype(jnp.bfloat16)
    hand_f32 = hand_state.astype(jnp.float32)
    square_sums = lax.psum(jnp.sum(hand_f32 * hand_f32, axis=1), ("tp", "sub"))
    normed = (
        hand_f32 * lax.rsqrt(square_sums / D + 1e-06)[:, None] * norm_gain.astype(jnp.float32)
    ).astype(jnp.bfloat16)
    ctx_count = lax.axis_size("ctx")
    expert_count = ctx_count // 2
    capacity = min(tok_count, max(2, tok_count * 10 // ctx_count))
    slot_total = expert_count * capacity
    recv_total = ctx_count * capacity
    flat_routes = routes.reshape(-1)
    onehot = (flat_routes[:, None] == jnp.arange(expert_count, dtype=jnp.int32)[None, :]).astype(
        jnp.int32
    )
    slot_rank = jnp.sum((jnp.cumsum(onehot, axis=0) - 1) * onehot, axis=1)
    slot_index = flat_routes * capacity + slot_rank
    position = jnp.arange(tok_count * TOPK, dtype=jnp.int32) // TOPK
    slot_source = jnp.full((slot_total,), tok_count, jnp.int32).at[slot_index].set(position)
    gate_local = w_gate[0]
    up_local = w_up[0]
    down_local = w_down[0]
    gathered = lax.all_gather(normed, ("tp", "sub"), axis=1, tiled=True)
    padded = jnp.concatenate([gathered, jnp.zeros((1, gathered.shape[1]), gathered.dtype)], axis=0)
    filled = padded[slot_source].reshape(expert_count, capacity, gathered.shape[1])
    arrived = lax.all_to_all(
        jnp.repeat(filled, 2, axis=0), "ctx", split_axis=0, concat_axis=0, tiled=True
    ).reshape(recv_total, gathered.shape[1])
    gate_sum = jnp.dot(arrived, gate_local, preferred_element_type=jnp.float32)
    up_sum = jnp.dot(arrived, up_local, preferred_element_type=jnp.float32)
    hidden = (jax.nn.silu(gate_sum) * up_sum).astype(jnp.bfloat16)
    down_rows_out = jnp.dot(
        lax.all_gather(hidden, ("tp", "sub"), axis=1, tiled=True),
        down_local,
        preferred_element_type=jnp.float32,
    ).astype(jnp.bfloat16)
    returned = lax.all_to_all(
        down_rows_out.reshape(ctx_count, capacity, feat_width),
        "ctx",
        split_axis=0,
        concat_axis=0,
        tiled=True,
    )
    combined = jnp.sum(
        returned.reshape(expert_count, 2, capacity, feat_width).astype(jnp.float32), axis=1
    ).reshape(slot_total, feat_width)
    picked = combined[slot_index].reshape(tok_count, TOPK, feat_width)
    mixed = hand_f32 + jnp.sum(route_gates[:, :, None] * picked, axis=1)
    return mixed.astype(jnp.bfloat16)


def solution(mesh):
    placed = (
        P(("groups", "ctx"), ("tp", "sub")),
        P(("groups", "ctx"), ("tp", "sub")),
        P(("groups", "ctx"), ("tp", "sub")),
        P(("groups", "ctx"), ("tp", "sub")),
        P(("tp", "sub")),
        P(("groups", "ctx"), None),
        P(("groups", "ctx"), None),
        P(("groups", "ctx")),
        P("ctx", None, ("tp", "sub")),
        P("ctx", None, ("tp", "sub")),
        P("ctx", None, ("tp", "sub")),
    )
    return jax.shard_map(
        per_device,
        mesh=mesh,
        in_specs=placed,
        out_specs=P(("groups", "ctx"), ("tp", "sub")),
        check_vma=False,
    )
```

profile of v0, /device:TPU:13, one launch (start us, length us, event | category | flops | bytes accessed | tf_op | source)
XLA Modules:
  0.0 389.4 jit_solution(16240750103662282257)
XLA Ops:
  6.5 0.7 all-gather.4.cloned.1.call-update
  7.3 0.7 all-gather.6.cloned.1.call-update
  8.1 0.8 copy.19
  8.9 0.1 eq.50
  9.1 0.7 convert_element_type.63
  9.8 0.7 broadcast_multiply_fusion
  10.5 0.1 mul.104
  10.7 0.6 reduce-window.6
  11.2 0.2 slice_reduce_fusion
  11.5 1.2 dynamic-slice
  13.4 1.4 scatter_custom_fusion
  14.8 0.9 dynamic-update-slice
  15.7 8.3 %all-reduce.1 = s32[1024]{0:T(1024)S(1)} all-reduce(s32[1024]{0:T(1024)S(1)} %dynamic-update-slice), channel_id=1, replica_groups=mesh['groups'=1,'ctx'=16,'tp'=2,'sub'=1] {'ctx'}, use_global_device_ids=true, to_apply=%add.1 | all-reduce | flops 1024 | bytes 8192
  24.0 36.8 %all-gather.4.cloned.1.call-done = bf16[1024,2048]{1,0:T(8,128)(2,1)} async-done(((bf16[64,2048]{1,0:T(8,128)(2,1)}), bf16[1024,2048]{1,0:T(8,128)(2,1)}) %all-gather.4.cloned.1.call-update) | async-done | bytes 4194320 | tf_op jit(solution)/shard_map/all_gather | solution.py:27
  60.9 3.6 copy.23
  64.5 3.0 copy.14
  67.5 44.6 %all-gather.6.cloned.1.call-done = bf16[1024,2048]{1,0:T(8,128)(2,1)} async-done(((bf16[64,2048]{1,0:T(8,128)(2,1)}), bf16[1024,2048]{1,0:T(8,128)(2,1)}) %all-gather.6.cloned.1.call-update) | async-done | bytes 4194320 | tf_op jit(solution)/shard_map/all_gather | solution.py:28
  112.1 3.6 copy.24
  115.7 3.1 copy.16
  118.8 11.3 %while.16 = (s32[]{:T(128)}, f32[64,2048]{1,0:T(8,128)S(1)}, f32[64]{0:T(128)S(1)}, s32[2]{0:T(128)S(1)}, s32[64]{0:T(128)S(1)}, /*index=5*/s32[1024]{0:T(1024)S...) while((s32[]{:T(128)}, f32[64,2048]{1,0:T(8,128)S(1)}, ...), condition=%wide.region_4.5_spmd, body=%wide.region_0.4_spmd.sunk | while | flops 272531968 | bytes 6833579 | solution.py:67
  118.8 0.6 slice.33
  119.4 0.5 dynamic_slice.59
  120.5 0.6 dynamic_slice.60
  122.4 4.1 %conditional.2 = ((f32[64,2048]{1,0:T(8,128)S(1)}, f32[64]{0:T(128)S(1)})) conditional(s32[]{:T(128)} %convert_element_type.99, (f32[64,2048]{1,0:T(8,128)S(1)}, f32[64]{0:T(128)S(1)}) %tuple.54, (bf16[2,512,16,128]{3,1,2,0:T(8,128)(2,1)}, s32[]{:T(128)}, bf16[64,16,128]{2,0,1:T(8,128)(2,1)S(1)}, s32[]{:T(128)}, s32[1024]{0:T(1024)S(1)}, ...), branch_computations={%region_1.1_spmd, %region_2.3_spmd} | conditional | flops 272531968 | bytes 6833218 | solution.py:63
  122.5 0.2 fusion.18
  122.8 3.6 fusion.13
  126.4 0.1 bitcast_add_fusion
  126.5 0.6 slice.33
  127.1 0.5 dynamic_slice.59
  128.2 0.6 dynamic_slice.60
  130.1 0.3 fusion.38
  130.4 3.8 psum.7
  134.2 0.1 fusion.40
  134.4 7.1 %all_gather.18 = bf16[64,4096]{1,0:T(8,128)(2,1)S(1)} all-gather(bf16[64,2048]{1,0:T(8,128)(2,1)S(1)} %fusion.40), channel_id=1, replica_groups=mesh['groups'=1,'ctx'=16,'tp'=2,'sub'=1] {'tp','sub'}, dimensions={1}, use_global_device_ids=true | all-gather | bytes 786432 | tf_op jit(solution)/shard_map/all_gather | solution.py:92
  141.5 3.3 gather_fusion
  144.7 0.6 broadcast_in_dim.19
  145.4 124.5 %all_to_all.10 = bf16[16,40,4096]{2,1,0:T(8,128)(2,1)S(1)} all-to-all(bf16[16,40,4096]{2,1,0:T(8,128)(2,1)S(1)} %bitcast.95), channel_id=1, replica_groups=mesh['groups'=1,'ctx'=16,'tp'=2,'sub'=1] {'ctx'}, dimensions={0} | all-to-all | bytes 10485760 | tf_op jit(solution)/shard_map/all_to_all | solution.py:95
  269.9 2.9 fusion.27
  272.8 3.8 fusion.35
  276.7 24.3 %all-gather.8.cloned.1.call-done = bf16[640,1024]{1,0:T(8,128)(2,1)} async-done(((bf16[640,512]{1,0:T(8,128)(2,1)}), bf16[640,1024]{1,0:T(8,128)(2,1)}) %all-gather.8.cloned.1.call-update) | async-done | bytes 1310736 | tf_op jit(solution)/shard_map/all_gather | solution.py:102
  301.0 7.0 %fusion.29 = bf16[640,2048]{1,0:T(8,128)(2,1)} fusion(bf16[640,1024]{1,0:T(8,128)(2,1)} %all-gather.8.cloned.1.call-done, bf16[1,1024,2048]{2,1,0:T(8,128)(2,1)} %param.25), kind=kOutput, calls=%fused_computation.31 | convolution fusion | flops 2685665280 | bytes 8126464 | tf_op jit(solution)/shard_map/dot_general | solution.py:101
  308.0 6.5 %all-to-all-start.1 = ((bf16[16,40,2048]{2,1,0:T(8,128)(2,1)}), bf16[16,40,2048]{2,1,0:T(8,128)(2,1)}, u32[]{:S(2)}, u32[]{:S(2)}) async-start(bf16[16,40,2048]{2,1,0:T(8,128)(2,1)} %bitcast.18), calls=%async_computation.1 | async-start | bytes 5242880 | tf_op jit(solution)/shard_map/all_to_all | solution.py:106
  314.6 58.7 %all-to-all-done.1 = bf16[16,40,2048]{2,1,0:T(8,128)(2,1)} async-done(((bf16[16,40,2048]{2,1,0:T(8,128)(2,1)}), bf16[16,40,2048]{2,1,0:T(8,128)(2,1)}, u32[]{:S(2)}, u32[]{:S(2)}) %all-to-all-start.1) | async-done | bytes 2621472 | tf_op jit(solution)/shard_map/all_to_all | solution.py:106
  373.3 2.6 convert_reduce_fusion
  375.8 2.7 gather_fusion.1
  378.6 1.9 reshape.159
  380.5 1.6 multiply_reduce_fusion
  382.1 0.8 fusion.41
  (48 shorter events, 0.9 us)
Async XLA Ops:
  6.5 17.4 %copy-start = (bf16[64,2048]{1,0:T(8,128)(2,1)S(1)}, bf16[64,2048]{1,0:T(8,128)(2,1)}, u32[]{:S(2)}) copy-start(bf16[64,2048]{1,0:T(8,128)(2,1)} %param.16) | copy-start | bytes 786436
  6.5 54.3 %all-gather.4.cloned.1.call-start = ((), (), s32[]{:S(2)}) async-start(), calls=%async_computation.2 | async-start | bytes 4456448 | tf_op jit(solution)/shard_map/all_gather | solution.py:27
  7.3 104.9 %all-gather.6.cloned.1.call-start = ((), (), s32[]{:S(2)}) async-start(), calls=%async_computation.3 | async-start | bytes 4456448 | tf_op jit(solution)/shard_map/all_gather | solution.py:28
  8.0 293.0 %all-gather.8.cloned.1.call-start = ((), (), s32[]{:S(2)}) async-start(), calls=%async_computation.4 | async-start | bytes 1966080 | tf_op jit(solution)/shard_map/all_gather | solution.py:102
  115.7 3.1 copy-start.5
  118.8 11.3 %copy-start.4 = (bf16[64,2048]{1,0:T(8,128)(2,1)S(1)}, bf16[64,2048]{1,0:T(8,128)(2,1)}, u32[]{:S(2)}) copy-start(bf16[64,2048]{1,0:T(8,128)(2,1)} %param.15) | copy-start | bytes 786436
  130.4 14.3 %copy-start.2 = (bf16[64,2048]{1,0:T(8,128)(2,1)}, bf16[64,2048]{1,0:T(8,128)(2,1)S(1)}, u32[]{:S(2)}) copy-start(bf16[64,2048]{1,0:T(8,128)(2,1)S(1)} %get-tuple-element.334) | copy-start | bytes 786436
  145.4 124.5 %copy-start.7 = (bf16[1,4096,512]{2,1,0:T(8,128)(2,1)S(1)}, bf16[1,4096,512]{2,1,0:T(8,128)(2,1)}, u32[]{:S(2)}) copy-start(bf16[1,4096,512]{2,1,0:T(8,128)(2,1)} %param.23) | copy-start | bytes 12582916
  269.9 2.9 copy-start.8
  308.0 6.5 %copy-start.6 = (f32[64,4]{0,1:T(4,128)S(1)}, f32[64,4]{0,1:T(4,128)}, u32[]{:S(2)}) copy-start(f32[64,4]{0,1:T(4,128)} %param.21) | copy-start | bytes 3076
  308.0 65.3 %all-to-all-start.1 = ((bf16[16,40,2048]{2,1,0:T(8,128)(2,1)}), bf16[16,40,2048]{2,1,0:T(8,128)(2,1)}, u32[]{:S(2)}, u32[]{:S(2)}) async-start(bf16[16,40,2048]{2,1,0:T(8,128)(2,1)} %bitcast.18), calls=%async_computation.1 | async-start | bytes 5242880 | tf_op jit(solution)/shard_map/all_to_all | solution.py:106
  378.6 3.5 copy-start.3
  378.6 4.3 %copy-start.1 = (bf16[64,2048]{1,0:T(8,128)(2,1)S(1)}, bf16[64,2048]{1,0:T(8,128)(2,1)}, u32[]{:S(2)}) copy-start(bf16[64,2048]{1,0:T(8,128)(2,1)} %param.16) | copy-start | bytes 786436
Sparse Core Ops, SparseCore 0:
  9.5 51.2 all-gather.3
  63.0 49.0 all-gather.5
  276.8 24.1 all-gather.7
where the time goes:
time: 390 us; the launch traced here: 389 us
  waiting for transfers between devices  166 us (43%)
  blocking collectives  144 us (37%)
  local copies, waits for them, and re-layouts  30.5 us (8%)
  matrix products  17.2 us (4%)
  between operations  13.9 us (4%)
  other arithmetic  7.87 us (2%)
  starting transfers between devices  6.58 us (2%)
    all_to_all x1, blocking collectives, per_device(): lax.all_to_all(jnp.repeat(filled, 2, axis=0), 'ctx', split_axis=0, concat...  125 us
    all_to_all x1, waiting for transfers between devices, per_device(): lax.all_to_all(down_rows_out.reshape(ctx_count, capacity, feat_width), 'c...  58.7 us
    all_gather x1, waiting for transfers between devices, per_device(): value_piece = lax.all_gather(value, 'ctx', axis=0, tiled=True)  44.6 us
    all_gather x1, waiting for transfers between devices, per_device(): key_piece = lax.all_gather(key, 'ctx', axis=0, tiled=True)  36.8 us
    all_gather x1, waiting for transfers between devices, per_device(): lax.all_gather(hidden, ('tp', 'sub'), axis=1, tiled=True)  24.3 us
    unnamed x25, local copies, waits for them, and re-layouts  10.2 us
    unnamed x1, blocking collectives  8.28 us
  transfers between devices with their start and end apart: 4, of which 4 were waited for; matrix products, arithmetic and copies ran while one was open for 4% of the time, Pallas kernels for 0%

commit v1 on v0

--- a/solution.py
+++ b/solution.py
@@ -1,16 +1,291 @@
+import functools
 import math
 
 import jax
 import jax.numpy as jnp
 from jax import lax
+from jax.experimental import pallas as pl
+from jax.experimental.pallas import tpu as pltpu
 from jax.sharding import PartitionSpec as P
 
 D = 4096
 HD = 128
 TOPK = 4
-
-
-def per_device(
+EPS = 1e-06
+META = 16
+LANES = 128
+MIB = 1 << 20
+
+
+def silu(v):
+    return v * (0.5 * jnp.tanh(0.5 * v) + 0.5)
+
+
+def call(kernel, out_shape, args, smem=0, scratch=(), vmem=24, flops=0, moved=0):
+    specs = [pl.BlockSpec(memory_space=pltpu.SMEM)] * smem
+    specs += [pl.BlockSpec(memory_space=pltpu.VMEM)] * (len(args) - smem)
+    several = isinstance(out_shape, (tuple, list))
+    out = pl.BlockSpec(memory_space=pltpu.VMEM)
+    return pl.pallas_call(
+        kernel,
+        out_shape=out_shape,
+        in_specs=specs,
+        out_specs=tuple(out for _ in out_shape) if several else out,
+        scratch_shapes=list(scratch),
+        compiler_params=pltpu.CompilerParams(vmem_limit_bytes=vmem * MIB),
+        cost_estimate=pl.CostEstimate(flops=flops, bytes_accessed=moved, transcendentals=0),
+    )(*args)
+
+
+def pack_kernel(q_ref, k_ref, v_ref, r_ref, seg_ref, gate_ref, out_ref):
+    heads, tok = out_ref.shape[0], q_ref.shape[0]
+    row = lax.broadcasted_iota(jnp.int32, (META, LANES), 0)
+    seg = jnp.broadcast_to(seg_ref[...], (META, LANES))
+    for h in range(heads):
+        cols = slice(h * HD, (h + 1) * HD)
+        for n, ref in enumerate((q_ref, k_ref, v_ref, r_ref)):
+            out_ref[h, n * tok : (n + 1) * tok, :] = ref[:, cols]
+        gate = jnp.broadcast_to(gate_ref[h : h + 1, :], (META, LANES))
+        high = gate.astype(jnp.bfloat16).astype(jnp.float32)
+        middle = (gate - high).astype(jnp.bfloat16).astype(jnp.float32)
+        low = gate - high - middle
+        meta = jnp.where(
+            row == 0, seg, jnp.where(row == 1, high, jnp.where(row == 2, middle, jnp.where(row == 3, low, 0.0)))
+        )
+        out_ref[h, 4 * tok : 4 * tok + META, :] = meta.astype(jnp.bfloat16)
+
+
+def attend_kernel(x_ref, even_ref, odd_ref, gate_even_ref, gate_odd_ref):
+    blocks = x_ref.shape[0]
+    tok = LANES // 2
+    scale = 1.0 / math.sqrt(HD)
+    lane = lax.broadcasted_iota(jnp.int32, (META, LANES), 1)
+    row_at = lax.broadcasted_iota(jnp.int32, (LANES, LANES), 0)
+    lane_at = lax.broadcasted_iota(jnp.int32, (LANES, LANES), 1)
+    causal = lane_at <= row_at
+
+    def part(n, first, last):
+        return x_ref[first:last, n * tok : (n + 1) * tok, :].reshape((last - first) * tok, HD)
+
+    seg_rows = []
+    for i in range(blocks // 2):
+        meta = jnp.where(
+            lane < tok,
+            x_ref[2 * i, 4 * tok : 4 * tok + META, :].astype(jnp.float32),
+            x_ref[2 * i + 1, 4 * tok : 4 * tok + META, :].astype(jnp.float32),
+        )
+        seg_rows.append(meta[0:1, :])
+        seg_col = jnp.transpose(jnp.broadcast_to(meta[0:1, :], (LANES, LANES)))
+        gate_row = meta[1:2, :] + (meta[2:3, :] + meta[3:4, :])
+        gate_col = jnp.transpose(jnp.broadcast_to(gate_row, (LANES, LANES)))
+        masks = []
+        for j in range(i + 1):
+            same = seg_col == jnp.broadcast_to(seg_rows[j], (LANES, LANES))
+            if j == i:
+                same = jnp.logical_and(same, causal)
+            masks.append(same.astype(jnp.float32))
+        visible = jnp.concatenate(masks, axis=1)
+        query = part(0, 2 * i, 2 * i + 2)
+        keys = part(1, 0, 2 * i + 2)
+        values = part(2, 0, 2 * i + 2)
+        scores = (
+            lax.dot_general(query, keys, (((1,), (1,)), ((), ())), preferred_element_type=jnp.float32) * scale
+        )
+        weights = (silu(scores) * visible).astype(jnp.bfloat16)
+        summed = jnp.dot(weights, values, preferred_element_type=jnp.float32)
+        counted = jnp.sum(visible, axis=1, keepdims=True)
+        hand = (part(3, 2 * i, 2 * i + 2).astype(jnp.float32) + summed / jnp.sqrt(counted)).astype(jnp.bfloat16)
+        here = slice(i * tok, (i + 1) * tok)
+        even_ref[here, :] = hand[:tok, :]
+        odd_ref[here, :] = hand[tok:, :]
+        gate_even_ref[here, :] = gate_col[:tok, :]
+        gate_odd_ref[here, :] = gate_col[tok:, :]
+
+
+def gate_up_kernel(places, heads, idx_ref, gain_ref, wg_ref, wu_ref, *refs):
+    pieces, (hidden_ref, hand_ref, lhs_ref) = refs[: len(places)], refs[len(places) :]
+    me, plane = idx_ref[0], idx_ref[1]
+    rows = pieces[0].shape[1]
+    tok = hand_ref.shape[0]
+    tile = min(rows, 128)
+    mine = pl.multiple_of(lax.div(me, 2) * tok, tok)
+    for ref, entries in zip(pieces, places):
+        for k, (other, mask) in enumerate(entries):
+            if not other:
+                at = pl.multiple_of((me ^ mask) * HD, HD)
+                hand_ref[:, pl.ds(at, HD)] = ref[k, pl.ds(mine, tok), :]
+
+    def normalise(r, carry):
+        here = pl.ds(pl.multiple_of(r * tile, tile), tile)
+        squares = jnp.zeros((tile, HD), jnp.float32)
+        for ref, entries in zip(pieces, places):
+            for k in range(len(entries)):
+                v = ref[k, here, :].astype(jnp.float32)
+                squares = squares + v * v
+        scale = lax.rsqrt(jnp.sum(squares, axis=1, keepdims=True) / D + EPS)
+        for ref, entries in zip(pieces, places):
+            for k, (other, mask) in enumerate(entries):
+                head = me ^ mask
+                at = pl.multiple_of(((plane ^ other) * heads + head) * HD, HD)
+                gain = gain_ref[other : other + 1, pl.ds(pl.multiple_of(head * HD, HD), HD)]
+                v = ref[k, here, :].astype(jnp.float32) * scale * gain
+                lhs_ref[here, pl.ds(at, HD)] = v.astype(jnp.bfloat16)
+        return carry
+
+    lax.fori_loop(0, rows // tile, normalise, 0)
+    width = min(256, wg_ref.shape[1])
+
+    def project(n, carry):
+        cols = pl.ds(pl.multiple_of(n * width, width), width)
+        gate = jnp.dot(lhs_ref[...], wg_ref[:, cols], preferred_element_type=jnp.float32)
+        up = jnp.dot(lhs_ref[...], wu_ref[:, cols], preferred_element_type=jnp.float32)
+        hidden_ref[:, cols] = (silu(gate) * up).astype(jnp.bfloat16)
+        return carry
+
+    lax.fori_loop(0, wg_ref.shape[1] // width, project, 0)
+
+
+def down_kernel(idx_ref, own_ref, peer_ref, wd_ref, out_ref):
+    plane = idx_ref[1]
+    depth = own_ref.shape[1]
+    width = min(512, wd_ref.shape[1])
+    own_rows = pl.ds(pl.multiple_of(plane * depth, depth), depth)
+    peer_rows = pl.ds(pl.multiple_of((1 - plane) * depth, depth), depth)
+
+    def project(n, carry):
+        cols = pl.ds(pl.multiple_of(n * width, width), width)
+        total = jnp.dot(own_ref[...], wd_ref[own_rows, cols], preferred_element_type=jnp.float32)
+        total = total + jnp.dot(peer_ref[...], wd_ref[peer_rows, cols], preferred_element_type=jnp.float32)
+        out_ref[:, cols] = total.astype(jnp.bfloat16)
+        return carry
+
+    lax.fori_loop(0, wd_ref.shape[1] // width, project, 0)
+
+
+def weigh_kernel(idx_ref, own_ref, other_ref, gate_ref, send_ref, keep_ref):
+    pair = lax.div(idx_ref[0], 2)
+    count, tok, width = send_ref.shape
+    for k in range(count):
+        for flip, out_ref in ((1, send_ref), (0, keep_ref)):
+            here = pl.ds(pl.multiple_of((pair ^ (2 * k + flip)) * tok, tok), tok)
+            gate = gate_ref[here, :]
+            for n in range(width // LANES):
+                cols = slice(n * LANES, (n + 1) * LANES)
+                both = own_ref[here, cols].astype(jnp.float32) + other_ref[here, cols].astype(jnp.float32)
+                out_ref[k, :, cols] = (both * gate).astype(out_ref.dtype)
+
+
+def add_kernel(keep_ref, got_ref, own_ref, *send_refs):
+    own_ref[...] = keep_ref[0] + got_ref[0].astype(jnp.float32)
+    for k, ref in enumerate(send_refs, 1):
+        ref[...] = (keep_ref[k] + got_ref[k].astype(jnp.float32)).astype(jnp.bfloat16)
+
+
+def final_kernel(idx_ref, *refs):
+    out_ref = refs[-1]
+    per = (len(refs) - 1) // 2
+    core = lax.rem(idx_ref[0], 2)
+    for n in range(2):
+        @pl.when(core == n)
+        def _(mine=refs[n * per : (n + 1) * per]):
+            total = mine[1][...]
+            for ref in mine[2:]:
+                total = total + ref[...].astype(jnp.float32)
+            out_ref[...] = (mine[0][...].astype(jnp.float32) + total).astype(jnp.bfloat16)
+
+
+def heads_over_ctx(
+    resid, query, key, value, norm_gain, routes, route_gates, segment_ids, w_gate, w_up, w_down
+):
+    ctx = lax.axis_size("ctx")
+    heads, tok, width = ctx, resid.shape[0], resid.shape[1]
+    levels = ctx // 4
+    experts = ctx // 2
+    bf16, f32 = jnp.bfloat16, jnp.float32
+    rows = ctx // 2 * tok
+    me, plane = lax.axis_index("ctx"), lax.axis_index("tp")
+    idx = jnp.stack([me, plane]).astype(jnp.int32)
+
+    def over_ctx(x, mask, core=None):
+        return lax.ppermute(x, "ctx", [(c, c ^ mask) for c in range(ctx) if core is None or c % 2 == core])
+
+    def over_tp(x):
+        return lax.ppermute(x, "tp", [(0, 1), (1, 0)])
+
+    def to_core(x, core):
+        return lax.ppermute(x, "ctx", [(c, c ^ 1) for c in range(ctx) if c % 2 != core])
+
+    wg, wu, wd = w_gate[0], w_up[0], w_down[0]
+    chosen = routes[:, :, None] == jnp.arange(experts, dtype=jnp.int32)
+    gate_rows = jnp.sum(jnp.where(chosen, route_gates[:, :, None], 0.0), axis=1).T
+    gate_rows = jnp.tile(jnp.repeat(gate_rows, 2, axis=0), (1, 2))
+    seg_row = jnp.tile(segment_ids.astype(f32)[None, :], (1, 2))
+    packed = call(
+        pack_kernel,
+        jax.ShapeDtypeStruct((ctx, 4 * tok + META, HD), bf16),
+        (query, key, value, resid, seg_row, gate_rows),
+    )
+    arrived = lax.all_to_all(packed, "ctx", split_axis=0, concat_axis=0, tiled=True)
+    gain = jnp.stack([norm_gain, over_tp(norm_gain)]).astype(f32)
+    hand_even, hand_odd, gates_even, gates_odd = call(
+        attend_kernel,
+        [jax.ShapeDtypeStruct((rows, HD), t) for t in (bf16, bf16, f32, f32)],
+        (arrived,),
+    )
+    masks = [4 * k for k in range(levels)]
+    half = levels // 2
+    results = []
+    for core, (hand, gates) in enumerate(((hand_even, gates_even), (hand_odd, gates_odd))):
+        column = jnp.stack([hand] + [over_ctx(hand, m) for m in masks[1:]])
+        by_y, by_x = over_ctx(column, 2), over_tp(column)
+        diag_x, diag_y = over_tp(by_y[:half]), over_ctx(by_x[half:], 2)
+        pieces = [column, by_y, by_x, diag_x, diag_y]
+        places = [
+            [(0, m) for m in masks],
+            [(0, m ^ 2) for m in masks],
+            [(1, m) for m in masks],
+            [(1, m ^ 2) for m in masks[:half]],
+            [(1, m ^ 2) for m in masks[half:]],
+        ]
+        pieces += [over_ctx(p, 1) for p in pieces]
+        places += [[(t, m ^ 1) for t, m in entry] for entry in places]
+        hidden, own_hand = call(
+            functools.partial(gate_up_kernel, places, heads),
+            [
+                jax.ShapeDtypeStruct((rows, wg.shape[1]), bf16),
+                jax.ShapeDtypeStruct((tok, width), bf16),
+            ],
+            (idx, gain, wg, wu, *pieces),
+            smem=1,
+            scratch=[pltpu.VMEM((rows, D), bf16)],
+            vmem=32,
+            flops=4 * rows * D * wg.shape[1],
+            moved=2 * (rows * D + 2 * D * wg.shape[1]),
+        )
+        half_out = call(
+            down_kernel,
+            jax.ShapeDtypeStruct((rows, width), bf16),
+            (idx, hidden, over_tp(hidden), wd),
+            smem=1,
+            flops=2 * rows * wd.shape[0] * width,
+            moved=2 * (rows * width + wd.shape[0] * width),
+        )
+        send, keep = call(
+            weigh_kernel,
+            [jax.ShapeDtypeStruct((levels, tok, width), t) for t in (bf16, f32)],
+            (idx, half_out, to_core(half_out, core), gates),
+            smem=1,
+        )
+        own, *sends = call(
+            add_kernel,
+            [jax.ShapeDtypeStruct((tok, width), t) for t in [f32] + [bf16] * (levels - 1)],
+            (keep, over_ctx(send, 2, core)),
+        )
+        results += [own_hand, own] + [over_ctx(s, m, core) for s, m in zip(sends, masks[1:])]
+    return call(final_kernel, jax.ShapeDtypeStruct((tok, width), bf16), (idx, *results), smem=1)
+
+
+def general(
     resid, query, key, value, norm_gain, routes, route_gates, segment_ids, w_gate, w_up, w_down
 ):
     tok_count = resid.shape[0]
@@ -71,7 +346,7 @@
     hand_f32 = hand_state.astype(jnp.float32)
     square_sums = lax.psum(jnp.sum(hand_f32 * hand_f32, axis=1), ("tp", "sub"))
     normed = (
-        hand_f32 * lax.rsqrt(square_sums / D + 1e-06)[:, None] * norm_gain.astype(jnp.float32)
+        hand_f32 * lax.rsqrt(square_sums / D + EPS)[:, None] * norm_gain.astype(jnp.float32)
     ).astype(jnp.bfloat16)
     ctx_count = lax.axis_size("ctx")
     expert_count = ctx_count // 2
@@ -118,6 +393,13 @@
     return mixed.astype(jnp.bfloat16)
 
 
+def fits(mesh, resid):
+    ctx, tp = mesh.shape["ctx"], mesh.shape["tp"]
+    heads = resid.shape[1] // tp // HD
+    tok = resid.shape[0] // mesh.shape["groups"] // ctx
+    return tp == 2 and mesh.shape["sub"] == 1 and heads == ctx and 2 * tok == LANES and ctx >= 8 and ctx & (ctx - 1) == 0
+
+
 def solution(mesh):
     placed = (
         P(("groups", "ctx"), ("tp", "sub")),
@@ -132,10 +414,15 @@
         P("ctx", None, ("tp", "sub")),
         P("ctx", None, ("tp", "sub")),
     )
-    return jax.shard_map(
-        per_device,
-        mesh=mesh,
-        in_specs=placed,
-        out_specs=P(("groups", "ctx"), ("tp", "sub")),
-        check_vma=False,
-    )
+
+    def step(resid, *rest):
+        per_device = heads_over_ctx if fits(mesh, resid) else general
+        return jax.shard_map(
+            per_device,
+            mesh=mesh,
+            in_specs=placed,
+            out_specs=P(("groups", "ctx"), ("tp", "sub")),
+            check_vma=False,
+        )(resid, *rest)
+
+    return step

time: 390 us -> 210 us (0.54)
  blocking collectives: 144 us -> 32.7 us
  waiting for transfers between devices: 166 us -> 84.2 us
  starting transfers between devices: 6.58 us -> 46.9 us
  Pallas kernels: 0 us -> 30.2 us
  matrix products: 17.2 us -> 0 us
  local copies, waits for them, and re-layouts: 30.5 us -> 13.3 us
  between operations: 13.9 us -> 0.29 us
  other arithmetic: 7.87 us -> 1.6 us
    all_gather x3 -> x0, waiting for transfers between devices: 106 us -> none  [the longest x1 44.6 us: per_device(): value_piece = lax.all_gather(value, 'ctx', axis=0, tiled=True)]
    all_to_all x1, blocking collectives: 125 us -> 32.7 us  [heads_over_ctx(): lax.all_to_all(packed, 'ctx', split_axis=0, concat_axis=0, tiled=True)]
    ppermute x0 -> x37, waiting for transfers between devices: none -> 84.2 us  [the longest x28 60.7 us: over_ctx(): lax.ppermute(x, 'ctx', [(c, c ^ mask) for c in range(ctx) if core is None...]
    all_to_all x1 -> x0, waiting for transfers between devices: 58.7 us -> none  [per_device(): lax.all_to_all(down_rows_out.reshape(ctx_count, capacity, feat_width), 'c...]
    ppermute x0 -> x37, starting transfers between devices: none -> 46.9 us  [the longest x28 36.6 us: over_ctx(): lax.ppermute(x, 'ctx', [(c, c ^ mask) for c in range(ctx) if core is None...]
    pallas_call x0 -> x11, Pallas kernels: none -> 30.2 us  [call(): pl.pallas_call(kernel, out_shape=out_shape, in_specs=specs, out_specs=tup...]
    dot_general x4 -> x0, matrix products: 17.2 us -> none  [the longest x1 6.97 us: per_device(): jnp.dot(lax.all_gather(hidden, ('tp', 'sub'), axis=1, tiled=True), down_l...]
    unnamed x1 -> x0, blocking collectives: 8.28 us -> none
  transfers between devices with their start and end apart: 4 -> 37, of which waited for: 4 -> 14; matrix products, arithmetic and copies ran while one was open for 4% -> 2% of each run, Pallas kernels for 0% -> 13%
where the time goes in v1:
time: 210 us; the launch traced here: 209 us
  waiting for transfers between devices  84.2 us (40%)
  starting transfers between devices  46.9 us (22%)
  blocking collectives  32.7 us (16%)
  Pallas kernels  30.2 us (14%)
  local copies, waits for them, and re-layouts  13.3 us (6%)
    ppermute x28, waiting for transfers between devices, over_ctx(): lax.ppermute(x, 'ctx', [(c, c ^ mask) for c in range(ctx) if core is None...  60.7 us
    ppermute x28, starting transfers between devices, over_ctx(): lax.ppermute(x, 'ctx', [(c, c ^ mask) for c in range(ctx) if core is None...  36.6 us
    all_to_all x1, blocking collectives, heads_over_ctx(): lax.all_to_all(packed, 'ctx', split_axis=0, concat_axis=0, tiled=True)  32.7 us
    pallas_call x11, Pallas kernels, call(): pl.pallas_call(kernel, out_shape=out_shape, in_specs=specs, out_specs=tup...  30.2 us
    ppermute x7, waiting for transfers between devices, over_tp(): return lax.ppermute(x, 'tp', [(0, 1), (1, 0)])  20.6 us
    unnamed x20, local copies, waits for them, and re-layouts  10 us
    ppermute x7, starting transfers between devices, over_tp(): return lax.ppermute(x, 'tp', [(0, 1), (1, 0)])  5.56 us
    ppermute x2, starting transfers between devices, to_core(): lax.ppermute(x, 'ctx', [(c, c ^ 1) for c in range(ctx) if c % 2 != core])  4.68 us
  transfers between devices with their start and end apart: 37, of which 14 were waited for; matrix products, arithmetic and copies ran while one was open for 2% of the time, Pallas kernels for 13%

profile of v1, /device:TPU:13, one launch (start us, length us, event | category | flops | bytes accessed | tf_op | source)
XLA Modules:
  0.0 209.2 jit_solution(14479440452822899551)
XLA Ops:
  1.6 0.9 copy-done
  2.5 0.9 copy-done.1
  3.5 0.9 copy-done.2
  5.6 32.7 %all_to_all.5.x_ref = bf16[16,272,128]{2,1,0:T(8,128)(2,1)S(1)} all-to-all(bf16[16,272,128]{2,1,0:T(8,128)(2,1)S(1)} %shard_map.109), channel_id=1, replica_groups=mesh['groups'=1,'ctx'=16,'tp'=2,'sub'=1] {'ctx'}, dimensions={0} | all-to-all | bytes 2228224 | tf_op jit(solution)/shard_map/all_to_all | solution.py:228
  38.3 1.7 shard_map.110
  40.3 2.9 %collective-permute-start.2 = (bf16[512,128]{1,0:T(8,128)(2,1)S(1)}, bf16[512,128]{1,0:T(8,128)(2,1)S(1)}, u32[]{:S(2)}, u32[]{:S(2)}) collective-permute-start(bf16[512,128]{1,0:T(8,128)(2,1)S(1)} %get-tuple-element.25), channel_id=1, source_target_pairs={{0,16},{2,18},{4,20},{6,22},{8,24},{10,26},{12,28},{14,30},{16,0},... | collective-permute-start | bytes 393224 | tf_op jit(solution)/shard_map/ppermute | solution.py:210
  43.7 3.1 %collective-permute-start.20 = (bf16[512,128]{1,0:T(8,128)(2,1)S(1)}, bf16[512,128]{1,0:T(8,128)(2,1)S(1)}, u32[]{:S(2)}, u32[]{:S(2)}) collective-permute-start(bf16[512,128]{1,0:T(8,128)(2,1)S(1)} %get-tuple-element.35), channel_id=1, source_target_pairs={{0,16},{2,18},{4,20},{6,22},{8,24},{10,26},{12,28},{14,30},{16,0},... | collective-permute-start | bytes 393224 | tf_op jit(solution)/shard_map/ppermute | solution.py:210
  46.8 2.9 %collective-permute-done.3 = bf16[512,128]{1,0:T(8,128)(2,1)S(1)} collective-permute-done((bf16[512,128]{1,0:T(8,128)(2,1)S(1)}, bf16[512,128]{1,0:T(8,128)(2,1)S(1)}, u32[]{:S(2)}, u32[]{:S(2)}) %collective-permute-start.3) | collective-permute-done | bytes 131104 | tf_op jit(solution)/shard_map/ppermute | solution.py:210
  49.7 2.1 collective-permute-done.2
  51.9 1.1 collective-permute-start.4
  52.9 1.2 collective-permute-start.5
  54.2 7.5 %collective-permute-done.21 = bf16[512,128]{1,0:T(8,128)(2,1)S(1)} collective-permute-done((bf16[512,128]{1,0:T(8,128)(2,1)S(1)}, bf16[512,128]{1,0:T(8,128)(2,1)S(1)}, u32[]{:S(2)}, u32[]{:S(2)}) %collective-permute-start.21) | collective-permute-done | bytes 131104 | tf_op jit(solution)/shard_map/ppermute | solution.py:210
  62.6 1.1 collective-permute-start.22
  63.7 1.5 collective-permute-start.8
  65.3 1.2 collective-permute-start.23
  66.8 12.6 %collective-permute-done = bf16[2048]{0:T(1024)(128)(2,1)S(1)} collective-permute-done((bf16[2048]{0:T(1024)(128)(2,1)S(1)}, bf16[2048]{0:T(1024)(128)(2,1)S(1)}, u32[]{:S(2)}, u32[]{:S(2)}) %collective-permute-start) | collective-permute-done | bytes 4128 | tf_op jit(solution)/shard_map/ppermute | solution.py:213
  79.4 1.2 collective-permute-start.6
  80.6 1.7 collective-permute-start.9
  82.4 1.7 slice.17
  87.0 1.0 collective-permute-start.25
  88.0 5.3 %collective-permute-done.7.refs_4_ = bf16[2,512,128]{2,1,0:T(8,128)(2,1)} collective-permute-done((bf16[2,512,128]{2,1,0:T(8,128)(2,1)}, bf16[2,512,128]{2,1,0:T(8,128)(2,1)}, u32[]{:S(2)}, u32[]{:S(2)}) %collective-permute-start.7) | collective-permute-done | bytes 262176 | tf_op jit(solution)/shard_map/ppermute | solution.py:210
  93.3 2.2 %collective-permute-start.11 = (bf16[2,512,128]{2,1,0:T(8,128)(2,1)}, bf16[2,512,128]{2,1,0:T(8,128)(2,1)S(1)}, u32[]{:S(2)}, u32[]{:S(2)}) collective-permute-start(bf16[2,512,128]{2,1,0:T(8,128)(2,1)} %collective-permute-done.6.refs_3_), channel_id=1, source_target_pairs={{0,2},{2,0},{4,6},{6,4},{8,10},{10,8},{12,14},{14,12},{16,18},{18,... | collective-permute-start | bytes 786440 | tf_op jit(solution)/shard_map/ppermute | solution.py:210
  95.6 3.3 %collective-permute-done.25.refs_4_ = bf16[2,512,128]{2,1,0:T(8,128)(2,1)} collective-permute-done((bf16[2,512,128]{2,1,0:T(8,128)(2,1)}, bf16[2,512,128]{2,1,0:T(8,128)(2,1)}, u32[]{:S(2)}, u32[]{:S(2)}) %collective-permute-start.25) | collective-permute-done | bytes 262176 | tf_op jit(solution)/shard_map/ppermute | solution.py:210
  98.9 1.3 collective-permute-start.26
  101.3 2.2 %copy-done.4 = bf16[1,4096,512]{2,1,0:T(8,128)(2,1)S(1)} copy-done((bf16[1,4096,512]{2,1,0:T(8,128)(2,1)S(1)}, bf16[1,4096,512]{2,1,0:T(8,128)(2,1)}, u32[]{:S(2)}) %copy-start.4) | copy-done | bytes 4194328
  103.5 2.2 %copy-done.5 = bf16[1,4096,512]{2,1,0:T(8,128)(2,1)S(1)} copy-done((bf16[1,4096,512]{2,1,0:T(8,128)(2,1)S(1)}, bf16[1,4096,512]{2,1,0:T(8,128)(2,1)}, u32[]{:S(2)}) %copy-start.5) | copy-done | bytes 4194328
  105.7 1.0 copy-done.8
  106.8 8.9 %shard_map.111 = (bf16[512,512]{1,0:T(8,128)(2,1)S(1)}, bf16[64,2048]{1,0:T(8,128)(2,1)S(1)}) custom-call(s32[2]{0:T(128)S(1)} %pad_add_fusion.idx_ref, f32[2,2048]{1,0:T(2,128)S(1)} %maximum_convert_fusion.gain_ref, bf16[4096,512]{1,0:T(8,128)(2,1)S(1)} %bitcast.17, bf16[4096,512]{1,0:T(8,128)(2,1)S(1)} %bitcast.19, ...), custom_call_target="tpu_custom_call" | custom-call | flops 4294967296 | bytes 12582912 | tf_op jit(solution)/shard_map/pallas_call | solution.py:29
  116.0 8.5 %shard_map.115 = (bf16[512,512]{1,0:T(8,128)(2,1)S(1)}, bf16[64,2048]{1,0:T(8,128)(2,1)S(1)}) custom-call(s32[2]{0:T(128)S(1)} %pad_add_fusion.idx_ref, f32[2,2048]{1,0:T(2,128)S(1)} %maximum_convert_fusion.gain_ref, bf16[4096,512]{1,0:T(8,128)(2,1)S(1)} %bitcast.18, bf16[4096,512]{1,0:T(8,128)(2,1)S(1)} %bitcast.20, ...), custom_call_target="tpu_custom_call" | custom-call | flops 4294967296 | bytes 12582912 | tf_op jit(solution)/shard_map/pallas_call | solution.py:29
  124.5 1.1 collective-permute-start.31
  125.6 3.6 %collective-permute-done.13.peer_ref = bf16[512,512]{1,0:T(8,128)(2,1)S(1)} collective-permute-done((bf16[512,512]{1,0:T(8,128)(2,1)S(1)}, bf16[512,512]{1,0:T(8,128)(2,1)S(1)}, u32[]{:S(2)}, u32[]{:S(2)}) %collective-permute-start.13) | collective-permute-done | bytes 524320 | tf_op jit(solution)/shard_map/ppermute | solution.py:213
  129.2 3.4 %shard_map.112.own_ref = bf16[512,2048]{1,0:T(8,128)(2,1)S(1)} custom-call(s32[2]{0:T(128)S(1)} %pad_add_fusion.idx_ref, bf16[512,512]{1,0:T(8,128)(2,1)S(1)} %get-tuple-element.27.own_ref, bf16[512,512]{1,0:T(8,128)(2,1)S(1)} %collective-permute-done.13.peer_ref, bf16[1024,2048]{1,0:T(8,128)(2,1)S(1)} %bitcast.21), custom_call_target="tpu_custom_call" | custom-call | flops 2147483648 | bytes 6291456 | tf_op jit(solution)/shard_map/pallas_call | solution.py:29
  132.6 3.4 %collective-permute-start.14 = (bf16[512,2048]{1,0:T(8,128)(2,1)S(1)}, bf16[512,2048]{1,0:T(8,128)(2,1)S(1)}, u32[]{:S(2)}, u32[]{:S(2)}) collective-permute-start(bf16[512,2048]{1,0:T(8,128)(2,1)S(1)} %shard_map.112.own_ref), channel_id=1, source_target_pairs={{2,0},{6,4},{10,8},{14,12},{18,16},{22,20},{26,24},{30,28},{3,1},{... | collective-permute-start | bytes 6291464 | tf_op jit(solution)/shard_map/ppermute | solution.py:216
  136.0 4.4 %collective-permute-done.31.peer_ref = bf16[512,512]{1,0:T(8,128)(2,1)S(1)} collective-permute-done((bf16[512,512]{1,0:T(8,128)(2,1)S(1)}, bf16[512,512]{1,0:T(8,128)(2,1)S(1)}, u32[]{:S(2)}, u32[]{:S(2)}) %collective-permute-start.31) | collective-permute-done | bytes 524320 | tf_op jit(solution)/shard_map/ppermute | solution.py:213
  140.5 3.4 %shard_map.116.own_ref = bf16[512,2048]{1,0:T(8,128)(2,1)S(1)} custom-call(s32[2]{0:T(128)S(1)} %pad_add_fusion.idx_ref, bf16[512,512]{1,0:T(8,128)(2,1)S(1)} %get-tuple-element.37.own_ref, bf16[512,512]{1,0:T(8,128)(2,1)S(1)} %collective-permute-done.31.peer_ref, bf16[1024,2048]{1,0:T(8,128)(2,1)S(1)} %bitcast.22), custom_call_target="tpu_custom_call" | custom-call | flops 2147483648 | bytes 6291456 | tf_op jit(solution)/shard_map/pallas_call | solution.py:29
  143.8 1.3 collective-permute-start.32
  145.2 1.2 shard_map.113
  147.1 2.8 %collective-permute-done.32.other_ref = bf16[512,2048]{1,0:T(8,128)(2,1)S(1)} collective-permute-done((bf16[512,2048]{1,0:T(8,128)(2,1)S(1)}, bf16[512,2048]{1,0:T(8,128)(2,1)S(1)}, u32[]{:S(2)}, u32[]{:S(2)}) %collective-permute-start.32) | collective-permute-done | bytes 2097184 | tf_op jit(solution)/shard_map/ppermute | solution.py:216
  149.9 1.2 shard_map.117
  151.1 2.4 %collective-permute-start.33 = (bf16[4,64,2048]{2,1,0:T(8,128)(2,1)S(1)}, bf16[4,64,2048]{2,1,0:T(8,128)(2,1)S(1)}, u32[]{:S(2)}, u32[]{:S(2)}) collective-permute-start(bf16[4,64,2048]{2,1,0:T(8,128)(2,1)S(1)} %get-tuple-element.40), channel_id=1, source_target_pairs={{2,6},{6,2},{10,14},{14,10},{18,22},{22,18},{26,30},{30,26},{3,7},... | collective-permute-start | bytes 3145736 | tf_op jit(solution)/shard_map/ppermute | solution.py:210
  155.7 19.1 %collective-permute-done.33.got_ref = bf16[4,64,2048]{2,1,0:T(8,128)(2,1)S(1)} collective-permute-done((bf16[4,64,2048]{2,1,0:T(8,128)(2,1)S(1)}, bf16[4,64,2048]{2,1,0:T(8,128)(2,1)S(1)}, u32[]{:S(2)}, u32[]{:S(2)}) %collective-permute-start.33) | collective-permute-done | bytes 1048608 | tf_op jit(solution)/shard_map/ppermute | solution.py:210
  175.1 8.2 %collective-permute-start.34 = (bf16[64,2048]{1,0:T(8,128)(2,1)S(1)}, bf16[64,2048]{1,0:T(8,128)(2,1)S(1)}, u32[]{:S(2)}, u32[]{:S(2)}) collective-permute-start(bf16[64,2048]{1,0:T(8,128)(2,1)S(1)} %get-tuple-element.42), channel_id=1, source_target_pairs={{2,10},{6,14},{10,2},{14,6},{18,26},{22,30},{26,18},{30,22},{3,11}... | collective-permute-start | bytes 786440 | tf_op jit(solution)/shard_map/ppermute | solution.py:210
  183.2 1.9 collective-permute-start.35
  185.2 3.1 %collective-permute-start.36 = (bf16[64,2048]{1,0:T(8,128)(2,1)S(1)}, bf16[64,2048]{1,0:T(8,128)(2,1)S(1)}, u32[]{:S(2)}, u32[]{:S(2)}) collective-permute-start(bf16[64,2048]{1,0:T(8,128)(2,1)S(1)} %get-tuple-element.44), channel_id=1, source_target_pairs={{2,26},{6,30},{10,18},{14,22},{18,10},{22,14},{26,2},{30,6},{3,27}... | collective-permute-start | bytes 786440 | tf_op jit(solution)/shard_map/ppermute | solution.py:210
  188.3 1.4 collective-permute-done.34.refs_7_
  189.7 12.5 %collective-permute-done.35.refs_8_ = bf16[64,2048]{1,0:T(8,128)(2,1)S(1)} collective-permute-done((bf16[64,2048]{1,0:T(8,128)(2,1)S(1)}, bf16[64,2048]{1,0:T(8,128)(2,1)S(1)}, u32[]{:S(2)}, u32[]{:S(2)}) %collective-permute-start.35) | collective-permute-done | bytes 262176 | tf_op jit(solution)/shard_map/ppermute | solution.py:210
  202.2 5.6 %collective-permute-done.36.refs_9_ = bf16[64,2048]{1,0:T(8,128)(2,1)S(1)} collective-permute-done((bf16[64,2048]{1,0:T(8,128)(2,1)S(1)}, bf16[64,2048]{1,0:T(8,128)(2,1)S(1)}, u32[]{:S(2)}, u32[]{:S(2)}) %collective-permute-start.36) | collective-permute-done | bytes 262176 | tf_op jit(solution)/shard_map/ppermute | solution.py:210
  207.8 1.4 shard_map.119
  (75 shorter events, 12.5 us)
Async XLA Ops:
  1.6 1.0 copy-start
  2.5 0.9 copy-start.1
  3.5 0.9 copy-start.2
  4.4 0.9 copy-start.3
  38.3 28.2 %copy-start.9 = (bf16[2048]{0:T(1024)(128)(2,1)S(1)}, bf16[2048]{0:T(1024)(128)(2,1)}, u32[]{:S(2)}) copy-start(bf16[2048]{0:T(1024)(128)(2,1)} %param.15) | copy-start | bytes 12292
  40.0 9.7 %collective-permute-start.3 = (bf16[512,128]{1,0:T(8,128)(2,1)S(1)}, bf16[512,128]{1,0:T(8,128)(2,1)S(1)}, u32[]{:S(2)}, u32[]{:S(2)}) collective-permute-start(bf16[512,128]{1,0:T(8,128)(2,1)S(1)} %get-tuple-element.25), channel_id=1, source_target_pairs={{0,24},{2,26},{4,28},{6,30},{8,16},{10,18},{12,20},{14,22},{16,8},... | collective-permute-start | bytes 393224 | tf_op jit(solution)/shard_map/ppermute | solution.py:210
  40.3 11.5 %collective-permute-start.2 = (bf16[512,128]{1,0:T(8,128)(2,1)S(1)}, bf16[512,128]{1,0:T(8,128)(2,1)S(1)}, u32[]{:S(2)}, u32[]{:S(2)}) collective-permute-start(bf16[512,128]{1,0:T(8,128)(2,1)S(1)} %get-tuple-element.25), channel_id=1, source_target_pairs={{0,16},{2,18},{4,20},{6,22},{8,24},{10,26},{12,28},{14,30},{16,0},... | collective-permute-start | bytes 393224 | tf_op jit(solution)/shard_map/ppermute | solution.py:210
  43.2 8.5 %collective-permute-start.1 = (bf16[512,128]{1,0:T(8,128)(2,1)S(1)}, bf16[512,128]{1,0:T(8,128)(2,1)S(1)}, u32[]{:S(2)}, u32[]{:S(2)}) collective-permute-start(bf16[512,128]{1,0:T(8,128)(2,1)S(1)} %get-tuple-element.25), channel_id=1, source_target_pairs={{0,8},{2,10},{4,12},{6,14},{8,0},{10,2},{12,4},{14,6},{16,24},{18,... | collective-permute-start | bytes 393224 | tf_op jit(solution)/shard_map/ppermute | solution.py:210
  43.2 18.4 %collective-permute-start.21 = (bf16[512,128]{1,0:T(8,128)(2,1)S(1)}, bf16[512,128]{1,0:T(8,128)(2,1)S(1)}, u32[]{:S(2)}, u32[]{:S(2)}) collective-permute-start(bf16[512,128]{1,0:T(8,128)(2,1)S(1)} %get-tuple-element.35), channel_id=1, source_target_pairs={{0,24},{2,26},{4,28},{6,30},{8,16},{10,18},{12,20},{14,22},{16,8},... | collective-permute-start | bytes 393224 | tf_op jit(solution)/shard_map/ppermute | solution.py:210
  43.7 18.9 %collective-permute-start.20 = (bf16[512,128]{1,0:T(8,128)(2,1)S(1)}, bf16[512,128]{1,0:T(8,128)(2,1)S(1)}, u32[]{:S(2)}, u32[]{:S(2)}) collective-permute-start(bf16[512,128]{1,0:T(8,128)(2,1)S(1)} %get-tuple-element.35), channel_id=1, source_target_pairs={{0,16},{2,18},{4,20},{6,22},{8,24},{10,26},{12,28},{14,30},{16,0},... | collective-permute-start | bytes 393224 | tf_op jit(solution)/shard_map/ppermute | solution.py:210
  49.7 12.8 %collective-permute-start.19 = (bf16[512,128]{1,0:T(8,128)(2,1)S(1)}, bf16[512,128]{1,0:T(8,128)(2,1)S(1)}, u32[]{:S(2)}, u32[]{:S(2)}) collective-permute-start(bf16[512,128]{1,0:T(8,128)(2,1)S(1)} %get-tuple-element.35), channel_id=1, source_target_pairs={{0,8},{2,10},{4,12},{6,14},{8,0},{10,2},{12,4},{14,6},{16,24},{18,... | collective-permute-start | bytes 393224 | tf_op jit(solution)/shard_map/ppermute | solution.py:210
  51.9 14.6 %collective-permute-start.4 = (bf16[4,512,128]{2,1,0:T(8,128)(2,1)S(1)}, bf16[4,512,128]{2,1,0:T(8,128)(2,1)S(1)}, u32[]{:S(2)}, u32[]{:S(2)}) collective-permute-start(bf16[4,512,128]{2,1,0:T(8,128)(2,1)S(1)} %pad_maximum_fusion.refs_0_), channel_id=1, source_target_pairs={{0,4},{2,6},{4,0},{6,2},{8,12},{10,14},{12,8},{14,10},{16,20},{18,... | collective-permute-start | bytes 1572872 | tf_op jit(solution)/shard_map/ppermute | solution.py:210
  52.9 27.6 %collective-permute-start.5 = (bf16[4,512,128]{2,1,0:T(8,128)(2,1)S(1)}, bf16[4,512,128]{2,1,0:T(8,128)(2,1)}, u32[]{:S(2)}, u32[]{:S(2)}) collective-permute-start(bf16[4,512,128]{2,1,0:T(8,128)(2,1)S(1)} %pad_maximum_fusion.refs_0_), channel_id=1, source_target_pairs={{0,1},{1,0},{2,3},{3,2},{4,5},{5,4},{6,7},{7,6},{8,9},{9,8},{10,11... | collective-permute-start | bytes 1572872 | tf_op jit(solution)/shard_map/ppermute | solution.py:213
  62.6 19.7 %collective-permute-start.22 = (bf16[4,512,128]{2,1,0:T(8,128)(2,1)S(1)}, bf16[4,512,128]{2,1,0:T(8,128)(2,1)S(1)}, u32[]{:S(2)}, u32[]{:S(2)}) collective-permute-start(bf16[4,512,128]{2,1,0:T(8,128)(2,1)S(1)} %pad_maximum_fusion.1.refs_0_), channel_id=1, source_target_pairs={{0,4},{2,6},{4,0},{6,2},{8,12},{10,14},{12,8},{14,10},{16,20},{18,... | collective-permute-start | bytes 1572872 | tf_op jit(solution)/shard_map/ppermute | solution.py:210
  63.7 21.0 %collective-permute-start.8 = (bf16[4,512,128]{2,1,0:T(8,128)(2,1)S(1)}, bf16[4,512,128]{2,1,0:T(8,128)(2,1)S(1)}, u32[]{:S(2)}, u32[]{:S(2)}) collective-permute-start(bf16[4,512,128]{2,1,0:T(8,128)(2,1)S(1)} %pad_maximum_fusion.refs_0_), channel_id=1, source_target_pairs={{0,2},{2,0},{4,6},{6,4},{8,10},{10,8},{12,14},{14,12},{16,18},{18,... | collective-permute-start | bytes 1572872 | tf_op jit(solution)/shard_map/ppermute | solution.py:210
  65.3 20.7 %collective-permute-start.23 = (bf16[4,512,128]{2,1,0:T(8,128)(2,1)S(1)}, bf16[4,512,128]{2,1,0:T(8,128)(2,1)S(1)}, u32[]{:S(2)}, u32[]{:S(2)}) collective-permute-start(bf16[4,512,128]{2,1,0:T(8,128)(2,1)S(1)} %pad_maximum_fusion.1.refs_0_), channel_id=1, source_target_pairs={{0,1},{1,0},{2,3},{3,2},{4,5},{5,4},{6,7},{7,6},{8,9},{9,8},{10,11... | collective-permute-start | bytes 1572872 | tf_op jit(solution)/shard_map/ppermute | solution.py:213
  66.5 12.9 %collective-permute-start = (bf16[2048]{0:T(1024)(128)(2,1)S(1)}, bf16[2048]{0:T(1024)(128)(2,1)S(1)}, u32[]{:S(2)}, u32[]{:S(2)}) collective-permute-start(bf16[2048]{0:T(1024)(128)(2,1)S(1)} %copy-done.9), channel_id=1, source_target_pairs={{0,1},{1,0},{2,3},{3,2},{4,5},{5,4},{6,7},{7,6},{8,9},{9,8},{10,11... | collective-permute-start | bytes 12296 | tf_op jit(solution)/shard_map/ppermute | solution.py:213
  79.4 7.6 %collective-permute-start.6 = (bf16[2,512,128]{2,1,0:T(8,128)(2,1)S(1)}, bf16[2,512,128]{2,1,0:T(8,128)(2,1)}, u32[]{:S(2)}, u32[]{:S(2)}) collective-permute-start(bf16[2,512,128]{2,1,0:T(8,128)(2,1)S(1)} %slice.16), channel_id=1, source_target_pairs={{0,1},{1,0},{2,3},{3,2},{4,5},{5,4},{6,7},{7,6},{8,9},{9,8},{10,11... | collective-permute-start | bytes 786440 | tf_op jit(solution)/shard_map/ppermute | solution.py:213
  80.6 19.6 %collective-permute-start.9 = (bf16[4,512,128]{2,1,0:T(8,128)(2,1)S(1)}, bf16[4,512,128]{2,1,0:T(8,128)(2,1)}, u32[]{:S(2)}, u32[]{:S(2)}) collective-permute-start(bf16[4,512,128]{2,1,0:T(8,128)(2,1)S(1)} %collective-permute-done.4.refs_1_), channel_id=1, source_target_pairs={{0,2},{2,0},{4,6},{6,4},{8,10},{10,8},{12,14},{14,12},{16,18},{18,... | collective-permute-start | bytes 1572872 | tf_op jit(solution)/shard_map/ppermute | solution.py:210
  82.3 17.9 %collective-permute-start.10 = (bf16[4,512,128]{2,1,0:T(8,128)(2,1)}, bf16[4,512,128]{2,1,0:T(8,128)(2,1)}, u32[]{:S(2)}, u32[]{:S(2)}) collective-permute-start(bf16[4,512,128]{2,1,0:T(8,128)(2,1)} %collective-permute-done.5.refs_2_), channel_id=1, source_target_pairs={{0,2},{2,0},{4,6},{6,4},{8,10},{10,8},{12,14},{14,12},{16,18},{18,... | collective-permute-start | bytes 1572872 | tf_op jit(solution)/shard_map/ppermute | solution.py:210
  84.8 0.8 copy-start.7
  85.6 7.8 %collective-permute-start.7 = (bf16[2,512,128]{2,1,0:T(8,128)(2,1)}, bf16[2,512,128]{2,1,0:T(8,128)(2,1)}, u32[]{:S(2)}, u32[]{:S(2)}) collective-permute-start(bf16[2,512,128]{2,1,0:T(8,128)(2,1)} %slice.17), channel_id=1, source_target_pairs={{0,4},{2,6},{4,0},{6,2},{8,12},{10,14},{12,8},{14,10},{16,20},{18,... | collective-permute-start | bytes 786440 | tf_op jit(solution)/shard_map/ppermute | solution.py:210
  86.0 9.5 %collective-permute-start.24 = (bf16[2,512,128]{2,1,0:T(8,128)(2,1)}, bf16[2,512,128]{2,1,0:T(8,128)(2,1)S(1)}, u32[]{:S(2)}, u32[]{:S(2)}) collective-permute-start(bf16[2,512,128]{2,1,0:T(8,128)(2,1)} %slice.18), channel_id=1, source_target_pairs={{0,1},{1,0},{2,3},{3,2},{4,5},{5,4},{6,7},{7,6},{8,9},{9,8},{10,11... | collective-permute-start | bytes 786440 | tf_op jit(solution)/shard_map/ppermute | solution.py:213
  87.0 11.9 %collective-permute-start.25 = (bf16[2,512,128]{2,1,0:T(8,128)(2,1)}, bf16[2,512,128]{2,1,0:T(8,128)(2,1)}, u32[]{:S(2)}, u32[]{:S(2)}) collective-permute-start(bf16[2,512,128]{2,1,0:T(8,128)(2,1)} %slice.19), channel_id=1, source_target_pairs={{0,4},{2,6},{4,0},{6,2},{8,12},{10,14},{12,8},{14,10},{16,20},{18,... | collective-permute-start | bytes 786440 | tf_op jit(solution)/shard_map/ppermute | solution.py:210
  93.3 7.4 %collective-permute-start.11 = (bf16[2,512,128]{2,1,0:T(8,128)(2,1)}, bf16[2,512,128]{2,1,0:T(8,128)(2,1)S(1)}, u32[]{:S(2)}, u32[]{:S(2)}) collective-permute-start(bf16[2,512,128]{2,1,0:T(8,128)(2,1)} %collective-permute-done.6.refs_3_), channel_id=1, source_target_pairs={{0,2},{2,0},{4,6},{6,4},{8,10},{10,8},{12,14},{14,12},{16,18},{18,... | collective-permute-start | bytes 786440 | tf_op jit(solution)/shard_map/ppermute | solution.py:210
  95.5 5.4 %collective-permute-start.12 = (bf16[2,512,128]{2,1,0:T(8,128)(2,1)}, bf16[2,512,128]{2,1,0:T(8,128)(2,1)S(1)}, u32[]{:S(2)}, u32[]{:S(2)}) collective-permute-start(bf16[2,512,128]{2,1,0:T(8,128)(2,1)} %collective-permute-done.7.refs_4_), channel_id=1, source_target_pairs={{0,2},{2,0},{4,6},{6,4},{8,10},{10,8},{12,14},{14,12},{16,18},{18,... | collective-permute-start | bytes 786440 | tf_op jit(solution)/shard_map/ppermute | solution.py:210
  98.9 16.7 %collective-permute-start.26 = (bf16[4,512,128]{2,1,0:T(8,128)(2,1)S(1)}, bf16[4,512,128]{2,1,0:T(8,128)(2,1)S(1)}, u32[]{:S(2)}, u32[]{:S(2)}) collective-permute-start(bf16[4,512,128]{2,1,0:T(8,128)(2,1)S(1)} %pad_maximum_fusion.1.refs_0_), channel_id=1, source_target_pairs={{0,2},{2,0},{4,6},{6,4},{8,10},{10,8},{12,14},{14,12},{16,18},{18,... | collective-permute-start | bytes 1572872 | tf_op jit(solution)/shard_map/ppermute | solution.py:210
  100.2 15.8 %collective-permute-start.27 = (bf16[4,512,128]{2,1,0:T(8,128)(2,1)S(1)}, bf16[4,512,128]{2,1,0:T(8,128)(2,1)S(1)}, u32[]{:S(2)}, u32[]{:S(2)}) collective-permute-start(bf16[4,512,128]{2,1,0:T(8,128)(2,1)S(1)} %collective-permute-done.22.refs_1_), channel_id=1, source_target_pairs={{0,2},{2,0},{4,6},{6,4},{8,10},{10,8},{12,14},{14,12},{16,18},{18,... | collective-permute-start | bytes 1572872 | tf_op jit(solution)/shard_map/ppermute | solution.py:210
  100.2 15.8 %collective-permute-start.28 = (bf16[4,512,128]{2,1,0:T(8,128)(2,1)S(1)}, bf16[4,512,128]{2,1,0:T(8,128)(2,1)S(1)}, u32[]{:S(2)}, u32[]{:S(2)}) collective-permute-start(bf16[4,512,128]{2,1,0:T(8,128)(2,1)S(1)} %collective-permute-done.23.refs_2_), channel_id=1, source_target_pairs={{0,2},{2,0},{4,6},{6,4},{8,10},{10,8},{12,14},{14,12},{16,18},{18,... | collective-permute-start | bytes 1572872 | tf_op jit(solution)/shard_map/ppermute | solution.py:210
  100.8 15.2 %collective-permute-start.29 = (bf16[2,512,128]{2,1,0:T(8,128)(2,1)S(1)}, bf16[2,512,128]{2,1,0:T(8,128)(2,1)S(1)}, u32[]{:S(2)}, u32[]{:S(2)}) collective-permute-start(bf16[2,512,128]{2,1,0:T(8,128)(2,1)S(1)} %collective-permute-done.24.refs_3_), channel_id=1, source_target_pairs={{0,2},{2,0},{4,6},{6,4},{8,10},{10,8},{12,14},{14,12},{16,18},{18,... | collective-permute-start | bytes 786440 | tf_op jit(solution)/shard_map/ppermute | solution.py:210
  100.9 15.1 %collective-permute-start.30 = (bf16[2,512,128]{2,1,0:T(8,128)(2,1)}, bf16[2,512,128]{2,1,0:T(8,128)(2,1)S(1)}, u32[]{:S(2)}, u32[]{:S(2)}) collective-permute-start(bf16[2,512,128]{2,1,0:T(8,128)(2,1)} %collective-permute-done.25.refs_4_), channel_id=1, source_target_pairs={{0,2},{2,0},{4,6},{6,4},{8,10},{10,8},{12,14},{14,12},{16,18},{18,... | collective-permute-start | bytes 786440 | tf_op jit(solution)/shard_map/ppermute | solution.py:210
  101.3 2.2 %copy-start.4 = (bf16[1,4096,512]{2,1,0:T(8,128)(2,1)S(1)}, bf16[1,4096,512]{2,1,0:T(8,128)(2,1)}, u32[]{:S(2)}) copy-start(bf16[1,4096,512]{2,1,0:T(8,128)(2,1)} %param.19) | copy-start | bytes 12582916
  103.5 2.2 %copy-start.5 = (bf16[1,4096,512]{2,1,0:T(8,128)(2,1)S(1)}, bf16[1,4096,512]{2,1,0:T(8,128)(2,1)}, u32[]{:S(2)}) copy-start(bf16[1,4096,512]{2,1,0:T(8,128)(2,1)} %param.20) | copy-start | bytes 12582916
  105.7 1.0 copy-start.8
  115.7 13.6 %copy-start.6 = (bf16[1,1024,2048]{2,1,0:T(8,128)(2,1)S(1)}, bf16[1,1024,2048]{2,1,0:T(8,128)(2,1)}, u32[]{:S(2)}) copy-start(bf16[1,1024,2048]{2,1,0:T(8,128)(2,1)} %param.21) | copy-start | bytes 12582916
  115.7 13.6 %collective-permute-start.13 = (bf16[512,512]{1,0:T(8,128)(2,1)S(1)}, bf16[512,512]{1,0:T(8,128)(2,1)S(1)}, u32[]{:S(2)}, u32[]{:S(2)}) collective-permute-start(bf16[512,512]{1,0:T(8,128)(2,1)S(1)} %get-tuple-element.27.own_ref), channel_id=1, source_target_pairs={{0,1},{1,0},{2,3},{3,2},{4,5},{5,4},{6,7},{7,6},{8,9},{9,8},{10,11... | collective-permute-start | bytes 1572872 | tf_op jit(solution)/shard_map/ppermute | solution.py:213
  124.5 15.9 %collective-permute-start.31 = (bf16[512,512]{1,0:T(8,128)(2,1)S(1)}, bf16[512,512]{1,0:T(8,128)(2,1)S(1)}, u32[]{:S(2)}, u32[]{:S(2)}) collective-permute-start(bf16[512,512]{1,0:T(8,128)(2,1)S(1)} %get-tuple-element.37.own_ref), channel_id=1, source_target_pairs={{0,1},{1,0},{2,3},{3,2},{4,5},{5,4},{6,7},{7,6},{8,9},{9,8},{10,11... | collective-permute-start | bytes 1572872 | tf_op jit(solution)/shard_map/ppermute | solution.py:213
  132.6 12.5 %collective-permute-start.14 = (bf16[512,2048]{1,0:T(8,128)(2,1)S(1)}, bf16[512,2048]{1,0:T(8,128)(2,1)S(1)}, u32[]{:S(2)}, u32[]{:S(2)}) collective-permute-start(bf16[512,2048]{1,0:T(8,128)(2,1)S(1)} %shard_map.112.own_ref), channel_id=1, source_target_pairs={{2,0},{6,4},{10,8},{14,12},{18,16},{22,20},{26,24},{30,28},{3,1},{... | collective-permute-start | bytes 6291464 | tf_op jit(solution)/shard_map/ppermute | solution.py:216
  143.8 6.1 %collective-permute-start.32 = (bf16[512,2048]{1,0:T(8,128)(2,1)S(1)}, bf16[512,2048]{1,0:T(8,128)(2,1)S(1)}, u32[]{:S(2)}, u32[]{:S(2)}) collective-permute-start(bf16[512,2048]{1,0:T(8,128)(2,1)S(1)} %shard_map.116.own_ref), channel_id=1, source_target_pairs={{0,2},{4,6},{8,10},{12,14},{16,18},{20,22},{24,26},{28,30},{1,3},{... | collective-permute-start | bytes 6291464 | tf_op jit(solution)/shard_map/ppermute | solution.py:216
  146.3 7.1 %collective-permute-start.15 = (bf16[4,64,2048]{2,1,0:T(8,128)(2,1)S(1)}, bf16[4,64,2048]{2,1,0:T(8,128)(2,1)S(1)}, u32[]{:S(2)}, u32[]{:S(2)}) collective-permute-start(bf16[4,64,2048]{2,1,0:T(8,128)(2,1)S(1)} %get-tuple-element.30), channel_id=1, source_target_pairs={{0,4},{4,0},{8,12},{12,8},{16,20},{20,16},{24,28},{28,24},{1,5},{5... | collective-permute-start | bytes 3145736 | tf_op jit(solution)/shard_map/ppermute | solution.py:210
  151.1 23.8 %collective-permute-start.33 = (bf16[4,64,2048]{2,1,0:T(8,128)(2,1)S(1)}, bf16[4,64,2048]{2,1,0:T(8,128)(2,1)S(1)}, u32[]{:S(2)}, u32[]{:S(2)}) collective-permute-start(bf16[4,64,2048]{2,1,0:T(8,128)(2,1)S(1)} %get-tuple-element.40), channel_id=1, source_target_pairs={{2,6},{6,2},{10,14},{14,10},{18,22},{22,18},{26,30},{30,26},{3,7},... | collective-permute-start | bytes 3145736 | tf_op jit(solution)/shard_map/ppermute | solution.py:210
  153.7 31.5 %collective-permute-start.16 = (bf16[64,2048]{1,0:T(8,128)(2,1)S(1)}, bf16[64,2048]{1,0:T(8,128)(2,1)S(1)}, u32[]{:S(2)}, u32[]{:S(2)}) collective-permute-start(bf16[64,2048]{1,0:T(8,128)(2,1)S(1)} %get-tuple-element.32), channel_id=1, source_target_pairs={{0,8},{4,12},{8,0},{12,4},{16,24},{20,28},{24,16},{28,20},{1,9},{5... | collective-permute-start | bytes 786440 | tf_op jit(solution)/shard_map/ppermute | solution.py:210
  154.3 33.9 %collective-permute-start.17 = (bf16[64,2048]{1,0:T(8,128)(2,1)S(1)}, bf16[64,2048]{1,0:T(8,128)(2,1)S(1)}, u32[]{:S(2)}, u32[]{:S(2)}) collective-permute-start(bf16[64,2048]{1,0:T(8,128)(2,1)S(1)} %get-tuple-element.33), channel_id=1, source_target_pairs={{0,16},{4,20},{8,24},{12,28},{16,0},{20,4},{24,8},{28,12},{1,17},{... | collective-permute-start | bytes 786440 | tf_op jit(solution)/shard_map/ppermute | solution.py:210
  155.0 33.3 %collective-permute-start.18 = (bf16[64,2048]{1,0:T(8,128)(2,1)S(1)}, bf16[64,2048]{1,0:T(8,128)(2,1)S(1)}, u32[]{:S(2)}, u32[]{:S(2)}) collective-permute-start(bf16[64,2048]{1,0:T(8,128)(2,1)S(1)} %get-tuple-element.34), channel_id=1, source_target_pairs={{0,24},{4,28},{8,16},{12,20},{16,8},{20,12},{24,0},{28,4},{1,25},{... | collective-permute-start | bytes 786440 | tf_op jit(solution)/shard_map/ppermute | solution.py:210
  175.1 14.6 %collective-permute-start.34 = (bf16[64,2048]{1,0:T(8,128)(2,1)S(1)}, bf16[64,2048]{1,0:T(8,128)(2,1)S(1)}, u32[]{:S(2)}, u32[]{:S(2)}) collective-permute-start(bf16[64,2048]{1,0:T(8,128)(2,1)S(1)} %get-tuple-element.42), channel_id=1, source_target_pairs={{2,10},{6,14},{10,2},{14,6},{18,26},{22,30},{26,18},{30,22},{3,11}... | collective-permute-start | bytes 786440 | tf_op jit(solution)/shard_map/ppermute | solution.py:210
  183.2 19.0 %collective-permute-start.35 = (bf16[64,2048]{1,0:T(8,128)(2,1)S(1)}, bf16[64,2048]{1,0:T(8,128)(2,1)S(1)}, u32[]{:S(2)}, u32[]{:S(2)}) collective-permute-start(bf16[64,2048]{1,0:T(8,128)(2,1)S(1)} %get-tuple-element.43), channel_id=1, source_target_pairs={{2,18},{6,22},{10,26},{14,30},{18,2},{22,6},{26,10},{30,14},{3,19}... | collective-permute-start | bytes 786440 | tf_op jit(solution)/shard_map/ppermute | solution.py:210
  185.2 22.6 %collective-permute-start.36 = (bf16[64,2048]{1,0:T(8,128)(2,1)S(1)}, bf16[64,2048]{1,0:T(8,128)(2,1)S(1)}, u32[]{:S(2)}, u32[]{:S(2)}) collective-permute-start(bf16[64,2048]{1,0:T(8,128)(2,1)S(1)} %get-tuple-element.44), channel_id=1, source_target_pairs={{2,26},{6,30},{10,18},{14,22},{18,10},{22,14},{26,2},{30,6},{3,27}... | collective-permute-start | bytes 786440 | tf_op jit(solution)/shard_map/ppermute | solution.py:210

commit v2 on v1

--- a/solution.py
+++ b/solution.py
@@ -21,15 +21,14 @@
     return v * (0.5 * jnp.tanh(0.5 * v) + 0.5)
 
 
-def call(kernel, out_shape, args, smem=0, scratch=(), vmem=24, flops=0, moved=0):
-    specs = [pl.BlockSpec(memory_space=pltpu.SMEM)] * smem
-    specs += [pl.BlockSpec(memory_space=pltpu.VMEM)] * (len(args) - smem)
+def call(kernel, out_shape, args, smem=0, hbm=(), scratch=(), vmem=16, flops=0, moved=0):
+    spaces = [pltpu.SMEM if n < smem else pl.ANY if n in hbm else pltpu.VMEM for n in range(len(args))]
     several = isinstance(out_shape, (tuple, list))
     out = pl.BlockSpec(memory_space=pltpu.VMEM)
     return pl.pallas_call(
         kernel,
         out_shape=out_shape,
-        in_specs=specs,
+        in_specs=[pl.BlockSpec(memory_space=space) for space in spaces],
         out_specs=tuple(out for _ in out_shape) if several else out,
         scratch_shapes=list(scratch),
         compiler_params=pltpu.CompilerParams(vmem_limit_bytes=vmem * MIB),
@@ -37,47 +36,86 @@
     )(*args)
 
 
-def pack_kernel(q_ref, k_ref, v_ref, r_ref, seg_ref, gate_ref, out_ref):
+def pack_kernel(seg_ref, route_ref, gate_ref, q_ref, k_ref, v_ref, r_ref, out_ref, held_ref, sems):
     heads, tok = out_ref.shape[0], q_ref.shape[0]
-    row = lax.broadcasted_iota(jnp.int32, (META, LANES), 0)
-    seg = jnp.broadcast_to(seg_ref[...], (META, LANES))
-    for h in range(heads):
-        cols = slice(h * HD, (h + 1) * HD)
-        for n, ref in enumerate((q_ref, k_ref, v_ref, r_ref)):
-            out_ref[h, n * tok : (n + 1) * tok, :] = ref[:, cols]
-        gate = jnp.broadcast_to(gate_ref[h : h + 1, :], (META, LANES))
+    copies = [pltpu.make_async_copy(ref, held_ref.at[n], sems.at[n]) for n, ref in enumerate((q_ref, k_ref, v_ref, r_ref))]
+    for copy in copies:
+        copy.start()
+    row = lax.broadcasted_iota(jnp.int32, (META, tok), 0)
+    seg = jnp.broadcast_to(seg_ref[...].astype(jnp.float32), (META, tok))
+    parts = []
+    for e in range(heads // 2):
+        gate = jnp.sum(jnp.where(route_ref[...] == e, gate_ref[...], 0.0), axis=0, keepdims=True)
+        gate = jnp.broadcast_to(gate, (META, tok))
         high = gate.astype(jnp.bfloat16).astype(jnp.float32)
         middle = (gate - high).astype(jnp.bfloat16).astype(jnp.float32)
-        low = gate - high - middle
-        meta = jnp.where(
-            row == 0, seg, jnp.where(row == 1, high, jnp.where(row == 2, middle, jnp.where(row == 3, low, 0.0)))
-        )
-        out_ref[h, 4 * tok : 4 * tok + META, :] = meta.astype(jnp.bfloat16)
-
-
-def attend_kernel(x_ref, even_ref, odd_ref, gate_even_ref, gate_odd_ref):
+        parts.append((high, middle, gate - high - middle))
+    out_ref[:, 4 * tok :, :] = jnp.zeros((heads, META, HD), jnp.bfloat16)
+    for h in range(heads):
+        meta = jnp.where(row == 0, seg, 0.0)
+        for n, piece in enumerate(parts[h // 2] + parts[h // 2 ^ 1], 1):
+            meta = jnp.where(row == n, piece, meta)
+        out_ref[h, 4 * tok :, 0:tok] = meta.astype(jnp.bfloat16)
+    for n, copy in enumerate(copies):
+        copy.wait()
+        for h in range(heads):
+            out_ref[h, n * tok : (n + 1) * tok, :] = held_ref[n, :, h * HD : (h + 1) * HD]
+
+
+def attend_kernel(capacity, x_ref, even_ref, odd_ref, pick_even_ref, pick_odd_ref, gate_even_ref, gate_odd_ref):
     blocks = x_ref.shape[0]
     tok = LANES // 2
+    levels = blocks // 4
     scale = 1.0 / math.sqrt(HD)
     lane = lax.broadcasted_iota(jnp.int32, (META, LANES), 1)
     row_at = lax.broadcasted_iota(jnp.int32, (LANES, LANES), 0)
     lane_at = lax.broadcasted_iota(jnp.int32, (LANES, LANES), 1)
     causal = lane_at <= row_at
+    span = levels * tok
+    slots = levels * capacity
+    earlier_at = lax.broadcasted_iota(jnp.int32, (span, span), 0)
+    later_at = lax.broadcasted_iota(jnp.int32, (span, span), 1)
+    earlier = jnp.logical_and(earlier_at < later_at, earlier_at // tok == later_at // tok)
+    earlier = earlier.astype(jnp.float32).astype(jnp.bfloat16)
+    slot_at = lax.broadcasted_iota(jnp.int32, (slots, span), 0).astype(jnp.float32)
+    base = (lax.broadcasted_iota(jnp.int32, (1, span), 1) // tok * capacity).astype(jnp.float32)
 
     def part(n, first, last):
         return x_ref[first:last, n * tok : (n + 1) * tok, :].reshape((last - first) * tok, HD)
 
+    def scalars(first, second):
+        left = x_ref[first, 4 * tok :, :].astype(jnp.float32)
+        right = pltpu.roll(x_ref[second, 4 * tok :, :].astype(jnp.float32), tok, 1)
+        return jnp.where(lane < tok, left, right)
+
+    def gate_of(meta, which):
+        first = 1 + 3 * which
+        return meta[first : first + 1, :] + (meta[first + 1 : first + 2, :] + meta[first + 2 : first + 3, :])
+
+    def down_rows(row):
+        return jnp.transpose(jnp.broadcast_to(row, (LANES, LANES)))
+
+    for y in range(2):
+        for odd, (pick_ref, gate_ref) in enumerate(((pick_even_ref, gate_even_ref), (pick_odd_ref, gate_odd_ref))):
+            metas = [scalars(4 * z + 2 * y + odd, 4 * z + 4 + 2 * y + odd) for z in range(0, levels, 2)]
+            for which in range(2):
+                rows = [gate_of(meta, which) for meta in metas]
+                for n, row in enumerate(rows):
+                    gate_ref[which, y * span + n * LANES : y * span + (n + 1) * LANES, :] = down_rows(row)
+                named = (jnp.concatenate(rows, axis=1) > 0.0).astype(jnp.float32)
+                rank = jnp.dot(
+                    jnp.broadcast_to(named, (META, span)).astype(jnp.bfloat16),
+                    earlier,
+                    preferred_element_type=jnp.float32,
+                )[0:1, :]
+                target = jnp.broadcast_to(jnp.where(named > 0.0, base + rank, -1.0), (slots, span))
+                pick = (slot_at == target).astype(jnp.float32).astype(jnp.bfloat16)
+                pick_ref[which, y * slots : (y + 1) * slots, :] = pick
+
     seg_rows = []
     for i in range(blocks // 2):
-        meta = jnp.where(
-            lane < tok,
-            x_ref[2 * i, 4 * tok : 4 * tok + META, :].astype(jnp.float32),
-            x_ref[2 * i + 1, 4 * tok : 4 * tok + META, :].astype(jnp.float32),
-        )
-        seg_rows.append(meta[0:1, :])
-        seg_col = jnp.transpose(jnp.broadcast_to(meta[0:1, :], (LANES, LANES)))
-        gate_row = meta[1:2, :] + (meta[2:3, :] + meta[3:4, :])
-        gate_col = jnp.transpose(jnp.broadcast_to(gate_row, (LANES, LANES)))
+        seg_rows.append(scalars(2 * i, 2 * i + 1)[0:1, :])
+        seg_col = down_rows(seg_rows[i])
         masks = []
         for j in range(i + 1):
             same = seg_col == jnp.broadcast_to(seg_rows[j], (LANES, LANES))
@@ -95,25 +133,49 @@
         summed = jnp.dot(weights, values, preferred_element_type=jnp.float32)
         counted = jnp.sum(visible, axis=1, keepdims=True)
         hand = (part(3, 2 * i, 2 * i + 2).astype(jnp.float32) + summed / jnp.sqrt(counted)).astype(jnp.bfloat16)
-        here = slice(i * tok, (i + 1) * tok)
-        even_ref[here, :] = hand[:tok, :]
-        odd_ref[here, :] = hand[tok:, :]
-        gate_even_ref[here, :] = gate_col[:tok, :]
-        gate_odd_ref[here, :] = gate_col[tok:, :]
-
-
-def gate_up_kernel(places, heads, idx_ref, gain_ref, wg_ref, wu_ref, *refs):
-    pieces, (hidden_ref, hand_ref, lhs_ref) = refs[: len(places)], refs[len(places) :]
+        at = (i % 2 * levels + i // 2) * tok
+        even_ref[at : at + tok, :] = hand[:tok, :]
+        odd_ref[at : at + tok, :] = hand[tok:, :]
+
+
+def compact_kernel(idx_ref, pick_ref, *refs):
+    pieces, (mine_ref, theirs_ref) = refs[:-2], refs[-2:]
+    me = idx_ref[0]
+    levels = len(pieces)
+    slots, span = pick_ref.shape[1] // 2, pick_ref.shape[2]
+    tok = span // levels
+    z, y = lax.div(me, 4), lax.rem(lax.div(me, 2), 2)
+    for group in range(2):
+        block = jnp.concatenate([p[group * span : (group + 1) * span, :] for p in pieces], axis=1)
+        for which, out_ref in enumerate((mine_ref, theirs_ref)):
+            here = slice(group * slots, (group + 1) * slots)
+            rows = jnp.dot(pick_ref[which, here, :], block, preferred_element_type=jnp.float32).astype(jnp.bfloat16)
+            for k in range(levels):
+                out_ref[k, here, :] = rows[:, k * HD : (k + 1) * HD]
+    for which, out_ref in enumerate((mine_ref, theirs_ref)):
+        own = pl.ds(pl.multiple_of(((y ^ which) * levels + z) * tok, tok), tok)
+        for k in range(levels):
+            out_ref[k, 2 * slots :, :] = pieces[k][own, :]
+
+
+def gate_up_kernel(places, heads, idx_ref, wg_ref, wu_ref, gain_ref, *refs):
+    pieces, (hidden_ref, hand_ref, lhs_ref, wg_held, wu_held, sems) = refs[: len(places)], refs[len(places) :]
     me, plane = idx_ref[0], idx_ref[1]
-    rows = pieces[0].shape[1]
-    tok = hand_ref.shape[0]
-    tile = min(rows, 128)
-    mine = pl.multiple_of(lax.div(me, 2) * tok, tok)
+    rows, tok = hidden_ref.shape[0], hand_ref.shape[0]
+    width = min(256, wg_ref.shape[1])
+    steps = wg_ref.shape[1] // width
+    copies = []
+    for n in range(steps):
+        cols = slice(n * width, (n + 1) * width)
+        for m, (ref, held) in enumerate(((wg_ref, wg_held), (wu_ref, wu_held))):
+            copies.append(pltpu.make_async_copy(ref.at[:, cols], held.at[:, cols], sems.at[2 * n + m]))
+            copies[-1].start()
+    tile = rows // 2
     for ref, entries in zip(pieces, places):
         for k, (other, mask) in enumerate(entries):
             if not other:
                 at = pl.multiple_of((me ^ mask) * HD, HD)
-                hand_ref[:, pl.ds(at, HD)] = ref[k, pl.ds(mine, tok), :]
+                hand_ref[:, pl.ds(at, HD)] = ref[k, rows : rows + tok, :]
 
     def normalise(r, carry):
         here = pl.ds(pl.multiple_of(r * tile, tile), tile)
@@ -133,52 +195,75 @@
         return carry
 
     lax.fori_loop(0, rows // tile, normalise, 0)
-    width = min(256, wg_ref.shape[1])
-
-    def project(n, carry):
-        cols = pl.ds(pl.multiple_of(n * width, width), width)
-        gate = jnp.dot(lhs_ref[...], wg_ref[:, cols], preferred_element_type=jnp.float32)
-        up = jnp.dot(lhs_ref[...], wu_ref[:, cols], preferred_element_type=jnp.float32)
+    for n in range(steps):
+        cols = slice(n * width, (n + 1) * width)
+        copies[2 * n].wait()
+        gate = jnp.dot(lhs_ref[...], wg_held[:, cols], preferred_element_type=jnp.float32)
+        copies[2 * n + 1].wait()
+        up = jnp.dot(lhs_ref[...], wu_held[:, cols], preferred_element_type=jnp.float32)
         hidden_ref[:, cols] = (silu(gate) * up).astype(jnp.bfloat16)
-        return carry
-
-    lax.fori_loop(0, wg_ref.shape[1] // width, project, 0)
-
-
-def down_kernel(idx_ref, own_ref, peer_ref, wd_ref, out_ref):
+
+
+def down_kernel(idx_ref, wd_ref, own_ref, peer_ref, out_ref, wd_held, sems):
     plane = idx_ref[1]
     depth = own_ref.shape[1]
     width = min(512, wd_ref.shape[1])
+    steps = wd_ref.shape[1] // width
+    copies = []
+    for n in range(steps):
+        cols = slice(n * width, (n + 1) * width)
+        copies.append(pltpu.make_async_copy(wd_ref.at[:, cols], wd_held.at[:, cols], sems.at[n]))
+        copies[-1].start()
     own_rows = pl.ds(pl.multiple_of(plane * depth, depth), depth)
     peer_rows = pl.ds(pl.multiple_of((1 - plane) * depth, depth), depth)
-
-    def project(n, carry):
-        cols = pl.ds(pl.multiple_of(n * width, width), width)
-        total = jnp.dot(own_ref[...], wd_ref[own_rows, cols], preferred_element_type=jnp.float32)
-        total = total + jnp.dot(peer_ref[...], wd_ref[peer_rows, cols], preferred_element_type=jnp.float32)
+    for n in range(steps):
+        cols = slice(n * width, (n + 1) * width)
+        copies[n].wait()
+        total = jnp.dot(own_ref[...], wd_held[own_rows, cols], preferred_element_type=jnp.float32)
+        total = total + jnp.dot(peer_ref[...], wd_held[peer_rows, cols], preferred_element_type=jnp.float32)
         out_ref[:, cols] = total.astype(jnp.bfloat16)
-        return carry
-
-    lax.fori_loop(0, wd_ref.shape[1] // width, project, 0)
-
-
-def weigh_kernel(idx_ref, own_ref, other_ref, gate_ref, send_ref, keep_ref):
-    pair = lax.div(idx_ref[0], 2)
-    count, tok, width = send_ref.shape
-    for k in range(count):
-        for flip, out_ref in ((1, send_ref), (0, keep_ref)):
-            here = pl.ds(pl.multiple_of((pair ^ (2 * k + flip)) * tok, tok), tok)
-            gate = gate_ref[here, :]
-            for n in range(width // LANES):
-                cols = slice(n * LANES, (n + 1) * LANES)
-                both = own_ref[here, cols].astype(jnp.float32) + other_ref[here, cols].astype(jnp.float32)
-                out_ref[k, :, cols] = (both * gate).astype(out_ref.dtype)
-
-
-def add_kernel(keep_ref, got_ref, own_ref, *send_refs):
-    own_ref[...] = keep_ref[0] + got_ref[0].astype(jnp.float32)
+
+
+def pair_kernel(idx_ref, own_ref, other_ref, send_ref):
+    slots = send_ref.shape[0]
+    y = lax.rem(lax.div(idx_ref[0], 2), 2)
+    theirs = pl.ds(pl.multiple_of((1 - y) * slots, slots), slots)
+    both = own_ref[theirs, :].astype(jnp.float32) + other_ref[theirs, :].astype(jnp.float32)
+    send_ref[...] = both.astype(jnp.bfloat16)
+
+
+def spread(pick, rows):
+    return lax.dot_general(pick, rows, (((0,), (0,)), ((), ())), preferred_element_type=jnp.float32)
+
+
+def weigh_kernel(idx_ref, pick_ref, gate_ref, own_ref, other_ref, keep_ref):
+    slots, span = pick_ref.shape[1] // 2, pick_ref.shape[2]
+    y = lax.rem(lax.div(idx_ref[0], 2), 2)
+    mine = pl.ds(pl.multiple_of(y * slots, slots), slots)
+    gate = gate_ref[0, pl.ds(pl.multiple_of(y * span, span), span), :]
+    pick = pick_ref[0, mine, :]
+    width = 4 * LANES
+    for n in range(own_ref.shape[1] // width):
+        cols = slice(n * width, (n + 1) * width)
+        total = spread(pick, own_ref[mine, cols]) + spread(pick, other_ref[mine, cols])
+        keep_ref[:, cols] = total * jnp.concatenate([gate] * (width // LANES), axis=1)
+
+
+def add_kernel(idx_ref, pick_ref, gate_ref, keep_ref, got_ref, own_ref, *refs):
+    send_refs, total_ref = refs[:-1], refs[-1]
+    slots, span = pick_ref.shape[1] // 2, pick_ref.shape[2]
+    tok = own_ref.shape[0]
+    z, y = lax.div(idx_ref[0], 4), lax.rem(lax.div(idx_ref[0], 2), 2)
+    gate = gate_ref[1, pl.ds(pl.multiple_of(y * span, span), span), :]
+    pick = pick_ref[1, pl.ds(pl.multiple_of(y * slots, slots), slots), :]
+    width = 4 * LANES
+    for n in range(got_ref.shape[1] // width):
+        cols = slice(n * width, (n + 1) * width)
+        more = spread(pick, got_ref[:, cols]) * jnp.concatenate([gate] * (width // LANES), axis=1)
+        total_ref[:, cols] = keep_ref[:, cols] + more
+    own_ref[...] = total_ref[pl.ds(pl.multiple_of(z * tok, tok), tok), :]
     for k, ref in enumerate(send_refs, 1):
-        ref[...] = (keep_ref[k] + got_ref[k].astype(jnp.float32)).astype(jnp.bfloat16)
+        ref[...] = total_ref[pl.ds(pl.multiple_of((z ^ k) * tok, tok), tok), :].astype(jnp.bfloat16)
 
 
 def final_kernel(idx_ref, *refs):
@@ -200,12 +285,15 @@
     ctx = lax.axis_size("ctx")
     heads, tok, width = ctx, resid.shape[0], resid.shape[1]
     levels = ctx // 4
-    experts = ctx // 2
     bf16, f32 = jnp.bfloat16, jnp.float32
     rows = ctx // 2 * tok
+    span, slots = levels * tok, levels * block_slots(ctx, tok)
     me, plane = lax.axis_index("ctx"), lax.axis_index("tp")
     idx = jnp.stack([me, plane]).astype(jnp.int32)
 
+    def shape(*dims, dtype=bf16):
+        return jax.ShapeDtypeStruct(dims, dtype)
+
     def over_ctx(x, mask, core=None):
         return lax.ppermute(x, "ctx", [(c, c ^ mask) for c in range(ctx) if core is None or c % 2 == core])
 
@@ -216,73 +304,68 @@
         return lax.ppermute(x, "ctx", [(c, c ^ 1) for c in range(ctx) if c % 2 != core])
 
     wg, wu, wd = w_gate[0], w_up[0], w_down[0]
-    chosen = routes[:, :, None] == jnp.arange(experts, dtype=jnp.int32)
-    gate_rows = jnp.sum(jnp.where(chosen, route_gates[:, :, None], 0.0), axis=1).T
-    gate_rows = jnp.tile(jnp.repeat(gate_rows, 2, axis=0), (1, 2))
-    seg_row = jnp.tile(segment_ids.astype(f32)[None, :], (1, 2))
+    hidden_width = wg.shape[1]
     packed = call(
         pack_kernel,
-        jax.ShapeDtypeStruct((ctx, 4 * tok + META, HD), bf16),
-        (query, key, value, resid, seg_row, gate_rows),
+        shape(ctx, 4 * tok + META, HD),
+        (segment_ids[None, :], routes.T, route_gates.T, query, key, value, resid),
+        hbm=(3, 4, 5, 6),
+        scratch=[pltpu.VMEM((4, tok, width), bf16), pltpu.SemaphoreType.DMA((4,))],
     )
+    gain = over_tp(norm_gain)
     arrived = lax.all_to_all(packed, "ctx", split_axis=0, concat_axis=0, tiled=True)
-    gain = jnp.stack([norm_gain, over_tp(norm_gain)]).astype(f32)
-    hand_even, hand_odd, gates_even, gates_odd = call(
-        attend_kernel,
-        [jax.ShapeDtypeStruct((rows, HD), t) for t in (bf16, bf16, f32, f32)],
+    arrived, gain = lax.optimization_barrier((arrived, gain))
+    gain = jnp.stack([norm_gain, gain]).astype(f32)
+    hands = call(
+        functools.partial(attend_kernel, block_slots(ctx, tok)),
+        [shape(rows, HD)] * 2 + [shape(2, 2 * slots, span)] * 2 + [shape(2, 2 * span, LANES, dtype=f32)] * 2,
         (arrived,),
     )
     masks = [4 * k for k in range(levels)]
-    half = levels // 2
     results = []
-    for core, (hand, gates) in enumerate(((hand_even, gates_even), (hand_odd, gates_odd))):
-        column = jnp.stack([hand] + [over_ctx(hand, m) for m in masks[1:]])
-        by_y, by_x = over_ctx(column, 2), over_tp(column)
-        diag_x, diag_y = over_tp(by_y[:half]), over_ctx(by_x[half:], 2)
-        pieces = [column, by_y, by_x, diag_x, diag_y]
-        places = [
-            [(0, m) for m in masks],
-            [(0, m ^ 2) for m in masks],
-            [(1, m) for m in masks],
-            [(1, m ^ 2) for m in masks[:half]],
-            [(1, m ^ 2) for m in masks[half:]],
-        ]
+    for core in range(2):
+        hand, pick, gates = hands[core::2]
+        column = [hand] + [over_ctx(hand, m) for m in masks[1:]]
+        mine, theirs = call(compact_kernel, [shape(levels, 2 * slots + tok, HD)] * 2, (idx, pick, *column), smem=1)
+        by_y = over_ctx(theirs, 2)
+        pieces = [mine, by_y, over_tp(mine[:, : 2 * slots]), over_tp(by_y[:, : 2 * slots])]
+        places = [[(t, m ^ f) for m in masks] for t, f in ((0, 0), (0, 2), (1, 0), (1, 2))]
         pieces += [over_ctx(p, 1) for p in pieces]
         places += [[(t, m ^ 1) for t, m in entry] for entry in places]
         hidden, own_hand = call(
             functools.partial(gate_up_kernel, places, heads),
-            [
-                jax.ShapeDtypeStruct((rows, wg.shape[1]), bf16),
-                jax.ShapeDtypeStruct((tok, width), bf16),
-            ],
-            (idx, gain, wg, wu, *pieces),
+            [shape(2 * slots, hidden_width), shape(tok, width)],
+            (idx, wg, wu, gain, *pieces),
             smem=1,
-            scratch=[pltpu.VMEM((rows, D), bf16)],
+            hbm=(1, 2),
+            scratch=[pltpu.VMEM((2 * slots, D), bf16), pltpu.VMEM(wg.shape, bf16), pltpu.VMEM(wu.shape, bf16)]
+            + [pltpu.SemaphoreType.DMA((2 * (hidden_width // min(256, hidden_width)),))],
             vmem=32,
-            flops=4 * rows * D * wg.shape[1],
-            moved=2 * (rows * D + 2 * D * wg.shape[1]),
+            flops=8 * slots * D * hidden_width,
+            moved=2 * (2 * slots * D + 2 * D * hidden_width),
         )
         half_out = call(
             down_kernel,
-            jax.ShapeDtypeStruct((rows, width), bf16),
-            (idx, hidden, over_tp(hidden), wd),
+            shape(2 * slots, width),
+            (idx, wd, hidden, over_tp(hidden)),
             smem=1,
-            flops=2 * rows * wd.shape[0] * width,
-            moved=2 * (rows * width + wd.shape[0] * width),
+            hbm=(1,),
+            scratch=[pltpu.VMEM(wd.shape, bf16), pltpu.SemaphoreType.DMA((width // min(512, width),))],
+            flops=4 * slots * wd.shape[0] * width,
+            moved=2 * (2 * slots * width + wd.shape[0] * width),
         )
-        send, keep = call(
-            weigh_kernel,
-            [jax.ShapeDtypeStruct((levels, tok, width), t) for t in (bf16, f32)],
-            (idx, half_out, to_core(half_out, core), gates),
-            smem=1,
-        )
+        other = to_core(half_out, core)
+        got = over_ctx(call(pair_kernel, shape(slots, width), (idx, half_out, other), smem=1), 2, core)
+        keep = call(weigh_kernel, shape(span, width, dtype=f32), (idx, pick, gates, half_out, other), smem=1)
         own, *sends = call(
             add_kernel,
-            [jax.ShapeDtypeStruct((tok, width), t) for t in [f32] + [bf16] * (levels - 1)],
-            (keep, over_ctx(send, 2, core)),
+            [shape(tok, width, dtype=f32)] + [shape(tok, width)] * (levels - 1),
+            (idx, pick, gates, keep, got),
+            smem=1,
+            scratch=[pltpu.VMEM((span, width), f32)],
         )
         results += [own_hand, own] + [over_ctx(s, m, core) for s, m in zip(sends, masks[1:])]
-    return call(final_kernel, jax.ShapeDtypeStruct((tok, width), bf16), (idx, *results), smem=1)
+    return call(final_kernel, shape(tok, width), (idx, *results), smem=1)
 
 
 def general(
@@ -350,7 +433,7 @@
     ).astype(jnp.bfloat16)
     ctx_count = lax.axis_size("ctx")
     expert_count = ctx_count // 2
-    capacity = min(tok_count, max(2, tok_count * 10 // ctx_count))
+    capacity = block_slots(ctx_count, tok_count)
     slot_total = expert_count * capacity
     recv_total = ctx_count * capacity
     flat_routes = routes.reshape(-1)
@@ -393,11 +476,17 @@
     return mixed.astype(jnp.bfloat16)
 
 
+def block_slots(ctx, tok):
+    return min(tok, max(2, tok * 10 // ctx))
+
+
 def fits(mesh, resid):
     ctx, tp = mesh.shape["ctx"], mesh.shape["tp"]
     heads = resid.shape[1] // tp // HD
     tok = resid.shape[0] // mesh.shape["groups"] // ctx
-    return tp == 2 and mesh.shape["sub"] == 1 and heads == ctx and 2 * tok == LANES and ctx >= 8 and ctx & (ctx - 1) == 0
+    slots = ctx // 4 * block_slots(ctx, tok)
+    whole = heads == ctx and 2 * tok == LANES and slots % 16 == 0
+    return tp == 2 and mesh.shape["sub"] == 1 and whole and ctx >= 8 and ctx & (ctx - 1) == 0
 
 
 def solution(mesh):

time: 210 us -> 190 us (0.905)
  blocking collectives: 32.7 us -> 0 us
  starting transfers between devices: 46.9 us -> 55.3 us
  Pallas kernels: 30.2 us -> 37.1 us
  local copies, waits for them, and re-layouts: 13.3 us -> 8.12 us
  waiting for transfers between devices: 84.2 us -> 87.7 us
    all_to_all x1 -> x0, blocking collectives: 32.7 us -> none  [heads_over_ctx(): lax.all_to_all(packed, 'ctx', split_axis=0, concat_axis=0, tiled=True)]
    all_to_all x0 -> x1, waiting for transfers between devices: none -> 23.5 us  [heads_over_ctx(): lax.all_to_all(packed, 'ctx', split_axis=0, concat_axis=0, tiled=True)]
    ppermute x28 -> x24, waiting for transfers between devices: 60.7 us -> 48 us  [over_ctx(): lax.ppermute(x, 'ctx', [(c, c ^ mask) for c in range(ctx) if core is None...]
    ppermute x7, waiting for transfers between devices: 20.6 us -> 13.5 us  [over_tp(): return lax.ppermute(x, 'tp', [(0, 1), (1, 0)])]
    pallas_call x11 -> x15, Pallas kernels: 30.2 us -> 37.1 us  [call(): pl.pallas_call(kernel, out_shape=out_shape, in_specs=[pl.BlockSpec(memory...]
    all_to_all x0 -> x1, starting transfers between devices: none -> 6.57 us  [heads_over_ctx(): lax.all_to_all(packed, 'ctx', split_axis=0, concat_axis=0, tiled=True)]
    slice x4, local copies, waits for them, and re-layouts: 3.12 us -> 0.09 us  [the longest x2 0.04 us: heads_over_ctx(): by_y[:, :2 * slots]]
    unnamed x20 -> x24, local copies, waits for them, and re-layouts: 10 us -> 8.02 us
  transfers between devices with their start and end apart: 37 -> 34, of which waited for: 14 -> 16; matrix products, arithmetic and copies ran while one was open for 2% -> 0% of each run, Pallas kernels for 13% -> 17%
where the time goes in v2:
time: 190 us; the launch traced here: 189 us
  waiting for transfers between devices  87.7 us (46%)
  starting transfers between devices  55.3 us (29%)
  Pallas kernels  37.1 us (20%)
  local copies, waits for them, and re-layouts  8.12 us (4%)
    ppermute x24, waiting for transfers between devices, over_ctx(): lax.ppermute(x, 'ctx', [(c, c ^ mask) for c in range(ctx) if core is None...  48 us
    ppermute x24, starting transfers between devices, over_ctx(): lax.ppermute(x, 'ctx', [(c, c ^ mask) for c in range(ctx) if core is None...  37.4 us
    pallas_call x15, Pallas kernels, call(): pl.pallas_call(kernel, out_shape=out_shape, in_specs=[pl.BlockSpec(memory...  37.1 us
    all_to_all x1, waiting for transfers between devices, heads_over_ctx(): lax.all_to_all(packed, 'ctx', split_axis=0, concat_axis=0, tiled=True)  23.5 us
    ppermute x7, waiting for transfers between devices, over_tp(): return lax.ppermute(x, 'tp', [(0, 1), (1, 0)])  13.5 us
    unnamed x24, local copies, waits for them, and re-layouts  8.02 us
    ppermute x7, starting transfers between devices, over_tp(): return lax.ppermute(x, 'tp', [(0, 1), (1, 0)])  6.97 us
    all_to_all x1, starting transfers between devices, heads_over_ctx(): lax.all_to_all(packed, 'ctx', split_axis=0, concat_axis=0, tiled=True)  6.57 us
  transfers between devices with their start and end apart: 34, of which 16 were waited for; matrix products, arithmetic and copies ran while one was open for 0% of the time, Pallas kernels for 17%

profile of v2, /device:TPU:13, one launch (start us, length us, event | category | flops | bytes accessed | tf_op | source)
XLA Modules:
  0.0 188.8 jit_solution(8366640146248518671)
XLA Ops:
  5.8 1.4 shard_map.109
  7.2 6.6 %all-to-all-start = ((bf16[16,272,128]{2,1,0:T(8,128)(2,1)}), bf16[16,272,128]{2,1,0:T(8,128)(2,1)S(1)}, u32[]{:S(2)}, u32[]{:S(2)}) async-start(bf16[16,272,128]{2,1,0:T(8,128)(2,1)} %shard_map.109), calls=%async_computation | async-start | bytes 2228224 | tf_op jit(solution)/shard_map/all_to_all | solution.py:316
  13.8 1.3 collective-permute-start
  15.1 1.5 collective-permute-done
  16.6 23.5 %all-to-all-done.x_ref = bf16[16,272,128]{2,1,0:T(8,128)(2,1)S(1)} async-done(((bf16[16,272,128]{2,1,0:T(8,128)(2,1)}), bf16[16,272,128]{2,1,0:T(8,128)(2,1)S(1)}, u32[]{:S(2)}, u32[]{:S(2)}) %all-to-all-start) | async-done | bytes 1114144 | tf_op jit(solution)/shard_map/all_to_all | solution.py:316
  40.1 2.0 %shard_map.110 = (bf16[512,128]{1,0:T(8,128)(2,1)S(1)}, bf16[512,128]{1,0:T(8,128)(2,1)S(1)}, bf16[2,320,256]{2,1,0:T(8,128)(2,1)S(1)}, bf16[2,320,256]{2,1,0:T(...) custom-call(bf16[16,272,128]{2,1,0:T(8,128)(2,1)S(1)} %all-to-all-done.x_ref), custom_call_target="tpu_custom_call" | custom-call | tf_op jit(solution)/shard_map/pallas_call | solution.py:28
  42.2 1.1 collective-permute-start.2
  43.3 1.5 collective-permute-start.3
  44.8 1.0 collective-permute-start.17
  45.8 1.0 collective-permute-start.18
  47.1 1.4 collective-permute-start.19
  48.5 1.1 collective-permute-done.2.refs_2_
  49.6 12.5 %collective-permute-done.3.refs_3_ = bf16[512,128]{1,0:T(8,128)(2,1)S(1)} collective-permute-done((bf16[512,128]{1,0:T(8,128)(2,1)S(1)}, bf16[512,128]{1,0:T(8,128)(2,1)S(1)}, u32[]{:S(2)}, u32[]{:S(2)}) %collective-permute-start.3) | collective-permute-done | bytes 131104 | tf_op jit(solution)/shard_map/ppermute | solution.py:298
  63.7 4.1 %collective-permute-done.19.refs_3_ = bf16[512,128]{1,0:T(8,128)(2,1)S(1)} collective-permute-done((bf16[512,128]{1,0:T(8,128)(2,1)S(1)}, bf16[512,128]{1,0:T(8,128)(2,1)S(1)}, u32[]{:S(2)}, u32[]{:S(2)}) %collective-permute-start.19) | collective-permute-done | bytes 131104 | tf_op jit(solution)/shard_map/ppermute | solution.py:298
  69.3 1.3 collective-permute-start.5
  71.7 1.3 collective-permute-start.6
  73.0 5.7 %collective-permute-start.7 = (bf16[4,384,128]{2,1,0:T(8,128)(2,1)S(1)}, bf16[4,384,128]{2,1,0:T(8,128)(2,1)S(1)}, u32[]{:S(2)}, u32[]{:S(2)}) collective-permute-start(bf16[4,384,128]{2,1,0:T(8,128)(2,1)S(1)} %get-tuple-element.33.refs_0_), channel_id=1, source_target_pairs={{0,2},{2,0},{4,6},{6,4},{8,10},{10,8},{12,14},{14,12},{16,18},{18,... | collective-permute-start | bytes 1179656 | tf_op jit(solution)/shard_map/ppermute | solution.py:298
  78.8 2.3 %collective-permute-start.8 = (bf16[4,384,128]{2,1,0:T(8,128)(2,1)S(1)}, bf16[4,384,128]{2,1,0:T(8,128)(2,1)S(1)}, u32[]{:S(2)}, u32[]{:S(2)}) collective-permute-start(bf16[4,384,128]{2,1,0:T(8,128)(2,1)S(1)} %collective-permute-done.4.refs_1_), channel_id=1, source_target_pairs={{0,2},{2,0},{4,6},{6,4},{8,10},{10,8},{12,14},{14,12},{16,18},{18,... | collective-permute-start | bytes 1179656 | tf_op jit(solution)/shard_map/ppermute | solution.py:298
  81.1 2.0 %collective-permute-start.9 = (bf16[4,320,128]{2,1,0:T(8,128)(2,1)S(1)}, bf16[4,320,128]{2,1,0:T(8,128)(2,1)S(1)}, u32[]{:S(2)}, u32[]{:S(2)}) collective-permute-start(bf16[4,320,128]{2,1,0:T(8,128)(2,1)S(1)} %collective-permute-done.5.refs_2_), channel_id=1, source_target_pairs={{0,2},{2,0},{4,6},{6,4},{8,10},{10,8},{12,14},{14,12},{16,18},{18,... | collective-permute-start | bytes 983048 | tf_op jit(solution)/shard_map/ppermute | solution.py:298
  83.1 1.4 collective-permute-done.21.refs_2_
  84.5 1.2 collective-permute-start.22
  85.7 5.8 %collective-permute-done.6.refs_3_ = bf16[4,320,128]{2,1,0:T(8,128)(2,1)S(1)} collective-permute-done((bf16[4,320,128]{2,1,0:T(8,128)(2,1)S(1)}, bf16[4,320,128]{2,1,0:T(8,128)(2,1)S(1)}, u32[]{:S(2)}, u32[]{:S(2)}) %collective-permute-start.6) | collective-permute-done | bytes 327712 | tf_op jit(solution)/shard_map/ppermute | solution.py:301
  91.5 3.6 %collective-permute-start.10 = (bf16[4,320,128]{2,1,0:T(8,128)(2,1)S(1)}, bf16[4,320,128]{2,1,0:T(8,128)(2,1)S(1)}, u32[]{:S(2)}, u32[]{:S(2)}) collective-permute-start(bf16[4,320,128]{2,1,0:T(8,128)(2,1)S(1)} %collective-permute-done.6.refs_3_), channel_id=1, source_target_pairs={{0,2},{2,0},{4,6},{6,4},{8,10},{10,8},{12,14},{14,12},{16,18},{18,... | collective-permute-start | bytes 983048 | tf_op jit(solution)/shard_map/ppermute | solution.py:298
  95.8 2.8 %collective-permute-done.22.refs_3_ = bf16[4,320,128]{2,1,0:T(8,128)(2,1)S(1)} collective-permute-done((bf16[4,320,128]{2,1,0:T(8,128)(2,1)S(1)}, bf16[4,320,128]{2,1,0:T(8,128)(2,1)S(1)}, u32[]{:S(2)}, u32[]{:S(2)}) %collective-permute-start.22) | collective-permute-done | bytes 327712 | tf_op jit(solution)/shard_map/ppermute | solution.py:301
  98.6 2.0 %collective-permute-start.24 = (bf16[4,384,128]{2,1,0:T(8,128)(2,1)S(1)}, bf16[4,384,128]{2,1,0:T(8,128)(2,1)S(1)}, u32[]{:S(2)}, u32[]{:S(2)}) collective-permute-start(bf16[4,384,128]{2,1,0:T(8,128)(2,1)S(1)} %collective-permute-done.20.refs_1_), channel_id=1, source_target_pairs={{0,2},{2,0},{4,6},{6,4},{8,10},{10,8},{12,14},{14,12},{16,18},{18,... | collective-permute-start | bytes 1179656 | tf_op jit(solution)/shard_map/ppermute | solution.py:298
  100.6 2.2 %copy-done.2 = bf16[1,4096,512]{2,1,0:T(8,128)(2,1)S(1)} copy-done((bf16[1,4096,512]{2,1,0:T(8,128)(2,1)S(1)}, bf16[1,4096,512]{2,1,0:T(8,128)(2,1)}, u32[]{:S(2)}) %copy-start.2) | copy-done | bytes 4194328
  102.8 8.9 %shard_map.112 = (bf16[320,512]{1,0:T(8,128)(2,1)S(1)}, bf16[64,2048]{1,0:T(8,128)(2,1)S(1)}) custom-call(s32[2]{0:T(128)S(1)} %pad_add_fusion.idx_ref, bf16[4096,512]{1,0:T(8,128)(2,1)S(1)} %bitcast.10, bf16[4096,512]{1,0:T(8,128)(2,1)S(1)} %bitcast.12, f32[2,2048]{1,0:T(2,128)S(1)} %maximum_convert_fusion.gain_ref, ...), custom_call_target="tpu_custom_call" | custom-call | flops 2684354560 | bytes 11010048 | tf_op jit(solution)/shard_map/pallas_call | solution.py:28
  111.7 1.3 collective-permute-start.11
  113.1 9.1 %shard_map.118 = (bf16[320,512]{1,0:T(8,128)(2,1)S(1)}, bf16[64,2048]{1,0:T(8,128)(2,1)S(1)}) custom-call(s32[2]{0:T(128)S(1)} %pad_add_fusion.idx_ref, bf16[4096,512]{1,0:T(8,128)(2,1)S(1)} %bitcast.11, bf16[4096,512]{1,0:T(8,128)(2,1)S(1)} %bitcast.13, f32[2,2048]{1,0:T(2,128)S(1)} %maximum_convert_fusion.gain_ref, ...), custom_call_target="tpu_custom_call" | custom-call | flops 2684354560 | bytes 11010048 | tf_op jit(solution)/shard_map/pallas_call | solution.py:28
  122.5 3.2 %shard_map.113.own_ref = bf16[320,2048]{1,0:T(8,128)(2,1)S(1)} custom-call(s32[2]{0:T(128)S(1)} %pad_add_fusion.idx_ref, bf16[1024,2048]{1,0:T(8,128)(2,1)S(1)} %bitcast.8, bf16[320,512]{1,0:T(8,128)(2,1)S(1)} %get-tuple-element.37.own_ref, bf16[320,512]{1,0:T(8,128)(2,1)S(1)} %collective-permute-done.11.peer_ref), custom_call_target="tpu_custom_call" | custom-call | flops 1342177280 | bytes 5505024 | tf_op jit(solution)/shard_map/pallas_call | solution.py:28
  125.7 3.0 %collective-permute-start.12 = (bf16[320,2048]{1,0:T(8,128)(2,1)S(1)}, bf16[320,2048]{1,0:T(8,128)(2,1)S(1)}, u32[]{:S(2)}, u32[]{:S(2)}) collective-permute-start(bf16[320,2048]{1,0:T(8,128)(2,1)S(1)} %shard_map.113.own_ref), channel_id=1, source_target_pairs={{2,0},{6,4},{10,8},{14,12},{18,16},{22,20},{26,24},{30,28},{3,1},{... | collective-permute-start | bytes 3932168 | tf_op jit(solution)/shard_map/ppermute | solution.py:304
  128.8 1.9 %collective-permute-done.27.peer_ref = bf16[320,512]{1,0:T(8,128)(2,1)S(1)} collective-permute-done((bf16[320,512]{1,0:T(8,128)(2,1)S(1)}, bf16[320,512]{1,0:T(8,128)(2,1)S(1)}, u32[]{:S(2)}, u32[]{:S(2)}) %collective-permute-start.27) | collective-permute-done | bytes 327712 | tf_op jit(solution)/shard_map/ppermute | solution.py:301
  130.7 3.2 %shard_map.119.own_ref = bf16[320,2048]{1,0:T(8,128)(2,1)S(1)} custom-call(s32[2]{0:T(128)S(1)} %pad_add_fusion.idx_ref, bf16[1024,2048]{1,0:T(8,128)(2,1)S(1)} %bitcast.9, bf16[320,512]{1,0:T(8,128)(2,1)S(1)} %get-tuple-element.48.own_ref, bf16[320,512]{1,0:T(8,128)(2,1)S(1)} %collective-permute-done.27.peer_ref), custom_call_target="tpu_custom_call" | custom-call | flops 1342177280 | bytes 5505024 | tf_op jit(solution)/shard_map/pallas_call | solution.py:28
  133.9 1.3 collective-permute-start.28
  136.6 2.7 %collective-permute-done.28.other_ref = bf16[320,2048]{1,0:T(8,128)(2,1)S(1)} collective-permute-done((bf16[320,2048]{1,0:T(8,128)(2,1)S(1)}, bf16[320,2048]{1,0:T(8,128)(2,1)S(1)}, u32[]{:S(2)}, u32[]{:S(2)}) %collective-permute-start.28) | collective-permute-done | bytes 1310752 | tf_op jit(solution)/shard_map/ppermute | solution.py:304
  140.1 2.8 %collective-permute-start.29 = (bf16[160,2048]{1,0:T(8,128)(2,1)S(1)}, bf16[160,2048]{1,0:T(8,128)(2,1)S(1)}, u32[]{:S(2)}, u32[]{:S(2)}) collective-permute-start(bf16[160,2048]{1,0:T(8,128)(2,1)S(1)} %shard_map.121), channel_id=1, source_target_pairs={{2,6},{6,2},{10,14},{14,10},{18,22},{22,18},{26,30},{30,26},{3,7},... | collective-permute-start | bytes 1966088 | tf_op jit(solution)/shard_map/ppermute | solution.py:298
  142.9 1.3 shard_map.114.keep_ref
  144.2 1.1 shard_map.116
  146.0 1.3 shard_map.120.keep_ref
  148.7 7.8 %collective-permute-done.29.got_ref = bf16[160,2048]{1,0:T(8,128)(2,1)S(1)} collective-permute-done((bf16[160,2048]{1,0:T(8,128)(2,1)S(1)}, bf16[160,2048]{1,0:T(8,128)(2,1)S(1)}, u32[]{:S(2)}, u32[]{:S(2)}) %collective-permute-start.29) | collective-permute-done | bytes 655392 | tf_op jit(solution)/shard_map/ppermute | solution.py:298
  156.5 1.1 shard_map.122
  157.6 1.9 %collective-permute-start.30 = (bf16[64,2048]{1,0:T(8,128)(2,1)S(1)}, bf16[64,2048]{1,0:T(8,128)(2,1)S(1)}, u32[]{:S(2)}, u32[]{:S(2)}) collective-permute-start(bf16[64,2048]{1,0:T(8,128)(2,1)S(1)} %get-tuple-element.50), channel_id=1, source_target_pairs={{2,10},{6,14},{10,2},{14,6},{18,26},{22,30},{26,18},{30,22},{3,11}... | collective-permute-start | bytes 786440 | tf_op jit(solution)/shard_map/ppermute | solution.py:298
  159.5 2.6 %collective-permute-start.31 = (bf16[64,2048]{1,0:T(8,128)(2,1)S(1)}, bf16[64,2048]{1,0:T(8,128)(2,1)S(1)}, u32[]{:S(2)}, u32[]{:S(2)}) collective-permute-start(bf16[64,2048]{1,0:T(8,128)(2,1)S(1)} %get-tuple-element.51), channel_id=1, source_target_pairs={{2,18},{6,22},{10,26},{14,30},{18,2},{22,6},{26,10},{30,14},{3,19}... | collective-permute-start | bytes 786440 | tf_op jit(solution)/shard_map/ppermute | solution.py:298
  162.2 3.8 %collective-permute-start.32 = (bf16[64,2048]{1,0:T(8,128)(2,1)S(1)}, bf16[64,2048]{1,0:T(8,128)(2,1)S(1)}, u32[]{:S(2)}, u32[]{:S(2)}) collective-permute-start(bf16[64,2048]{1,0:T(8,128)(2,1)S(1)} %get-tuple-element.52), channel_id=1, source_target_pairs={{2,26},{6,30},{10,18},{14,22},{18,10},{22,14},{26,2},{30,6},{3,27}... | collective-permute-start | bytes 786440 | tf_op jit(solution)/shard_map/ppermute | solution.py:298
  166.0 1.8 collective-permute-done.30.refs_7_
  167.8 11.1 %collective-permute-done.31.refs_8_ = bf16[64,2048]{1,0:T(8,128)(2,1)S(1)} collective-permute-done((bf16[64,2048]{1,0:T(8,128)(2,1)S(1)}, bf16[64,2048]{1,0:T(8,128)(2,1)S(1)}, u32[]{:S(2)}, u32[]{:S(2)}) %collective-permute-start.31) | collective-permute-done | bytes 262176 | tf_op jit(solution)/shard_map/ppermute | solution.py:298
  178.9 8.5 %collective-permute-done.32.refs_9_ = bf16[64,2048]{1,0:T(8,128)(2,1)S(1)} collective-permute-done((bf16[64,2048]{1,0:T(8,128)(2,1)S(1)}, bf16[64,2048]{1,0:T(8,128)(2,1)S(1)}, u32[]{:S(2)}, u32[]{:S(2)}) %collective-permute-start.32) | collective-permute-done | bytes 262176 | tf_op jit(solution)/shard_map/ppermute | solution.py:298
  187.4 1.4 shard_map.123
  (67 shorter events, 15.6 us)
Async XLA Ops:
  0.0 0.9 copy-start.4
  1.0 0.9 copy-start.5
  1.9 0.9 copy-start.6
  2.9 0.9 copy-start.7
  3.8 0.7 copy-start.8
  4.5 0.7 copy-start.9
  5.2 0.7 copy-start.10
  7.2 6.6 %copy-start.11 = (bf16[2048]{0:T(1024)(128)(2,1)S(1)}, bf16[2048]{0:T(1024)(128)(2,1)}, u32[]{:S(2)}) copy-start(bf16[2048]{0:T(1024)(128)(2,1)} %param.15) | copy-start | bytes 12292
  7.2 32.9 %all-to-all-start = ((bf16[16,272,128]{2,1,0:T(8,128)(2,1)}), bf16[16,272,128]{2,1,0:T(8,128)(2,1)S(1)}, u32[]{:S(2)}, u32[]{:S(2)}) async-start(bf16[16,272,128]{2,1,0:T(8,128)(2,1)} %shard_map.109), calls=%async_computation | async-start | bytes 2228224 | tf_op jit(solution)/shard_map/all_to_all | solution.py:316
  13.8 2.8 %collective-permute-start = (bf16[2048]{0:T(1024)(128)(2,1)S(1)}, bf16[2048]{0:T(1024)(128)(2,1)S(1)}, u32[]{:S(2)}, u32[]{:S(2)}) collective-permute-start(bf16[2048]{0:T(1024)(128)(2,1)S(1)} %copy-done.11), channel_id=1, source_target_pairs={{0,1},{1,0},{2,3},{3,2},{4,5},{5,4},{6,7},{7,6},{8,9},{9,8},{10,11... | collective-permute-start | bytes 12296 | tf_op jit(solution)/shard_map/ppermute | solution.py:301
  42.1 5.0 %collective-permute-start.1 = (bf16[512,128]{1,0:T(8,128)(2,1)S(1)}, bf16[512,128]{1,0:T(8,128)(2,1)S(1)}, u32[]{:S(2)}, u32[]{:S(2)}) collective-permute-start(bf16[512,128]{1,0:T(8,128)(2,1)S(1)} %get-tuple-element.32.refs_0_), channel_id=1, source_target_pairs={{0,8},{2,10},{4,12},{6,14},{8,0},{10,2},{12,4},{14,6},{16,24},{18,... | collective-permute-start | bytes 393224 | tf_op jit(solution)/shard_map/ppermute | solution.py:298
  42.2 7.4 %collective-permute-start.2 = (bf16[512,128]{1,0:T(8,128)(2,1)S(1)}, bf16[512,128]{1,0:T(8,128)(2,1)S(1)}, u32[]{:S(2)}, u32[]{:S(2)}) collective-permute-start(bf16[512,128]{1,0:T(8,128)(2,1)S(1)} %get-tuple-element.32.refs_0_), channel_id=1, source_target_pairs={{0,16},{2,18},{4,20},{6,22},{8,24},{10,26},{12,28},{14,30},{16,0},... | collective-permute-start | bytes 393224 | tf_op jit(solution)/shard_map/ppermute | solution.py:298
  43.3 18.8 %collective-permute-start.3 = (bf16[512,128]{1,0:T(8,128)(2,1)S(1)}, bf16[512,128]{1,0:T(8,128)(2,1)S(1)}, u32[]{:S(2)}, u32[]{:S(2)}) collective-permute-start(bf16[512,128]{1,0:T(8,128)(2,1)S(1)} %get-tuple-element.32.refs_0_), channel_id=1, source_target_pairs={{0,24},{2,26},{4,28},{6,30},{8,16},{10,18},{12,20},{14,22},{16,8},... | collective-permute-start | bytes 393224 | tf_op jit(solution)/shard_map/ppermute | solution.py:298
  44.8 18.8 %collective-permute-start.17 = (bf16[512,128]{1,0:T(8,128)(2,1)S(1)}, bf16[512,128]{1,0:T(8,128)(2,1)S(1)}, u32[]{:S(2)}, u32[]{:S(2)}) collective-permute-start(bf16[512,128]{1,0:T(8,128)(2,1)S(1)} %get-tuple-element.43.refs_0_), channel_id=1, source_target_pairs={{0,8},{2,10},{4,12},{6,14},{8,0},{10,2},{12,4},{14,6},{16,24},{18,... | collective-permute-start | bytes 393224 | tf_op jit(solution)/shard_map/ppermute | solution.py:298
  45.8 17.9 %collective-permute-start.18 = (bf16[512,128]{1,0:T(8,128)(2,1)S(1)}, bf16[512,128]{1,0:T(8,128)(2,1)S(1)}, u32[]{:S(2)}, u32[]{:S(2)}) collective-permute-start(bf16[512,128]{1,0:T(8,128)(2,1)S(1)} %get-tuple-element.43.refs_0_), channel_id=1, source_target_pairs={{0,16},{2,18},{4,20},{6,22},{8,24},{10,26},{12,28},{14,30},{16,0},... | collective-permute-start | bytes 393224 | tf_op jit(solution)/shard_map/ppermute | solution.py:298
  47.1 20.7 %collective-permute-start.19 = (bf16[512,128]{1,0:T(8,128)(2,1)S(1)}, bf16[512,128]{1,0:T(8,128)(2,1)S(1)}, u32[]{:S(2)}, u32[]{:S(2)}) collective-permute-start(bf16[512,128]{1,0:T(8,128)(2,1)S(1)} %get-tuple-element.43.refs_0_), channel_id=1, source_target_pairs={{0,24},{2,26},{4,28},{6,30},{8,16},{10,18},{12,20},{14,22},{16,8},... | collective-permute-start | bytes 393224 | tf_op jit(solution)/shard_map/ppermute | solution.py:298
  62.2 38.5 %copy-start.1 = (bf16[1,4096,512]{2,1,0:T(8,128)(2,1)S(1)}, bf16[1,4096,512]{2,1,0:T(8,128)(2,1)}, u32[]{:S(2)}) copy-start(bf16[1,4096,512]{2,1,0:T(8,128)(2,1)} %param.19) | copy-start | bytes 12582916
  63.0 8.7 %collective-permute-start.4 = (bf16[4,384,128]{2,1,0:T(8,128)(2,1)S(1)}, bf16[4,384,128]{2,1,0:T(8,128)(2,1)S(1)}, u32[]{:S(2)}, u32[]{:S(2)}) collective-permute-start(bf16[4,384,128]{2,1,0:T(8,128)(2,1)S(1)} %get-tuple-element.34), channel_id=1, source_target_pairs={{0,4},{2,6},{4,0},{6,2},{8,12},{10,14},{12,8},{14,10},{16,20},{18,... | collective-permute-start | bytes 1179656 | tf_op jit(solution)/shard_map/ppermute | solution.py:298
  68.7 12.4 %collective-permute-start.20 = (bf16[4,384,128]{2,1,0:T(8,128)(2,1)S(1)}, bf16[4,384,128]{2,1,0:T(8,128)(2,1)S(1)}, u32[]{:S(2)}, u32[]{:S(2)}) collective-permute-start(bf16[4,384,128]{2,1,0:T(8,128)(2,1)S(1)} %get-tuple-element.45), channel_id=1, source_target_pairs={{0,4},{2,6},{4,0},{6,2},{8,12},{10,14},{12,8},{14,10},{16,20},{18,... | collective-permute-start | bytes 1179656 | tf_op jit(solution)/shard_map/ppermute | solution.py:298
  69.3 9.5 %collective-permute-start.5 = (bf16[4,320,128]{2,1,0:T(8,128)(2,1)S(1)}, bf16[4,320,128]{2,1,0:T(8,128)(2,1)S(1)}, u32[]{:S(2)}, u32[]{:S(2)}) collective-permute-start(bf16[4,320,128]{2,1,0:T(8,128)(2,1)S(1)} %slice.12), channel_id=1, source_target_pairs={{0,1},{1,0},{2,3},{3,2},{4,5},{5,4},{6,7},{7,6},{8,9},{9,8},{10,11... | collective-permute-start | bytes 983048 | tf_op jit(solution)/shard_map/ppermute | solution.py:301
  70.6 13.9 %collective-permute-start.21 = (bf16[4,320,128]{2,1,0:T(8,128)(2,1)S(1)}, bf16[4,320,128]{2,1,0:T(8,128)(2,1)S(1)}, u32[]{:S(2)}, u32[]{:S(2)}) collective-permute-start(bf16[4,320,128]{2,1,0:T(8,128)(2,1)S(1)} %slice.14), channel_id=1, source_target_pairs={{0,1},{1,0},{2,3},{3,2},{4,5},{5,4},{6,7},{7,6},{8,9},{9,8},{10,11... | collective-permute-start | bytes 983048 | tf_op jit(solution)/shard_map/ppermute | solution.py:301
  71.7 19.8 %collective-permute-start.6 = (bf16[4,320,128]{2,1,0:T(8,128)(2,1)S(1)}, bf16[4,320,128]{2,1,0:T(8,128)(2,1)S(1)}, u32[]{:S(2)}, u32[]{:S(2)}) collective-permute-start(bf16[4,320,128]{2,1,0:T(8,128)(2,1)S(1)} %slice.16), channel_id=1, source_target_pairs={{0,1},{1,0},{2,3},{3,2},{4,5},{5,4},{6,7},{7,6},{8,9},{9,8},{10,11... | collective-permute-start | bytes 983048 | tf_op jit(solution)/shard_map/ppermute | solution.py:301
  73.0 22.2 %collective-permute-start.7 = (bf16[4,384,128]{2,1,0:T(8,128)(2,1)S(1)}, bf16[4,384,128]{2,1,0:T(8,128)(2,1)S(1)}, u32[]{:S(2)}, u32[]{:S(2)}) collective-permute-start(bf16[4,384,128]{2,1,0:T(8,128)(2,1)S(1)} %get-tuple-element.33.refs_0_), channel_id=1, source_target_pairs={{0,2},{2,0},{4,6},{6,4},{8,10},{10,8},{12,14},{14,12},{16,18},{18,... | collective-permute-start | bytes 1179656 | tf_op jit(solution)/shard_map/ppermute | solution.py:298
  78.8 21.8 %collective-permute-start.8 = (bf16[4,384,128]{2,1,0:T(8,128)(2,1)S(1)}, bf16[4,384,128]{2,1,0:T(8,128)(2,1)S(1)}, u32[]{:S(2)}, u32[]{:S(2)}) collective-permute-start(bf16[4,384,128]{2,1,0:T(8,128)(2,1)S(1)} %collective-permute-done.4.refs_1_), channel_id=1, source_target_pairs={{0,2},{2,0},{4,6},{6,4},{8,10},{10,8},{12,14},{14,12},{16,18},{18,... | collective-permute-start | bytes 1179656 | tf_op jit(solution)/shard_map/ppermute | solution.py:298
  81.1 14.2 %collective-permute-start.9 = (bf16[4,320,128]{2,1,0:T(8,128)(2,1)S(1)}, bf16[4,320,128]{2,1,0:T(8,128)(2,1)S(1)}, u32[]{:S(2)}, u32[]{:S(2)}) collective-permute-start(bf16[4,320,128]{2,1,0:T(8,128)(2,1)S(1)} %collective-permute-done.5.refs_2_), channel_id=1, source_target_pairs={{0,2},{2,0},{4,6},{6,4},{8,10},{10,8},{12,14},{14,12},{16,18},{18,... | collective-permute-start | bytes 983048 | tf_op jit(solution)/shard_map/ppermute | solution.py:298
  84.5 14.0 %collective-permute-start.22 = (bf16[4,320,128]{2,1,0:T(8,128)(2,1)S(1)}, bf16[4,320,128]{2,1,0:T(8,128)(2,1)S(1)}, u32[]{:S(2)}, u32[]{:S(2)}) collective-permute-start(bf16[4,320,128]{2,1,0:T(8,128)(2,1)S(1)} %slice.17), channel_id=1, source_target_pairs={{0,1},{1,0},{2,3},{3,2},{4,5},{5,4},{6,7},{7,6},{8,9},{9,8},{10,11... | collective-permute-start | bytes 983048 | tf_op jit(solution)/shard_map/ppermute | solution.py:301
  91.5 9.1 %collective-permute-start.10 = (bf16[4,320,128]{2,1,0:T(8,128)(2,1)S(1)}, bf16[4,320,128]{2,1,0:T(8,128)(2,1)S(1)}, u32[]{:S(2)}, u32[]{:S(2)}) collective-permute-start(bf16[4,320,128]{2,1,0:T(8,128)(2,1)S(1)} %collective-permute-done.6.refs_3_), channel_id=1, source_target_pairs={{0,2},{2,0},{4,6},{6,4},{8,10},{10,8},{12,14},{14,12},{16,18},{18,... | collective-permute-start | bytes 983048 | tf_op jit(solution)/shard_map/ppermute | solution.py:298
  95.2 17.9 %collective-permute-start.23 = (bf16[4,384,128]{2,1,0:T(8,128)(2,1)S(1)}, bf16[4,384,128]{2,1,0:T(8,128)(2,1)S(1)}, u32[]{:S(2)}, u32[]{:S(2)}) collective-permute-start(bf16[4,384,128]{2,1,0:T(8,128)(2,1)S(1)} %get-tuple-element.44.refs_0_), channel_id=1, source_target_pairs={{0,2},{2,0},{4,6},{6,4},{8,10},{10,8},{12,14},{14,12},{16,18},{18,... | collective-permute-start | bytes 1179656 | tf_op jit(solution)/shard_map/ppermute | solution.py:298
  95.3 17.8 %collective-permute-start.25 = (bf16[4,320,128]{2,1,0:T(8,128)(2,1)S(1)}, bf16[4,320,128]{2,1,0:T(8,128)(2,1)S(1)}, u32[]{:S(2)}, u32[]{:S(2)}) collective-permute-start(bf16[4,320,128]{2,1,0:T(8,128)(2,1)S(1)} %collective-permute-done.21.refs_2_), channel_id=1, source_target_pairs={{0,2},{2,0},{4,6},{6,4},{8,10},{10,8},{12,14},{14,12},{16,18},{18,... | collective-permute-start | bytes 983048 | tf_op jit(solution)/shard_map/ppermute | solution.py:298
  98.6 14.5 %collective-permute-start.24 = (bf16[4,384,128]{2,1,0:T(8,128)(2,1)S(1)}, bf16[4,384,128]{2,1,0:T(8,128)(2,1)S(1)}, u32[]{:S(2)}, u32[]{:S(2)}) collective-permute-start(bf16[4,384,128]{2,1,0:T(8,128)(2,1)S(1)} %collective-permute-done.20.refs_1_), channel_id=1, source_target_pairs={{0,2},{2,0},{4,6},{6,4},{8,10},{10,8},{12,14},{14,12},{16,18},{18,... | collective-permute-start | bytes 1179656 | tf_op jit(solution)/shard_map/ppermute | solution.py:298
  100.6 12.5 %collective-permute-start.26 = (bf16[4,320,128]{2,1,0:T(8,128)(2,1)S(1)}, bf16[4,320,128]{2,1,0:T(8,128)(2,1)S(1)}, u32[]{:S(2)}, u32[]{:S(2)}) collective-permute-start(bf16[4,320,128]{2,1,0:T(8,128)(2,1)S(1)} %collective-permute-done.22.refs_3_), channel_id=1, source_target_pairs={{0,2},{2,0},{4,6},{6,4},{8,10},{10,8},{12,14},{14,12},{16,18},{18,... | collective-permute-start | bytes 983048 | tf_op jit(solution)/shard_map/ppermute | solution.py:298
  100.6 2.2 %copy-start.2 = (bf16[1,4096,512]{2,1,0:T(8,128)(2,1)S(1)}, bf16[1,4096,512]{2,1,0:T(8,128)(2,1)}, u32[]{:S(2)}) copy-start(bf16[1,4096,512]{2,1,0:T(8,128)(2,1)} %param.20) | copy-start | bytes 12582916
  102.8 10.2 %copy-start.3 = (bf16[1,4096,512]{2,1,0:T(8,128)(2,1)S(1)}, bf16[1,4096,512]{2,1,0:T(8,128)(2,1)}, u32[]{:S(2)}) copy-start(bf16[1,4096,512]{2,1,0:T(8,128)(2,1)} %param.20) | copy-start | bytes 12582916
  111.7 10.8 %copy-start = (bf16[1,1024,2048]{2,1,0:T(8,128)(2,1)S(1)}, bf16[1,1024,2048]{2,1,0:T(8,128)(2,1)}, u32[]{:S(2)}) copy-start(bf16[1,1024,2048]{2,1,0:T(8,128)(2,1)} %param.21) | copy-start | bytes 12582916
  111.7 10.7 %collective-permute-start.11 = (bf16[320,512]{1,0:T(8,128)(2,1)S(1)}, bf16[320,512]{1,0:T(8,128)(2,1)S(1)}, u32[]{:S(2)}, u32[]{:S(2)}) collective-permute-start(bf16[320,512]{1,0:T(8,128)(2,1)S(1)} %get-tuple-element.37.own_ref), channel_id=1, source_target_pairs={{0,1},{1,0},{2,3},{3,2},{4,5},{5,4},{6,7},{7,6},{8,9},{9,8},{10,11... | collective-permute-start | bytes 983048 | tf_op jit(solution)/shard_map/ppermute | solution.py:301
  122.1 8.5 %collective-permute-start.27 = (bf16[320,512]{1,0:T(8,128)(2,1)S(1)}, bf16[320,512]{1,0:T(8,128)(2,1)S(1)}, u32[]{:S(2)}, u32[]{:S(2)}) collective-permute-start(bf16[320,512]{1,0:T(8,128)(2,1)S(1)} %get-tuple-element.48.own_ref), channel_id=1, source_target_pairs={{0,1},{1,0},{2,3},{3,2},{4,5},{5,4},{6,7},{7,6},{8,9},{9,8},{10,11... | collective-permute-start | bytes 983048 | tf_op jit(solution)/shard_map/ppermute | solution.py:301
  125.7 9.5 %collective-permute-start.12 = (bf16[320,2048]{1,0:T(8,128)(2,1)S(1)}, bf16[320,2048]{1,0:T(8,128)(2,1)S(1)}, u32[]{:S(2)}, u32[]{:S(2)}) collective-permute-start(bf16[320,2048]{1,0:T(8,128)(2,1)S(1)} %shard_map.113.own_ref), channel_id=1, source_target_pairs={{2,0},{6,4},{10,8},{14,12},{18,16},{22,20},{26,24},{30,28},{3,1},{... | collective-permute-start | bytes 3932168 | tf_op jit(solution)/shard_map/ppermute | solution.py:304
  133.9 5.5 %collective-permute-start.28 = (bf16[320,2048]{1,0:T(8,128)(2,1)S(1)}, bf16[320,2048]{1,0:T(8,128)(2,1)S(1)}, u32[]{:S(2)}, u32[]{:S(2)}) collective-permute-start(bf16[320,2048]{1,0:T(8,128)(2,1)S(1)} %shard_map.119.own_ref), channel_id=1, source_target_pairs={{0,2},{4,6},{8,10},{12,14},{16,18},{20,22},{24,26},{28,30},{1,3},{... | collective-permute-start | bytes 3932168 | tf_op jit(solution)/shard_map/ppermute | solution.py:304
  135.9 8.3 %collective-permute-start.13 = (bf16[160,2048]{1,0:T(8,128)(2,1)S(1)}, bf16[160,2048]{1,0:T(8,128)(2,1)S(1)}, u32[]{:S(2)}, u32[]{:S(2)}) collective-permute-start(bf16[160,2048]{1,0:T(8,128)(2,1)S(1)} %shard_map.115), channel_id=1, source_target_pairs={{0,4},{4,0},{8,12},{12,8},{16,20},{20,16},{24,28},{28,24},{1,5},{5... | collective-permute-start | bytes 1966088 | tf_op jit(solution)/shard_map/ppermute | solution.py:298
  140.1 16.4 %collective-permute-start.29 = (bf16[160,2048]{1,0:T(8,128)(2,1)S(1)}, bf16[160,2048]{1,0:T(8,128)(2,1)S(1)}, u32[]{:S(2)}, u32[]{:S(2)}) collective-permute-start(bf16[160,2048]{1,0:T(8,128)(2,1)S(1)} %shard_map.121), channel_id=1, source_target_pairs={{2,6},{6,2},{10,14},{14,10},{18,22},{22,18},{26,30},{30,26},{3,7},... | collective-permute-start | bytes 1966088 | tf_op jit(solution)/shard_map/ppermute | solution.py:298
  145.3 16.8 %collective-permute-start.14 = (bf16[64,2048]{1,0:T(8,128)(2,1)S(1)}, bf16[64,2048]{1,0:T(8,128)(2,1)S(1)}, u32[]{:S(2)}, u32[]{:S(2)}) collective-permute-start(bf16[64,2048]{1,0:T(8,128)(2,1)S(1)} %get-tuple-element.39), channel_id=1, source_target_pairs={{0,8},{4,12},{8,0},{12,4},{16,24},{20,28},{24,16},{28,20},{1,9},{5... | collective-permute-start | bytes 786440 | tf_op jit(solution)/shard_map/ppermute | solution.py:298
  147.3 18.7 %collective-permute-start.15 = (bf16[64,2048]{1,0:T(8,128)(2,1)S(1)}, bf16[64,2048]{1,0:T(8,128)(2,1)S(1)}, u32[]{:S(2)}, u32[]{:S(2)}) collective-permute-start(bf16[64,2048]{1,0:T(8,128)(2,1)S(1)} %get-tuple-element.40), channel_id=1, source_target_pairs={{0,16},{4,20},{8,24},{12,28},{16,0},{20,4},{24,8},{28,12},{1,17},{... | collective-permute-start | bytes 786440 | tf_op jit(solution)/shard_map/ppermute | solution.py:298
  148.0 18.0 %collective-permute-start.16 = (bf16[64,2048]{1,0:T(8,128)(2,1)S(1)}, bf16[64,2048]{1,0:T(8,128)(2,1)S(1)}, u32[]{:S(2)}, u32[]{:S(2)}) collective-permute-start(bf16[64,2048]{1,0:T(8,128)(2,1)S(1)} %get-tuple-element.41), channel_id=1, source_target_pairs={{0,24},{4,28},{8,16},{12,20},{16,8},{20,12},{24,0},{28,4},{1,25},{... | collective-permute-start | bytes 786440 | tf_op jit(solution)/shard_map/ppermute | solution.py:298
  157.6 10.2 %collective-permute-start.30 = (bf16[64,2048]{1,0:T(8,128)(2,1)S(1)}, bf16[64,2048]{1,0:T(8,128)(2,1)S(1)}, u32[]{:S(2)}, u32[]{:S(2)}) collective-permute-start(bf16[64,2048]{1,0:T(8,128)(2,1)S(1)} %get-tuple-element.50), channel_id=1, source_target_pairs={{2,10},{6,14},{10,2},{14,6},{18,26},{22,30},{26,18},{30,22},{3,11}... | collective-permute-start | bytes 786440 | tf_op jit(solution)/shard_map/ppermute | solution.py:298
  159.5 19.4 %collective-permute-start.31 = (bf16[64,2048]{1,0:T(8,128)(2,1)S(1)}, bf16[64,2048]{1,0:T(8,128)(2,1)S(1)}, u32[]{:S(2)}, u32[]{:S(2)}) collective-permute-start(bf16[64,2048]{1,0:T(8,128)(2,1)S(1)} %get-tuple-element.51), channel_id=1, source_target_pairs={{2,18},{6,22},{10,26},{14,30},{18,2},{22,6},{26,10},{30,14},{3,19}... | collective-permute-start | bytes 786440 | tf_op jit(solution)/shard_map/ppermute | solution.py:298
  162.2 25.2 %collective-permute-start.32 = (bf16[64,2048]{1,0:T(8,128)(2,1)S(1)}, bf16[64,2048]{1,0:T(8,128)(2,1)S(1)}, u32[]{:S(2)}, u32[]{:S(2)}) collective-permute-start(bf16[64,2048]{1,0:T(8,128)(2,1)S(1)} %get-tuple-element.52), channel_id=1, source_target_pairs={{2,26},{6,30},{10,18},{14,22},{18,10},{22,14},{26,2},{30,6},{3,27}... | collective-permute-start | bytes 786440 | tf_op jit(solution)/shard_map/ppermute | solution.py:298

commit v3 on v2

--- a/solution.py
+++ b/solution.py
@@ -22,7 +22,7 @@
 
 
 def call(kernel, out_shape, args, smem=0, hbm=(), scratch=(), vmem=16, flops=0, moved=0):
-    spaces = [pltpu.SMEM if n < smem else pl.ANY if n in hbm else pltpu.VMEM for n in range(len(args))]
+    spaces = [pltpu.SMEM if n < smem else pltpu.HBM if n in hbm else pltpu.VMEM for n in range(len(args))]
     several = isinstance(out_shape, (tuple, list))
     out = pl.BlockSpec(memory_space=pltpu.VMEM)
     return pl.pallas_call(
@@ -32,7 +32,6 @@
         out_specs=tuple(out for _ in out_shape) if several else out,
         scratch_shapes=list(scratch),
         compiler_params=pltpu.CompilerParams(vmem_limit_bytes=vmem * MIB),
-        cost_estimate=pl.CostEstimate(flops=flops, bytes_accessed=moved, transcendentals=0),
     )(*args)
 
 
@@ -159,17 +158,10 @@
 
 
 def gate_up_kernel(places, heads, idx_ref, wg_ref, wu_ref, gain_ref, *refs):
-    pieces, (hidden_ref, hand_ref, lhs_ref, wg_held, wu_held, sems) = refs[: len(places)], refs[len(places) :]
+    pieces, (hidden_ref, hand_ref, lhs_ref) = refs[: len(places)], refs[len(places) :]
     me, plane = idx_ref[0], idx_ref[1]
     rows, tok = hidden_ref.shape[0], hand_ref.shape[0]
     width = min(256, wg_ref.shape[1])
-    steps = wg_ref.shape[1] // width
-    copies = []
-    for n in range(steps):
-        cols = slice(n * width, (n + 1) * width)
-        for m, (ref, held) in enumerate(((wg_ref, wg_held), (wu_ref, wu_held))):
-            copies.append(pltpu.make_async_copy(ref.at[:, cols], held.at[:, cols], sems.at[2 * n + m]))
-            copies[-1].start()
     tile = rows // 2
     for ref, entries in zip(pieces, places):
         for k, (other, mask) in enumerate(entries):
@@ -195,33 +187,25 @@
         return carry
 
     lax.fori_loop(0, rows // tile, normalise, 0)
-    for n in range(steps):
+    for n in range(wg_ref.shape[1] // width):
         cols = slice(n * width, (n + 1) * width)
-        copies[2 * n].wait()
-        gate = jnp.dot(lhs_ref[...], wg_held[:, cols], preferred_element_type=jnp.float32)
-        copies[2 * n + 1].wait()
-        up = jnp.dot(lhs_ref[...], wu_held[:, cols], preferred_element_type=jnp.float32)
+        gate = jnp.dot(lhs_ref[...], wg_ref[:, cols], preferred_element_type=jnp.float32)
+        up = jnp.dot(lhs_ref[...], wu_ref[:, cols], preferred_element_type=jnp.float32)
         hidden_ref[:, cols] = (silu(gate) * up).astype(jnp.bfloat16)
 
 
-def down_kernel(idx_ref, wd_ref, own_ref, peer_ref, out_ref, wd_held, sems):
-    plane = idx_ref[1]
-    depth = own_ref.shape[1]
-    width = min(512, wd_ref.shape[1])
-    steps = wd_ref.shape[1] // width
-    copies = []
-    for n in range(steps):
-        cols = slice(n * width, (n + 1) * width)
-        copies.append(pltpu.make_async_copy(wd_ref.at[:, cols], wd_held.at[:, cols], sems.at[n]))
-        copies[-1].start()
+def down_kernel(flip, idx_ref, wd_ref, own_ref, peer_ref, out_ref):
+    core, plane = lax.rem(idx_ref[0], 2), idx_ref[1]
+    depth, total_width = own_ref.shape[1], out_ref.shape[1]
+    width = min(512, total_width)
+    first = (core ^ flip) * total_width
     own_rows = pl.ds(pl.multiple_of(plane * depth, depth), depth)
     peer_rows = pl.ds(pl.multiple_of((1 - plane) * depth, depth), depth)
-    for n in range(steps):
-        cols = slice(n * width, (n + 1) * width)
-        copies[n].wait()
-        total = jnp.dot(own_ref[...], wd_held[own_rows, cols], preferred_element_type=jnp.float32)
-        total = total + jnp.dot(peer_ref[...], wd_held[peer_rows, cols], preferred_element_type=jnp.float32)
-        out_ref[:, cols] = total.astype(jnp.bfloat16)
+    for n in range(total_width // width):
+        cols = pl.ds(pl.multiple_of(first + n * width, width), width)
+        total = jnp.dot(own_ref[...], wd_ref[own_rows, cols], preferred_element_type=jnp.float32)
+        total = total + jnp.dot(peer_ref[...], wd_ref[peer_rows, cols], preferred_element_type=jnp.float32)
+        out_ref[:, n * width : (n + 1) * width] = total.astype(jnp.bfloat16)
 
 
 def pair_kernel(idx_ref, own_ref, other_ref, send_ref):
@@ -266,17 +250,27 @@
         ref[...] = total_ref[pl.ds(pl.multiple_of((z ^ k) * tok, tok), tok), :].astype(jnp.bfloat16)
 
 
+def sum_kernel(own_ref, *refs):
+    total = own_ref[...]
+    for ref in refs[:-1]:
+        total = total + ref[...].astype(jnp.float32)
+    refs[-1][...] = total.astype(refs[-1].dtype)
+
+
 def final_kernel(idx_ref, *refs):
     out_ref = refs[-1]
-    per = (len(refs) - 1) // 2
     core = lax.rem(idx_ref[0], 2)
     for n in range(2):
+        hand_ref, own_ref, other_ref = refs[3 * n : 3 * n + 3]
+        half = own_ref.shape[1]
+
         @pl.when(core == n)
-        def _(mine=refs[n * per : (n + 1) * per]):
-            total = mine[1][...]
-            for ref in mine[2:]:
-                total = total + ref[...].astype(jnp.float32)
-            out_ref[...] = (mine[0][...].astype(jnp.float32) + total).astype(jnp.bfloat16)
+        def _(hand_ref=hand_ref, halves=(own_ref, other_ref) if n == 0 else (other_ref, own_ref)):
+            for m, ref in enumerate(halves):
+                cols = slice(m * half, (m + 1) * half)
+                out_ref[:, cols] = (hand_ref[:, cols].astype(jnp.float32) + ref[...].astype(jnp.float32)).astype(
+                    jnp.bfloat16
+                )
 
 
 def heads_over_ctx(
@@ -300,20 +294,25 @@
     def over_tp(x):
         return lax.ppermute(x, "tp", [(0, 1), (1, 0)])
 
+    def across(x):
+        pairs = [(2 * c + t, 2 * (c ^ 2) + (t ^ 1)) for c in range(ctx) for t in range(2)]
+        return lax.ppermute(x, ("ctx", "tp"), pairs)
+
     def to_core(x, core):
         return lax.ppermute(x, "ctx", [(c, c ^ 1) for c in range(ctx) if c % 2 != core])
 
-    wg, wu, wd = w_gate[0], w_up[0], w_down[0]
-    hidden_width = wg.shape[1]
     packed = call(
         pack_kernel,
         shape(ctx, 4 * tok + META, HD),
         (segment_ids[None, :], routes.T, route_gates.T, query, key, value, resid),
         hbm=(3, 4, 5, 6),
         scratch=[pltpu.VMEM((4, tok, width), bf16), pltpu.SemaphoreType.DMA((4,))],
+        vmem=60,
     )
     gain = over_tp(norm_gain)
     arrived = lax.all_to_all(packed, "ctx", split_axis=0, concat_axis=0, tiled=True)
+    wg, wu, wd = w_gate[0], w_up[0], w_down[0]
+    hidden_width = wg.shape[1]
     arrived, gain = lax.optimization_barrier((arrived, gain))
     gain = jnp.stack([norm_gain, gain]).astype(f32)
     hands = call(
@@ -322,13 +321,21 @@
         (arrived,),
     )
     masks = [4 * k for k in range(levels)]
-    results = []
+    half = width // 2
+    results, waited = [], None
     for core in range(2):
         hand, pick, gates = hands[core::2]
+        if waited is not None:
+            hand, waited = lax.optimization_barrier((hand, waited))
         column = [hand] + [over_ctx(hand, m) for m in masks[1:]]
+        if waited is None:
+            column[:-1] = lax.optimization_barrier(column[:-1])
+            waited = column[0]
         mine, theirs = call(compact_kernel, [shape(levels, 2 * slots + tok, HD)] * 2, (idx, pick, *column), smem=1)
-        by_y = over_ctx(theirs, 2)
-        pieces = [mine, by_y, over_tp(mine[:, : 2 * slots]), over_tp(by_y[:, : 2 * slots])]
+        pieces = [over_ctx(theirs, 2), over_tp(mine[:, : 2 * slots]), across(theirs[:, : 2 * slots])]
+        pieces = [mine] + pieces
+        if core:
+            *pieces, hidden = lax.optimization_barrier((*pieces, hidden))
         places = [[(t, m ^ f) for m in masks] for t, f in ((0, 0), (0, 2), (1, 0), (1, 2))]
         pieces += [over_ctx(p, 1) for p in pieces]
         places += [[(t, m ^ 1) for t, m in entry] for entry in places]
@@ -337,34 +344,35 @@
             [shape(2 * slots, hidden_width), shape(tok, width)],
             (idx, wg, wu, gain, *pieces),
             smem=1,
-            hbm=(1, 2),
-            scratch=[pltpu.VMEM((2 * slots, D), bf16), pltpu.VMEM(wg.shape, bf16), pltpu.VMEM(wu.shape, bf16)]
-            + [pltpu.SemaphoreType.DMA((2 * (hidden_width // min(256, hidden_width)),))],
-            vmem=32,
+            scratch=[pltpu.VMEM((2 * slots, D), bf16)],
             flops=8 * slots * D * hidden_width,
             moved=2 * (2 * slots * D + 2 * D * hidden_width),
         )
-        half_out = call(
-            down_kernel,
-            shape(2 * slots, width),
-            (idx, wd, hidden, over_tp(hidden)),
-            smem=1,
-            hbm=(1,),
-            scratch=[pltpu.VMEM(wd.shape, bf16), pltpu.SemaphoreType.DMA((width // min(512, width),))],
-            flops=4 * slots * wd.shape[0] * width,
-            moved=2 * (2 * slots * width + wd.shape[0] * width),
-        )
-        other = to_core(half_out, core)
-        got = over_ctx(call(pair_kernel, shape(slots, width), (idx, half_out, other), smem=1), 2, core)
-        keep = call(weigh_kernel, shape(span, width, dtype=f32), (idx, pick, gates, half_out, other), smem=1)
+        peer = over_tp(hidden)
+
+        def down(flip):
+            return call(
+                functools.partial(down_kernel, flip),
+                shape(2 * slots, half),
+                (idx, wd, hidden, peer),
+                smem=1,
+                flops=4 * slots * wd.shape[0] * half,
+                moved=2 * (2 * slots * half + wd.shape[0] * half),
+            )
+
+        other = over_ctx(down(1), 1)
+        half_out = down(0)
+        got = over_ctx(call(pair_kernel, shape(slots, half), (idx, half_out, other), smem=1), 2)
+        keep = call(weigh_kernel, shape(span, half, dtype=f32), (idx, pick, gates, half_out, other), smem=1)
         own, *sends = call(
             add_kernel,
-            [shape(tok, width, dtype=f32)] + [shape(tok, width)] * (levels - 1),
+            [shape(tok, half, dtype=f32)] + [shape(tok, half)] * (levels - 1),
             (idx, pick, gates, keep, got),
             smem=1,
-            scratch=[pltpu.VMEM((span, width), f32)],
+            scratch=[pltpu.VMEM((span, half), f32)],
         )
-        results += [own_hand, own] + [over_ctx(s, m, core) for s, m in zip(sends, masks[1:])]
+        summed = call(sum_kernel, shape(tok, half), (own, *[over_ctx(s, m) for s, m in zip(sends, masks[1:])]))
+        results += [own_hand, summed, to_core(summed, core)]
     return call(final_kernel, shape(tok, width), (idx, *results), smem=1)
 
 

time: 190 us -> 158 us (0.83)
  waiting for transfers between devices: 87.7 us -> 73 us
  Pallas kernels: 37.1 us -> 29.6 us
  local copies, waits for them, and re-layouts: 8.12 us -> 2.31 us
  starting transfers between devices: 55.3 us -> 51.8 us
    ppermute x24 -> x26, waiting for transfers between devices: 48 us -> 31 us  [over_ctx(): lax.ppermute(x, 'ctx', [(c, c ^ mask) for c in range(ctx) if core is None...]
    ppermute x24 -> x26, starting transfers between devices: 37.4 us -> 26.6 us  [over_ctx(): lax.ppermute(x, 'ctx', [(c, c ^ mask) for c in range(ctx) if core is None...]
    pallas_call x15 -> x19, Pallas kernels: 37.1 us -> 29.6 us  [call(): pl.pallas_call(kernel, out_shape=out_shape, in_specs=[pl.BlockSpec(memory...]
    ppermute x2, starting transfers between devices: 4.33 us -> 11.4 us  [to_core(): lax.ppermute(x, 'ctx', [(c, c ^ 1) for c in range(ctx) if c % 2 != core])]
    ppermute x0 -> x2, waiting for transfers between devices: none -> 6.53 us  [across(): return lax.ppermute(x, ('ctx', 'tp'), pairs)]
    unnamed x24 -> x10, local copies, waits for them, and re-layouts: 8.02 us -> 2.2 us
    ppermute x7 -> x5, waiting for transfers between devices: 13.5 us -> 9.4 us  [over_tp(): return lax.ppermute(x, 'tp', [(0, 1), (1, 0)])]
    ppermute x0 -> x2, starting transfers between devices: none -> 2.26 us  [across(): return lax.ppermute(x, ('ctx', 'tp'), pairs)]
  transfers between devices with their start and end apart: 34 -> 36, of which waited for: 16 -> 19; matrix products, arithmetic and copies ran while one was open for 0% -> 0% of each run, Pallas kernels for 17% -> 14%
where the time goes in v3:
time: 158 us; the launch traced here: 157 us
  waiting for transfers between devices  73 us (46%)
  starting transfers between devices  51.8 us (33%)
  Pallas kernels  29.6 us (19%)
  local copies, waits for them, and re-layouts  2.31 us (1%)
    ppermute x26, waiting for transfers between devices, over_ctx(): lax.ppermute(x, 'ctx', [(c, c ^ mask) for c in range(ctx) if core is None...  31 us
    pallas_call x19, Pallas kernels, call(): pl.pallas_call(kernel, out_shape=out_shape, in_specs=[pl.BlockSpec(memory...  29.6 us
    ppermute x26, starting transfers between devices, over_ctx(): lax.ppermute(x, 'ctx', [(c, c ^ mask) for c in range(ctx) if core is None...  26.6 us
    all_to_all x1, waiting for transfers between devices, heads_over_ctx(): lax.all_to_all(packed, 'ctx', split_axis=0, concat_axis=0, tiled=True)  23.5 us
    ppermute x2, starting transfers between devices, to_core(): lax.ppermute(x, 'ctx', [(c, c ^ 1) for c in range(ctx) if c % 2 != core])  11.4 us
    ppermute x5, waiting for transfers between devices, over_tp(): return lax.ppermute(x, 'tp', [(0, 1), (1, 0)])  9.4 us
    all_to_all x1, starting transfers between devices, heads_over_ctx(): lax.all_to_all(packed, 'ctx', split_axis=0, concat_axis=0, tiled=True)  6.57 us
    ppermute x2, waiting for transfers between devices, across(): return lax.ppermute(x, ('ctx', 'tp'), pairs)  6.53 us
  transfers between devices with their start and end apart: 36, of which 19 were waited for; matrix products, arithmetic and copies ran while one was open for 0% of the time, Pallas kernels for 14%

profile of v3, /device:TPU:13, one launch (start us, length us, event | category | flops | bytes accessed | tf_op | source)
XLA Modules:
  0.0 157.1 jit_solution(2923713067660253926)
XLA Ops:
  0.0 3.0 %shard_map.109 = bf16[16,272,128]{2,1,0:T(8,128)(2,1)} custom-call(s32[1,64]{1,0:T(1,128)} %bitcast.18, s32[4,64]{1,0:T(4,128)} %bitcast.16, f32[4,64]{1,0:T(4,128)} %bitcast.17, bf16[64,2048]{1,0:T(8,128)(2,1)} %q_ref.1, bf16[64,2048]{1,0:T(8,128)(2,1)} %k_ref.1, bf16[64,2048]{1,0:T(8,128)(2,1)} %v_ref.1, bf16[64,2048]{1,0:T(8,128)(2,1)} %r_ref.1), custom_call_target="tpu_custom_call" | custom-call | tf_op jit(solution)/shard_map/pallas_call | solution.py:28
  3.0 6.6 %all-to-all-start = ((bf16[16,272,128]{2,1,0:T(8,128)(2,1)}), bf16[16,272,128]{2,1,0:T(8,128)(2,1)S(1)}, u32[]{:S(2)}, u32[]{:S(2)}) async-start(bf16[16,272,128]{2,1,0:T(8,128)(2,1)} %shard_map.109), calls=%async_computation | async-start | bytes 2228224 | tf_op jit(solution)/shard_map/all_to_all | solution.py:313
  9.6 1.3 collective-permute-start
  10.9 1.5 collective-permute-done
  12.4 23.5 %all-to-all-done.x_ref = bf16[16,272,128]{2,1,0:T(8,128)(2,1)S(1)} async-done(((bf16[16,272,128]{2,1,0:T(8,128)(2,1)}), bf16[16,272,128]{2,1,0:T(8,128)(2,1)S(1)}, u32[]{:S(2)}, u32[]{:S(2)}) %all-to-all-start) | async-done | bytes 1114144 | tf_op jit(solution)/shard_map/all_to_all | solution.py:313
  35.9 2.0 %shard_map.110 = (bf16[512,128]{1,0:T(8,128)(2,1)S(1)}, bf16[512,128]{1,0:T(8,128)(2,1)S(1)}, bf16[2,320,256]{2,1,0:T(8,128)(2,1)S(1)}, bf16[2,320,256]{2,1,0:T(...) custom-call(bf16[16,272,128]{2,1,0:T(8,128)(2,1)S(1)} %all-to-all-done.x_ref), custom_call_target="tpu_custom_call" | custom-call | tf_op jit(solution)/shard_map/pallas_call | solution.py:28
  38.0 1.2 collective-permute-start.2
  39.2 1.5 collective-permute-start.3
  40.7 2.2 %collective-permute-done.1.refs_1_ = bf16[512,128]{1,0:T(8,128)(2,1)S(1)} collective-permute-done((bf16[512,128]{1,0:T(8,128)(2,1)S(1)}, bf16[512,128]{1,0:T(8,128)(2,1)S(1)}, u32[]{:S(2)}, u32[]{:S(2)}) %collective-permute-start.1) | collective-permute-done | bytes 131104 | tf_op jit(solution)/shard_map/ppermute | solution.py:292
  42.9 2.5 %collective-permute-done.2.refs_2_ = bf16[512,128]{1,0:T(8,128)(2,1)S(1)} collective-permute-done((bf16[512,128]{1,0:T(8,128)(2,1)S(1)}, bf16[512,128]{1,0:T(8,128)(2,1)S(1)}, u32[]{:S(2)}, u32[]{:S(2)}) %collective-permute-start.2) | collective-permute-done | bytes 131104 | tf_op jit(solution)/shard_map/ppermute | solution.py:292
  45.4 6.9 %collective-permute-done.3.refs_3_ = bf16[512,128]{1,0:T(8,128)(2,1)S(1)} collective-permute-done((bf16[512,128]{1,0:T(8,128)(2,1)S(1)}, bf16[512,128]{1,0:T(8,128)(2,1)S(1)}, u32[]{:S(2)}, u32[]{:S(2)}) %collective-permute-start.3) | collective-permute-done | bytes 131104 | tf_op jit(solution)/shard_map/ppermute | solution.py:292
  53.2 1.2 collective-permute-start.5
  55.1 1.4 collective-permute-start.7
  56.5 1.3 collective-permute-start.6
  57.8 1.4 collective-permute-done.18.refs_1_
  59.3 2.0 %collective-permute-done.5.refs_2_ = bf16[4,320,128]{2,1,0:T(8,128)(2,1)S(1)} collective-permute-done((bf16[4,320,128]{2,1,0:T(8,128)(2,1)S(1)}, bf16[4,320,128]{2,1,0:T(8,128)(2,1)S(1)}, u32[]{:S(2)}, u32[]{:S(2)}) %collective-permute-start.5) | collective-permute-done | bytes 327712 | tf_op jit(solution)/shard_map/ppermute | solution.py:295
  61.3 3.9 %collective-permute-start.9 = (bf16[4,320,128]{2,1,0:T(8,128)(2,1)S(1)}, bf16[4,320,128]{2,1,0:T(8,128)(2,1)S(1)}, u32[]{:S(2)}, u32[]{:S(2)}) collective-permute-start(bf16[4,320,128]{2,1,0:T(8,128)(2,1)S(1)} %collective-permute-done.5.refs_2_), channel_id=1, source_target_pairs={{0,2},{2,0},{4,6},{6,4},{8,10},{10,8},{12,14},{14,12},{16,18},{18,... | collective-permute-start | bytes 983048 | tf_op jit(solution)/shard_map/ppermute | solution.py:292
  65.2 5.4 %collective-permute-done.4.refs_1_ = bf16[4,384,128]{2,1,0:T(8,128)(2,1)S(1)} collective-permute-done((bf16[4,384,128]{2,1,0:T(8,128)(2,1)S(1)}, bf16[4,384,128]{2,1,0:T(8,128)(2,1)S(1)}, u32[]{:S(2)}, u32[]{:S(2)}) %collective-permute-start.4) | collective-permute-done | bytes 393248 | tf_op jit(solution)/shard_map/ppermute | solution.py:292
  70.6 2.4 %collective-permute-start.8 = (bf16[4,384,128]{2,1,0:T(8,128)(2,1)S(1)}, bf16[4,384,128]{2,1,0:T(8,128)(2,1)S(1)}, u32[]{:S(2)}, u32[]{:S(2)}) collective-permute-start(bf16[4,384,128]{2,1,0:T(8,128)(2,1)S(1)} %collective-permute-done.4.refs_1_), channel_id=1, source_target_pairs={{0,2},{2,0},{4,6},{6,4},{8,10},{10,8},{12,14},{14,12},{16,18},{18,... | collective-permute-start | bytes 1179656 | tf_op jit(solution)/shard_map/ppermute | solution.py:292
  74.6 1.6 collective-permute-start.10
  76.4 1.0 collective-permute-start.23
  77.5 2.2 %copy-done.2 = bf16[1,4096,512]{2,1,0:T(8,128)(2,1)S(1)} copy-done((bf16[1,4096,512]{2,1,0:T(8,128)(2,1)S(1)}, bf16[1,4096,512]{2,1,0:T(8,128)(2,1)}, u32[]{:S(2)}) %copy-start.2) | copy-done | bytes 4194328
  79.7 5.3 %shard_map.112 = (bf16[320,512]{1,0:T(8,128)(2,1)S(1)}, bf16[64,2048]{1,0:T(8,128)(2,1)S(1)}) custom-call(s32[2]{0:T(128)S(1)} %pad_add_fusion.idx_ref, bf16[4096,512]{1,0:T(8,128)(2,1)S(1)} %bitcast.12, bf16[4096,512]{1,0:T(8,128)(2,1)S(1)} %bitcast.14, f32[2,2048]{1,0:T(2,128)S(1)} %maximum_convert_fusion.gain_ref, ...), custom_call_target="tpu_custom_call" | custom-call | tf_op jit(solution)/shard_map/pallas_call | solution.py:28
  85.7 6.5 %collective-permute-done.23.refs_3_ = bf16[4,320,128]{2,1,0:T(8,128)(2,1)S(1)} collective-permute-done((bf16[4,320,128]{2,1,0:T(8,128)(2,1)S(1)}, bf16[4,320,128]{2,1,0:T(8,128)(2,1)S(1)}, u32[]{:S(2)}, u32[]{:S(2)}) %collective-permute-start.23) | collective-permute-done | bytes 327712 | tf_op jit(solution)/shard_map/ppermute | solution.py:299
  93.6 1.1 collective-permute-start.11
  95.9 5.5 %shard_map.120 = (bf16[320,512]{1,0:T(8,128)(2,1)S(1)}, bf16[64,2048]{1,0:T(8,128)(2,1)S(1)}) custom-call(s32[2]{0:T(128)S(1)} %pad_add_fusion.idx_ref, bf16[4096,512]{1,0:T(8,128)(2,1)S(1)} %bitcast.13, bf16[4096,512]{1,0:T(8,128)(2,1)S(1)} %bitcast.15, f32[2,2048]{1,0:T(2,128)S(1)} %maximum_convert_fusion.gain_ref, ...), custom_call_target="tpu_custom_call" | custom-call | tf_op jit(solution)/shard_map/pallas_call | solution.py:28
  101.3 1.2 collective-permute-start.28
  102.5 1.4 shard_map.114
  103.9 1.2 collective-permute-start.12
  105.2 5.1 %collective-permute-done.28.peer_ref = bf16[320,512]{1,0:T(8,128)(2,1)S(1)} collective-permute-done((bf16[320,512]{1,0:T(8,128)(2,1)S(1)}, bf16[320,512]{1,0:T(8,128)(2,1)S(1)}, u32[]{:S(2)}, u32[]{:S(2)}) %collective-permute-start.28) | collective-permute-done | bytes 327712 | tf_op jit(solution)/shard_map/ppermute | solution.py:295
  110.3 1.4 shard_map.122
  111.7 1.3 collective-permute-start.29
  113.0 1.4 shard_map.113.own_ref
  115.0 1.7 %collective-permute-start.13 = (bf16[160,1024]{1,0:T(8,128)(2,1)S(1)}, bf16[160,1024]{1,0:T(8,128)(2,1)S(1)}, u32[]{:S(2)}, u32[]{:S(2)}) collective-permute-start(bf16[160,1024]{1,0:T(8,128)(2,1)S(1)} %shard_map.116), channel_id=1, source_target_pairs={{0,4},{2,6},{4,0},{6,2},{8,12},{10,14},{12,8},{14,10},{16,20},{18,... | collective-permute-start | bytes 983048 | tf_op jit(solution)/shard_map/ppermute | solution.py:292
  116.8 1.4 shard_map.121.own_ref
  118.9 1.0 shard_map.115.keep_ref
  119.9 4.9 %collective-permute-done.13.got_ref = bf16[160,1024]{1,0:T(8,128)(2,1)S(1)} collective-permute-done((bf16[160,1024]{1,0:T(8,128)(2,1)S(1)}, bf16[160,1024]{1,0:T(8,128)(2,1)S(1)}, u32[]{:S(2)}, u32[]{:S(2)}) %collective-permute-start.13) | collective-permute-done | bytes 327712 | tf_op jit(solution)/shard_map/ppermute | solution.py:292
  125.7 2.5 %collective-permute-start.14 = (bf16[64,1024]{1,0:T(8,128)(2,1)S(1)}, bf16[64,1024]{1,0:T(8,128)(2,1)S(1)}, u32[]{:S(2)}, u32[]{:S(2)}) collective-permute-start(bf16[64,1024]{1,0:T(8,128)(2,1)S(1)} %get-tuple-element.50), channel_id=1, source_target_pairs={{0,8},{2,10},{4,12},{6,14},{8,0},{10,2},{12,4},{14,6},{16,24},{18,... | collective-permute-start | bytes 393224 | tf_op jit(solution)/shard_map/ppermute | solution.py:292
  128.5 1.0 collective-permute-start.16
  129.5 1.0 shard_map.123.keep_ref
  130.5 1.3 collective-permute-done.30.got_ref
  132.7 2.5 %collective-permute-start.31 = (bf16[64,1024]{1,0:T(8,128)(2,1)S(1)}, bf16[64,1024]{1,0:T(8,128)(2,1)S(1)}, u32[]{:S(2)}, u32[]{:S(2)}) collective-permute-start(bf16[64,1024]{1,0:T(8,128)(2,1)S(1)} %get-tuple-element.66), channel_id=1, source_target_pairs={{0,8},{2,10},{4,12},{6,14},{8,0},{10,2},{12,4},{14,6},{16,24},{18,... | collective-permute-start | bytes 393224 | tf_op jit(solution)/shard_map/ppermute | solution.py:292
  135.5 1.0 collective-permute-start.33
  136.5 4.6 %collective-permute-done.16.refs_2_ = bf16[64,1024]{1,0:T(8,128)(2,1)S(1)} collective-permute-done((bf16[64,1024]{1,0:T(8,128)(2,1)S(1)}, bf16[64,1024]{1,0:T(8,128)(2,1)S(1)}, u32[]{:S(2)}, u32[]{:S(2)}) %collective-permute-start.16) | collective-permute-done | bytes 131104 | tf_op jit(solution)/shard_map/ppermute | solution.py:292
  141.2 10.2 %collective-permute-start.17 = (bf16[64,1024]{1,0:T(8,128)(2,1)S(1)}, bf16[64,1024]{1,0:T(8,128)(2,1)S(1)}, u32[]{:S(2)}, u32[]{:S(2)}) collective-permute-start(bf16[64,1024]{1,0:T(8,128)(2,1)S(1)} %shard_map.118.refs_1_), channel_id=1, source_target_pairs={{2,0},{6,4},{10,8},{14,12},{18,16},{22,20},{26,24},{30,28},{3,1},{... | collective-permute-start | bytes 393224 | tf_op jit(solution)/shard_map/ppermute | solution.py:302
  151.9 1.3 collective-permute-start.34
  153.2 2.6 %collective-permute-done.34.refs_5_ = bf16[64,1024]{1,0:T(8,128)(2,1)S(1)} collective-permute-done((bf16[64,1024]{1,0:T(8,128)(2,1)S(1)}, bf16[64,1024]{1,0:T(8,128)(2,1)S(1)}, u32[]{:S(2)}, u32[]{:S(2)}) %collective-permute-start.34) | collective-permute-done | bytes 131104 | tf_op jit(solution)/shard_map/ppermute | solution.py:302
  155.8 1.3 shard_map.127
  (61 shorter events, 11.3 us)
Async XLA Ops:
  0.0 9.6 %copy-start.4 = (bf16[2048]{0:T(1024)(128)(2,1)S(1)}, bf16[2048]{0:T(1024)(128)(2,1)}, u32[]{:S(2)}) copy-start(bf16[2048]{0:T(1024)(128)(2,1)} %param.15) | copy-start | bytes 12292
  3.0 32.9 %all-to-all-start = ((bf16[16,272,128]{2,1,0:T(8,128)(2,1)}), bf16[16,272,128]{2,1,0:T(8,128)(2,1)S(1)}, u32[]{:S(2)}, u32[]{:S(2)}) async-start(bf16[16,272,128]{2,1,0:T(8,128)(2,1)} %shard_map.109), calls=%async_computation | async-start | bytes 2228224 | tf_op jit(solution)/shard_map/all_to_all | solution.py:313
  9.6 2.8 %collective-permute-start = (bf16[2048]{0:T(1024)(128)(2,1)S(1)}, bf16[2048]{0:T(1024)(128)(2,1)S(1)}, u32[]{:S(2)}, u32[]{:S(2)}) collective-permute-start(bf16[2048]{0:T(1024)(128)(2,1)S(1)} %copy-done.4), channel_id=1, source_target_pairs={{0,1},{1,0},{2,3},{3,2},{4,5},{5,4},{6,7},{7,6},{8,9},{9,8},{10,11... | collective-permute-start | bytes 12296 | tf_op jit(solution)/shard_map/ppermute | solution.py:295
  37.9 5.0 %collective-permute-start.1 = (bf16[512,128]{1,0:T(8,128)(2,1)S(1)}, bf16[512,128]{1,0:T(8,128)(2,1)S(1)}, u32[]{:S(2)}, u32[]{:S(2)}) collective-permute-start(bf16[512,128]{1,0:T(8,128)(2,1)S(1)} %get-tuple-element.41.refs_0_), channel_id=1, source_target_pairs={{0,8},{2,10},{4,12},{6,14},{8,0},{10,2},{12,4},{14,6},{16,24},{18,... | collective-permute-start | bytes 393224 | tf_op jit(solution)/shard_map/ppermute | solution.py:292
  38.0 7.4 %collective-permute-start.2 = (bf16[512,128]{1,0:T(8,128)(2,1)S(1)}, bf16[512,128]{1,0:T(8,128)(2,1)S(1)}, u32[]{:S(2)}, u32[]{:S(2)}) collective-permute-start(bf16[512,128]{1,0:T(8,128)(2,1)S(1)} %get-tuple-element.41.refs_0_), channel_id=1, source_target_pairs={{0,16},{2,18},{4,20},{6,22},{8,24},{10,26},{12,28},{14,30},{16,0},... | collective-permute-start | bytes 393224 | tf_op jit(solution)/shard_map/ppermute | solution.py:292
  39.2 13.2 %collective-permute-start.3 = (bf16[512,128]{1,0:T(8,128)(2,1)S(1)}, bf16[512,128]{1,0:T(8,128)(2,1)S(1)}, u32[]{:S(2)}, u32[]{:S(2)}) collective-permute-start(bf16[512,128]{1,0:T(8,128)(2,1)S(1)} %get-tuple-element.41.refs_0_), channel_id=1, source_target_pairs={{0,24},{2,26},{4,28},{6,30},{8,16},{10,18},{12,20},{14,22},{16,8},... | collective-permute-start | bytes 393224 | tf_op jit(solution)/shard_map/ppermute | solution.py:292
  40.6 36.8 %copy-start.1 = (bf16[1,4096,512]{2,1,0:T(8,128)(2,1)S(1)}, bf16[1,4096,512]{2,1,0:T(8,128)(2,1)}, u32[]{:S(2)}) copy-start(bf16[1,4096,512]{2,1,0:T(8,128)(2,1)} %param.19) | copy-start | bytes 12582916
  53.2 8.1 %collective-permute-start.5 = (bf16[4,320,128]{2,1,0:T(8,128)(2,1)S(1)}, bf16[4,320,128]{2,1,0:T(8,128)(2,1)S(1)}, u32[]{:S(2)}, u32[]{:S(2)}) collective-permute-start(bf16[4,320,128]{2,1,0:T(8,128)(2,1)S(1)} %slice.12), channel_id=1, source_target_pairs={{0,1},{1,0},{2,3},{3,2},{4,5},{5,4},{6,7},{7,6},{8,9},{9,8},{10,11... | collective-permute-start | bytes 983048 | tf_op jit(solution)/shard_map/ppermute | solution.py:295
  54.5 16.1 %collective-permute-start.4 = (bf16[4,384,128]{2,1,0:T(8,128)(2,1)S(1)}, bf16[4,384,128]{2,1,0:T(8,128)(2,1)S(1)}, u32[]{:S(2)}, u32[]{:S(2)}) collective-permute-start(bf16[4,384,128]{2,1,0:T(8,128)(2,1)S(1)} %get-tuple-element.45), channel_id=1, source_target_pairs={{0,4},{2,6},{4,0},{6,2},{8,12},{10,14},{12,8},{14,10},{16,20},{18,... | collective-permute-start | bytes 1179656 | tf_op jit(solution)/shard_map/ppermute | solution.py:292
  55.1 4.1 %collective-permute-start.18 = (bf16[512,128]{1,0:T(8,128)(2,1)S(1)}, bf16[512,128]{1,0:T(8,128)(2,1)S(1)}, u32[]{:S(2)}, u32[]{:S(2)}) collective-permute-start(bf16[512,128]{1,0:T(8,128)(2,1)S(1)} %get-tuple-element.55.refs_0_), channel_id=1, source_target_pairs={{0,8},{2,10},{4,12},{6,14},{8,0},{10,2},{12,4},{14,6},{16,24},{18,... | collective-permute-start | bytes 393224 | tf_op jit(solution)/shard_map/ppermute | solution.py:292
  55.1 21.1 %collective-permute-start.7 = (bf16[4,384,128]{2,1,0:T(8,128)(2,1)S(1)}, bf16[4,384,128]{2,1,0:T(8,128)(2,1)S(1)}, u32[]{:S(2)}, u32[]{:S(2)}) collective-permute-start(bf16[4,384,128]{2,1,0:T(8,128)(2,1)S(1)} %get-tuple-element.44.refs_0_), channel_id=1, source_target_pairs={{0,2},{2,0},{4,6},{6,4},{8,10},{10,8},{12,14},{14,12},{16,18},{18,... | collective-permute-start | bytes 1179656 | tf_op jit(solution)/shard_map/ppermute | solution.py:292
  56.5 18.1 %collective-permute-start.6 = (bf16[4,320,128]{2,1,0:T(8,128)(2,1)S(1)}, bf16[4,320,128]{2,1,0:T(8,128)(2,1)S(1)}, u32[]{:S(2)}, u32[]{:S(2)}) collective-permute-start(bf16[4,320,128]{2,1,0:T(8,128)(2,1)S(1)} %slice.13), channel_id=1, source_target_pairs={{0,5},{1,4},{2,7},{3,6},{4,1},{5,0},{6,3},{7,2},{8,13},{9,12},{10,... | collective-permute-start | bytes 983048 | tf_op jit(solution)/shard_map/ppermute | solution.py:299
  59.2 5.9 %collective-permute-start.19 = (bf16[512,128]{1,0:T(8,128)(2,1)S(1)}, bf16[512,128]{1,0:T(8,128)(2,1)S(1)}, u32[]{:S(2)}, u32[]{:S(2)}) collective-permute-start(bf16[512,128]{1,0:T(8,128)(2,1)S(1)} %get-tuple-element.55.refs_0_), channel_id=1, source_target_pairs={{0,16},{2,18},{4,20},{6,22},{8,24},{10,26},{12,28},{14,30},{16,0},... | collective-permute-start | bytes 393224 | tf_op jit(solution)/shard_map/ppermute | solution.py:292
  61.3 15.1 %collective-permute-start.9 = (bf16[4,320,128]{2,1,0:T(8,128)(2,1)S(1)}, bf16[4,320,128]{2,1,0:T(8,128)(2,1)S(1)}, u32[]{:S(2)}, u32[]{:S(2)}) collective-permute-start(bf16[4,320,128]{2,1,0:T(8,128)(2,1)S(1)} %collective-permute-done.5.refs_2_), channel_id=1, source_target_pairs={{0,2},{2,0},{4,6},{6,4},{8,10},{10,8},{12,14},{14,12},{16,18},{18,... | collective-permute-start | bytes 983048 | tf_op jit(solution)/shard_map/ppermute | solution.py:292
  65.2 7.9 %collective-permute-start.20 = (bf16[512,128]{1,0:T(8,128)(2,1)S(1)}, bf16[512,128]{1,0:T(8,128)(2,1)S(1)}, u32[]{:S(2)}, u32[]{:S(2)}) collective-permute-start(bf16[512,128]{1,0:T(8,128)(2,1)S(1)} %get-tuple-element.55.refs_0_), channel_id=1, source_target_pairs={{0,24},{2,26},{4,28},{6,30},{8,16},{10,18},{12,20},{14,22},{16,8},... | collective-permute-start | bytes 393224 | tf_op jit(solution)/shard_map/ppermute | solution.py:292
  70.6 6.9 %collective-permute-start.8 = (bf16[4,384,128]{2,1,0:T(8,128)(2,1)S(1)}, bf16[4,384,128]{2,1,0:T(8,128)(2,1)S(1)}, u32[]{:S(2)}, u32[]{:S(2)}) collective-permute-start(bf16[4,384,128]{2,1,0:T(8,128)(2,1)S(1)} %collective-permute-done.4.refs_1_), channel_id=1, source_target_pairs={{0,2},{2,0},{4,6},{6,4},{8,10},{10,8},{12,14},{14,12},{16,18},{18,... | collective-permute-start | bytes 1179656 | tf_op jit(solution)/shard_map/ppermute | solution.py:292
  73.9 18.3 %collective-permute-start.21 = (bf16[4,384,128]{2,1,0:T(8,128)(2,1)S(1)}, bf16[4,384,128]{2,1,0:T(8,128)(2,1)S(1)}, u32[]{:S(2)}, u32[]{:S(2)}) collective-permute-start(bf16[4,384,128]{2,1,0:T(8,128)(2,1)S(1)} %get-tuple-element.57), channel_id=1, source_target_pairs={{0,4},{2,6},{4,0},{6,2},{8,12},{10,14},{12,8},{14,10},{16,20},{18,... | collective-permute-start | bytes 1179656 | tf_op jit(solution)/shard_map/ppermute | solution.py:292
  74.6 2.8 %collective-permute-start.10 = (bf16[4,320,128]{2,1,0:T(8,128)(2,1)S(1)}, bf16[4,320,128]{2,1,0:T(8,128)(2,1)S(1)}, u32[]{:S(2)}, u32[]{:S(2)}) collective-permute-start(bf16[4,320,128]{2,1,0:T(8,128)(2,1)S(1)} %collective-permute-done.6.refs_3_), channel_id=1, source_target_pairs={{0,2},{2,0},{4,6},{6,4},{8,10},{10,8},{12,14},{14,12},{16,18},{18,... | collective-permute-start | bytes 983048 | tf_op jit(solution)/shard_map/ppermute | solution.py:292
  76.3 9.4 %collective-permute-start.22 = (bf16[4,320,128]{2,1,0:T(8,128)(2,1)S(1)}, bf16[4,320,128]{2,1,0:T(8,128)(2,1)S(1)}, u32[]{:S(2)}, u32[]{:S(2)}) collective-permute-start(bf16[4,320,128]{2,1,0:T(8,128)(2,1)S(1)} %slice.14), channel_id=1, source_target_pairs={{0,1},{1,0},{2,3},{3,2},{4,5},{5,4},{6,7},{7,6},{8,9},{9,8},{10,11... | collective-permute-start | bytes 983048 | tf_op jit(solution)/shard_map/ppermute | solution.py:295
  76.4 15.8 %collective-permute-start.23 = (bf16[4,320,128]{2,1,0:T(8,128)(2,1)S(1)}, bf16[4,320,128]{2,1,0:T(8,128)(2,1)S(1)}, u32[]{:S(2)}, u32[]{:S(2)}) collective-permute-start(bf16[4,320,128]{2,1,0:T(8,128)(2,1)S(1)} %slice.15), channel_id=1, source_target_pairs={{0,5},{1,4},{2,7},{3,6},{4,1},{5,0},{6,3},{7,2},{8,13},{9,12},{10,... | collective-permute-start | bytes 983048 | tf_op jit(solution)/shard_map/ppermute | solution.py:299
  77.5 2.2 %copy-start.2 = (bf16[1,4096,512]{2,1,0:T(8,128)(2,1)S(1)}, bf16[1,4096,512]{2,1,0:T(8,128)(2,1)}, u32[]{:S(2)}) copy-start(bf16[1,4096,512]{2,1,0:T(8,128)(2,1)} %param.20) | copy-start | bytes 12582916
  79.6 16.2 %copy-start.3 = (bf16[1,4096,512]{2,1,0:T(8,128)(2,1)S(1)}, bf16[1,4096,512]{2,1,0:T(8,128)(2,1)}, u32[]{:S(2)}) copy-start(bf16[1,4096,512]{2,1,0:T(8,128)(2,1)} %param.20) | copy-start | bytes 12582916
  92.2 10.3 %copy-start = (bf16[1,1024,2048]{2,1,0:T(8,128)(2,1)S(1)}, bf16[1,1024,2048]{2,1,0:T(8,128)(2,1)}, u32[]{:S(2)}) copy-start(bf16[1,1024,2048]{2,1,0:T(8,128)(2,1)} %param.21) | copy-start | bytes 12582916
  92.2 3.7 %collective-permute-start.24 = (bf16[4,384,128]{2,1,0:T(8,128)(2,1)S(1)}, bf16[4,384,128]{2,1,0:T(8,128)(2,1)S(1)}, u32[]{:S(2)}, u32[]{:S(2)}) collective-permute-start(bf16[4,384,128]{2,1,0:T(8,128)(2,1)S(1)} %get-tuple-element.58.refs_0_), channel_id=1, source_target_pairs={{0,2},{2,0},{4,6},{6,4},{8,10},{10,8},{12,14},{14,12},{16,18},{18,... | collective-permute-start | bytes 1179656 | tf_op jit(solution)/shard_map/ppermute | solution.py:292
  93.0 2.9 %collective-permute-start.25 = (bf16[4,384,128]{2,1,0:T(8,128)(2,1)S(1)}, bf16[4,384,128]{2,1,0:T(8,128)(2,1)S(1)}, u32[]{:S(2)}, u32[]{:S(2)}) collective-permute-start(bf16[4,384,128]{2,1,0:T(8,128)(2,1)S(1)} %collective-permute-done.21.refs_1_), channel_id=1, source_target_pairs={{0,2},{2,0},{4,6},{6,4},{8,10},{10,8},{12,14},{14,12},{16,18},{18,... | collective-permute-start | bytes 1179656 | tf_op jit(solution)/shard_map/ppermute | solution.py:292
  93.1 2.3 %collective-permute-start.26 = (bf16[4,320,128]{2,1,0:T(8,128)(2,1)S(1)}, bf16[4,320,128]{2,1,0:T(8,128)(2,1)S(1)}, u32[]{:S(2)}, u32[]{:S(2)}) collective-permute-start(bf16[4,320,128]{2,1,0:T(8,128)(2,1)S(1)} %collective-permute-done.22.refs_2_), channel_id=1, source_target_pairs={{0,2},{2,0},{4,6},{6,4},{8,10},{10,8},{12,14},{14,12},{16,18},{18,... | collective-permute-start | bytes 983048 | tf_op jit(solution)/shard_map/ppermute | solution.py:292
  93.5 2.3 %collective-permute-start.27 = (bf16[4,320,128]{2,1,0:T(8,128)(2,1)S(1)}, bf16[4,320,128]{2,1,0:T(8,128)(2,1)S(1)}, u32[]{:S(2)}, u32[]{:S(2)}) collective-permute-start(bf16[4,320,128]{2,1,0:T(8,128)(2,1)S(1)} %collective-permute-done.23.refs_3_), channel_id=1, source_target_pairs={{0,2},{2,0},{4,6},{6,4},{8,10},{10,8},{12,14},{14,12},{16,18},{18,... | collective-permute-start | bytes 983048 | tf_op jit(solution)/shard_map/ppermute | solution.py:292
  93.6 9.0 %collective-permute-start.11 = (bf16[320,512]{1,0:T(8,128)(2,1)S(1)}, bf16[320,512]{1,0:T(8,128)(2,1)S(1)}, u32[]{:S(2)}, u32[]{:S(2)}) collective-permute-start(bf16[320,512]{1,0:T(8,128)(2,1)S(1)} %get-tuple-element.48.own_ref), channel_id=1, source_target_pairs={{0,1},{1,0},{2,3},{3,2},{4,5},{5,4},{6,7},{7,6},{8,9},{9,8},{10,11... | collective-permute-start | bytes 983048 | tf_op jit(solution)/shard_map/ppermute | solution.py:295
  101.3 9.0 %collective-permute-start.28 = (bf16[320,512]{1,0:T(8,128)(2,1)S(1)}, bf16[320,512]{1,0:T(8,128)(2,1)S(1)}, u32[]{:S(2)}, u32[]{:S(2)}) collective-permute-start(bf16[320,512]{1,0:T(8,128)(2,1)S(1)} %get-tuple-element.64.own_ref), channel_id=1, source_target_pairs={{0,1},{1,0},{2,3},{3,2},{4,5},{5,4},{6,7},{7,6},{8,9},{9,8},{10,11... | collective-permute-start | bytes 983048 | tf_op jit(solution)/shard_map/ppermute | solution.py:295
  103.9 10.5 %collective-permute-start.12 = (bf16[320,1024]{1,0:T(8,128)(2,1)S(1)}, bf16[320,1024]{1,0:T(8,128)(2,1)S(1)}, u32[]{:S(2)}, u32[]{:S(2)}) collective-permute-start(bf16[320,1024]{1,0:T(8,128)(2,1)S(1)} %shard_map.114), channel_id=1, source_target_pairs={{0,2},{2,0},{4,6},{6,4},{8,10},{10,8},{12,14},{14,12},{16,18},{18,... | collective-permute-start | bytes 1966088 | tf_op jit(solution)/shard_map/ppermute | solution.py:292
  111.7 6.5 %collective-permute-start.29 = (bf16[320,1024]{1,0:T(8,128)(2,1)S(1)}, bf16[320,1024]{1,0:T(8,128)(2,1)S(1)}, u32[]{:S(2)}, u32[]{:S(2)}) collective-permute-start(bf16[320,1024]{1,0:T(8,128)(2,1)S(1)} %shard_map.122), channel_id=1, source_target_pairs={{0,2},{2,0},{4,6},{6,4},{8,10},{10,8},{12,14},{14,12},{16,18},{18,... | collective-permute-start | bytes 1966088 | tf_op jit(solution)/shard_map/ppermute | solution.py:292
  115.0 9.7 %collective-permute-start.13 = (bf16[160,1024]{1,0:T(8,128)(2,1)S(1)}, bf16[160,1024]{1,0:T(8,128)(2,1)S(1)}, u32[]{:S(2)}, u32[]{:S(2)}) collective-permute-start(bf16[160,1024]{1,0:T(8,128)(2,1)S(1)} %shard_map.116), channel_id=1, source_target_pairs={{0,4},{2,6},{4,0},{6,2},{8,12},{10,14},{12,8},{14,10},{16,20},{18,... | collective-permute-start | bytes 983048 | tf_op jit(solution)/shard_map/ppermute | solution.py:292
  118.8 13.0 %collective-permute-start.30 = (bf16[160,1024]{1,0:T(8,128)(2,1)S(1)}, bf16[160,1024]{1,0:T(8,128)(2,1)S(1)}, u32[]{:S(2)}, u32[]{:S(2)}) collective-permute-start(bf16[160,1024]{1,0:T(8,128)(2,1)S(1)} %shard_map.124), channel_id=1, source_target_pairs={{0,4},{2,6},{4,0},{6,2},{8,12},{10,14},{12,8},{14,10},{16,20},{18,... | collective-permute-start | bytes 983048 | tf_op jit(solution)/shard_map/ppermute | solution.py:292
  125.7 9.8 %collective-permute-start.14 = (bf16[64,1024]{1,0:T(8,128)(2,1)S(1)}, bf16[64,1024]{1,0:T(8,128)(2,1)S(1)}, u32[]{:S(2)}, u32[]{:S(2)}) collective-permute-start(bf16[64,1024]{1,0:T(8,128)(2,1)S(1)} %get-tuple-element.50), channel_id=1, source_target_pairs={{0,8},{2,10},{4,12},{6,14},{8,0},{10,2},{12,4},{14,6},{16,24},{18,... | collective-permute-start | bytes 393224 | tf_op jit(solution)/shard_map/ppermute | solution.py:292
  128.2 8.3 %collective-permute-start.15 = (bf16[64,1024]{1,0:T(8,128)(2,1)S(1)}, bf16[64,1024]{1,0:T(8,128)(2,1)S(1)}, u32[]{:S(2)}, u32[]{:S(2)}) collective-permute-start(bf16[64,1024]{1,0:T(8,128)(2,1)S(1)} %get-tuple-element.51), channel_id=1, source_target_pairs={{0,16},{2,18},{4,20},{6,22},{8,24},{10,26},{12,28},{14,30},{16,0},... | collective-permute-start | bytes 393224 | tf_op jit(solution)/shard_map/ppermute | solution.py:292
  128.5 12.6 %collective-permute-start.16 = (bf16[64,1024]{1,0:T(8,128)(2,1)S(1)}, bf16[64,1024]{1,0:T(8,128)(2,1)S(1)}, u32[]{:S(2)}, u32[]{:S(2)}) collective-permute-start(bf16[64,1024]{1,0:T(8,128)(2,1)S(1)} %get-tuple-element.52), channel_id=1, source_target_pairs={{0,24},{2,26},{4,28},{6,30},{8,16},{10,18},{12,20},{14,22},{16,8},... | collective-permute-start | bytes 393224 | tf_op jit(solution)/shard_map/ppermute | solution.py:292
  132.7 18.6 %collective-permute-start.31 = (bf16[64,1024]{1,0:T(8,128)(2,1)S(1)}, bf16[64,1024]{1,0:T(8,128)(2,1)S(1)}, u32[]{:S(2)}, u32[]{:S(2)}) collective-permute-start(bf16[64,1024]{1,0:T(8,128)(2,1)S(1)} %get-tuple-element.66), channel_id=1, source_target_pairs={{0,8},{2,10},{4,12},{6,14},{8,0},{10,2},{12,4},{14,6},{16,24},{18,... | collective-permute-start | bytes 393224 | tf_op jit(solution)/shard_map/ppermute | solution.py:292
  135.2 16.1 %collective-permute-start.32 = (bf16[64,1024]{1,0:T(8,128)(2,1)S(1)}, bf16[64,1024]{1,0:T(8,128)(2,1)S(1)}, u32[]{:S(2)}, u32[]{:S(2)}) collective-permute-start(bf16[64,1024]{1,0:T(8,128)(2,1)S(1)} %get-tuple-element.67), channel_id=1, source_target_pairs={{0,16},{2,18},{4,20},{6,22},{8,24},{10,26},{12,28},{14,30},{16,0},... | collective-permute-start | bytes 393224 | tf_op jit(solution)/shard_map/ppermute | solution.py:292
  135.5 16.4 %collective-permute-start.33 = (bf16[64,1024]{1,0:T(8,128)(2,1)S(1)}, bf16[64,1024]{1,0:T(8,128)(2,1)S(1)}, u32[]{:S(2)}, u32[]{:S(2)}) collective-permute-start(bf16[64,1024]{1,0:T(8,128)(2,1)S(1)} %get-tuple-element.68), channel_id=1, source_target_pairs={{0,24},{2,26},{4,28},{6,30},{8,16},{10,18},{12,20},{14,22},{16,8},... | collective-permute-start | bytes 393224 | tf_op jit(solution)/shard_map/ppermute | solution.py:292
  141.2 12.1 %collective-permute-start.17 = (bf16[64,1024]{1,0:T(8,128)(2,1)S(1)}, bf16[64,1024]{1,0:T(8,128)(2,1)S(1)}, u32[]{:S(2)}, u32[]{:S(2)}) collective-permute-start(bf16[64,1024]{1,0:T(8,128)(2,1)S(1)} %shard_map.118.refs_1_), channel_id=1, source_target_pairs={{2,0},{6,4},{10,8},{14,12},{18,16},{22,20},{26,24},{30,28},{3,1},{... | collective-permute-start | bytes 393224 | tf_op jit(solution)/shard_map/ppermute | solution.py:302
  151.9 3.9 %collective-permute-start.34 = (bf16[64,1024]{1,0:T(8,128)(2,1)S(1)}, bf16[64,1024]{1,0:T(8,128)(2,1)S(1)}, u32[]{:S(2)}, u32[]{:S(2)}) collective-permute-start(bf16[64,1024]{1,0:T(8,128)(2,1)S(1)} %shard_map.126.refs_4_), channel_id=1, source_target_pairs={{0,2},{4,6},{8,10},{12,14},{16,18},{20,22},{24,26},{28,30},{1,3},{... | collective-permute-start | bytes 393224 | tf_op jit(solution)/shard_map/ppermute | solution.py:302

commit v4 on v3

--- a/solution.py
+++ b/solution.py
@@ -15,13 +15,14 @@
 META = 16
 LANES = 128
 MIB = 1 << 20
+PARTS = 4
 
 
 def silu(v):
     return v * (0.5 * jnp.tanh(0.5 * v) + 0.5)
 
 
-def call(kernel, out_shape, args, smem=0, hbm=(), scratch=(), vmem=16, flops=0, moved=0):
+def call(kernel, out_shape, args, smem=0, hbm=(), scratch=(), vmem=8, flops=0, moved=0):
     spaces = [pltpu.SMEM if n < smem else pltpu.HBM if n in hbm else pltpu.VMEM for n in range(len(args))]
     several = isinstance(out_shape, (tuple, list))
     out = pl.BlockSpec(memory_space=pltpu.VMEM)
@@ -138,9 +139,10 @@
 
 
 def compact_kernel(idx_ref, pick_ref, *refs):
-    pieces, (mine_ref, theirs_ref) = refs[:-2], refs[-2:]
+    mine_ref, theirs_ref = refs[-2:]
     me = idx_ref[0]
-    levels = len(pieces)
+    levels = mine_ref.shape[0]
+    pieces = refs[:levels]
     slots, span = pick_ref.shape[1] // 2, pick_ref.shape[2]
     tok = span // levels
     z, y = lax.div(me, 4), lax.rem(lax.div(me, 2), 2)
@@ -157,80 +159,125 @@
             out_ref[k, 2 * slots :, :] = pieces[k][own, :]
 
 
-def gate_up_kernel(places, heads, idx_ref, wg_ref, wu_ref, gain_ref, *refs):
-    pieces, (hidden_ref, hand_ref, lhs_ref) = refs[: len(places)], refs[len(places) :]
-    me, plane = idx_ref[0], idx_ref[1]
-    rows, tok = hidden_ref.shape[0], hand_ref.shape[0]
-    width = min(256, wg_ref.shape[1])
+def thirds(value):
+    high = value.astype(jnp.bfloat16)
+    rest = value - high.astype(jnp.float32)
+    middle = rest.astype(jnp.bfloat16)
+    return high, middle, (rest - middle.astype(jnp.float32)).astype(jnp.bfloat16)
+
+
+def scale_kernel(places, idx_ref, gain_ref, *refs):
+    pieces, out_ref = refs[: len(places)], refs[-1]
+    me = idx_ref[0]
+    heads = gain_ref.shape[1] // HD
+    rows, tok = pieces[-1].shape[1], pieces[0].shape[1] - pieces[-1].shape[1]
+    width = sum(map(len, places)) * HD
     tile = rows // 2
-    for ref, entries in zip(pieces, places):
-        for k, (other, mask) in enumerate(entries):
-            if not other:
-                at = pl.multiple_of((me ^ mask) * HD, HD)
-                hand_ref[:, pl.ds(at, HD)] = ref[k, rows : rows + tok, :]
-
-    def normalise(r, carry):
-        here = pl.ds(pl.multiple_of(r * tile, tile), tile)
+    for r in range(rows // tile):
+        here = slice(r * tile, (r + 1) * tile)
         squares = jnp.zeros((tile, HD), jnp.float32)
+        n = 0
         for ref, entries in zip(pieces, places):
-            for k in range(len(entries)):
+            for k, (other, low, back) in enumerate(entries):
+                head = lax.rem((me ^ low) + heads - 4 * back, heads)
+                gain = gain_ref[other : other + 1, pl.ds(pl.multiple_of(head * HD, HD), HD)]
                 v = ref[k, here, :].astype(jnp.float32)
                 squares = squares + v * v
-        scale = lax.rsqrt(jnp.sum(squares, axis=1, keepdims=True) / D + EPS)
-        for ref, entries in zip(pieces, places):
-            for k, (other, mask) in enumerate(entries):
-                head = me ^ mask
-                at = pl.multiple_of(((plane ^ other) * heads + head) * HD, HD)
-                gain = gain_ref[other : other + 1, pl.ds(pl.multiple_of(head * HD, HD), HD)]
-                v = ref[k, here, :].astype(jnp.float32) * scale * gain
-                lhs_ref[here, pl.ds(at, HD)] = v.astype(jnp.bfloat16)
-        return carry
-
-    lax.fori_loop(0, rows // tile, normalise, 0)
+                out_ref[here, n : n + HD] = (v * gain).astype(jnp.bfloat16)
+                if not other and r == 0:
+                    out_ref[rows:, n : n + HD] = ref[k, rows : rows + tok, :]
+                n += HD
+        lane = lax.broadcasted_iota(jnp.int32, (tile, HD), 1)
+        high, middle, low = thirds(jnp.broadcast_to(jnp.sum(squares, axis=1, keepdims=True), (tile, HD)))
+        parts = jnp.where(lane == 0, high, jnp.where(lane == 1, middle, jnp.where(lane == 2, low, 0)))
+        out_ref[here, width:] = parts.astype(jnp.bfloat16)
+
+
+def row_offsets(places, heads, me, plane, flip):
+    found = []
+    for other, low, back in (entry for entries in places for entry in entries):
+        head = lax.rem((me ^ low ^ flip) + heads - 4 * back, heads)
+        found.append((other, pl.multiple_of(head * HD, HD), pl.multiple_of(((plane ^ other) * heads + head) * HD, HD)))
+    return found
+
+
+def half_projection(lhs, offsets, weight_ref, cols):
+    weights = jnp.concatenate([weight_ref[pl.ds(at, HD), cols] for *_, at in offsets], axis=0)
+    return jnp.dot(lhs, weights, preferred_element_type=jnp.float32)
+
+
+def first_kernel(places, heads, idx_ref, wg_ref, wu_ref, lhs_ref, gate_ref, up_ref):
+    rows = gate_ref.shape[0]
+    offsets = row_offsets(places, heads, idx_ref[0], idx_ref[1], 0)
+    width = min(256, wg_ref.shape[1])
     for n in range(wg_ref.shape[1] // width):
         cols = slice(n * width, (n + 1) * width)
-        gate = jnp.dot(lhs_ref[...], wg_ref[:, cols], preferred_element_type=jnp.float32)
-        up = jnp.dot(lhs_ref[...], wu_ref[:, cols], preferred_element_type=jnp.float32)
+        lhs = lhs_ref[0:rows, 0 : len(offsets) * HD]
+        gate_ref[:, cols] = half_projection(lhs, offsets, wg_ref, cols)
+        up_ref[:, cols] = half_projection(lhs, offsets, wu_ref, cols)
+
+
+def second_kernel(places, heads, idx_ref, wg_ref, wu_ref, own_ref, lhs_ref, gate_ref, up_ref, hidden_ref, hand_ref):
+    rows = gate_ref.shape[0]
+    me, plane = idx_ref[0], idx_ref[1]
+    for flip, ref in enumerate((own_ref, lhs_ref)):
+        for n, (other, at, _) in enumerate(row_offsets(places, heads, me, plane, flip)):
+            if not other:
+                hand_ref[:, pl.ds(at, HD)] = ref[rows:, n * HD : (n + 1) * HD]
+    offsets = row_offsets(places, heads, me, plane, 1)
+    last = len(offsets) * HD
+    squares = own_ref[0:rows, last:].astype(jnp.float32) + lhs_ref[0:rows, last:].astype(jnp.float32)
+    scale = lax.rsqrt(jnp.sum(squares, axis=1, keepdims=True) / D + EPS)
+    width = min(256, wg_ref.shape[1])
+    for n in range(wg_ref.shape[1] // width):
+        cols = slice(n * width, (n + 1) * width)
+        lhs = lhs_ref[0:rows, 0:last]
+        gate = (gate_ref[:, cols] + half_projection(lhs, offsets, wg_ref, cols)) * scale
+        up = (up_ref[:, cols] + half_projection(lhs, offsets, wu_ref, cols)) * scale
         hidden_ref[:, cols] = (silu(gate) * up).astype(jnp.bfloat16)
 
 
-def down_kernel(flip, idx_ref, wd_ref, own_ref, peer_ref, out_ref):
+def down_kernel(flip, parts, idx_ref, wd_ref, own_ref, peer_ref, *refs):
+    out_refs = refs[-parts:]
     core, plane = lax.rem(idx_ref[0], 2), idx_ref[1]
-    depth, total_width = own_ref.shape[1], out_ref.shape[1]
-    width = min(512, total_width)
+    depth, width = own_ref.shape[1], out_refs[0].shape[1]
+    total_width = parts * width
     first = (core ^ flip) * total_width
     own_rows = pl.ds(pl.multiple_of(plane * depth, depth), depth)
     peer_rows = pl.ds(pl.multiple_of((1 - plane) * depth, depth), depth)
-    for n in range(total_width // width):
+    for n, out_ref in enumerate(out_refs):
         cols = pl.ds(pl.multiple_of(first + n * width, width), width)
         total = jnp.dot(own_ref[...], wd_ref[own_rows, cols], preferred_element_type=jnp.float32)
         total = total + jnp.dot(peer_ref[...], wd_ref[peer_rows, cols], preferred_element_type=jnp.float32)
-        out_ref[:, n * width : (n + 1) * width] = total.astype(jnp.bfloat16)
-
-
-def pair_kernel(idx_ref, own_ref, other_ref, send_ref):
+        out_ref[...] = total.astype(jnp.bfloat16)
+
+
+def pair_kernel(parts, idx_ref, *refs):
+    send_ref = refs[-1]
     slots = send_ref.shape[0]
     y = lax.rem(lax.div(idx_ref[0], 2), 2)
     theirs = pl.ds(pl.multiple_of((1 - y) * slots, slots), slots)
-    both = own_ref[theirs, :].astype(jnp.float32) + other_ref[theirs, :].astype(jnp.float32)
-    send_ref[...] = both.astype(jnp.bfloat16)
+    width = refs[0].shape[1]
+    for n in range(parts):
+        both = refs[n][theirs, :].astype(jnp.float32) + refs[parts + n][theirs, :].astype(jnp.float32)
+        send_ref[:, n * width : (n + 1) * width] = both.astype(jnp.bfloat16)
 
 
 def spread(pick, rows):
     return lax.dot_general(pick, rows, (((0,), (0,)), ((), ())), preferred_element_type=jnp.float32)
 
 
-def weigh_kernel(idx_ref, pick_ref, gate_ref, own_ref, other_ref, keep_ref):
+def weigh_kernel(parts, idx_ref, pick_ref, gate_ref, *refs):
     slots, span = pick_ref.shape[1] // 2, pick_ref.shape[2]
     y = lax.rem(lax.div(idx_ref[0], 2), 2)
     mine = pl.ds(pl.multiple_of(y * slots, slots), slots)
     gate = gate_ref[0, pl.ds(pl.multiple_of(y * span, span), span), :]
     pick = pick_ref[0, mine, :]
-    width = 4 * LANES
-    for n in range(own_ref.shape[1] // width):
+    width = refs[0].shape[1]
+    for n in range(parts):
         cols = slice(n * width, (n + 1) * width)
-        total = spread(pick, own_ref[mine, cols]) + spread(pick, other_ref[mine, cols])
-        keep_ref[:, cols] = total * jnp.concatenate([gate] * (width // LANES), axis=1)
+        total = spread(pick, refs[n][mine, :]) + spread(pick, refs[parts + n][mine, :])
+        refs[-1][:, cols] = total * jnp.concatenate([gate] * (width // LANES), axis=1)
 
 
 def add_kernel(idx_ref, pick_ref, gate_ref, keep_ref, got_ref, own_ref, *refs):
@@ -247,7 +294,8 @@
         total_ref[:, cols] = keep_ref[:, cols] + more
     own_ref[...] = total_ref[pl.ds(pl.multiple_of(z * tok, tok), tok), :]
     for k, ref in enumerate(send_refs, 1):
-        ref[...] = total_ref[pl.ds(pl.multiple_of((z ^ k) * tok, tok), tok), :].astype(jnp.bfloat16)
+        there = lax.rem(z + k, len(send_refs) + 1)
+        ref[...] = total_ref[pl.ds(pl.multiple_of(there * tok, tok), tok), :].astype(jnp.bfloat16)
 
 
 def sum_kernel(own_ref, *refs):
@@ -290,6 +338,9 @@
 
     def over_ctx(x, mask, core=None):
         return lax.ppermute(x, "ctx", [(c, c ^ mask) for c in range(ctx) if core is None or c % 2 == core])
+
+    def along_z(x, steps):
+        return lax.ppermute(x, "ctx", [(c, (c + 4 * steps) % ctx) for c in range(ctx)])
 
     def over_tp(x):
         return lax.ppermute(x, "tp", [(0, 1), (1, 0)])
@@ -320,50 +371,68 @@
         [shape(rows, HD)] * 2 + [shape(2, 2 * slots, span)] * 2 + [shape(2, 2 * span, LANES, dtype=f32)] * 2,
         (arrived,),
     )
-    masks = [4 * k for k in range(levels)]
     half = width // 2
-    results, waited = [], None
-    for core in range(2):
-        hand, pick, gates = hands[core::2]
-        if waited is not None:
-            hand, waited = lax.optimization_barrier((hand, waited))
-        column = [hand] + [over_ctx(hand, m) for m in masks[1:]]
-        if waited is None:
-            column[:-1] = lax.optimization_barrier(column[:-1])
-            waited = column[0]
-        mine, theirs = call(compact_kernel, [shape(levels, 2 * slots + tok, HD)] * 2, (idx, pick, *column), smem=1)
-        pieces = [over_ctx(theirs, 2), over_tp(mine[:, : 2 * slots]), across(theirs[:, : 2 * slots])]
-        pieces = [mine] + pieces
-        if core:
-            *pieces, hidden = lax.optimization_barrier((*pieces, hidden))
-        places = [[(t, m ^ f) for m in masks] for t, f in ((0, 0), (0, 2), (1, 0), (1, 2))]
-        pieces += [over_ctx(p, 1) for p in pieces]
-        places += [[(t, m ^ 1) for t, m in entry] for entry in places]
+    columns = []
+    for hand in hands[:2]:
+        if columns:
+            hand, columns[0][1] = lax.optimization_barrier((hand, columns[0][1]))
+        columns.append([hand] + [along_z(hand, k) for k in range(1, levels)])
+    places = [[(t, f, k) for k in range(levels)] for t, f in ((0, 0), (0, 2), (1, 0), (1, 2))]
+    pieces, compacted = [], []
+    for pick, column in zip(hands[2:4], columns):
+        mine, theirs = call(
+            compact_kernel, [shape(levels, 2 * slots + tok, HD)] * 2, (idx, pick, *column, *compacted), smem=1
+        )
+        compacted = [theirs]
+        pieces.append([mine, over_ctx(theirs, 2), over_tp(mine[:, : 2 * slots]), across(theirs[:, : 2 * slots])])
+    fronts, after = [], pieces[1][0]
+    for got in pieces:
+        mixed = call(
+            functools.partial(scale_kernel, places),
+            shape(2 * slots + tok, (4 * levels + 1) * HD),
+            (idx, gain, *got, after),
+            smem=1,
+        )
+        sums = call(
+            functools.partial(first_kernel, places, heads),
+            [shape(2 * slots, hidden_width, dtype=f32)] * 2,
+            (idx, wg, wu, mixed),
+            smem=1,
+        )
         hidden, own_hand = call(
-            functools.partial(gate_up_kernel, places, heads),
+            functools.partial(second_kernel, places, heads),
             [shape(2 * slots, hidden_width), shape(tok, width)],
-            (idx, wg, wu, gain, *pieces),
+            (idx, wg, wu, mixed, over_ctx(mixed, 1), *sums),
             smem=1,
-            scratch=[pltpu.VMEM((2 * slots, D), bf16)],
-            flops=8 * slots * D * hidden_width,
-            moved=2 * (2 * slots * D + 2 * D * hidden_width),
-        )
-        peer = over_tp(hidden)
-
-        def down(flip):
-            return call(
-                functools.partial(down_kernel, flip),
-                shape(2 * slots, half),
-                (idx, wd, hidden, peer),
-                smem=1,
-                flops=4 * slots * wd.shape[0] * half,
-                moved=2 * (2 * slots * half + wd.shape[0] * half),
-            )
-
-        other = over_ctx(down(1), 1)
-        half_out = down(0)
-        got = over_ctx(call(pair_kernel, shape(slots, half), (idx, half_out, other), smem=1), 2)
-        keep = call(weigh_kernel, shape(span, half, dtype=f32), (idx, pick, gates, half_out, other), smem=1)
+        )
+        fronts.append((hidden, over_tp(hidden), own_hand))
+        after = hidden
+    half = width // 2
+    results, after, added = [], [fronts[1][0]], [fronts[1][1]]
+
+    def down(flip, *args):
+        return call(
+            functools.partial(down_kernel, flip, PARTS),
+            [shape(2 * slots, half // PARTS)] * PARTS,
+            (idx, wd, *args),
+            smem=1,
+        )
+
+    for core, (hidden, peer, own_hand) in enumerate(fronts):
+        pick, gates = hands[2 + core], hands[4 + core]
+        other = [over_ctx(part, 1) for part in down(1, hidden, peer, *after)]
+        half_out = down(0, hidden, peer)
+        send = call(
+            functools.partial(pair_kernel, PARTS), shape(slots, half), (idx, *half_out, *other, *added), smem=1
+        )
+        after = [send]
+        got = over_ctx(send, 2)
+        keep = call(
+            functools.partial(weigh_kernel, PARTS),
+            shape(span, half, dtype=f32),
+            (idx, pick, gates, *half_out, *other),
+            smem=1,
+        )
         own, *sends = call(
             add_kernel,
             [shape(tok, half, dtype=f32)] + [shape(tok, half)] * (levels - 1),
@@ -371,7 +440,8 @@
             smem=1,
             scratch=[pltpu.VMEM((span, half), f32)],
         )
-        summed = call(sum_kernel, shape(tok, half), (own, *[over_ctx(s, m) for s, m in zip(sends, masks[1:])]))
+        added = [own]
+        summed = call(sum_kernel, shape(tok, half, dtype=f32), (own, *[along_z(s, k) for k, s in enumerate(sends, 1)]))
         results += [own_hand, summed, to_core(summed, core)]
     return call(final_kernel, shape(tok, width), (idx, *results), smem=1)
 

time: 158 us -> 152 us (0.962)
  starting transfers between devices: 51.8 us -> 37.5 us
  waiting for transfers between devices: 73 us -> 81 us
    ppermute x0 -> x12, waiting for transfers between devices: none -> 33.1 us  [along_z(): lax.ppermute(x, 'ctx', [(c, (c + 4 * steps) % ctx) for c in range(ctx)])]
    ppermute x26 -> x14, waiting for transfers between devices: 31 us -> 5.95 us  [over_ctx(): lax.ppermute(x, 'ctx', [(c, c ^ mask) for c in range(ctx) if core is None...]
    ppermute x26 -> x14, starting transfers between devices: 26.6 us -> 6.65 us  [over_ctx(): lax.ppermute(x, 'ctx', [(c, c ^ mask) for c in range(ctx) if core is None...]
    ppermute x0 -> x12, starting transfers between devices: none -> 11.4 us  [along_z(): lax.ppermute(x, 'ctx', [(c, (c + 4 * steps) % ctx) for c in range(ctx)])]
    ppermute x2, starting transfers between devices: 11.4 us -> 3.8 us  [to_core(): lax.ppermute(x, 'ctx', [(c, c ^ 1) for c in range(ctx) if c % 2 != core])]
    pallas_call x19 -> x23, Pallas kernels: 29.6 us -> 29.5 us  [call(): pl.pallas_call(kernel, out_shape=out_shape, in_specs=[pl.BlockSpec(memory...]
  transfers between devices with their start and end apart: 36 -> 36, of which waited for: 19 -> 19; matrix products, arithmetic and copies ran while one was open for 0% -> 0% of each run, Pallas kernels for 14% -> 13%
where the time goes in v4:
time: 152 us; the launch traced here: 151 us
  waiting for transfers between devices  81 us (53%)
  starting transfers between devices  37.5 us (25%)
  Pallas kernels  29.5 us (19%)
  local copies, waits for them, and re-layouts  2.31 us (2%)
    ppermute x12, waiting for transfers between devices, along_z(): lax.ppermute(x, 'ctx', [(c, (c + 4 * steps) % ctx) for c in range(ctx)])  33.1 us
    pallas_call x23, Pallas kernels, call(): pl.pallas_call(kernel, out_shape=out_shape, in_specs=[pl.BlockSpec(memory...  29.5 us
    all_to_all x1, waiting for transfers between devices, heads_over_ctx(): lax.all_to_all(packed, 'ctx', split_axis=0, concat_axis=0, tiled=True)  23.5 us
    ppermute x12, starting transfers between devices, along_z(): lax.ppermute(x, 'ctx', [(c, (c + 4 * steps) % ctx) for c in range(ctx)])  11.4 us
    ppermute x5, waiting for transfers between devices, over_tp(): return lax.ppermute(x, 'tp', [(0, 1), (1, 0)])  8.14 us
    ppermute x2, waiting for transfers between devices, across(): return lax.ppermute(x, ('ctx', 'tp'), pairs)  8.1 us
    ppermute x14, starting transfers between devices, over_ctx(): lax.ppermute(x, 'ctx', [(c, c ^ mask) for c in range(ctx) if core is None...  6.65 us
    all_to_all x1, starting transfers between devices, heads_over_ctx(): lax.all_to_all(packed, 'ctx', split_axis=0, concat_axis=0, tiled=True)  6.57 us
  transfers between devices with their start and end apart: 36, of which 19 were waited for; matrix products, arithmetic and copies ran while one was open for 0% of the time, Pallas kernels for 13%

profile of v4, /device:TPU:13, one launch (start us, length us, event | category | flops | bytes accessed | tf_op | source)
XLA Modules:
  0.0 150.8 jit_solution(17888780284325739201)
XLA Ops:
  0.0 3.0 %shard_map.109 = bf16[16,272,128]{2,1,0:T(8,128)(2,1)} custom-call(s32[1,64]{1,0:T(1,128)} %bitcast.22, s32[4,64]{1,0:T(4,128)} %bitcast.20, f32[4,64]{1,0:T(4,128)} %bitcast.21, bf16[64,2048]{1,0:T(8,128)(2,1)} %q_ref.1, bf16[64,2048]{1,0:T(8,128)(2,1)} %k_ref.1, bf16[64,2048]{1,0:T(8,128)(2,1)} %v_ref.1, bf16[64,2048]{1,0:T(8,128)(2,1)} %r_ref.1), custom_call_target="tpu_custom_call" | custom-call | tf_op jit(solution)/shard_map/pallas_call | solution.py:29
  3.0 6.6 %all-to-all-start = ((bf16[16,272,128]{2,1,0:T(8,128)(2,1)}), bf16[16,272,128]{2,1,0:T(8,128)(2,1)S(1)}, u32[]{:S(2)}, u32[]{:S(2)}) async-start(bf16[16,272,128]{2,1,0:T(8,128)(2,1)} %shard_map.109), calls=%async_computation | async-start | bytes 2228224 | tf_op jit(solution)/shard_map/all_to_all | solution.py:364
  9.6 1.3 collective-permute-start
  10.9 1.5 %collective-permute-done = bf16[2048]{0:T(1024)(128)(2,1)S(1)} collective-permute-done((bf16[2048]{0:T(1024)(128)(2,1)S(1)}, bf16[2048]{0:T(1024)(128)(2,1)S(1)}, u32[]{:S(2)}, u32[]{:S(2)}) %collective-permute-start) | collective-permute-done | bytes 4128 | tf_op jit(solution)/shard_map/ppermute | solution.py:346
  12.4 23.5 %all-to-all-done.x_ref = bf16[16,272,128]{2,1,0:T(8,128)(2,1)S(1)} async-done(((bf16[16,272,128]{2,1,0:T(8,128)(2,1)}), bf16[16,272,128]{2,1,0:T(8,128)(2,1)S(1)}, u32[]{:S(2)}, u32[]{:S(2)}) %all-to-all-start) | async-done | bytes 1114144 | tf_op jit(solution)/shard_map/all_to_all | solution.py:364
  36.0 2.0 %shard_map.110 = (bf16[512,128]{1,0:T(8,128)(2,1)S(1)}, bf16[512,128]{1,0:T(8,128)(2,1)S(1)}, bf16[2,320,256]{2,1,0:T(8,128)(2,1)S(1)}, bf16[2,320,256]{2,1,0:T(...) custom-call(bf16[16,272,128]{2,1,0:T(8,128)(2,1)S(1)} %all-to-all-done.x_ref), custom_call_target="tpu_custom_call" | custom-call | tf_op jit(solution)/shard_map/pallas_call | solution.py:29
  38.0 1.2 collective-permute-start.2
  39.2 1.4 collective-permute-start.3
  40.6 2.3 %collective-permute-done.1.refs_1_ = bf16[512,128]{1,0:T(8,128)(2,1)S(1)} collective-permute-done((bf16[512,128]{1,0:T(8,128)(2,1)S(1)}, bf16[512,128]{1,0:T(8,128)(2,1)S(1)}, u32[]{:S(2)}, u32[]{:S(2)}) %collective-permute-start.1) | collective-permute-done | bytes 131104 | tf_op jit(solution)/shard_map/ppermute | solution.py:343
  42.9 6.4 %collective-permute-done.2.refs_2_ = bf16[512,128]{1,0:T(8,128)(2,1)S(1)} collective-permute-done((bf16[512,128]{1,0:T(8,128)(2,1)S(1)}, bf16[512,128]{1,0:T(8,128)(2,1)S(1)}, u32[]{:S(2)}, u32[]{:S(2)}) %collective-permute-start.2) | collective-permute-done | bytes 131104 | tf_op jit(solution)/shard_map/ppermute | solution.py:343
  49.3 2.2 %collective-permute-done.3.refs_3_ = bf16[512,128]{1,0:T(8,128)(2,1)S(1)} collective-permute-done((bf16[512,128]{1,0:T(8,128)(2,1)S(1)}, bf16[512,128]{1,0:T(8,128)(2,1)S(1)}, u32[]{:S(2)}, u32[]{:S(2)}) %collective-permute-start.3) | collective-permute-done | bytes 131104 | tf_op jit(solution)/shard_map/ppermute | solution.py:343
  52.5 2.4 %collective-permute-start.6 = (bf16[4,320,128]{2,1,0:T(8,128)(2,1)S(1)}, bf16[4,320,128]{2,1,0:T(8,128)(2,1)S(1)}, u32[]{:S(2)}, u32[]{:S(2)}) collective-permute-start(bf16[4,320,128]{2,1,0:T(8,128)(2,1)S(1)} %slice.13), channel_id=1, source_target_pairs={{0,5},{1,4},{2,7},{3,6},{4,1},{5,0},{6,3},{7,2},{8,13},{9,12},{10,... | collective-permute-start | bytes 983048 | tf_op jit(solution)/shard_map/ppermute | solution.py:350
  57.8 2.6 %collective-permute-done.8.refs_2_ = bf16[512,128]{1,0:T(8,128)(2,1)S(1)} collective-permute-done((bf16[512,128]{1,0:T(8,128)(2,1)S(1)}, bf16[512,128]{1,0:T(8,128)(2,1)S(1)}, u32[]{:S(2)}, u32[]{:S(2)}) %collective-permute-start.8) | collective-permute-done | bytes 131104 | tf_op jit(solution)/shard_map/ppermute | solution.py:343
  60.4 6.3 %collective-permute-done.9.refs_3_ = bf16[512,128]{1,0:T(8,128)(2,1)S(1)} collective-permute-done((bf16[512,128]{1,0:T(8,128)(2,1)S(1)}, bf16[512,128]{1,0:T(8,128)(2,1)S(1)}, u32[]{:S(2)}, u32[]{:S(2)}) %collective-permute-start.9) | collective-permute-done | bytes 131104 | tf_op jit(solution)/shard_map/ppermute | solution.py:343
  67.6 1.7 %collective-permute-done.5.refs_2_ = bf16[4,320,128]{2,1,0:T(8,128)(2,1)S(1)} collective-permute-done((bf16[4,320,128]{2,1,0:T(8,128)(2,1)S(1)}, bf16[4,320,128]{2,1,0:T(8,128)(2,1)S(1)}, u32[]{:S(2)}, u32[]{:S(2)}) %collective-permute-start.5) | collective-permute-done | bytes 327712 | tf_op jit(solution)/shard_map/ppermute | solution.py:346
  70.7 1.4 collective-permute-start.10
  72.2 1.3 collective-permute-start.13
  73.5 1.4 collective-permute-start.14
  74.9 2.2 %copy-done.1 = bf16[1,4096,512]{2,1,0:T(8,128)(2,1)S(1)} copy-done((bf16[1,4096,512]{2,1,0:T(8,128)(2,1)S(1)}, bf16[1,4096,512]{2,1,0:T(8,128)(2,1)}, u32[]{:S(2)}) %copy-start.1) | copy-done | bytes 4194328
  77.1 2.1 %shard_map.114 = (f32[320,512]{1,0:T(8,128)S(1)}, f32[320,512]{1,0:T(8,128)S(1)}) custom-call(s32[2]{0:T(128)S(1)} %pad_add_fusion.idx_ref, bf16[4096,512]{1,0:T(8,128)(2,1)S(1)} %bitcast.8, bf16[4096,512]{1,0:T(8,128)(2,1)S(1)} %bitcast.12, bf16[384,2176]{1,0:T(8,128)(2,1)S(1)} %shard_map.113.lhs_ref.own_ref), custom_call_target="tpu_custom_call" | custom-call | tf_op jit(solution)/shard_map/pallas_call | solution.py:29
  79.2 2.2 %shard_map.115 = (bf16[320,512]{1,0:T(8,128)(2,1)S(1)}, bf16[64,2048]{1,0:T(8,128)(2,1)S(1)}) custom-call(s32[2]{0:T(128)S(1)} %pad_add_fusion.idx_ref, bf16[4096,512]{1,0:T(8,128)(2,1)S(1)} %bitcast.9, bf16[4096,512]{1,0:T(8,128)(2,1)S(1)} %bitcast.13, bf16[384,2176]{1,0:T(8,128)(2,1)S(1)} %shard_map.113.lhs_ref.own_ref, ...), custom_call_target="tpu_custom_call" | custom-call | tf_op jit(solution)/shard_map/pallas_call | solution.py:29
  81.3 8.1 %collective-permute-done.14.refs_3_ = bf16[4,320,128]{2,1,0:T(8,128)(2,1)S(1)} collective-permute-done((bf16[4,320,128]{2,1,0:T(8,128)(2,1)S(1)}, bf16[4,320,128]{2,1,0:T(8,128)(2,1)S(1)}, u32[]{:S(2)}, u32[]{:S(2)}) %collective-permute-start.14) | collective-permute-done | bytes 327712 | tf_op jit(solution)/shard_map/ppermute | solution.py:350
  89.4 1.0 shard_map.117.lhs_ref.own_ref
  90.5 1.3 collective-permute-start.15
  91.8 1.2 collective-permute-start.11
  93.0 2.1 %shard_map.118 = (f32[320,512]{1,0:T(8,128)S(1)}, f32[320,512]{1,0:T(8,128)S(1)}) custom-call(s32[2]{0:T(128)S(1)} %pad_add_fusion.idx_ref, bf16[4096,512]{1,0:T(8,128)(2,1)S(1)} %bitcast.10, bf16[4096,512]{1,0:T(8,128)(2,1)S(1)} %bitcast.14, bf16[384,2176]{1,0:T(8,128)(2,1)S(1)} %shard_map.117.lhs_ref.own_ref), custom_call_target="tpu_custom_call" | custom-call | tf_op jit(solution)/shard_map/pallas_call | solution.py:29
  95.1 2.2 %shard_map.119 = (bf16[320,512]{1,0:T(8,128)(2,1)S(1)}, bf16[64,2048]{1,0:T(8,128)(2,1)S(1)}) custom-call(s32[2]{0:T(128)S(1)} %pad_add_fusion.idx_ref, bf16[4096,512]{1,0:T(8,128)(2,1)S(1)} %bitcast.11, bf16[4096,512]{1,0:T(8,128)(2,1)S(1)} %bitcast.15, bf16[384,2176]{1,0:T(8,128)(2,1)S(1)} %shard_map.117.lhs_ref.own_ref, ...), custom_call_target="tpu_custom_call" | custom-call | tf_op jit(solution)/shard_map/pallas_call | solution.py:29
  97.3 1.1 collective-permute-start.20
  98.4 2.7 %collective-permute-done.11.peer_ref = bf16[320,512]{1,0:T(8,128)(2,1)S(1)} collective-permute-done((bf16[320,512]{1,0:T(8,128)(2,1)S(1)}, bf16[320,512]{1,0:T(8,128)(2,1)S(1)}, u32[]{:S(2)}, u32[]{:S(2)}) %collective-permute-start.11) | collective-permute-done | bytes 327712 | tf_op jit(solution)/shard_map/ppermute | solution.py:346
  101.1 1.4 shard_map.120
  102.5 1.4 collective-permute-start.16
  104.4 1.4 shard_map.116
  105.9 2.2 %collective-permute-done.20.refs_8_.peer_ref = bf16[320,512]{1,0:T(8,128)(2,1)S(1)} collective-permute-done((bf16[320,512]{1,0:T(8,128)(2,1)S(1)}, bf16[320,512]{1,0:T(8,128)(2,1)S(1)}, u32[]{:S(2)}, u32[]{:S(2)}) %collective-permute-start.20) | collective-permute-done | bytes 327712 | tf_op jit(solution)/shard_map/ppermute | solution.py:346
  108.8 1.4 shard_map.126
  110.2 1.2 collective-permute-start.26
  113.0 1.4 shard_map.125
  114.4 2.7 %collective-permute-done.21.got_ref = bf16[160,1024]{1,0:T(8,128)(2,1)S(1)} collective-permute-done((bf16[160,1024]{1,0:T(8,128)(2,1)S(1)}, bf16[160,1024]{1,0:T(8,128)(2,1)S(1)}, u32[]{:S(2)}, u32[]{:S(2)}) %collective-permute-start.21) | collective-permute-done | bytes 327712 | tf_op jit(solution)/shard_map/ppermute | solution.py:340
  118.9 1.4 collective-permute-start.22
  121.3 2.2 %collective-permute-start.23 = (bf16[64,1024]{1,0:T(8,128)(2,1)S(1)}, bf16[64,1024]{1,0:T(8,128)(2,1)S(1)}, u32[]{:S(2)}, u32[]{:S(2)}) collective-permute-start(bf16[64,1024]{1,0:T(8,128)(2,1)S(1)} %get-tuple-element.81), channel_id=1, source_target_pairs={{0,16},{2,18},{4,20},{6,22},{8,24},{10,26},{12,28},{14,30},{16,0},... | collective-permute-start | bytes 393224 | tf_op jit(solution)/shard_map/ppermute | solution.py:343
  123.5 2.8 %collective-permute-done.30.got_ref = bf16[160,1024]{1,0:T(8,128)(2,1)S(1)} collective-permute-done((bf16[160,1024]{1,0:T(8,128)(2,1)S(1)}, bf16[160,1024]{1,0:T(8,128)(2,1)S(1)}, u32[]{:S(2)}, u32[]{:S(2)}) %collective-permute-start.30) | collective-permute-done | bytes 327712 | tf_op jit(solution)/shard_map/ppermute | solution.py:340
  127.3 1.2 collective-permute-start.31
  128.5 2.4 %collective-permute-start.32 = (bf16[64,1024]{1,0:T(8,128)(2,1)S(1)}, bf16[64,1024]{1,0:T(8,128)(2,1)S(1)}, u32[]{:S(2)}, u32[]{:S(2)}) collective-permute-start(bf16[64,1024]{1,0:T(8,128)(2,1)S(1)} %get-tuple-element.95), channel_id=1, source_target_pairs={{0,16},{2,18},{4,20},{6,22},{8,24},{10,26},{12,28},{14,30},{16,0},... | collective-permute-start | bytes 393224 | tf_op jit(solution)/shard_map/ppermute | solution.py:343
  131.6 8.8 %collective-permute-done.24.refs_2_ = bf16[64,1024]{1,0:T(8,128)(2,1)S(1)} collective-permute-done((bf16[64,1024]{1,0:T(8,128)(2,1)S(1)}, bf16[64,1024]{1,0:T(8,128)(2,1)S(1)}, u32[]{:S(2)}, u32[]{:S(2)}) %collective-permute-start.24) | collective-permute-done | bytes 131104 | tf_op jit(solution)/shard_map/ppermute | solution.py:343
  140.5 2.5 %collective-permute-start.25 = (f32[64,1024]{1,0:T(8,128)S(1)}, f32[64,1024]{1,0:T(8,128)S(1)}, u32[]{:S(2)}, u32[]{:S(2)}) collective-permute-start(f32[64,1024]{1,0:T(8,128)S(1)} %shard_map.124.refs_1_), channel_id=1, source_target_pairs={{2,0},{6,4},{10,8},{14,12},{18,16},{22,20},{26,24},{30,28},{3,1},{... | collective-permute-start | bytes 786440 | tf_op jit(solution)/shard_map/ppermute | solution.py:353
  143.0 3.0 %collective-permute-done.33.refs_2_ = bf16[64,1024]{1,0:T(8,128)(2,1)S(1)} collective-permute-done((bf16[64,1024]{1,0:T(8,128)(2,1)S(1)}, bf16[64,1024]{1,0:T(8,128)(2,1)S(1)}, u32[]{:S(2)}, u32[]{:S(2)}) %collective-permute-start.33) | collective-permute-done | bytes 131104 | tf_op jit(solution)/shard_map/ppermute | solution.py:343
  146.1 1.3 collective-permute-start.34
  147.4 2.1 %collective-permute-done.34.refs_5_ = f32[64,1024]{1,0:T(8,128)S(1)} collective-permute-done((f32[64,1024]{1,0:T(8,128)S(1)}, f32[64,1024]{1,0:T(8,128)S(1)}, u32[]{:S(2)}, u32[]{:S(2)}) %collective-permute-start.34) | collective-permute-done | bytes 262176 | tf_op jit(solution)/shard_map/ppermute | solution.py:353
  149.5 1.3 shard_map.131
  (65 shorter events, 13.7 us)
Async XLA Ops:
  0.0 9.6 %copy-start.4 = (bf16[2048]{0:T(1024)(128)(2,1)S(1)}, bf16[2048]{0:T(1024)(128)(2,1)}, u32[]{:S(2)}) copy-start(bf16[2048]{0:T(1024)(128)(2,1)} %param.15) | copy-start | bytes 12292
  3.0 32.9 %all-to-all-start = ((bf16[16,272,128]{2,1,0:T(8,128)(2,1)}), bf16[16,272,128]{2,1,0:T(8,128)(2,1)S(1)}, u32[]{:S(2)}, u32[]{:S(2)}) async-start(bf16[16,272,128]{2,1,0:T(8,128)(2,1)} %shard_map.109), calls=%async_computation | async-start | bytes 2228224 | tf_op jit(solution)/shard_map/all_to_all | solution.py:364
  9.6 2.8 %collective-permute-start = (bf16[2048]{0:T(1024)(128)(2,1)S(1)}, bf16[2048]{0:T(1024)(128)(2,1)S(1)}, u32[]{:S(2)}, u32[]{:S(2)}) collective-permute-start(bf16[2048]{0:T(1024)(128)(2,1)S(1)} %copy-done.4), channel_id=1, source_target_pairs={{0,1},{1,0},{2,3},{3,2},{4,5},{5,4},{6,7},{7,6},{8,9},{9,8},{10,11... | collective-permute-start | bytes 12296 | tf_op jit(solution)/shard_map/ppermute | solution.py:346
  38.0 4.9 %collective-permute-start.1 = (bf16[512,128]{1,0:T(8,128)(2,1)S(1)}, bf16[512,128]{1,0:T(8,128)(2,1)S(1)}, u32[]{:S(2)}, u32[]{:S(2)}) collective-permute-start(bf16[512,128]{1,0:T(8,128)(2,1)S(1)} %get-tuple-element.54.refs_0_), channel_id=1, source_target_pairs={{0,8},{2,10},{4,12},{6,14},{8,16},{10,18},{12,20},{14,22},{16,24},... | collective-permute-start | bytes 393224 | tf_op jit(solution)/shard_map/ppermute | solution.py:343
  38.0 11.3 %collective-permute-start.2 = (bf16[512,128]{1,0:T(8,128)(2,1)S(1)}, bf16[512,128]{1,0:T(8,128)(2,1)S(1)}, u32[]{:S(2)}, u32[]{:S(2)}) collective-permute-start(bf16[512,128]{1,0:T(8,128)(2,1)S(1)} %get-tuple-element.54.refs_0_), channel_id=1, source_target_pairs={{0,16},{2,18},{4,20},{6,22},{8,24},{10,26},{12,28},{14,30},{16,0},... | collective-permute-start | bytes 393224 | tf_op jit(solution)/shard_map/ppermute | solution.py:343
  39.2 12.3 %collective-permute-start.3 = (bf16[512,128]{1,0:T(8,128)(2,1)S(1)}, bf16[512,128]{1,0:T(8,128)(2,1)S(1)}, u32[]{:S(2)}, u32[]{:S(2)}) collective-permute-start(bf16[512,128]{1,0:T(8,128)(2,1)S(1)} %get-tuple-element.54.refs_0_), channel_id=1, source_target_pairs={{0,24},{2,26},{4,28},{6,30},{8,0},{10,2},{12,4},{14,6},{16,8},{18,... | collective-permute-start | bytes 393224 | tf_op jit(solution)/shard_map/ppermute | solution.py:343
  52.4 17.3 %collective-permute-start.4 = (bf16[4,384,128]{2,1,0:T(8,128)(2,1)S(1)}, bf16[4,384,128]{2,1,0:T(8,128)(2,1)S(1)}, u32[]{:S(2)}, u32[]{:S(2)}) collective-permute-start(bf16[4,384,128]{2,1,0:T(8,128)(2,1)S(1)} %get-tuple-element.58.refs_4_), channel_id=1, source_target_pairs={{0,4},{2,6},{4,0},{6,2},{8,12},{10,14},{12,8},{14,10},{16,20},{18,... | collective-permute-start | bytes 1179656 | tf_op jit(solution)/shard_map/ppermute | solution.py:340
  52.5 4.6 %collective-permute-start.7 = (bf16[512,128]{1,0:T(8,128)(2,1)S(1)}, bf16[512,128]{1,0:T(8,128)(2,1)S(1)}, u32[]{:S(2)}, u32[]{:S(2)}) collective-permute-start(bf16[512,128]{1,0:T(8,128)(2,1)S(1)} %get-tuple-element.60.refs_0_), channel_id=1, source_target_pairs={{0,8},{2,10},{4,12},{6,14},{8,16},{10,18},{12,20},{14,22},{16,24},... | collective-permute-start | bytes 393224 | tf_op jit(solution)/shard_map/ppermute | solution.py:343
  52.5 15.0 %collective-permute-start.6 = (bf16[4,320,128]{2,1,0:T(8,128)(2,1)S(1)}, bf16[4,320,128]{2,1,0:T(8,128)(2,1)S(1)}, u32[]{:S(2)}, u32[]{:S(2)}) collective-permute-start(bf16[4,320,128]{2,1,0:T(8,128)(2,1)S(1)} %slice.13), channel_id=1, source_target_pairs={{0,5},{1,4},{2,7},{3,6},{4,1},{5,0},{6,3},{7,2},{8,13},{9,12},{10,... | collective-permute-start | bytes 983048 | tf_op jit(solution)/shard_map/ppermute | solution.py:350
  55.0 14.3 %collective-permute-start.5 = (bf16[4,320,128]{2,1,0:T(8,128)(2,1)S(1)}, bf16[4,320,128]{2,1,0:T(8,128)(2,1)S(1)}, u32[]{:S(2)}, u32[]{:S(2)}) collective-permute-start(bf16[4,320,128]{2,1,0:T(8,128)(2,1)S(1)} %slice.12), channel_id=1, source_target_pairs={{0,1},{1,0},{2,3},{3,2},{4,5},{5,4},{6,7},{7,6},{8,9},{9,8},{10,11... | collective-permute-start | bytes 983048 | tf_op jit(solution)/shard_map/ppermute | solution.py:346
  55.3 5.1 %collective-permute-start.8 = (bf16[512,128]{1,0:T(8,128)(2,1)S(1)}, bf16[512,128]{1,0:T(8,128)(2,1)S(1)}, u32[]{:S(2)}, u32[]{:S(2)}) collective-permute-start(bf16[512,128]{1,0:T(8,128)(2,1)S(1)} %get-tuple-element.60.refs_0_), channel_id=1, source_target_pairs={{0,16},{2,18},{4,20},{6,22},{8,24},{10,26},{12,28},{14,30},{16,0},... | collective-permute-start | bytes 393224 | tf_op jit(solution)/shard_map/ppermute | solution.py:343
  57.1 9.6 %collective-permute-start.9 = (bf16[512,128]{1,0:T(8,128)(2,1)S(1)}, bf16[512,128]{1,0:T(8,128)(2,1)S(1)}, u32[]{:S(2)}, u32[]{:S(2)}) collective-permute-start(bf16[512,128]{1,0:T(8,128)(2,1)S(1)} %get-tuple-element.60.refs_0_), channel_id=1, source_target_pairs={{0,24},{2,26},{4,28},{6,30},{8,0},{10,2},{12,4},{14,6},{16,8},{18,... | collective-permute-start | bytes 393224 | tf_op jit(solution)/shard_map/ppermute | solution.py:343
  69.7 5.2 %copy-start = (bf16[1,4096,512]{2,1,0:T(8,128)(2,1)S(1)}, bf16[1,4096,512]{2,1,0:T(8,128)(2,1)}, u32[]{:S(2)}) copy-start(bf16[1,4096,512]{2,1,0:T(8,128)(2,1)} %param.19) | copy-start | bytes 12582916
  70.7 8.4 %collective-permute-start.10 = (bf16[384,2176]{1,0:T(8,128)(2,1)S(1)}, bf16[384,2176]{1,0:T(8,128)(2,1)S(1)}, u32[]{:S(2)}, u32[]{:S(2)}) collective-permute-start(bf16[384,2176]{1,0:T(8,128)(2,1)S(1)} %shard_map.113.lhs_ref.own_ref), channel_id=1, source_target_pairs={{0,2},{2,0},{4,6},{6,4},{8,10},{10,8},{12,14},{14,12},{16,18},{18,... | collective-permute-start | bytes 5013512 | tf_op jit(solution)/shard_map/ppermute | solution.py:340
  72.1 17.3 %collective-permute-start.12 = (bf16[4,384,128]{2,1,0:T(8,128)(2,1)S(1)}, bf16[4,384,128]{2,1,0:T(8,128)(2,1)S(1)}, u32[]{:S(2)}, u32[]{:S(2)}) collective-permute-start(bf16[4,384,128]{2,1,0:T(8,128)(2,1)S(1)} %get-tuple-element.71), channel_id=1, source_target_pairs={{0,4},{2,6},{4,0},{6,2},{8,12},{10,14},{12,8},{14,10},{16,20},{18,... | collective-permute-start | bytes 1179656 | tf_op jit(solution)/shard_map/ppermute | solution.py:340
  72.2 9.2 %collective-permute-start.13 = (bf16[4,320,128]{2,1,0:T(8,128)(2,1)S(1)}, bf16[4,320,128]{2,1,0:T(8,128)(2,1)S(1)}, u32[]{:S(2)}, u32[]{:S(2)}) collective-permute-start(bf16[4,320,128]{2,1,0:T(8,128)(2,1)S(1)} %slice.14), channel_id=1, source_target_pairs={{0,1},{1,0},{2,3},{3,2},{4,5},{5,4},{6,7},{7,6},{8,9},{9,8},{10,11... | collective-permute-start | bytes 983048 | tf_op jit(solution)/shard_map/ppermute | solution.py:346
  73.5 16.0 %collective-permute-start.14 = (bf16[4,320,128]{2,1,0:T(8,128)(2,1)S(1)}, bf16[4,320,128]{2,1,0:T(8,128)(2,1)S(1)}, u32[]{:S(2)}, u32[]{:S(2)}) collective-permute-start(bf16[4,320,128]{2,1,0:T(8,128)(2,1)S(1)} %slice.15), channel_id=1, source_target_pairs={{0,5},{1,4},{2,7},{3,6},{4,1},{5,0},{6,3},{7,2},{8,13},{9,12},{10,... | collective-permute-start | bytes 983048 | tf_op jit(solution)/shard_map/ppermute | solution.py:350
  74.9 2.2 %copy-start.1 = (bf16[1,4096,512]{2,1,0:T(8,128)(2,1)S(1)}, bf16[1,4096,512]{2,1,0:T(8,128)(2,1)}, u32[]{:S(2)}) copy-start(bf16[1,4096,512]{2,1,0:T(8,128)(2,1)} %param.20) | copy-start | bytes 12582916
  79.2 13.9 %copy-start.2 = (bf16[1,4096,512]{2,1,0:T(8,128)(2,1)S(1)}, bf16[1,4096,512]{2,1,0:T(8,128)(2,1)}, u32[]{:S(2)}) copy-start(bf16[1,4096,512]{2,1,0:T(8,128)(2,1)} %param.20) | copy-start | bytes 12582916
  90.5 4.6 %collective-permute-start.15 = (bf16[384,2176]{1,0:T(8,128)(2,1)S(1)}, bf16[384,2176]{1,0:T(8,128)(2,1)S(1)}, u32[]{:S(2)}, u32[]{:S(2)}) collective-permute-start(bf16[384,2176]{1,0:T(8,128)(2,1)S(1)} %shard_map.117.lhs_ref.own_ref), channel_id=1, source_target_pairs={{0,2},{2,0},{4,6},{6,4},{8,10},{10,8},{12,14},{14,12},{16,18},{18,... | collective-permute-start | bytes 5013512 | tf_op jit(solution)/shard_map/ppermute | solution.py:340
  91.8 9.3 %collective-permute-start.11 = (bf16[320,512]{1,0:T(8,128)(2,1)S(1)}, bf16[320,512]{1,0:T(8,128)(2,1)S(1)}, u32[]{:S(2)}, u32[]{:S(2)}) collective-permute-start(bf16[320,512]{1,0:T(8,128)(2,1)S(1)} %get-tuple-element.66.own_ref.refs_4_), channel_id=1, source_target_pairs={{0,1},{1,0},{2,3},{3,2},{4,5},{5,4},{6,7},{7,6},{8,9},{9,8},{10,11... | collective-permute-start | bytes 983048 | tf_op jit(solution)/shard_map/ppermute | solution.py:346
  95.1 6.0 %copy-start.3 = (bf16[1,1024,2048]{2,1,0:T(8,128)(2,1)S(1)}, bf16[1,1024,2048]{2,1,0:T(8,128)(2,1)}, u32[]{:S(2)}) copy-start(bf16[1,1024,2048]{2,1,0:T(8,128)(2,1)} %param.21) | copy-start | bytes 12582916
  97.3 10.8 %collective-permute-start.20 = (bf16[320,512]{1,0:T(8,128)(2,1)S(1)}, bf16[320,512]{1,0:T(8,128)(2,1)S(1)}, u32[]{:S(2)}, u32[]{:S(2)}) collective-permute-start(bf16[320,512]{1,0:T(8,128)(2,1)S(1)} %get-tuple-element.74.refs_0_.own_ref), channel_id=1, source_target_pairs={{0,1},{1,0},{2,3},{3,2},{4,5},{5,4},{6,7},{7,6},{8,9},{9,8},{10,11... | collective-permute-start | bytes 983048 | tf_op jit(solution)/shard_map/ppermute | solution.py:346
  102.5 3.4 %collective-permute-start.16 = (bf16[320,256]{1,0:T(8,128)(2,1)S(1)}, bf16[320,256]{1,0:T(8,128)(2,1)S(1)}, u32[]{:S(2)}, u32[]{:S(2)}) collective-permute-start(bf16[320,256]{1,0:T(8,128)(2,1)S(1)} %get-tuple-element.75), channel_id=1, source_target_pairs={{0,2},{2,0},{4,6},{6,4},{8,10},{10,8},{12,14},{14,12},{16,18},{18,... | collective-permute-start | bytes 491528 | tf_op jit(solution)/shard_map/ppermute | solution.py:340
  103.9 2.0 %collective-permute-start.17 = (bf16[320,256]{1,0:T(8,128)(2,1)S(1)}, bf16[320,256]{1,0:T(8,128)(2,1)S(1)}, u32[]{:S(2)}, u32[]{:S(2)}) collective-permute-start(bf16[320,256]{1,0:T(8,128)(2,1)S(1)} %get-tuple-element.76), channel_id=1, source_target_pairs={{0,2},{2,0},{4,6},{6,4},{8,10},{10,8},{12,14},{14,12},{16,18},{18,... | collective-permute-start | bytes 491528 | tf_op jit(solution)/shard_map/ppermute | solution.py:340
  103.9 2.0 %collective-permute-start.18 = (bf16[320,256]{1,0:T(8,128)(2,1)S(1)}, bf16[320,256]{1,0:T(8,128)(2,1)S(1)}, u32[]{:S(2)}, u32[]{:S(2)}) collective-permute-start(bf16[320,256]{1,0:T(8,128)(2,1)S(1)} %get-tuple-element.77), channel_id=1, source_target_pairs={{0,2},{2,0},{4,6},{6,4},{8,10},{10,8},{12,14},{14,12},{16,18},{18,... | collective-permute-start | bytes 491528 | tf_op jit(solution)/shard_map/ppermute | solution.py:340
  104.4 1.5 %collective-permute-start.19 = (bf16[320,256]{1,0:T(8,128)(2,1)S(1)}, bf16[320,256]{1,0:T(8,128)(2,1)S(1)}, u32[]{:S(2)}, u32[]{:S(2)}) collective-permute-start(bf16[320,256]{1,0:T(8,128)(2,1)S(1)} %get-tuple-element.78), channel_id=1, source_target_pairs={{0,2},{2,0},{4,6},{6,4},{8,10},{10,8},{12,14},{14,12},{16,18},{18,... | collective-permute-start | bytes 491528 | tf_op jit(solution)/shard_map/ppermute | solution.py:340
  108.7 8.4 %collective-permute-start.21 = (bf16[160,1024]{1,0:T(8,128)(2,1)S(1)}, bf16[160,1024]{1,0:T(8,128)(2,1)S(1)}, u32[]{:S(2)}, u32[]{:S(2)}) collective-permute-start(bf16[160,1024]{1,0:T(8,128)(2,1)S(1)} %shard_map.122.refs_0_), channel_id=1, source_target_pairs={{0,4},{2,6},{4,0},{6,2},{8,12},{10,14},{12,8},{14,10},{16,20},{18,... | collective-permute-start | bytes 983048 | tf_op jit(solution)/shard_map/ppermute | solution.py:340
  110.2 7.9 %collective-permute-start.26 = (bf16[320,256]{1,0:T(8,128)(2,1)S(1)}, bf16[320,256]{1,0:T(8,128)(2,1)S(1)}, u32[]{:S(2)}, u32[]{:S(2)}) collective-permute-start(bf16[320,256]{1,0:T(8,128)(2,1)S(1)} %get-tuple-element.89), channel_id=1, source_target_pairs={{0,2},{2,0},{4,6},{6,4},{8,10},{10,8},{12,14},{14,12},{16,18},{18,... | collective-permute-start | bytes 491528 | tf_op jit(solution)/shard_map/ppermute | solution.py:340
  111.4 6.7 %collective-permute-start.27 = (bf16[320,256]{1,0:T(8,128)(2,1)S(1)}, bf16[320,256]{1,0:T(8,128)(2,1)S(1)}, u32[]{:S(2)}, u32[]{:S(2)}) collective-permute-start(bf16[320,256]{1,0:T(8,128)(2,1)S(1)} %get-tuple-element.90), channel_id=1, source_target_pairs={{0,2},{2,0},{4,6},{6,4},{8,10},{10,8},{12,14},{14,12},{16,18},{18,... | collective-permute-start | bytes 491528 | tf_op jit(solution)/shard_map/ppermute | solution.py:340
  111.5 6.7 %collective-permute-start.28 = (bf16[320,256]{1,0:T(8,128)(2,1)S(1)}, bf16[320,256]{1,0:T(8,128)(2,1)S(1)}, u32[]{:S(2)}, u32[]{:S(2)}) collective-permute-start(bf16[320,256]{1,0:T(8,128)(2,1)S(1)} %get-tuple-element.91), channel_id=1, source_target_pairs={{0,2},{2,0},{4,6},{6,4},{8,10},{10,8},{12,14},{14,12},{16,18},{18,... | collective-permute-start | bytes 491528 | tf_op jit(solution)/shard_map/ppermute | solution.py:340
  111.9 6.2 %collective-permute-start.29 = (bf16[320,256]{1,0:T(8,128)(2,1)S(1)}, bf16[320,256]{1,0:T(8,128)(2,1)S(1)}, u32[]{:S(2)}, u32[]{:S(2)}) collective-permute-start(bf16[320,256]{1,0:T(8,128)(2,1)S(1)} %get-tuple-element.92), channel_id=1, source_target_pairs={{0,2},{2,0},{4,6},{6,4},{8,10},{10,8},{12,14},{14,12},{16,18},{18,... | collective-permute-start | bytes 491528 | tf_op jit(solution)/shard_map/ppermute | solution.py:340
  118.8 7.5 %collective-permute-start.30 = (bf16[160,1024]{1,0:T(8,128)(2,1)S(1)}, bf16[160,1024]{1,0:T(8,128)(2,1)S(1)}, u32[]{:S(2)}, u32[]{:S(2)}) collective-permute-start(bf16[160,1024]{1,0:T(8,128)(2,1)S(1)} %shard_map.128), channel_id=1, source_target_pairs={{0,4},{2,6},{4,0},{6,2},{8,12},{10,14},{12,8},{14,10},{16,20},{18,... | collective-permute-start | bytes 983048 | tf_op jit(solution)/shard_map/ppermute | solution.py:340
  118.9 11.9 %collective-permute-start.22 = (bf16[64,1024]{1,0:T(8,128)(2,1)S(1)}, bf16[64,1024]{1,0:T(8,128)(2,1)S(1)}, u32[]{:S(2)}, u32[]{:S(2)}) collective-permute-start(bf16[64,1024]{1,0:T(8,128)(2,1)S(1)} %get-tuple-element.80), channel_id=1, source_target_pairs={{0,8},{2,10},{4,12},{6,14},{8,16},{10,18},{12,20},{14,22},{16,24},... | collective-permute-start | bytes 393224 | tf_op jit(solution)/shard_map/ppermute | solution.py:343
  121.3 10.3 %collective-permute-start.23 = (bf16[64,1024]{1,0:T(8,128)(2,1)S(1)}, bf16[64,1024]{1,0:T(8,128)(2,1)S(1)}, u32[]{:S(2)}, u32[]{:S(2)}) collective-permute-start(bf16[64,1024]{1,0:T(8,128)(2,1)S(1)} %get-tuple-element.81), channel_id=1, source_target_pairs={{0,16},{2,18},{4,20},{6,22},{8,24},{10,26},{12,28},{14,30},{16,0},... | collective-permute-start | bytes 393224 | tf_op jit(solution)/shard_map/ppermute | solution.py:343
  123.5 16.9 %collective-permute-start.24 = (bf16[64,1024]{1,0:T(8,128)(2,1)S(1)}, bf16[64,1024]{1,0:T(8,128)(2,1)S(1)}, u32[]{:S(2)}, u32[]{:S(2)}) collective-permute-start(bf16[64,1024]{1,0:T(8,128)(2,1)S(1)} %get-tuple-element.82), channel_id=1, source_target_pairs={{0,24},{2,26},{4,28},{6,30},{8,0},{10,2},{12,4},{14,6},{16,8},{18,... | collective-permute-start | bytes 393224 | tf_op jit(solution)/shard_map/ppermute | solution.py:343
  127.3 15.7 %collective-permute-start.31 = (bf16[64,1024]{1,0:T(8,128)(2,1)S(1)}, bf16[64,1024]{1,0:T(8,128)(2,1)S(1)}, u32[]{:S(2)}, u32[]{:S(2)}) collective-permute-start(bf16[64,1024]{1,0:T(8,128)(2,1)S(1)} %get-tuple-element.94), channel_id=1, source_target_pairs={{0,8},{2,10},{4,12},{6,14},{8,16},{10,18},{12,20},{14,22},{16,24},... | collective-permute-start | bytes 393224 | tf_op jit(solution)/shard_map/ppermute | solution.py:343
  128.5 14.5 %collective-permute-start.32 = (bf16[64,1024]{1,0:T(8,128)(2,1)S(1)}, bf16[64,1024]{1,0:T(8,128)(2,1)S(1)}, u32[]{:S(2)}, u32[]{:S(2)}) collective-permute-start(bf16[64,1024]{1,0:T(8,128)(2,1)S(1)} %get-tuple-element.95), channel_id=1, source_target_pairs={{0,16},{2,18},{4,20},{6,22},{8,24},{10,26},{12,28},{14,30},{16,0},... | collective-permute-start | bytes 393224 | tf_op jit(solution)/shard_map/ppermute | solution.py:343
  130.8 15.2 %collective-permute-start.33 = (bf16[64,1024]{1,0:T(8,128)(2,1)S(1)}, bf16[64,1024]{1,0:T(8,128)(2,1)S(1)}, u32[]{:S(2)}, u32[]{:S(2)}) collective-permute-start(bf16[64,1024]{1,0:T(8,128)(2,1)S(1)} %get-tuple-element.96), channel_id=1, source_target_pairs={{0,24},{2,26},{4,28},{6,30},{8,0},{10,2},{12,4},{14,6},{16,8},{18,... | collective-permute-start | bytes 393224 | tf_op jit(solution)/shard_map/ppermute | solution.py:343
  140.5 6.9 %collective-permute-start.25 = (f32[64,1024]{1,0:T(8,128)S(1)}, f32[64,1024]{1,0:T(8,128)S(1)}, u32[]{:S(2)}, u32[]{:S(2)}) collective-permute-start(f32[64,1024]{1,0:T(8,128)S(1)} %shard_map.124.refs_1_), channel_id=1, source_target_pairs={{2,0},{6,4},{10,8},{14,12},{18,16},{22,20},{26,24},{30,28},{3,1},{... | collective-permute-start | bytes 786440 | tf_op jit(solution)/shard_map/ppermute | solution.py:353
  146.1 3.4 %collective-permute-start.34 = (f32[64,1024]{1,0:T(8,128)S(1)}, f32[64,1024]{1,0:T(8,128)S(1)}, u32[]{:S(2)}, u32[]{:S(2)}) collective-permute-start(f32[64,1024]{1,0:T(8,128)S(1)} %shard_map.130.refs_4_), channel_id=1, source_target_pairs={{0,2},{4,6},{8,10},{12,14},{16,18},{20,22},{24,26},{28,30},{1,3},{... | collective-permute-start | bytes 786440 | tf_op jit(solution)/shard_map/ppermute | solution.py:353

commit v5 on v4

--- a/solution.py
+++ b/solution.py
@@ -138,25 +138,52 @@
         odd_ref[at : at + tok, :] = hand[tok:, :]
 
 
+def near_kernel(pick_even_ref, pick_odd_ref, even_ref, odd_ref, mine_ref, theirs_ref):
+    slots, span = pick_even_ref.shape[1] // 2, pick_even_ref.shape[2]
+    for n, (pick_ref, ref) in enumerate(((pick_even_ref, even_ref), (pick_odd_ref, odd_ref))):
+        for group in range(2):
+            here = slice(group * slots, (group + 1) * slots)
+            block = ref[group * span : (group + 1) * span, :]
+            for which, out_ref in enumerate((mine_ref, theirs_ref)):
+                rows = jnp.dot(pick_ref[which, here, :], block, preferred_element_type=jnp.float32)
+                out_ref[n, here, :] = rows.astype(jnp.bfloat16)
+
+
 def compact_kernel(idx_ref, pick_ref, *refs):
-    mine_ref, theirs_ref = refs[-2:]
+    *out_refs, mine_own_ref, theirs_own_ref = refs[-4:]
     me = idx_ref[0]
-    levels = mine_ref.shape[0]
+    levels, tok = mine_own_ref.shape[:2]
     pieces = refs[:levels]
     slots, span = pick_ref.shape[1] // 2, pick_ref.shape[2]
-    tok = span // levels
     z, y = lax.div(me, 4), lax.rem(lax.div(me, 2), 2)
     for group in range(2):
         block = jnp.concatenate([p[group * span : (group + 1) * span, :] for p in pieces], axis=1)
-        for which, out_ref in enumerate((mine_ref, theirs_ref)):
+        for which, out_ref in enumerate(out_refs):
             here = slice(group * slots, (group + 1) * slots)
             rows = jnp.dot(pick_ref[which, here, :], block, preferred_element_type=jnp.float32).astype(jnp.bfloat16)
             for k in range(levels):
                 out_ref[k, here, :] = rows[:, k * HD : (k + 1) * HD]
-    for which, out_ref in enumerate((mine_ref, theirs_ref)):
+    for which, out_ref in enumerate((mine_own_ref, theirs_own_ref)):
         own = pl.ds(pl.multiple_of(((y ^ which) * levels + z) * tok, tok), tok)
         for k in range(levels):
-            out_ref[k, 2 * slots :, :] = pieces[k][own, :]
+            out_ref[k, :, :] = pieces[k][own, :]
+
+
+def gather_kernel(*refs):
+    out_ref = refs[-1]
+    for n in range(out_ref.shape[0]):
+        out_ref[n] = refs[n][...]
+
+
+def own_rows_kernel(idx_ref, even_ref, odd_ref, by_y_ref, keep_ref, send_ref):
+    core = lax.rem(idx_ref[0], 2)
+    levels = even_ref.shape[0]
+    for n, ref in enumerate((even_ref, odd_ref)):
+        for same, out_ref in ((True, keep_ref), (False, send_ref)):
+            @pl.when((core == n) == same)
+            def _(ref=ref, out_ref=out_ref, n=n):
+                out_ref[:levels] = ref[...]
+                out_ref[levels:] = by_y_ref[n]
 
 
 def thirds(value):
@@ -170,7 +197,7 @@
     pieces, out_ref = refs[: len(places)], refs[-1]
     me = idx_ref[0]
     heads = gain_ref.shape[1] // HD
-    rows, tok = pieces[-1].shape[1], pieces[0].shape[1] - pieces[-1].shape[1]
+    rows = out_ref.shape[0]
     width = sum(map(len, places)) * HD
     tile = rows // 2
     for r in range(rows // tile):
@@ -178,14 +205,12 @@
         squares = jnp.zeros((tile, HD), jnp.float32)
         n = 0
         for ref, entries in zip(pieces, places):
-            for k, (other, low, back) in enumerate(entries):
+            for k, other, low, back in entries:
                 head = lax.rem((me ^ low) + heads - 4 * back, heads)
                 gain = gain_ref[other : other + 1, pl.ds(pl.multiple_of(head * HD, HD), HD)]
                 v = ref[k, here, :].astype(jnp.float32)
                 squares = squares + v * v
                 out_ref[here, n : n + HD] = (v * gain).astype(jnp.bfloat16)
-                if not other and r == 0:
-                    out_ref[rows:, n : n + HD] = ref[k, rows : rows + tok, :]
                 n += HD
         lane = lax.broadcasted_iota(jnp.int32, (tile, HD), 1)
         high, middle, low = thirds(jnp.broadcast_to(jnp.sum(squares, axis=1, keepdims=True), (tile, HD)))
@@ -195,14 +220,14 @@
 
 def row_offsets(places, heads, me, plane, flip):
     found = []
-    for other, low, back in (entry for entries in places for entry in entries):
+    for _, other, low, back in (entry for entries in places for entry in entries):
         head = lax.rem((me ^ low ^ flip) + heads - 4 * back, heads)
-        found.append((other, pl.multiple_of(head * HD, HD), pl.multiple_of(((plane ^ other) * heads + head) * HD, HD)))
+        found.append(pl.multiple_of(((plane ^ other) * heads + head) * HD, HD))
     return found
 
 
 def half_projection(lhs, offsets, weight_ref, cols):
-    weights = jnp.concatenate([weight_ref[pl.ds(at, HD), cols] for *_, at in offsets], axis=0)
+    weights = jnp.concatenate([weight_ref[pl.ds(at, HD), cols] for at in offsets], axis=0)
     return jnp.dot(lhs, weights, preferred_element_type=jnp.float32)
 
 
@@ -217,13 +242,9 @@
         up_ref[:, cols] = half_projection(lhs, offsets, wu_ref, cols)
 
 
-def second_kernel(places, heads, idx_ref, wg_ref, wu_ref, own_ref, lhs_ref, gate_ref, up_ref, hidden_ref, hand_ref):
+def second_kernel(places, heads, idx_ref, wg_ref, wu_ref, own_ref, lhs_ref, gate_ref, up_ref, hidden_ref):
     rows = gate_ref.shape[0]
     me, plane = idx_ref[0], idx_ref[1]
-    for flip, ref in enumerate((own_ref, lhs_ref)):
-        for n, (other, at, _) in enumerate(row_offsets(places, heads, me, plane, flip)):
-            if not other:
-                hand_ref[:, pl.ds(at, HD)] = ref[rows:, n * HD : (n + 1) * HD]
     offsets = row_offsets(places, heads, me, plane, 1)
     last = len(offsets) * HD
     squares = own_ref[0:rows, last:].astype(jnp.float32) + lhs_ref[0:rows, last:].astype(jnp.float32)
@@ -306,19 +327,28 @@
 
 
 def final_kernel(idx_ref, *refs):
-    out_ref = refs[-1]
-    core = lax.rem(idx_ref[0], 2)
+    hand_refs, sum_refs, out_ref = refs[:2], refs[2:-1], refs[-1]
+    me = idx_ref[0]
+    core = lax.rem(me, 2)
+    levels = hand_refs[0].shape[0] // 2
+    heads = out_ref.shape[1] // HD
     for n in range(2):
-        hand_ref, own_ref, other_ref = refs[3 * n : 3 * n + 3]
+        own_ref, other_ref = sum_refs[2 * n : 2 * n + 2]
         half = own_ref.shape[1]
 
         @pl.when(core == n)
-        def _(hand_ref=hand_ref, halves=(own_ref, other_ref) if n == 0 else (other_ref, own_ref)):
-            for m, ref in enumerate(halves):
-                cols = slice(m * half, (m + 1) * half)
-                out_ref[:, cols] = (hand_ref[:, cols].astype(jnp.float32) + ref[...].astype(jnp.float32)).astype(
-                    jnp.bfloat16
-                )
+        def _(halves=(own_ref, other_ref) if n == 0 else (other_ref, own_ref)):
+            for flip, hand_ref in enumerate(hand_refs):
+                for low in range(2):
+                    for back in range(levels):
+                        head = lax.rem((me ^ (2 * low) ^ flip) + heads - 4 * back, heads)
+                        hand = hand_ref[low * levels + back].astype(jnp.float32)
+                        at = pl.multiple_of(head * HD, HD)
+                        inside = pl.multiple_of(lax.rem(head, heads // 2) * HD, HD)
+                        first = halves[0][:, pl.ds(inside, HD)].astype(jnp.float32)
+                        second = halves[1][:, pl.ds(inside, HD)].astype(jnp.float32)
+                        total = hand + jnp.where(head < heads // 2, first, second)
+                        out_ref[:, pl.ds(at, HD)] = total.astype(jnp.bfloat16)
 
 
 def heads_over_ctx(
@@ -377,35 +407,46 @@
         if columns:
             hand, columns[0][1] = lax.optimization_barrier((hand, columns[0][1]))
         columns.append([hand] + [along_z(hand, k) for k in range(1, levels)])
-    places = [[(t, f, k) for k in range(levels)] for t, f in ((0, 0), (0, 2), (1, 0), (1, 2))]
-    pieces, compacted = [], []
-    for pick, column in zip(hands[2:4], columns):
-        mine, theirs = call(
-            compact_kernel, [shape(levels, 2 * slots + tok, HD)] * 2, (idx, pick, *column, *compacted), smem=1
-        )
+    near = call(near_kernel, [shape(2, 2 * slots, HD)] * 2, (*hands[2:4], *hands[:2]))
+    near = [over_tp(near[0]), across(near[1])]
+    pieces, places, blocks, compacted = [], [], [], near
+    for core, (pick, column) in enumerate(zip(hands[2:4], columns)):
+        mine, theirs, *own_rows = call(
+            compact_kernel,
+            [shape(levels, 2 * slots, HD)] * 2 + [shape(levels, tok, HD)] * 2,
+            (idx, pick, *column, *compacted),
+            smem=1,
+        )
+        blocks.append(own_rows)
         compacted = [theirs]
-        pieces.append([mine, over_ctx(theirs, 2), over_tp(mine[:, : 2 * slots]), across(theirs[:, : 2 * slots])])
+        far = [over_tp(mine[1:]), across(theirs[1:])]
+        pieces.append([mine, over_ctx(theirs, 2), *far, *near])
+        places.append(
+            [[(k, 0, f, k) for k in range(levels)] for f in (0, 2)]
+            + [[(k - 1, 1, f, k) for k in range(1, levels)] for f in (0, 2)]
+            + [[(core, 1, f, 0)] for f in (0, 2)]
+        )
     fronts, after = [], pieces[1][0]
-    for got in pieces:
+    for got, where in zip(pieces, places):
         mixed = call(
-            functools.partial(scale_kernel, places),
-            shape(2 * slots + tok, (4 * levels + 1) * HD),
+            functools.partial(scale_kernel, where),
+            shape(2 * slots, (4 * levels + 1) * HD),
             (idx, gain, *got, after),
             smem=1,
         )
         sums = call(
-            functools.partial(first_kernel, places, heads),
+            functools.partial(first_kernel, where, heads),
             [shape(2 * slots, hidden_width, dtype=f32)] * 2,
             (idx, wg, wu, mixed),
             smem=1,
         )
-        hidden, own_hand = call(
-            functools.partial(second_kernel, places, heads),
-            [shape(2 * slots, hidden_width), shape(tok, width)],
+        hidden = call(
+            functools.partial(second_kernel, where, heads),
+            shape(2 * slots, hidden_width),
             (idx, wg, wu, mixed, over_ctx(mixed, 1), *sums),
             smem=1,
         )
-        fronts.append((hidden, over_tp(hidden), own_hand))
+        fronts.append((hidden, over_tp(hidden)))
         after = hidden
     half = width // 2
     results, after, added = [], [fronts[1][0]], [fronts[1][1]]
@@ -418,7 +459,14 @@
             smem=1,
         )
 
-    for core, (hidden, peer, own_hand) in enumerate(fronts):
+    by_y = call(gather_kernel, shape(2, levels, tok, HD), (blocks[0][1], blocks[1][1], fronts[1][0]))
+    keep_rows, send_rows = call(
+        own_rows_kernel,
+        [shape(2 * levels, tok, HD)] * 2,
+        (idx, blocks[0][0], blocks[1][0], over_ctx(by_y, 2)),
+        smem=1,
+    )
+    for core, (hidden, peer) in enumerate(fronts):
         pick, gates = hands[2 + core], hands[4 + core]
         other = [over_ctx(part, 1) for part in down(1, hidden, peer, *after)]
         half_out = down(0, hidden, peer)
@@ -442,8 +490,8 @@
         )
         added = [own]
         summed = call(sum_kernel, shape(tok, half, dtype=f32), (own, *[along_z(s, k) for k, s in enumerate(sends, 1)]))
-        results += [own_hand, summed, to_core(summed, core)]
-    return call(final_kernel, shape(tok, width), (idx, *results), smem=1)
+        results += [summed, to_core(summed, core)]
+    return call(final_kernel, shape(tok, width), (idx, keep_rows, over_ctx(send_rows, 1), *results), smem=1)
 
 
 def general(

time: 152 us -> 148 us (0.974)
  waiting for transfers between devices: 81 us -> 71.3 us
  starting transfers between devices: 37.5 us -> 42.9 us
    ppermute x14 -> x16, starting transfers between devices: 6.65 us -> 16.2 us  [over_ctx(): lax.ppermute(x, 'ctx', [(c, c ^ mask) for c in range(ctx) if core is None...]
    ppermute x12, starting transfers between devices: 11.4 us -> 7.17 us  [along_z(): lax.ppermute(x, 'ctx', [(c, (c + 4 * steps) % ctx) for c in range(ctx)])]
    ppermute x2 -> x3, waiting for transfers between devices: 8.1 us -> 4.41 us  [across(): return lax.ppermute(x, ('ctx', 'tp'), pairs)]
    ppermute x2, waiting for transfers between devices: 2.12 us -> 0.01 us  [to_core(): lax.ppermute(x, 'ctx', [(c, c ^ 1) for c in range(ctx) if c % 2 != core])]
    ppermute x12, waiting for transfers between devices: 33.1 us -> 31.1 us  [along_z(): lax.ppermute(x, 'ctx', [(c, (c + 4 * steps) % ctx) for c in range(ctx)])]
    ppermute x2 -> x3, starting transfers between devices: 3.81 us -> 2.34 us  [across(): return lax.ppermute(x, ('ctx', 'tp'), pairs)]
    ppermute x5 -> x6, starting transfers between devices: 5.24 us -> 6.53 us  [over_tp(): return lax.ppermute(x, 'tp', [(0, 1), (1, 0)])]
    ppermute x5 -> x6, waiting for transfers between devices: 8.14 us -> 7.14 us  [over_tp(): return lax.ppermute(x, 'tp', [(0, 1), (1, 0)])]
  transfers between devices with their start and end apart: 36 -> 40, of which waited for: 19 -> 17; matrix products, arithmetic and copies ran while one was open for 0% -> 0% of each run, Pallas kernels for 13% -> 14%
where the time goes in v5:
time: 148 us; the launch traced here: 147 us
  waiting for transfers between devices  71.3 us (48%)
  starting transfers between devices  42.9 us (29%)
  Pallas kernels  30.5 us (21%)
  local copies, waits for them, and re-layouts  2.29 us (2%)
    ppermute x12, waiting for transfers between devices, along_z(): lax.ppermute(x, 'ctx', [(c, (c + 4 * steps) % ctx) for c in range(ctx)])  31.1 us
    pallas_call x26, Pallas kernels, call(): pl.pallas_call(kernel, out_shape=out_shape, in_specs=[pl.BlockSpec(memory...  30.5 us
    all_to_all x1, waiting for transfers between devices, heads_over_ctx(): lax.all_to_all(packed, 'ctx', split_axis=0, concat_axis=0, tiled=True)  23.5 us
    ppermute x16, starting transfers between devices, over_ctx(): lax.ppermute(x, 'ctx', [(c, c ^ mask) for c in range(ctx) if core is None...  16.2 us
    ppermute x12, starting transfers between devices, along_z(): lax.ppermute(x, 'ctx', [(c, (c + 4 * steps) % ctx) for c in range(ctx)])  7.17 us
    ppermute x6, waiting for transfers between devices, over_tp(): return lax.ppermute(x, 'tp', [(0, 1), (1, 0)])  7.14 us
    all_to_all x1, starting transfers between devices, heads_over_ctx(): lax.all_to_all(packed, 'ctx', split_axis=0, concat_axis=0, tiled=True)  6.57 us
    ppermute x6, starting transfers between devices, over_tp(): return lax.ppermute(x, 'tp', [(0, 1), (1, 0)])  6.53 us
  transfers between devices with their start and end apart: 40, of which 17 were waited for; matrix products, arithmetic and copies ran while one was open for 0% of the time, Pallas kernels for 14%

profile of v5, /device:TPU:13, one launch (start us, length us, event | category | flops | bytes accessed | tf_op | source)
XLA Modules:
  0.0 147.5 jit_solution(3680465199462263124)
XLA Ops:
  0.0 3.0 %shard_map.109 = bf16[16,272,128]{2,1,0:T(8,128)(2,1)} custom-call(s32[1,64]{1,0:T(1,128)} %bitcast.22, s32[4,64]{1,0:T(4,128)} %bitcast.20, f32[4,64]{1,0:T(4,128)} %bitcast.21, bf16[64,2048]{1,0:T(8,128)(2,1)} %q_ref.1, bf16[64,2048]{1,0:T(8,128)(2,1)} %k_ref.1, bf16[64,2048]{1,0:T(8,128)(2,1)} %v_ref.1, bf16[64,2048]{1,0:T(8,128)(2,1)} %r_ref.1), custom_call_target="tpu_custom_call" | custom-call | tf_op jit(solution)/shard_map/pallas_call | solution.py:29
  3.1 6.6 %all-to-all-start = ((bf16[16,272,128]{2,1,0:T(8,128)(2,1)}), bf16[16,272,128]{2,1,0:T(8,128)(2,1)S(1)}, u32[]{:S(2)}, u32[]{:S(2)}) async-start(bf16[16,272,128]{2,1,0:T(8,128)(2,1)} %shard_map.109), calls=%async_computation | async-start | bytes 2228224 | tf_op jit(solution)/shard_map/all_to_all | solution.py:394
  9.6 1.3 collective-permute-start
  10.9 1.5 %collective-permute-done = bf16[2048]{0:T(1024)(128)(2,1)S(1)} collective-permute-done((bf16[2048]{0:T(1024)(128)(2,1)S(1)}, bf16[2048]{0:T(1024)(128)(2,1)S(1)}, u32[]{:S(2)}, u32[]{:S(2)}) %collective-permute-start) | collective-permute-done | bytes 4128 | tf_op jit(solution)/shard_map/ppermute | solution.py:376
  12.5 23.5 %all-to-all-done.x_ref = bf16[16,272,128]{2,1,0:T(8,128)(2,1)S(1)} async-done(((bf16[16,272,128]{2,1,0:T(8,128)(2,1)}), bf16[16,272,128]{2,1,0:T(8,128)(2,1)S(1)}, u32[]{:S(2)}, u32[]{:S(2)}) %all-to-all-start) | async-done | bytes 1114144 | tf_op jit(solution)/shard_map/all_to_all | solution.py:394
  36.0 2.0 %shard_map.110 = (bf16[512,128]{1,0:T(8,128)(2,1)S(1)}, bf16[512,128]{1,0:T(8,128)(2,1)S(1)}, bf16[2,320,256]{2,1,0:T(8,128)(2,1)S(1)}, bf16[2,320,256]{2,1,0:T(...) custom-call(bf16[16,272,128]{2,1,0:T(8,128)(2,1)S(1)} %all-to-all-done.x_ref), custom_call_target="tpu_custom_call" | custom-call | tf_op jit(solution)/shard_map/pallas_call | solution.py:29
  38.3 1.3 collective-permute-start.4
  39.6 1.1 collective-permute-start.5
  40.8 1.4 collective-permute-start.3
  43.2 2.4 %collective-permute-done.2.refs_2_ = bf16[512,128]{1,0:T(8,128)(2,1)S(1)} collective-permute-done((bf16[512,128]{1,0:T(8,128)(2,1)S(1)}, bf16[512,128]{1,0:T(8,128)(2,1)S(1)}, u32[]{:S(2)}, u32[]{:S(2)}) %collective-permute-start.2) | collective-permute-done | bytes 131104 | tf_op jit(solution)/shard_map/ppermute | solution.py:373
  45.6 8.4 %collective-permute-done.3.refs_3_ = bf16[512,128]{1,0:T(8,128)(2,1)S(1)} collective-permute-done((bf16[512,128]{1,0:T(8,128)(2,1)S(1)}, bf16[512,128]{1,0:T(8,128)(2,1)S(1)}, u32[]{:S(2)}, u32[]{:S(2)}) %collective-permute-start.3) | collective-permute-done | bytes 131104 | tf_op jit(solution)/shard_map/ppermute | solution.py:373
  54.9 1.6 %collective-permute-start.12 = (bf16[4,320,128]{2,1,0:T(8,128)(2,1)S(1)}, bf16[4,320,128]{2,1,0:T(8,128)(2,1)S(1)}, u32[]{:S(2)}, u32[]{:S(2)}) collective-permute-start(bf16[4,320,128]{2,1,0:T(8,128)(2,1)S(1)} %get-tuple-element.65.refs_4_), channel_id=1, source_target_pairs={{0,4},{2,6},{4,0},{6,2},{8,12},{10,14},{12,8},{14,10},{16,20},{18,... | collective-permute-start | bytes 983048 | tf_op jit(solution)/shard_map/ppermute | solution.py:370
  56.6 1.2 collective-permute-start.14
  58.7 7.7 %collective-permute-done.7.refs_2_ = bf16[512,128]{1,0:T(8,128)(2,1)S(1)} collective-permute-done((bf16[512,128]{1,0:T(8,128)(2,1)S(1)}, bf16[512,128]{1,0:T(8,128)(2,1)S(1)}, u32[]{:S(2)}, u32[]{:S(2)}) %collective-permute-start.7) | collective-permute-done | bytes 131104 | tf_op jit(solution)/shard_map/ppermute | solution.py:373
  68.4 1.0 shard_map.114.lhs_ref.own_ref
  69.5 2.1 %collective-permute-start.15 = (bf16[320,2176]{1,0:T(8,128)(2,1)S(1)}, bf16[320,2176]{1,0:T(8,128)(2,1)S(1)}, u32[]{:S(2)}, u32[]{:S(2)}) collective-permute-start(bf16[320,2176]{1,0:T(8,128)(2,1)S(1)} %shard_map.114.lhs_ref.own_ref), channel_id=1, source_target_pairs={{0,2},{2,0},{4,6},{6,4},{8,10},{10,8},{12,14},{14,12},{16,18},{18,... | collective-permute-start | bytes 4177928 | tf_op jit(solution)/shard_map/ppermute | solution.py:370
  71.6 1.5 collective-permute-start.9
  73.1 1.5 collective-permute-start.10
  74.6 2.2 %copy-done.1 = bf16[1,4096,512]{2,1,0:T(8,128)(2,1)S(1)} copy-done((bf16[1,4096,512]{2,1,0:T(8,128)(2,1)S(1)}, bf16[1,4096,512]{2,1,0:T(8,128)(2,1)}, u32[]{:S(2)}) %copy-start.1) | copy-done | bytes 4194328
  76.8 2.1 %shard_map.115 = (f32[320,512]{1,0:T(8,128)S(1)}, f32[320,512]{1,0:T(8,128)S(1)}) custom-call(s32[2]{0:T(128)S(1)} %pad_add_fusion.idx_ref, bf16[4096,512]{1,0:T(8,128)(2,1)S(1)} %bitcast.8, bf16[4096,512]{1,0:T(8,128)(2,1)S(1)} %bitcast.12, bf16[320,2176]{1,0:T(8,128)(2,1)S(1)} %shard_map.114.lhs_ref.own_ref), custom_call_target="tpu_custom_call" | custom-call | tf_op jit(solution)/shard_map/pallas_call | solution.py:29
  78.9 2.1 %shard_map.116.refs_6_.own_ref = bf16[320,512]{1,0:T(8,128)(2,1)S(1)} custom-call(s32[2]{0:T(128)S(1)} %pad_add_fusion.idx_ref, bf16[4096,512]{1,0:T(8,128)(2,1)S(1)} %bitcast.9, bf16[4096,512]{1,0:T(8,128)(2,1)S(1)} %bitcast.13, bf16[320,2176]{1,0:T(8,128)(2,1)S(1)} %shard_map.114.lhs_ref.own_ref, bf16[320,2176]{1,0:T(8,128)(2,1)S(1)} %collective-permute-done.15.lhs_ref, ...), custom_call_target="tpu_custom_call" | custom-call | tf_op jit(solution)/shard_map/pallas_call | solution.py:29
  81.0 4.4 %collective-permute-done.11.refs_3_ = bf16[3,320,128]{2,1,0:T(8,128)(2,1)S(1)} collective-permute-done((bf16[3,320,128]{2,1,0:T(8,128)(2,1)S(1)}, bf16[3,320,128]{2,1,0:T(8,128)(2,1)S(1)}, u32[]{:S(2)}, u32[]{:S(2)}) %collective-permute-start.11) | collective-permute-done | bytes 245792 | tf_op jit(solution)/shard_map/ppermute | solution.py:380
  86.4 1.7 %collective-permute-start.16 = (bf16[320,2176]{1,0:T(8,128)(2,1)S(1)}, bf16[320,2176]{1,0:T(8,128)(2,1)S(1)}, u32[]{:S(2)}, u32[]{:S(2)}) collective-permute-start(bf16[320,2176]{1,0:T(8,128)(2,1)S(1)} %shard_map.117.lhs_ref.own_ref), channel_id=1, source_target_pairs={{0,2},{2,0},{4,6},{6,4},{8,10},{10,8},{12,14},{14,12},{16,18},{18,... | collective-permute-start | bytes 4177928 | tf_op jit(solution)/shard_map/ppermute | solution.py:370
  88.1 1.4 collective-permute-start.19
  89.5 2.1 %shard_map.118 = (f32[320,512]{1,0:T(8,128)S(1)}, f32[320,512]{1,0:T(8,128)S(1)}) custom-call(s32[2]{0:T(128)S(1)} %pad_add_fusion.idx_ref, bf16[4096,512]{1,0:T(8,128)(2,1)S(1)} %bitcast.10, bf16[4096,512]{1,0:T(8,128)(2,1)S(1)} %bitcast.14, bf16[320,2176]{1,0:T(8,128)(2,1)S(1)} %shard_map.117.lhs_ref.own_ref), custom_call_target="tpu_custom_call" | custom-call | tf_op jit(solution)/shard_map/pallas_call | solution.py:29
  91.6 2.1 %shard_map.119.refs_2_.refs_0_.own_ref = bf16[320,512]{1,0:T(8,128)(2,1)S(1)} custom-call(s32[2]{0:T(128)S(1)} %pad_add_fusion.idx_ref, bf16[4096,512]{1,0:T(8,128)(2,1)S(1)} %bitcast.11, bf16[4096,512]{1,0:T(8,128)(2,1)S(1)} %bitcast.15, bf16[320,2176]{1,0:T(8,128)(2,1)S(1)} %shard_map.117.lhs_ref.own_ref, ...), custom_call_target="tpu_custom_call" | custom-call | tf_op jit(solution)/shard_map/pallas_call | solution.py:29
  94.5 2.9 %collective-permute-done.19.peer_ref = bf16[320,512]{1,0:T(8,128)(2,1)S(1)} collective-permute-done((bf16[320,512]{1,0:T(8,128)(2,1)S(1)}, bf16[320,512]{1,0:T(8,128)(2,1)S(1)}, u32[]{:S(2)}, u32[]{:S(2)}) %collective-permute-start.19) | collective-permute-done | bytes 327712 | tf_op jit(solution)/shard_map/ppermute | solution.py:376
  97.4 1.4 shard_map.123
  98.8 1.4 collective-permute-start.20
  100.8 1.4 shard_map.122
  102.2 2.2 %collective-permute-done.24.refs_8_.peer_ref = bf16[320,512]{1,0:T(8,128)(2,1)S(1)} collective-permute-done((bf16[320,512]{1,0:T(8,128)(2,1)S(1)}, bf16[320,512]{1,0:T(8,128)(2,1)S(1)}, u32[]{:S(2)}, u32[]{:S(2)}) %collective-permute-start.24) | collective-permute-done | bytes 327712 | tf_op jit(solution)/shard_map/ppermute | solution.py:376
  105.0 1.5 %collective-permute-start.25 = (bf16[160,1024]{1,0:T(8,128)(2,1)S(1)}, bf16[160,1024]{1,0:T(8,128)(2,1)S(1)}, u32[]{:S(2)}, u32[]{:S(2)}) collective-permute-start(bf16[160,1024]{1,0:T(8,128)(2,1)S(1)} %shard_map.125.refs_0_), channel_id=1, source_target_pairs={{0,4},{2,6},{4,0},{6,2},{8,12},{10,14},{12,8},{14,10},{16,20},{18,... | collective-permute-start | bytes 983048 | tf_op jit(solution)/shard_map/ppermute | solution.py:370
  106.6 1.4 shard_map.129
  108.0 1.2 collective-permute-start.30
  110.8 1.4 shard_map.128
  112.2 1.3 collective-permute-done.25.got_ref
  115.1 1.5 %collective-permute-start.34 = (bf16[160,1024]{1,0:T(8,128)(2,1)S(1)}, bf16[160,1024]{1,0:T(8,128)(2,1)S(1)}, u32[]{:S(2)}, u32[]{:S(2)}) collective-permute-start(bf16[160,1024]{1,0:T(8,128)(2,1)S(1)} %shard_map.131), channel_id=1, source_target_pairs={{0,4},{2,6},{4,0},{6,2},{8,12},{10,14},{12,8},{14,10},{16,20},{18,... | collective-permute-start | bytes 983048 | tf_op jit(solution)/shard_map/ppermute | solution.py:370
  118.6 1.5 collective-permute-start.28
  120.1 2.6 %collective-permute-done.34.got_ref = bf16[160,1024]{1,0:T(8,128)(2,1)S(1)} collective-permute-done((bf16[160,1024]{1,0:T(8,128)(2,1)S(1)}, bf16[160,1024]{1,0:T(8,128)(2,1)S(1)}, u32[]{:S(2)}, u32[]{:S(2)}) %collective-permute-start.34) | collective-permute-done | bytes 327712 | tf_op jit(solution)/shard_map/ppermute | solution.py:370
  123.7 1.2 collective-permute-start.36
  124.9 1.4 collective-permute-start.37
  126.3 1.3 collective-permute-start.17
  127.6 8.7 %collective-permute-done.28.refs_2_ = bf16[64,1024]{1,0:T(8,128)(2,1)S(1)} collective-permute-done((bf16[64,1024]{1,0:T(8,128)(2,1)S(1)}, bf16[64,1024]{1,0:T(8,128)(2,1)S(1)}, u32[]{:S(2)}, u32[]{:S(2)}) %collective-permute-start.28) | collective-permute-done | bytes 131104 | tf_op jit(solution)/shard_map/ppermute | solution.py:373
  136.3 2.8 %collective-permute-start.29 = (f32[64,1024]{1,0:T(8,128)S(1)}, f32[64,1024]{1,0:T(8,128)S(1)}, u32[]{:S(2)}, u32[]{:S(2)}) collective-permute-start(f32[64,1024]{1,0:T(8,128)S(1)} %shard_map.127.refs_2_), channel_id=1, source_target_pairs={{2,0},{6,4},{10,8},{14,12},{18,16},{22,20},{26,24},{30,28},{3,1},{... | collective-permute-start | bytes 786440 | tf_op jit(solution)/shard_map/ppermute | solution.py:383
  139.2 2.7 %collective-permute-done.37.refs_2_ = bf16[64,1024]{1,0:T(8,128)(2,1)S(1)} collective-permute-done((bf16[64,1024]{1,0:T(8,128)(2,1)S(1)}, bf16[64,1024]{1,0:T(8,128)(2,1)S(1)}, u32[]{:S(2)}, u32[]{:S(2)}) %collective-permute-start.37) | collective-permute-done | bytes 131104 | tf_op jit(solution)/shard_map/ppermute | solution.py:373
  142.0 1.3 collective-permute-start.38
  143.9 1.2 collective-permute-start.18
  146.0 1.4 shard_map.134
  (76 shorter events, 16.1 us)
Async XLA Ops:
  3.1 6.6 %copy-start.4 = (bf16[2048]{0:T(1024)(128)(2,1)S(1)}, bf16[2048]{0:T(1024)(128)(2,1)}, u32[]{:S(2)}) copy-start(bf16[2048]{0:T(1024)(128)(2,1)} %param.15) | copy-start | bytes 12292
  3.1 32.9 %all-to-all-start = ((bf16[16,272,128]{2,1,0:T(8,128)(2,1)}), bf16[16,272,128]{2,1,0:T(8,128)(2,1)S(1)}, u32[]{:S(2)}, u32[]{:S(2)}) async-start(bf16[16,272,128]{2,1,0:T(8,128)(2,1)} %shard_map.109), calls=%async_computation | async-start | bytes 2228224 | tf_op jit(solution)/shard_map/all_to_all | solution.py:394
  9.6 2.8 %collective-permute-start = (bf16[2048]{0:T(1024)(128)(2,1)S(1)}, bf16[2048]{0:T(1024)(128)(2,1)S(1)}, u32[]{:S(2)}, u32[]{:S(2)}) collective-permute-start(bf16[2048]{0:T(1024)(128)(2,1)S(1)} %copy-done.4), channel_id=1, source_target_pairs={{0,1},{1,0},{2,3},{3,2},{4,5},{5,4},{6,7},{7,6},{8,9},{9,8},{10,11... | collective-permute-start | bytes 12296 | tf_op jit(solution)/shard_map/ppermute | solution.py:376
  38.0 4.9 %collective-permute-start.1 = (bf16[512,128]{1,0:T(8,128)(2,1)S(1)}, bf16[512,128]{1,0:T(8,128)(2,1)S(1)}, u32[]{:S(2)}, u32[]{:S(2)}) collective-permute-start(bf16[512,128]{1,0:T(8,128)(2,1)S(1)} %get-tuple-element.57.even_ref.refs_0_), channel_id=1, source_target_pairs={{0,8},{2,10},{4,12},{6,14},{8,16},{10,18},{12,20},{14,22},{16,24},... | collective-permute-start | bytes 393224 | tf_op jit(solution)/shard_map/ppermute | solution.py:373
  38.3 15.7 %collective-permute-start.4 = (bf16[2,320,128]{2,1,0:T(8,128)(2,1)S(1)}, bf16[2,320,128]{2,1,0:T(8,128)(2,1)S(1)}, u32[]{:S(2)}, u32[]{:S(2)}) collective-permute-start(bf16[2,320,128]{2,1,0:T(8,128)(2,1)S(1)} %get-tuple-element.61), channel_id=1, source_target_pairs={{0,1},{1,0},{2,3},{3,2},{4,5},{5,4},{6,7},{7,6},{8,9},{9,8},{10,11... | collective-permute-start | bytes 491528 | tf_op jit(solution)/shard_map/ppermute | solution.py:376
  39.6 14.4 %collective-permute-start.5 = (bf16[2,320,128]{2,1,0:T(8,128)(2,1)S(1)}, bf16[2,320,128]{2,1,0:T(8,128)(2,1)S(1)}, u32[]{:S(2)}, u32[]{:S(2)}) collective-permute-start(bf16[2,320,128]{2,1,0:T(8,128)(2,1)S(1)} %get-tuple-element.62), channel_id=1, source_target_pairs={{0,5},{1,4},{2,7},{3,6},{4,1},{5,0},{6,3},{7,2},{8,13},{9,12},{10,... | collective-permute-start | bytes 491528 | tf_op jit(solution)/shard_map/ppermute | solution.py:380
  40.8 4.8 %collective-permute-start.2 = (bf16[512,128]{1,0:T(8,128)(2,1)S(1)}, bf16[512,128]{1,0:T(8,128)(2,1)S(1)}, u32[]{:S(2)}, u32[]{:S(2)}) collective-permute-start(bf16[512,128]{1,0:T(8,128)(2,1)S(1)} %get-tuple-element.57.even_ref.refs_0_), channel_id=1, source_target_pairs={{0,16},{2,18},{4,20},{6,22},{8,24},{10,26},{12,28},{14,30},{16,0},... | collective-permute-start | bytes 393224 | tf_op jit(solution)/shard_map/ppermute | solution.py:373
  40.8 13.3 %collective-permute-start.3 = (bf16[512,128]{1,0:T(8,128)(2,1)S(1)}, bf16[512,128]{1,0:T(8,128)(2,1)S(1)}, u32[]{:S(2)}, u32[]{:S(2)}) collective-permute-start(bf16[512,128]{1,0:T(8,128)(2,1)S(1)} %get-tuple-element.57.even_ref.refs_0_), channel_id=1, source_target_pairs={{0,24},{2,26},{4,28},{6,30},{8,0},{10,2},{12,4},{14,6},{16,8},{18,... | collective-permute-start | bytes 393224 | tf_op jit(solution)/shard_map/ppermute | solution.py:373
  42.9 15.3 %collective-permute-start.6 = (bf16[512,128]{1,0:T(8,128)(2,1)S(1)}, bf16[512,128]{1,0:T(8,128)(2,1)S(1)}, u32[]{:S(2)}, u32[]{:S(2)}) collective-permute-start(bf16[512,128]{1,0:T(8,128)(2,1)S(1)} %get-tuple-element.64.odd_ref.refs_0_), channel_id=1, source_target_pairs={{0,8},{2,10},{4,12},{6,14},{8,16},{10,18},{12,20},{14,22},{16,24},... | collective-permute-start | bytes 393224 | tf_op jit(solution)/shard_map/ppermute | solution.py:373
  54.9 13.5 %collective-permute-start.12 = (bf16[4,320,128]{2,1,0:T(8,128)(2,1)S(1)}, bf16[4,320,128]{2,1,0:T(8,128)(2,1)S(1)}, u32[]{:S(2)}, u32[]{:S(2)}) collective-permute-start(bf16[4,320,128]{2,1,0:T(8,128)(2,1)S(1)} %get-tuple-element.65.refs_4_), channel_id=1, source_target_pairs={{0,4},{2,6},{4,0},{6,2},{8,12},{10,14},{12,8},{14,10},{16,20},{18,... | collective-permute-start | bytes 983048 | tf_op jit(solution)/shard_map/ppermute | solution.py:370
  56.6 11.1 %collective-permute-start.14 = (bf16[3,320,128]{2,1,0:T(8,128)(2,1)S(1)}, bf16[3,320,128]{2,1,0:T(8,128)(2,1)S(1)}, u32[]{:S(2)}, u32[]{:S(2)}) collective-permute-start(bf16[3,320,128]{2,1,0:T(8,128)(2,1)S(1)} %slice.15), channel_id=1, source_target_pairs={{0,5},{1,4},{2,7},{3,6},{4,1},{5,0},{6,3},{7,2},{8,13},{9,12},{10,... | collective-permute-start | bytes 737288 | tf_op jit(solution)/shard_map/ppermute | solution.py:380
  57.8 10.4 %collective-permute-start.13 = (bf16[3,320,128]{2,1,0:T(8,128)(2,1)S(1)}, bf16[3,320,128]{2,1,0:T(8,128)(2,1)S(1)}, u32[]{:S(2)}, u32[]{:S(2)}) collective-permute-start(bf16[3,320,128]{2,1,0:T(8,128)(2,1)S(1)} %slice.14), channel_id=1, source_target_pairs={{0,1},{1,0},{2,3},{3,2},{4,5},{5,4},{6,7},{7,6},{8,9},{9,8},{10,11... | collective-permute-start | bytes 737288 | tf_op jit(solution)/shard_map/ppermute | solution.py:376
  58.2 8.3 %collective-permute-start.7 = (bf16[512,128]{1,0:T(8,128)(2,1)S(1)}, bf16[512,128]{1,0:T(8,128)(2,1)S(1)}, u32[]{:S(2)}, u32[]{:S(2)}) collective-permute-start(bf16[512,128]{1,0:T(8,128)(2,1)S(1)} %get-tuple-element.64.odd_ref.refs_0_), channel_id=1, source_target_pairs={{0,16},{2,18},{4,20},{6,22},{8,24},{10,26},{12,28},{14,30},{16,0},... | collective-permute-start | bytes 393224 | tf_op jit(solution)/shard_map/ppermute | solution.py:373
  58.3 8.6 %collective-permute-start.8 = (bf16[512,128]{1,0:T(8,128)(2,1)S(1)}, bf16[512,128]{1,0:T(8,128)(2,1)S(1)}, u32[]{:S(2)}, u32[]{:S(2)}) collective-permute-start(bf16[512,128]{1,0:T(8,128)(2,1)S(1)} %get-tuple-element.64.odd_ref.refs_0_), channel_id=1, source_target_pairs={{0,24},{2,26},{4,28},{6,30},{8,0},{10,2},{12,4},{14,6},{16,8},{18,... | collective-permute-start | bytes 393224 | tf_op jit(solution)/shard_map/ppermute | solution.py:373
  68.4 6.1 %copy-start = (bf16[1,4096,512]{2,1,0:T(8,128)(2,1)S(1)}, bf16[1,4096,512]{2,1,0:T(8,128)(2,1)}, u32[]{:S(2)}) copy-start(bf16[1,4096,512]{2,1,0:T(8,128)(2,1)} %param.19) | copy-start | bytes 12582916
  69.5 9.4 %collective-permute-start.15 = (bf16[320,2176]{1,0:T(8,128)(2,1)S(1)}, bf16[320,2176]{1,0:T(8,128)(2,1)S(1)}, u32[]{:S(2)}, u32[]{:S(2)}) collective-permute-start(bf16[320,2176]{1,0:T(8,128)(2,1)S(1)} %shard_map.114.lhs_ref.own_ref), channel_id=1, source_target_pairs={{0,2},{2,0},{4,6},{6,4},{8,10},{10,8},{12,14},{14,12},{16,18},{18,... | collective-permute-start | bytes 4177928 | tf_op jit(solution)/shard_map/ppermute | solution.py:370
  71.6 13.8 %collective-permute-start.9 = (bf16[4,320,128]{2,1,0:T(8,128)(2,1)S(1)}, bf16[4,320,128]{2,1,0:T(8,128)(2,1)S(1)}, u32[]{:S(2)}, u32[]{:S(2)}) collective-permute-start(bf16[4,320,128]{2,1,0:T(8,128)(2,1)S(1)} %get-tuple-element.71), channel_id=1, source_target_pairs={{0,4},{2,6},{4,0},{6,2},{8,12},{10,14},{12,8},{14,10},{16,20},{18,... | collective-permute-start | bytes 983048 | tf_op jit(solution)/shard_map/ppermute | solution.py:370
  73.1 7.9 %collective-permute-start.10 = (bf16[3,320,128]{2,1,0:T(8,128)(2,1)S(1)}, bf16[3,320,128]{2,1,0:T(8,128)(2,1)S(1)}, u32[]{:S(2)}, u32[]{:S(2)}) collective-permute-start(bf16[3,320,128]{2,1,0:T(8,128)(2,1)S(1)} %slice.12), channel_id=1, source_target_pairs={{0,1},{1,0},{2,3},{3,2},{4,5},{5,4},{6,7},{7,6},{8,9},{9,8},{10,11... | collective-permute-start | bytes 737288 | tf_op jit(solution)/shard_map/ppermute | solution.py:376
  74.6 10.8 %collective-permute-start.11 = (bf16[3,320,128]{2,1,0:T(8,128)(2,1)S(1)}, bf16[3,320,128]{2,1,0:T(8,128)(2,1)S(1)}, u32[]{:S(2)}, u32[]{:S(2)}) collective-permute-start(bf16[3,320,128]{2,1,0:T(8,128)(2,1)S(1)} %slice.13), channel_id=1, source_target_pairs={{0,5},{1,4},{2,7},{3,6},{4,1},{5,0},{6,3},{7,2},{8,13},{9,12},{10,... | collective-permute-start | bytes 737288 | tf_op jit(solution)/shard_map/ppermute | solution.py:380
  74.6 2.2 %copy-start.1 = (bf16[1,4096,512]{2,1,0:T(8,128)(2,1)S(1)}, bf16[1,4096,512]{2,1,0:T(8,128)(2,1)}, u32[]{:S(2)}) copy-start(bf16[1,4096,512]{2,1,0:T(8,128)(2,1)} %param.20) | copy-start | bytes 12582916
  78.8 10.7 %copy-start.2 = (bf16[1,4096,512]{2,1,0:T(8,128)(2,1)S(1)}, bf16[1,4096,512]{2,1,0:T(8,128)(2,1)}, u32[]{:S(2)}) copy-start(bf16[1,4096,512]{2,1,0:T(8,128)(2,1)} %param.20) | copy-start | bytes 12582916
  86.4 5.1 %collective-permute-start.16 = (bf16[320,2176]{1,0:T(8,128)(2,1)S(1)}, bf16[320,2176]{1,0:T(8,128)(2,1)S(1)}, u32[]{:S(2)}, u32[]{:S(2)}) collective-permute-start(bf16[320,2176]{1,0:T(8,128)(2,1)S(1)} %shard_map.117.lhs_ref.own_ref), channel_id=1, source_target_pairs={{0,2},{2,0},{4,6},{6,4},{8,10},{10,8},{12,14},{14,12},{16,18},{18,... | collective-permute-start | bytes 4177928 | tf_op jit(solution)/shard_map/ppermute | solution.py:370
  88.1 9.3 %collective-permute-start.19 = (bf16[320,512]{1,0:T(8,128)(2,1)S(1)}, bf16[320,512]{1,0:T(8,128)(2,1)S(1)}, u32[]{:S(2)}, u32[]{:S(2)}) collective-permute-start(bf16[320,512]{1,0:T(8,128)(2,1)S(1)} %shard_map.116.refs_6_.own_ref), channel_id=1, source_target_pairs={{0,1},{1,0},{2,3},{3,2},{4,5},{5,4},{6,7},{7,6},{8,9},{9,8},{10,11... | collective-permute-start | bytes 983048 | tf_op jit(solution)/shard_map/ppermute | solution.py:376
  91.6 5.8 %copy-start.3 = (bf16[1,1024,2048]{2,1,0:T(8,128)(2,1)S(1)}, bf16[1,1024,2048]{2,1,0:T(8,128)(2,1)}, u32[]{:S(2)}) copy-start(bf16[1,1024,2048]{2,1,0:T(8,128)(2,1)} %param.21) | copy-start | bytes 12582916
  93.7 10.7 %collective-permute-start.24 = (bf16[320,512]{1,0:T(8,128)(2,1)S(1)}, bf16[320,512]{1,0:T(8,128)(2,1)S(1)}, u32[]{:S(2)}, u32[]{:S(2)}) collective-permute-start(bf16[320,512]{1,0:T(8,128)(2,1)S(1)} %shard_map.119.refs_2_.refs_0_.own_ref), channel_id=1, source_target_pairs={{0,1},{1,0},{2,3},{3,2},{4,5},{5,4},{6,7},{7,6},{8,9},{9,8},{10,11... | collective-permute-start | bytes 983048 | tf_op jit(solution)/shard_map/ppermute | solution.py:376
  98.8 3.4 %collective-permute-start.20 = (bf16[320,256]{1,0:T(8,128)(2,1)S(1)}, bf16[320,256]{1,0:T(8,128)(2,1)S(1)}, u32[]{:S(2)}, u32[]{:S(2)}) collective-permute-start(bf16[320,256]{1,0:T(8,128)(2,1)S(1)} %get-tuple-element.84), channel_id=1, source_target_pairs={{0,2},{2,0},{4,6},{6,4},{8,10},{10,8},{12,14},{14,12},{16,18},{18,... | collective-permute-start | bytes 491528 | tf_op jit(solution)/shard_map/ppermute | solution.py:370
  100.2 2.0 %collective-permute-start.21 = (bf16[320,256]{1,0:T(8,128)(2,1)S(1)}, bf16[320,256]{1,0:T(8,128)(2,1)S(1)}, u32[]{:S(2)}, u32[]{:S(2)}) collective-permute-start(bf16[320,256]{1,0:T(8,128)(2,1)S(1)} %get-tuple-element.85), channel_id=1, source_target_pairs={{0,2},{2,0},{4,6},{6,4},{8,10},{10,8},{12,14},{14,12},{16,18},{18,... | collective-permute-start | bytes 491528 | tf_op jit(solution)/shard_map/ppermute | solution.py:370
  100.2 1.9 %collective-permute-start.22 = (bf16[320,256]{1,0:T(8,128)(2,1)S(1)}, bf16[320,256]{1,0:T(8,128)(2,1)S(1)}, u32[]{:S(2)}, u32[]{:S(2)}) collective-permute-start(bf16[320,256]{1,0:T(8,128)(2,1)S(1)} %get-tuple-element.86), channel_id=1, source_target_pairs={{0,2},{2,0},{4,6},{6,4},{8,10},{10,8},{12,14},{14,12},{16,18},{18,... | collective-permute-start | bytes 491528 | tf_op jit(solution)/shard_map/ppermute | solution.py:370
  100.7 1.5 %collective-permute-start.23 = (bf16[320,256]{1,0:T(8,128)(2,1)S(1)}, bf16[320,256]{1,0:T(8,128)(2,1)S(1)}, u32[]{:S(2)}, u32[]{:S(2)}) collective-permute-start(bf16[320,256]{1,0:T(8,128)(2,1)S(1)} %get-tuple-element.87), channel_id=1, source_target_pairs={{0,2},{2,0},{4,6},{6,4},{8,10},{10,8},{12,14},{14,12},{16,18},{18,... | collective-permute-start | bytes 491528 | tf_op jit(solution)/shard_map/ppermute | solution.py:370
  105.0 8.4 %collective-permute-start.25 = (bf16[160,1024]{1,0:T(8,128)(2,1)S(1)}, bf16[160,1024]{1,0:T(8,128)(2,1)S(1)}, u32[]{:S(2)}, u32[]{:S(2)}) collective-permute-start(bf16[160,1024]{1,0:T(8,128)(2,1)S(1)} %shard_map.125.refs_0_), channel_id=1, source_target_pairs={{0,4},{2,6},{4,0},{6,2},{8,12},{10,14},{12,8},{14,10},{16,20},{18,... | collective-permute-start | bytes 983048 | tf_op jit(solution)/shard_map/ppermute | solution.py:370
  108.0 6.5 %collective-permute-start.30 = (bf16[320,256]{1,0:T(8,128)(2,1)S(1)}, bf16[320,256]{1,0:T(8,128)(2,1)S(1)}, u32[]{:S(2)}, u32[]{:S(2)}) collective-permute-start(bf16[320,256]{1,0:T(8,128)(2,1)S(1)} %get-tuple-element.97), channel_id=1, source_target_pairs={{0,2},{2,0},{4,6},{6,4},{8,10},{10,8},{12,14},{14,12},{16,18},{18,... | collective-permute-start | bytes 491528 | tf_op jit(solution)/shard_map/ppermute | solution.py:370
  109.2 5.3 %collective-permute-start.31 = (bf16[320,256]{1,0:T(8,128)(2,1)S(1)}, bf16[320,256]{1,0:T(8,128)(2,1)S(1)}, u32[]{:S(2)}, u32[]{:S(2)}) collective-permute-start(bf16[320,256]{1,0:T(8,128)(2,1)S(1)} %get-tuple-element.98), channel_id=1, source_target_pairs={{0,2},{2,0},{4,6},{6,4},{8,10},{10,8},{12,14},{14,12},{16,18},{18,... | collective-permute-start | bytes 491528 | tf_op jit(solution)/shard_map/ppermute | solution.py:370
  109.3 5.2 %collective-permute-start.32 = (bf16[320,256]{1,0:T(8,128)(2,1)S(1)}, bf16[320,256]{1,0:T(8,128)(2,1)S(1)}, u32[]{:S(2)}, u32[]{:S(2)}) collective-permute-start(bf16[320,256]{1,0:T(8,128)(2,1)S(1)} %get-tuple-element.99), channel_id=1, source_target_pairs={{0,2},{2,0},{4,6},{6,4},{8,10},{10,8},{12,14},{14,12},{16,18},{18,... | collective-permute-start | bytes 491528 | tf_op jit(solution)/shard_map/ppermute | solution.py:370
  109.7 4.8 %collective-permute-start.33 = (bf16[320,256]{1,0:T(8,128)(2,1)S(1)}, bf16[320,256]{1,0:T(8,128)(2,1)S(1)}, u32[]{:S(2)}, u32[]{:S(2)}) collective-permute-start(bf16[320,256]{1,0:T(8,128)(2,1)S(1)} %get-tuple-element.100), channel_id=1, source_target_pairs={{0,2},{2,0},{4,6},{6,4},{8,10},{10,8},{12,14},{14,12},{16,18},{18,... | collective-permute-start | bytes 491528 | tf_op jit(solution)/shard_map/ppermute | solution.py:370
  115.1 7.5 %collective-permute-start.34 = (bf16[160,1024]{1,0:T(8,128)(2,1)S(1)}, bf16[160,1024]{1,0:T(8,128)(2,1)S(1)}, u32[]{:S(2)}, u32[]{:S(2)}) collective-permute-start(bf16[160,1024]{1,0:T(8,128)(2,1)S(1)} %shard_map.131), channel_id=1, source_target_pairs={{0,4},{2,6},{4,0},{6,2},{8,12},{10,14},{12,8},{14,10},{16,20},{18,... | collective-permute-start | bytes 983048 | tf_op jit(solution)/shard_map/ppermute | solution.py:370
  116.7 8.2 %collective-permute-start.26 = (bf16[64,1024]{1,0:T(8,128)(2,1)S(1)}, bf16[64,1024]{1,0:T(8,128)(2,1)S(1)}, u32[]{:S(2)}, u32[]{:S(2)}) collective-permute-start(bf16[64,1024]{1,0:T(8,128)(2,1)S(1)} %get-tuple-element.89), channel_id=1, source_target_pairs={{0,8},{2,10},{4,12},{6,14},{8,16},{10,18},{12,20},{14,22},{16,24},... | collective-permute-start | bytes 393224 | tf_op jit(solution)/shard_map/ppermute | solution.py:373
  117.7 8.6 %collective-permute-start.27 = (bf16[64,1024]{1,0:T(8,128)(2,1)S(1)}, bf16[64,1024]{1,0:T(8,128)(2,1)S(1)}, u32[]{:S(2)}, u32[]{:S(2)}) collective-permute-start(bf16[64,1024]{1,0:T(8,128)(2,1)S(1)} %get-tuple-element.90), channel_id=1, source_target_pairs={{0,16},{2,18},{4,20},{6,22},{8,24},{10,26},{12,28},{14,30},{16,0},... | collective-permute-start | bytes 393224 | tf_op jit(solution)/shard_map/ppermute | solution.py:373
  118.6 17.7 %collective-permute-start.28 = (bf16[64,1024]{1,0:T(8,128)(2,1)S(1)}, bf16[64,1024]{1,0:T(8,128)(2,1)S(1)}, u32[]{:S(2)}, u32[]{:S(2)}) collective-permute-start(bf16[64,1024]{1,0:T(8,128)(2,1)S(1)} %get-tuple-element.91), channel_id=1, source_target_pairs={{0,24},{2,26},{4,28},{6,30},{8,0},{10,2},{12,4},{14,6},{16,8},{18,... | collective-permute-start | bytes 393224 | tf_op jit(solution)/shard_map/ppermute | solution.py:373
  123.6 15.5 %collective-permute-start.35 = (bf16[64,1024]{1,0:T(8,128)(2,1)S(1)}, bf16[64,1024]{1,0:T(8,128)(2,1)S(1)}, u32[]{:S(2)}, u32[]{:S(2)}) collective-permute-start(bf16[64,1024]{1,0:T(8,128)(2,1)S(1)} %get-tuple-element.102), channel_id=1, source_target_pairs={{0,8},{2,10},{4,12},{6,14},{8,16},{10,18},{12,20},{14,22},{16,24},... | collective-permute-start | bytes 393224 | tf_op jit(solution)/shard_map/ppermute | solution.py:373
  123.7 15.5 %collective-permute-start.36 = (bf16[64,1024]{1,0:T(8,128)(2,1)S(1)}, bf16[64,1024]{1,0:T(8,128)(2,1)S(1)}, u32[]{:S(2)}, u32[]{:S(2)}) collective-permute-start(bf16[64,1024]{1,0:T(8,128)(2,1)S(1)} %get-tuple-element.103), channel_id=1, source_target_pairs={{0,16},{2,18},{4,20},{6,22},{8,24},{10,26},{12,28},{14,30},{16,0},... | collective-permute-start | bytes 393224 | tf_op jit(solution)/shard_map/ppermute | solution.py:373
  124.9 17.0 %collective-permute-start.37 = (bf16[64,1024]{1,0:T(8,128)(2,1)S(1)}, bf16[64,1024]{1,0:T(8,128)(2,1)S(1)}, u32[]{:S(2)}, u32[]{:S(2)}) collective-permute-start(bf16[64,1024]{1,0:T(8,128)(2,1)S(1)} %get-tuple-element.104), channel_id=1, source_target_pairs={{0,24},{2,26},{4,28},{6,30},{8,0},{10,2},{12,4},{14,6},{16,8},{18,... | collective-permute-start | bytes 393224 | tf_op jit(solution)/shard_map/ppermute | solution.py:373
  126.3 17.0 %collective-permute-start.17 = (bf16[2,4,64,128]{3,2,1,0:T(8,128)(2,1)S(1)}, bf16[2,4,64,128]{3,2,1,0:T(8,128)(2,1)S(1)}, u32[]{:S(2)}, u32[]{:S(2)}) collective-permute-start(bf16[2,4,64,128]{3,2,1,0:T(8,128)(2,1)S(1)} %shard_map.120), channel_id=1, source_target_pairs={{0,4},{2,6},{4,0},{6,2},{8,12},{10,14},{12,8},{14,10},{16,20},{18,... | collective-permute-start | bytes 393224 | tf_op jit(solution)/shard_map/ppermute | solution.py:370
  136.3 9.7 %collective-permute-start.29 = (f32[64,1024]{1,0:T(8,128)S(1)}, f32[64,1024]{1,0:T(8,128)S(1)}, u32[]{:S(2)}, u32[]{:S(2)}) collective-permute-start(f32[64,1024]{1,0:T(8,128)S(1)} %shard_map.127.refs_2_), channel_id=1, source_target_pairs={{2,0},{6,4},{10,8},{14,12},{18,16},{22,20},{26,24},{30,28},{3,1},{... | collective-permute-start | bytes 786440 | tf_op jit(solution)/shard_map/ppermute | solution.py:383
  142.0 4.1 %collective-permute-start.38 = (f32[64,1024]{1,0:T(8,128)S(1)}, f32[64,1024]{1,0:T(8,128)S(1)}, u32[]{:S(2)}, u32[]{:S(2)}) collective-permute-start(f32[64,1024]{1,0:T(8,128)S(1)} %shard_map.133.refs_4_), channel_id=1, source_target_pairs={{0,2},{4,6},{8,10},{12,14},{16,18},{20,22},{24,26},{28,30},{1,3},{... | collective-permute-start | bytes 786440 | tf_op jit(solution)/shard_map/ppermute | solution.py:383
  143.9 2.2 %collective-permute-start.18 = (bf16[8,64,128]{2,1,0:T(8,128)(2,1)S(1)}, bf16[8,64,128]{2,1,0:T(8,128)(2,1)S(1)}, u32[]{:S(2)}, u32[]{:S(2)}) collective-permute-start(bf16[8,64,128]{2,1,0:T(8,128)(2,1)S(1)} %get-tuple-element.78), channel_id=1, source_target_pairs={{0,2},{2,0},{4,6},{6,4},{8,10},{10,8},{12,14},{14,12},{16,18},{18,... | collective-permute-start | bytes 393224 | tf_op jit(solution)/shard_map/ppermute | solution.py:370

commit v6 on v5

--- a/solution.py
+++ b/solution.py
@@ -16,6 +16,7 @@
 LANES = 128
 MIB = 1 << 20
 PARTS = 4
+GROUPS = (((0, 1, 2, 3, 4, 5),), ((0, 2, 4), (1, 3, 5)))
 
 
 def silu(v):
@@ -231,28 +232,31 @@
     return jnp.dot(lhs, weights, preferred_element_type=jnp.float32)
 
 
-def first_kernel(places, heads, idx_ref, wg_ref, wu_ref, lhs_ref, gate_ref, up_ref):
+def project_kernel(places, heads, flip, idx_ref, wg_ref, wu_ref, lhs_ref, *refs):
+    *before, gate_ref, up_ref = refs
     rows = gate_ref.shape[0]
-    offsets = row_offsets(places, heads, idx_ref[0], idx_ref[1], 0)
+    offsets = row_offsets(places, heads, idx_ref[0], idx_ref[1], flip)
     width = min(256, wg_ref.shape[1])
     for n in range(wg_ref.shape[1] // width):
         cols = slice(n * width, (n + 1) * width)
         lhs = lhs_ref[0:rows, 0 : len(offsets) * HD]
-        gate_ref[:, cols] = half_projection(lhs, offsets, wg_ref, cols)
-        up_ref[:, cols] = half_projection(lhs, offsets, wu_ref, cols)
-
-
-def second_kernel(places, heads, idx_ref, wg_ref, wu_ref, own_ref, lhs_ref, gate_ref, up_ref, hidden_ref):
+        for m, (weight_ref, out_ref) in enumerate(((wg_ref, gate_ref), (wu_ref, up_ref))):
+            total = half_projection(lhs, offsets, weight_ref, cols)
+            out_ref[:, cols] = before[m][:, cols] + total if before else total
+
+
+def hidden_kernel(places, heads, idx_ref, wg_ref, wu_ref, gate_ref, up_ref, lhs_ref, *refs):
+    hidden_ref = refs[-1]
     rows = gate_ref.shape[0]
-    me, plane = idx_ref[0], idx_ref[1]
-    offsets = row_offsets(places, heads, me, plane, 1)
-    last = len(offsets) * HD
-    squares = own_ref[0:rows, last:].astype(jnp.float32) + lhs_ref[0:rows, last:].astype(jnp.float32)
+    offsets = row_offsets(places, heads, idx_ref[0], idx_ref[1], 1)
+    squares = jnp.zeros((rows, HD), jnp.float32)
+    for ref in (lhs_ref, *refs[:-1]):
+        squares = squares + ref[:, ref.shape[1] - HD :].astype(jnp.float32)
     scale = lax.rsqrt(jnp.sum(squares, axis=1, keepdims=True) / D + EPS)
     width = min(256, wg_ref.shape[1])
     for n in range(wg_ref.shape[1] // width):
         cols = slice(n * width, (n + 1) * width)
-        lhs = lhs_ref[0:rows, 0:last]
+        lhs = lhs_ref[0:rows, 0 : len(offsets) * HD]
         gate = (gate_ref[:, cols] + half_projection(lhs, offsets, wg_ref, cols)) * scale
         up = (up_ref[:, cols] + half_projection(lhs, offsets, wu_ref, cols)) * scale
         hidden_ref[:, cols] = (silu(gate) * up).astype(jnp.bfloat16)
@@ -418,32 +422,44 @@
             smem=1,
         )
         blocks.append(own_rows)
-        compacted = [theirs]
         far = [over_tp(mine[1:]), across(theirs[1:])]
         pieces.append([mine, over_ctx(theirs, 2), *far, *near])
+        compacted = pieces[0][1:4]
         places.append(
             [[(k, 0, f, k) for k in range(levels)] for f in (0, 2)]
             + [[(k - 1, 1, f, k) for k in range(1, levels)] for f in (0, 2)]
             + [[(core, 1, f, 0)] for f in (0, 2)]
         )
     fronts, after = [], pieces[1][0]
-    for got, where in zip(pieces, places):
-        mixed = call(
-            functools.partial(scale_kernel, where),
-            shape(2 * slots, (4 * levels + 1) * HD),
-            (idx, gain, *got, after),
-            smem=1,
-        )
-        sums = call(
-            functools.partial(first_kernel, where, heads),
-            [shape(2 * slots, hidden_width, dtype=f32)] * 2,
-            (idx, wg, wu, mixed),
-            smem=1,
-        )
+    for groups, got, where in zip(GROUPS, pieces, places):
+        sums, swapped = [], []
+        for group in groups:
+            chosen = [where[n] for n in group]
+            mixed = call(
+                functools.partial(scale_kernel, chosen),
+                shape(2 * slots, (sum(map(len, chosen)) + 1) * HD),
+                (idx, gain, *[got[n] for n in group], after),
+                smem=1,
+            )
+            sums = call(
+                functools.partial(project_kernel, chosen, heads, 0),
+                [shape(2 * slots, hidden_width, dtype=f32)] * 2,
+                (idx, wg, wu, mixed, *sums),
+                smem=1,
+            )
+            other = over_ctx(mixed, 1)
+            swapped += [mixed, other]
+            if group is not groups[-1]:
+                sums = call(
+                    functools.partial(project_kernel, chosen, heads, 1),
+                    [shape(2 * slots, hidden_width, dtype=f32)] * 2,
+                    (idx, wg, wu, other, *sums),
+                    smem=1,
+                )
         hidden = call(
-            functools.partial(second_kernel, where, heads),
+            functools.partial(hidden_kernel, chosen, heads),
             shape(2 * slots, hidden_width),
-            (idx, wg, wu, mixed, over_ctx(mixed, 1), *sums),
+            (idx, wg, wu, *sums, swapped[-1], *swapped[:-1]),
             smem=1,
         )
         fronts.append((hidden, over_tp(hidden)))

time: 148 us -> 147 us (level)
  waiting for transfers between devices: 71.3 us -> 66.1 us
  starting transfers between devices: 42.9 us -> 45 us
  Pallas kernels: 30.5 us -> 32.5 us
    ppermute x12, waiting for transfers between devices: 31.1 us -> 28.6 us  [along_z(): lax.ppermute(x, 'ctx', [(c, (c + 4 * steps) % ctx) for c in range(ctx)])]
    ppermute x16 -> x17, starting transfers between devices: 16.2 us -> 18.6 us  [over_ctx(): lax.ppermute(x, 'ctx', [(c, c ^ mask) for c in range(ctx) if core is None...]
    ppermute x2, starting transfers between devices: 4.12 us -> 6.21 us  [to_core(): lax.ppermute(x, 'ctx', [(c, c ^ 1) for c in range(ctx) if c % 2 != core])]
    pallas_call x26 -> x29, Pallas kernels: 30.5 us -> 32.5 us  [call(): pl.pallas_call(kernel, out_shape=out_shape, in_specs=[pl.BlockSpec(memory...]
    ppermute x12, starting transfers between devices: 7.17 us -> 5.5 us  [along_z(): lax.ppermute(x, 'ctx', [(c, (c + 4 * steps) % ctx) for c in range(ctx)])]
    ppermute x16 -> x17, waiting for transfers between devices: 5.1 us -> 4.68 us  [over_ctx(): lax.ppermute(x, 'ctx', [(c, c ^ mask) for c in range(ctx) if core is None...]
  transfers between devices with their start and end apart: 40 -> 41, of which waited for: 17 -> 16; matrix products, arithmetic and copies ran while one was open for 0% -> 0% of each run, Pallas kernels for 14% -> 16%
where the time goes in v6:
time: 147 us
  waiting for transfers between devices  66.1 us (45%)
  starting transfers between devices  45 us (31%)
  Pallas kernels  32.5 us (22%)
  local copies, waits for them, and re-layouts  2.29 us (2%)
    pallas_call x29, Pallas kernels, call(): pl.pallas_call(kernel, out_shape=out_shape, in_specs=[pl.BlockSpec(memory...  32.5 us
    ppermute x12, waiting for transfers between devices, along_z(): lax.ppermute(x, 'ctx', [(c, (c + 4 * steps) % ctx) for c in range(ctx)])  28.6 us
    all_to_all x1, waiting for transfers between devices, heads_over_ctx(): lax.all_to_all(packed, 'ctx', split_axis=0, concat_axis=0, tiled=True)  23.5 us
    ppermute x17, starting transfers between devices, over_ctx(): lax.ppermute(x, 'ctx', [(c, c ^ mask) for c in range(ctx) if core is None...  18.6 us
    ppermute x6, starting transfers between devices, over_tp(): return lax.ppermute(x, 'tp', [(0, 1), (1, 0)])  6.95 us
    all_to_all x1, starting transfers between devices, heads_over_ctx(): lax.all_to_all(packed, 'ctx', split_axis=0, concat_axis=0, tiled=True)  6.57 us
    ppermute x2, starting transfers between devices, to_core(): lax.ppermute(x, 'ctx', [(c, c ^ 1) for c in range(ctx) if c % 2 != core])  6.21 us
    ppermute x6, waiting for transfers between devices, over_tp(): return lax.ppermute(x, 'tp', [(0, 1), (1, 0)])  6.02 us
  transfers between devices with their start and end apart: 41, of which 16 were waited for; matrix products, arithmetic and copies ran while one was open for 0% of the time, Pallas kernels for 16%

profile of v6, /device:TPU:13, one launch (start us, length us, event | category | flops | bytes accessed | tf_op | source)
XLA Modules:
  0.0 146.5 jit_solution(13684711696034270373)
XLA Ops:
  0.0 3.0 %shard_map.109 = bf16[16,272,128]{2,1,0:T(8,128)(2,1)} custom-call(s32[1,64]{1,0:T(1,128)} %bitcast.26, s32[4,64]{1,0:T(4,128)} %bitcast.24, f32[4,64]{1,0:T(4,128)} %bitcast.25, bf16[64,2048]{1,0:T(8,128)(2,1)} %q_ref.1, bf16[64,2048]{1,0:T(8,128)(2,1)} %k_ref.1, bf16[64,2048]{1,0:T(8,128)(2,1)} %v_ref.1, bf16[64,2048]{1,0:T(8,128)(2,1)} %r_ref.1), custom_call_target="tpu_custom_call" | custom-call | tf_op jit(solution)/shard_map/pallas_call | solution.py:30
  3.0 6.6 %all-to-all-start = ((bf16[16,272,128]{2,1,0:T(8,128)(2,1)}), bf16[16,272,128]{2,1,0:T(8,128)(2,1)S(1)}, u32[]{:S(2)}, u32[]{:S(2)}) async-start(bf16[16,272,128]{2,1,0:T(8,128)(2,1)} %shard_map.109), calls=%async_computation | async-start | bytes 2228224 | tf_op jit(solution)/shard_map/all_to_all | solution.py:398
  9.6 1.3 collective-permute-start
  10.9 1.5 %collective-permute-done = bf16[2048]{0:T(1024)(128)(2,1)S(1)} collective-permute-done((bf16[2048]{0:T(1024)(128)(2,1)S(1)}, bf16[2048]{0:T(1024)(128)(2,1)S(1)}, u32[]{:S(2)}, u32[]{:S(2)}) %collective-permute-start) | collective-permute-done | bytes 4128 | tf_op jit(solution)/shard_map/ppermute | solution.py:380
  12.4 23.5 %all-to-all-done.x_ref = bf16[16,272,128]{2,1,0:T(8,128)(2,1)S(1)} async-done(((bf16[16,272,128]{2,1,0:T(8,128)(2,1)}), bf16[16,272,128]{2,1,0:T(8,128)(2,1)S(1)}, u32[]{:S(2)}, u32[]{:S(2)}) %all-to-all-start) | async-done | bytes 1114144 | tf_op jit(solution)/shard_map/all_to_all | solution.py:398
  36.0 2.0 %shard_map.110 = (bf16[512,128]{1,0:T(8,128)(2,1)S(1)}, bf16[512,128]{1,0:T(8,128)(2,1)S(1)}, bf16[2,320,256]{2,1,0:T(8,128)(2,1)S(1)}, bf16[2,320,256]{2,1,0:T(...) custom-call(bf16[16,272,128]{2,1,0:T(8,128)(2,1)S(1)} %all-to-all-done.x_ref), custom_call_target="tpu_custom_call" | custom-call | tf_op jit(solution)/shard_map/pallas_call | solution.py:30
  38.4 1.3 collective-permute-start.4
  39.6 1.1 collective-permute-start.5
  40.8 1.4 collective-permute-start.3
  43.2 2.4 %collective-permute-done.2.refs_2_ = bf16[512,128]{1,0:T(8,128)(2,1)S(1)} collective-permute-done((bf16[512,128]{1,0:T(8,128)(2,1)S(1)}, bf16[512,128]{1,0:T(8,128)(2,1)S(1)}, u32[]{:S(2)}, u32[]{:S(2)}) %collective-permute-start.2) | collective-permute-done | bytes 131104 | tf_op jit(solution)/shard_map/ppermute | solution.py:377
  45.6 8.4 %collective-permute-done.3.refs_3_ = bf16[512,128]{1,0:T(8,128)(2,1)S(1)} collective-permute-done((bf16[512,128]{1,0:T(8,128)(2,1)S(1)}, bf16[512,128]{1,0:T(8,128)(2,1)S(1)}, u32[]{:S(2)}, u32[]{:S(2)}) %collective-permute-start.3) | collective-permute-done | bytes 131104 | tf_op jit(solution)/shard_map/ppermute | solution.py:377
  54.9 1.7 %collective-permute-start.9 = (bf16[4,320,128]{2,1,0:T(8,128)(2,1)S(1)}, bf16[4,320,128]{2,1,0:T(8,128)(2,1)S(1)}, u32[]{:S(2)}, u32[]{:S(2)}) collective-permute-start(bf16[4,320,128]{2,1,0:T(8,128)(2,1)S(1)} %get-tuple-element.69), channel_id=1, source_target_pairs={{0,4},{2,6},{4,0},{6,2},{8,12},{10,14},{12,8},{14,10},{16,20},{18,... | collective-permute-start | bytes 983048 | tf_op jit(solution)/shard_map/ppermute | solution.py:374
  56.6 1.4 collective-permute-start.10
  58.6 7.7 %collective-permute-done.7.refs_2_ = bf16[512,128]{1,0:T(8,128)(2,1)S(1)} collective-permute-done((bf16[512,128]{1,0:T(8,128)(2,1)S(1)}, bf16[512,128]{1,0:T(8,128)(2,1)S(1)}, u32[]{:S(2)}, u32[]{:S(2)}) %collective-permute-start.7) | collective-permute-done | bytes 131104 | tf_op jit(solution)/shard_map/ppermute | solution.py:377
  66.7 1.1 collective-permute-done.11.refs_6_.refs_3_
  68.7 1.0 shard_map.114.lhs_ref.refs_0_
  69.8 2.7 %collective-permute-start.14 = (bf16[320,2176]{1,0:T(8,128)(2,1)S(1)}, bf16[320,2176]{1,0:T(8,128)(2,1)S(1)}, u32[]{:S(2)}, u32[]{:S(2)}) collective-permute-start(bf16[320,2176]{1,0:T(8,128)(2,1)S(1)} %shard_map.114.lhs_ref.refs_0_), channel_id=1, source_target_pairs={{0,2},{2,0},{4,6},{6,4},{8,10},{10,8},{12,14},{14,12},{16,18},{18,... | collective-permute-start | bytes 4177928 | tf_op jit(solution)/shard_map/ppermute | solution.py:374
  72.5 1.5 %collective-permute-start.12 = (bf16[4,320,128]{2,1,0:T(8,128)(2,1)S(1)}, bf16[4,320,128]{2,1,0:T(8,128)(2,1)S(1)}, u32[]{:S(2)}, u32[]{:S(2)}) collective-permute-start(bf16[4,320,128]{2,1,0:T(8,128)(2,1)S(1)} %get-tuple-element.75), channel_id=1, source_target_pairs={{0,4},{2,6},{4,0},{6,2},{8,12},{10,14},{12,8},{14,10},{16,20},{18,... | collective-permute-start | bytes 983048 | tf_op jit(solution)/shard_map/ppermute | solution.py:374
  74.0 1.4 collective-permute-start.15
  75.6 2.2 %copy-done.1 = bf16[1,4096,512]{2,1,0:T(8,128)(2,1)S(1)} copy-done((bf16[1,4096,512]{2,1,0:T(8,128)(2,1)S(1)}, bf16[1,4096,512]{2,1,0:T(8,128)(2,1)}, u32[]{:S(2)}) %copy-start.1) | copy-done | bytes 4194328
  77.7 2.1 %shard_map.115 = (f32[320,512]{1,0:T(8,128)S(1)}, f32[320,512]{1,0:T(8,128)S(1)}) custom-call(s32[2]{0:T(128)S(1)} %pad_add_fusion.idx_ref, bf16[4096,512]{1,0:T(8,128)(2,1)S(1)} %bitcast.8, bf16[4096,512]{1,0:T(8,128)(2,1)S(1)} %bitcast.14, bf16[320,2176]{1,0:T(8,128)(2,1)S(1)} %shard_map.114.lhs_ref.refs_0_), custom_call_target="tpu_custom_call" | custom-call | tf_op jit(solution)/shard_map/pallas_call | solution.py:30
  79.8 2.1 %shard_map.116.refs_3_.own_ref = bf16[320,512]{1,0:T(8,128)(2,1)S(1)} custom-call(s32[2]{0:T(128)S(1)} %pad_add_fusion.idx_ref, bf16[4096,512]{1,0:T(8,128)(2,1)S(1)} %bitcast.9, bf16[4096,512]{1,0:T(8,128)(2,1)S(1)} %bitcast.15, f32[320,512]{1,0:T(8,128)S(1)} %get-tuple-element.77.gate_ref, f32[320,512]{1,0:T(8,128)S(1)} %get-tuple-element.78.up_ref, ...), custom_call_target="tpu_custom_call" | custom-call | tf_op jit(solution)/shard_map/pallas_call | solution.py:30
  82.8 1.3 collective-permute-start.16
  84.1 2.2 %collective-permute-done.13.refs_1_ = bf16[3,320,128]{2,1,0:T(8,128)(2,1)S(1)} collective-permute-done((bf16[3,320,128]{2,1,0:T(8,128)(2,1)S(1)}, bf16[3,320,128]{2,1,0:T(8,128)(2,1)S(1)}, u32[]{:S(2)}, u32[]{:S(2)}) %collective-permute-start.13) | collective-permute-done | bytes 245792 | tf_op jit(solution)/shard_map/ppermute | solution.py:384
  87.1 1.7 %collective-permute-start.17 = (bf16[320,1152]{1,0:T(8,128)(2,1)S(1)}, bf16[320,1152]{1,0:T(8,128)(2,1)S(1)}, u32[]{:S(2)}, u32[]{:S(2)}) collective-permute-start(bf16[320,1152]{1,0:T(8,128)(2,1)S(1)} %shard_map.117.lhs_ref.refs_2_), channel_id=1, source_target_pairs={{0,2},{2,0},{4,6},{6,4},{8,10},{10,8},{12,14},{14,12},{16,18},{18,... | collective-permute-start | bytes 2211848 | tf_op jit(solution)/shard_map/ppermute | solution.py:374
  88.8 1.4 collective-permute-start.20
  90.2 1.4 shard_map.119
  91.6 1.4 shard_map.120
  93.0 1.4 shard_map.121
  94.4 1.4 shard_map.122.refs_2_.refs_0_.own_ref
  96.0 2.1 %collective-permute-done.20.peer_ref = bf16[320,512]{1,0:T(8,128)(2,1)S(1)} collective-permute-done((bf16[320,512]{1,0:T(8,128)(2,1)S(1)}, bf16[320,512]{1,0:T(8,128)(2,1)S(1)}, u32[]{:S(2)}, u32[]{:S(2)}) %collective-permute-start.20) | collective-permute-done | bytes 327712 | tf_op jit(solution)/shard_map/ppermute | solution.py:380
  98.1 1.4 shard_map.126
  101.0 1.4 shard_map.125
  102.5 2.4 %collective-permute-done.25.refs_8_.peer_ref = bf16[320,512]{1,0:T(8,128)(2,1)S(1)} collective-permute-done((bf16[320,512]{1,0:T(8,128)(2,1)S(1)}, bf16[320,512]{1,0:T(8,128)(2,1)S(1)}, u32[]{:S(2)}, u32[]{:S(2)}) %collective-permute-start.25) | collective-permute-done | bytes 327712 | tf_op jit(solution)/shard_map/ppermute | solution.py:380
  105.5 1.5 %collective-permute-start.26 = (bf16[160,1024]{1,0:T(8,128)(2,1)S(1)}, bf16[160,1024]{1,0:T(8,128)(2,1)S(1)}, u32[]{:S(2)}, u32[]{:S(2)}) collective-permute-start(bf16[160,1024]{1,0:T(8,128)(2,1)S(1)} %shard_map.128.refs_0_), channel_id=1, source_target_pairs={{0,4},{2,6},{4,0},{6,2},{8,12},{10,14},{12,8},{14,10},{16,20},{18,... | collective-permute-start | bytes 983048 | tf_op jit(solution)/shard_map/ppermute | solution.py:374
  107.0 1.4 shard_map.132
  108.5 1.5 %collective-permute-start.31 = (bf16[320,256]{1,0:T(8,128)(2,1)S(1)}, bf16[320,256]{1,0:T(8,128)(2,1)S(1)}, u32[]{:S(2)}, u32[]{:S(2)}) collective-permute-start(bf16[320,256]{1,0:T(8,128)(2,1)S(1)} %get-tuple-element.105), channel_id=1, source_target_pairs={{0,2},{2,0},{4,6},{6,4},{8,10},{10,8},{12,14},{14,12},{16,18},{18,... | collective-permute-start | bytes 491528 | tf_op jit(solution)/shard_map/ppermute | solution.py:374
  111.6 1.4 shard_map.131
  115.3 1.5 %collective-permute-start.35 = (bf16[160,1024]{1,0:T(8,128)(2,1)S(1)}, bf16[160,1024]{1,0:T(8,128)(2,1)S(1)}, u32[]{:S(2)}, u32[]{:S(2)}) collective-permute-start(bf16[160,1024]{1,0:T(8,128)(2,1)S(1)} %shard_map.134), channel_id=1, source_target_pairs={{0,4},{2,6},{4,0},{6,2},{8,12},{10,14},{12,8},{14,10},{16,20},{18,... | collective-permute-start | bytes 983048 | tf_op jit(solution)/shard_map/ppermute | solution.py:374
  117.9 1.5 %collective-permute-start.29 = (bf16[64,1024]{1,0:T(8,128)(2,1)S(1)}, bf16[64,1024]{1,0:T(8,128)(2,1)S(1)}, u32[]{:S(2)}, u32[]{:S(2)}) collective-permute-start(bf16[64,1024]{1,0:T(8,128)(2,1)S(1)} %get-tuple-element.99), channel_id=1, source_target_pairs={{0,24},{2,26},{4,28},{6,30},{8,0},{10,2},{12,4},{14,6},{16,8},{18,... | collective-permute-start | bytes 393224 | tf_op jit(solution)/shard_map/ppermute | solution.py:377
  119.4 3.0 %collective-permute-done.35.got_ref = bf16[160,1024]{1,0:T(8,128)(2,1)S(1)} collective-permute-done((bf16[160,1024]{1,0:T(8,128)(2,1)S(1)}, bf16[160,1024]{1,0:T(8,128)(2,1)S(1)}, u32[]{:S(2)}, u32[]{:S(2)}) %collective-permute-start.35) | collective-permute-done | bytes 327712 | tf_op jit(solution)/shard_map/ppermute | solution.py:374
  123.5 1.0 collective-permute-start.37
  125.2 1.3 collective-permute-start.18
  126.5 8.3 %collective-permute-done.29.refs_2_ = bf16[64,1024]{1,0:T(8,128)(2,1)S(1)} collective-permute-done((bf16[64,1024]{1,0:T(8,128)(2,1)S(1)}, bf16[64,1024]{1,0:T(8,128)(2,1)S(1)}, u32[]{:S(2)}, u32[]{:S(2)}) %collective-permute-start.29) | collective-permute-done | bytes 131104 | tf_op jit(solution)/shard_map/ppermute | solution.py:377
  134.8 4.9 %collective-permute-start.30 = (f32[64,1024]{1,0:T(8,128)S(1)}, f32[64,1024]{1,0:T(8,128)S(1)}, u32[]{:S(2)}, u32[]{:S(2)}) collective-permute-start(f32[64,1024]{1,0:T(8,128)S(1)} %shard_map.130.refs_2_), channel_id=1, source_target_pairs={{2,0},{6,4},{10,8},{14,12},{18,16},{22,20},{26,24},{30,28},{3,1},{... | collective-permute-start | bytes 786440 | tf_op jit(solution)/shard_map/ppermute | solution.py:387
  140.4 1.3 collective-permute-start.39
  142.3 1.8 %collective-permute-start.19 = (bf16[8,64,128]{2,1,0:T(8,128)(2,1)S(1)}, bf16[8,64,128]{2,1,0:T(8,128)(2,1)S(1)}, u32[]{:S(2)}, u32[]{:S(2)}) collective-permute-start(bf16[8,64,128]{2,1,0:T(8,128)(2,1)S(1)} %get-tuple-element.86), channel_id=1, source_target_pairs={{0,2},{2,0},{4,6},{6,4},{8,10},{10,8},{12,14},{14,12},{16,18},{18,... | collective-permute-start | bytes 393224 | tf_op jit(solution)/shard_map/ppermute | solution.py:374
  145.1 1.4 shard_map.137
  (81 shorter events, 17.1 us)
Async XLA Ops:
  3.0 6.6 %copy-start.4 = (bf16[2048]{0:T(1024)(128)(2,1)S(1)}, bf16[2048]{0:T(1024)(128)(2,1)}, u32[]{:S(2)}) copy-start(bf16[2048]{0:T(1024)(128)(2,1)} %param.15) | copy-start | bytes 12292
  3.0 32.9 %all-to-all-start = ((bf16[16,272,128]{2,1,0:T(8,128)(2,1)}), bf16[16,272,128]{2,1,0:T(8,128)(2,1)S(1)}, u32[]{:S(2)}, u32[]{:S(2)}) async-start(bf16[16,272,128]{2,1,0:T(8,128)(2,1)} %shard_map.109), calls=%async_computation | async-start | bytes 2228224 | tf_op jit(solution)/shard_map/all_to_all | solution.py:398
  9.6 2.8 %collective-permute-start = (bf16[2048]{0:T(1024)(128)(2,1)S(1)}, bf16[2048]{0:T(1024)(128)(2,1)S(1)}, u32[]{:S(2)}, u32[]{:S(2)}) collective-permute-start(bf16[2048]{0:T(1024)(128)(2,1)S(1)} %copy-done.4), channel_id=1, source_target_pairs={{0,1},{1,0},{2,3},{3,2},{4,5},{5,4},{6,7},{7,6},{8,9},{9,8},{10,11... | collective-permute-start | bytes 12296 | tf_op jit(solution)/shard_map/ppermute | solution.py:380
  38.0 5.0 %collective-permute-start.1 = (bf16[512,128]{1,0:T(8,128)(2,1)S(1)}, bf16[512,128]{1,0:T(8,128)(2,1)S(1)}, u32[]{:S(2)}, u32[]{:S(2)}) collective-permute-start(bf16[512,128]{1,0:T(8,128)(2,1)S(1)} %get-tuple-element.61.even_ref.refs_0_), channel_id=1, source_target_pairs={{0,8},{2,10},{4,12},{6,14},{8,16},{10,18},{12,20},{14,22},{16,24},... | collective-permute-start | bytes 393224 | tf_op jit(solution)/shard_map/ppermute | solution.py:377
  38.4 15.7 %collective-permute-start.4 = (bf16[2,320,128]{2,1,0:T(8,128)(2,1)S(1)}, bf16[2,320,128]{2,1,0:T(8,128)(2,1)S(1)}, u32[]{:S(2)}, u32[]{:S(2)}) collective-permute-start(bf16[2,320,128]{2,1,0:T(8,128)(2,1)S(1)} %get-tuple-element.65), channel_id=1, source_target_pairs={{0,1},{1,0},{2,3},{3,2},{4,5},{5,4},{6,7},{7,6},{8,9},{9,8},{10,11... | collective-permute-start | bytes 491528 | tf_op jit(solution)/shard_map/ppermute | solution.py:380
  39.6 14.4 %collective-permute-start.5 = (bf16[2,320,128]{2,1,0:T(8,128)(2,1)S(1)}, bf16[2,320,128]{2,1,0:T(8,128)(2,1)S(1)}, u32[]{:S(2)}, u32[]{:S(2)}) collective-permute-start(bf16[2,320,128]{2,1,0:T(8,128)(2,1)S(1)} %get-tuple-element.66), channel_id=1, source_target_pairs={{0,5},{1,4},{2,7},{3,6},{4,1},{5,0},{6,3},{7,2},{8,13},{9,12},{10,... | collective-permute-start | bytes 491528 | tf_op jit(solution)/shard_map/ppermute | solution.py:384
  40.8 4.8 %collective-permute-start.2 = (bf16[512,128]{1,0:T(8,128)(2,1)S(1)}, bf16[512,128]{1,0:T(8,128)(2,1)S(1)}, u32[]{:S(2)}, u32[]{:S(2)}) collective-permute-start(bf16[512,128]{1,0:T(8,128)(2,1)S(1)} %get-tuple-element.61.even_ref.refs_0_), channel_id=1, source_target_pairs={{0,16},{2,18},{4,20},{6,22},{8,24},{10,26},{12,28},{14,30},{16,0},... | collective-permute-start | bytes 393224 | tf_op jit(solution)/shard_map/ppermute | solution.py:377
  40.8 13.2 %collective-permute-start.3 = (bf16[512,128]{1,0:T(8,128)(2,1)S(1)}, bf16[512,128]{1,0:T(8,128)(2,1)S(1)}, u32[]{:S(2)}, u32[]{:S(2)}) collective-permute-start(bf16[512,128]{1,0:T(8,128)(2,1)S(1)} %get-tuple-element.61.even_ref.refs_0_), channel_id=1, source_target_pairs={{0,24},{2,26},{4,28},{6,30},{8,0},{10,2},{12,4},{14,6},{16,8},{18,... | collective-permute-start | bytes 393224 | tf_op jit(solution)/shard_map/ppermute | solution.py:377
  42.9 15.2 %collective-permute-start.6 = (bf16[512,128]{1,0:T(8,128)(2,1)S(1)}, bf16[512,128]{1,0:T(8,128)(2,1)S(1)}, u32[]{:S(2)}, u32[]{:S(2)}) collective-permute-start(bf16[512,128]{1,0:T(8,128)(2,1)S(1)} %get-tuple-element.68.odd_ref.refs_0_), channel_id=1, source_target_pairs={{0,8},{2,10},{4,12},{6,14},{8,16},{10,18},{12,20},{14,22},{16,24},... | collective-permute-start | bytes 393224 | tf_op jit(solution)/shard_map/ppermute | solution.py:377
  54.9 12.9 %collective-permute-start.9 = (bf16[4,320,128]{2,1,0:T(8,128)(2,1)S(1)}, bf16[4,320,128]{2,1,0:T(8,128)(2,1)S(1)}, u32[]{:S(2)}, u32[]{:S(2)}) collective-permute-start(bf16[4,320,128]{2,1,0:T(8,128)(2,1)S(1)} %get-tuple-element.69), channel_id=1, source_target_pairs={{0,4},{2,6},{4,0},{6,2},{8,12},{10,14},{12,8},{14,10},{16,20},{18,... | collective-permute-start | bytes 983048 | tf_op jit(solution)/shard_map/ppermute | solution.py:374
  56.6 10.1 %collective-permute-start.10 = (bf16[3,320,128]{2,1,0:T(8,128)(2,1)S(1)}, bf16[3,320,128]{2,1,0:T(8,128)(2,1)S(1)}, u32[]{:S(2)}, u32[]{:S(2)}) collective-permute-start(bf16[3,320,128]{2,1,0:T(8,128)(2,1)S(1)} %slice.12), channel_id=1, source_target_pairs={{0,1},{1,0},{2,3},{3,2},{4,5},{5,4},{6,7},{7,6},{8,9},{9,8},{10,11... | collective-permute-start | bytes 737288 | tf_op jit(solution)/shard_map/ppermute | solution.py:380
  58.1 9.8 %collective-permute-start.11 = (bf16[3,320,128]{2,1,0:T(8,128)(2,1)S(1)}, bf16[3,320,128]{2,1,0:T(8,128)(2,1)S(1)}, u32[]{:S(2)}, u32[]{:S(2)}) collective-permute-start(bf16[3,320,128]{2,1,0:T(8,128)(2,1)S(1)} %slice.13), channel_id=1, source_target_pairs={{0,5},{1,4},{2,7},{3,6},{4,1},{5,0},{6,3},{7,2},{8,13},{9,12},{10,... | collective-permute-start | bytes 737288 | tf_op jit(solution)/shard_map/ppermute | solution.py:384
  58.1 8.3 %collective-permute-start.7 = (bf16[512,128]{1,0:T(8,128)(2,1)S(1)}, bf16[512,128]{1,0:T(8,128)(2,1)S(1)}, u32[]{:S(2)}, u32[]{:S(2)}) collective-permute-start(bf16[512,128]{1,0:T(8,128)(2,1)S(1)} %get-tuple-element.68.odd_ref.refs_0_), channel_id=1, source_target_pairs={{0,16},{2,18},{4,20},{6,22},{8,24},{10,26},{12,28},{14,30},{16,0},... | collective-permute-start | bytes 393224 | tf_op jit(solution)/shard_map/ppermute | solution.py:377
  58.2 8.6 %collective-permute-start.8 = (bf16[512,128]{1,0:T(8,128)(2,1)S(1)}, bf16[512,128]{1,0:T(8,128)(2,1)S(1)}, u32[]{:S(2)}, u32[]{:S(2)}) collective-permute-start(bf16[512,128]{1,0:T(8,128)(2,1)S(1)} %get-tuple-element.68.odd_ref.refs_0_), channel_id=1, source_target_pairs={{0,24},{2,26},{4,28},{6,30},{8,0},{10,2},{12,4},{14,6},{16,8},{18,... | collective-permute-start | bytes 393224 | tf_op jit(solution)/shard_map/ppermute | solution.py:377
  68.7 6.8 %copy-start = (bf16[1,4096,512]{2,1,0:T(8,128)(2,1)S(1)}, bf16[1,4096,512]{2,1,0:T(8,128)(2,1)}, u32[]{:S(2)}) copy-start(bf16[1,4096,512]{2,1,0:T(8,128)(2,1)} %param.19) | copy-start | bytes 12582916
  69.8 10.0 %collective-permute-start.14 = (bf16[320,2176]{1,0:T(8,128)(2,1)S(1)}, bf16[320,2176]{1,0:T(8,128)(2,1)S(1)}, u32[]{:S(2)}, u32[]{:S(2)}) collective-permute-start(bf16[320,2176]{1,0:T(8,128)(2,1)S(1)} %shard_map.114.lhs_ref.refs_0_), channel_id=1, source_target_pairs={{0,2},{2,0},{4,6},{6,4},{8,10},{10,8},{12,14},{14,12},{16,18},{18,... | collective-permute-start | bytes 4177928 | tf_op jit(solution)/shard_map/ppermute | solution.py:374
  72.5 13.8 %collective-permute-start.12 = (bf16[4,320,128]{2,1,0:T(8,128)(2,1)S(1)}, bf16[4,320,128]{2,1,0:T(8,128)(2,1)S(1)}, u32[]{:S(2)}, u32[]{:S(2)}) collective-permute-start(bf16[4,320,128]{2,1,0:T(8,128)(2,1)S(1)} %get-tuple-element.75), channel_id=1, source_target_pairs={{0,4},{2,6},{4,0},{6,2},{8,12},{10,14},{12,8},{14,10},{16,20},{18,... | collective-permute-start | bytes 983048 | tf_op jit(solution)/shard_map/ppermute | solution.py:374
  74.0 8.0 %collective-permute-start.15 = (bf16[3,320,128]{2,1,0:T(8,128)(2,1)S(1)}, bf16[3,320,128]{2,1,0:T(8,128)(2,1)S(1)}, u32[]{:S(2)}, u32[]{:S(2)}) collective-permute-start(bf16[3,320,128]{2,1,0:T(8,128)(2,1)S(1)} %slice.15), channel_id=1, source_target_pairs={{0,1},{1,0},{2,3},{3,2},{4,5},{5,4},{6,7},{7,6},{8,9},{9,8},{10,11... | collective-permute-start | bytes 737288 | tf_op jit(solution)/shard_map/ppermute | solution.py:380
  75.5 10.8 %collective-permute-start.13 = (bf16[3,320,128]{2,1,0:T(8,128)(2,1)S(1)}, bf16[3,320,128]{2,1,0:T(8,128)(2,1)S(1)}, u32[]{:S(2)}, u32[]{:S(2)}) collective-permute-start(bf16[3,320,128]{2,1,0:T(8,128)(2,1)S(1)} %slice.14), channel_id=1, source_target_pairs={{0,5},{1,4},{2,7},{3,6},{4,1},{5,0},{6,3},{7,2},{8,13},{9,12},{10,... | collective-permute-start | bytes 737288 | tf_op jit(solution)/shard_map/ppermute | solution.py:384
  75.5 2.2 %copy-start.1 = (bf16[1,4096,512]{2,1,0:T(8,128)(2,1)S(1)}, bf16[1,4096,512]{2,1,0:T(8,128)(2,1)}, u32[]{:S(2)}) copy-start(bf16[1,4096,512]{2,1,0:T(8,128)(2,1)} %param.20) | copy-start | bytes 12582916
  79.8 10.4 %copy-start.2 = (bf16[1,4096,512]{2,1,0:T(8,128)(2,1)S(1)}, bf16[1,4096,512]{2,1,0:T(8,128)(2,1)}, u32[]{:S(2)}) copy-start(bf16[1,4096,512]{2,1,0:T(8,128)(2,1)} %param.20) | copy-start | bytes 12582916
  82.8 8.8 %collective-permute-start.16 = (bf16[320,1152]{1,0:T(8,128)(2,1)S(1)}, bf16[320,1152]{1,0:T(8,128)(2,1)S(1)}, u32[]{:S(2)}, u32[]{:S(2)}) collective-permute-start(bf16[320,1152]{1,0:T(8,128)(2,1)S(1)} %shard_map.118.lhs_ref.refs_0_), channel_id=1, source_target_pairs={{0,2},{2,0},{4,6},{6,4},{8,10},{10,8},{12,14},{14,12},{16,18},{18,... | collective-permute-start | bytes 2211848 | tf_op jit(solution)/shard_map/ppermute | solution.py:374
  87.1 7.3 %collective-permute-start.17 = (bf16[320,1152]{1,0:T(8,128)(2,1)S(1)}, bf16[320,1152]{1,0:T(8,128)(2,1)S(1)}, u32[]{:S(2)}, u32[]{:S(2)}) collective-permute-start(bf16[320,1152]{1,0:T(8,128)(2,1)S(1)} %shard_map.117.lhs_ref.refs_2_), channel_id=1, source_target_pairs={{0,2},{2,0},{4,6},{6,4},{8,10},{10,8},{12,14},{14,12},{16,18},{18,... | collective-permute-start | bytes 2211848 | tf_op jit(solution)/shard_map/ppermute | solution.py:374
  88.8 9.3 %collective-permute-start.20 = (bf16[320,512]{1,0:T(8,128)(2,1)S(1)}, bf16[320,512]{1,0:T(8,128)(2,1)S(1)}, u32[]{:S(2)}, u32[]{:S(2)}) collective-permute-start(bf16[320,512]{1,0:T(8,128)(2,1)S(1)} %shard_map.116.refs_3_.own_ref), channel_id=1, source_target_pairs={{0,1},{1,0},{2,3},{3,2},{4,5},{5,4},{6,7},{7,6},{8,9},{9,8},{10,11... | collective-permute-start | bytes 983048 | tf_op jit(solution)/shard_map/ppermute | solution.py:380
  94.4 3.7 %copy-start.3 = (bf16[1,1024,2048]{2,1,0:T(8,128)(2,1)S(1)}, bf16[1,1024,2048]{2,1,0:T(8,128)(2,1)}, u32[]{:S(2)}) copy-start(bf16[1,1024,2048]{2,1,0:T(8,128)(2,1)} %param.21) | copy-start | bytes 12582916
  95.9 9.0 %collective-permute-start.25 = (bf16[320,512]{1,0:T(8,128)(2,1)S(1)}, bf16[320,512]{1,0:T(8,128)(2,1)S(1)}, u32[]{:S(2)}, u32[]{:S(2)}) collective-permute-start(bf16[320,512]{1,0:T(8,128)(2,1)S(1)} %shard_map.122.refs_2_.refs_0_.own_ref), channel_id=1, source_target_pairs={{0,1},{1,0},{2,3},{3,2},{4,5},{5,4},{6,7},{7,6},{8,9},{9,8},{10,11... | collective-permute-start | bytes 983048 | tf_op jit(solution)/shard_map/ppermute | solution.py:380
  99.5 2.9 %collective-permute-start.21 = (bf16[320,256]{1,0:T(8,128)(2,1)S(1)}, bf16[320,256]{1,0:T(8,128)(2,1)S(1)}, u32[]{:S(2)}, u32[]{:S(2)}) collective-permute-start(bf16[320,256]{1,0:T(8,128)(2,1)S(1)} %get-tuple-element.92), channel_id=1, source_target_pairs={{0,2},{2,0},{4,6},{6,4},{8,10},{10,8},{12,14},{14,12},{16,18},{18,... | collective-permute-start | bytes 491528 | tf_op jit(solution)/shard_map/ppermute | solution.py:374
  100.4 2.0 %collective-permute-start.22 = (bf16[320,256]{1,0:T(8,128)(2,1)S(1)}, bf16[320,256]{1,0:T(8,128)(2,1)S(1)}, u32[]{:S(2)}, u32[]{:S(2)}) collective-permute-start(bf16[320,256]{1,0:T(8,128)(2,1)S(1)} %get-tuple-element.93), channel_id=1, source_target_pairs={{0,2},{2,0},{4,6},{6,4},{8,10},{10,8},{12,14},{14,12},{16,18},{18,... | collective-permute-start | bytes 491528 | tf_op jit(solution)/shard_map/ppermute | solution.py:374
  100.5 2.0 %collective-permute-start.23 = (bf16[320,256]{1,0:T(8,128)(2,1)S(1)}, bf16[320,256]{1,0:T(8,128)(2,1)S(1)}, u32[]{:S(2)}, u32[]{:S(2)}) collective-permute-start(bf16[320,256]{1,0:T(8,128)(2,1)S(1)} %get-tuple-element.94), channel_id=1, source_target_pairs={{0,2},{2,0},{4,6},{6,4},{8,10},{10,8},{12,14},{14,12},{16,18},{18,... | collective-permute-start | bytes 491528 | tf_op jit(solution)/shard_map/ppermute | solution.py:374
  100.9 1.5 %collective-permute-start.24 = (bf16[320,256]{1,0:T(8,128)(2,1)S(1)}, bf16[320,256]{1,0:T(8,128)(2,1)S(1)}, u32[]{:S(2)}, u32[]{:S(2)}) collective-permute-start(bf16[320,256]{1,0:T(8,128)(2,1)S(1)} %get-tuple-element.95), channel_id=1, source_target_pairs={{0,2},{2,0},{4,6},{6,4},{8,10},{10,8},{12,14},{14,12},{16,18},{18,... | collective-permute-start | bytes 491528 | tf_op jit(solution)/shard_map/ppermute | solution.py:374
  105.5 8.1 %collective-permute-start.26 = (bf16[160,1024]{1,0:T(8,128)(2,1)S(1)}, bf16[160,1024]{1,0:T(8,128)(2,1)S(1)}, u32[]{:S(2)}, u32[]{:S(2)}) collective-permute-start(bf16[160,1024]{1,0:T(8,128)(2,1)S(1)} %shard_map.128.refs_0_), channel_id=1, source_target_pairs={{0,4},{2,6},{4,0},{6,2},{8,12},{10,14},{12,8},{14,10},{16,20},{18,... | collective-permute-start | bytes 983048 | tf_op jit(solution)/shard_map/ppermute | solution.py:374
  108.5 6.1 %collective-permute-start.31 = (bf16[320,256]{1,0:T(8,128)(2,1)S(1)}, bf16[320,256]{1,0:T(8,128)(2,1)S(1)}, u32[]{:S(2)}, u32[]{:S(2)}) collective-permute-start(bf16[320,256]{1,0:T(8,128)(2,1)S(1)} %get-tuple-element.105), channel_id=1, source_target_pairs={{0,2},{2,0},{4,6},{6,4},{8,10},{10,8},{12,14},{14,12},{16,18},{18,... | collective-permute-start | bytes 491528 | tf_op jit(solution)/shard_map/ppermute | solution.py:374
  110.0 4.6 %collective-permute-start.32 = (bf16[320,256]{1,0:T(8,128)(2,1)S(1)}, bf16[320,256]{1,0:T(8,128)(2,1)S(1)}, u32[]{:S(2)}, u32[]{:S(2)}) collective-permute-start(bf16[320,256]{1,0:T(8,128)(2,1)S(1)} %get-tuple-element.106), channel_id=1, source_target_pairs={{0,2},{2,0},{4,6},{6,4},{8,10},{10,8},{12,14},{14,12},{16,18},{18,... | collective-permute-start | bytes 491528 | tf_op jit(solution)/shard_map/ppermute | solution.py:374
  110.1 4.5 %collective-permute-start.33 = (bf16[320,256]{1,0:T(8,128)(2,1)S(1)}, bf16[320,256]{1,0:T(8,128)(2,1)S(1)}, u32[]{:S(2)}, u32[]{:S(2)}) collective-permute-start(bf16[320,256]{1,0:T(8,128)(2,1)S(1)} %get-tuple-element.107), channel_id=1, source_target_pairs={{0,2},{2,0},{4,6},{6,4},{8,10},{10,8},{12,14},{14,12},{16,18},{18,... | collective-permute-start | bytes 491528 | tf_op jit(solution)/shard_map/ppermute | solution.py:374
  110.5 4.1 %collective-permute-start.34 = (bf16[320,256]{1,0:T(8,128)(2,1)S(1)}, bf16[320,256]{1,0:T(8,128)(2,1)S(1)}, u32[]{:S(2)}, u32[]{:S(2)}) collective-permute-start(bf16[320,256]{1,0:T(8,128)(2,1)S(1)} %get-tuple-element.108), channel_id=1, source_target_pairs={{0,2},{2,0},{4,6},{6,4},{8,10},{10,8},{12,14},{14,12},{16,18},{18,... | collective-permute-start | bytes 491528 | tf_op jit(solution)/shard_map/ppermute | solution.py:374
  115.3 7.2 %collective-permute-start.35 = (bf16[160,1024]{1,0:T(8,128)(2,1)S(1)}, bf16[160,1024]{1,0:T(8,128)(2,1)S(1)}, u32[]{:S(2)}, u32[]{:S(2)}) collective-permute-start(bf16[160,1024]{1,0:T(8,128)(2,1)S(1)} %shard_map.134), channel_id=1, source_target_pairs={{0,4},{2,6},{4,0},{6,2},{8,12},{10,14},{12,8},{14,10},{16,20},{18,... | collective-permute-start | bytes 983048 | tf_op jit(solution)/shard_map/ppermute | solution.py:374
  116.8 7.7 %collective-permute-start.27 = (bf16[64,1024]{1,0:T(8,128)(2,1)S(1)}, bf16[64,1024]{1,0:T(8,128)(2,1)S(1)}, u32[]{:S(2)}, u32[]{:S(2)}) collective-permute-start(bf16[64,1024]{1,0:T(8,128)(2,1)S(1)} %get-tuple-element.97), channel_id=1, source_target_pairs={{0,8},{2,10},{4,12},{6,14},{8,16},{10,18},{12,20},{14,22},{16,24},... | collective-permute-start | bytes 393224 | tf_op jit(solution)/shard_map/ppermute | solution.py:377
  117.8 7.4 %collective-permute-start.28 = (bf16[64,1024]{1,0:T(8,128)(2,1)S(1)}, bf16[64,1024]{1,0:T(8,128)(2,1)S(1)}, u32[]{:S(2)}, u32[]{:S(2)}) collective-permute-start(bf16[64,1024]{1,0:T(8,128)(2,1)S(1)} %get-tuple-element.98), channel_id=1, source_target_pairs={{0,16},{2,18},{4,20},{6,22},{8,24},{10,26},{12,28},{14,30},{16,0},... | collective-permute-start | bytes 393224 | tf_op jit(solution)/shard_map/ppermute | solution.py:377
  117.9 16.9 %collective-permute-start.29 = (bf16[64,1024]{1,0:T(8,128)(2,1)S(1)}, bf16[64,1024]{1,0:T(8,128)(2,1)S(1)}, u32[]{:S(2)}, u32[]{:S(2)}) collective-permute-start(bf16[64,1024]{1,0:T(8,128)(2,1)S(1)} %get-tuple-element.99), channel_id=1, source_target_pairs={{0,24},{2,26},{4,28},{6,30},{8,0},{10,2},{12,4},{14,6},{16,8},{18,... | collective-permute-start | bytes 393224 | tf_op jit(solution)/shard_map/ppermute | solution.py:377
  123.4 16.3 %collective-permute-start.36 = (bf16[64,1024]{1,0:T(8,128)(2,1)S(1)}, bf16[64,1024]{1,0:T(8,128)(2,1)S(1)}, u32[]{:S(2)}, u32[]{:S(2)}) collective-permute-start(bf16[64,1024]{1,0:T(8,128)(2,1)S(1)} %get-tuple-element.110), channel_id=1, source_target_pairs={{0,8},{2,10},{4,12},{6,14},{8,16},{10,18},{12,20},{14,22},{16,24},... | collective-permute-start | bytes 393224 | tf_op jit(solution)/shard_map/ppermute | solution.py:377
  123.5 16.3 %collective-permute-start.37 = (bf16[64,1024]{1,0:T(8,128)(2,1)S(1)}, bf16[64,1024]{1,0:T(8,128)(2,1)S(1)}, u32[]{:S(2)}, u32[]{:S(2)}) collective-permute-start(bf16[64,1024]{1,0:T(8,128)(2,1)S(1)} %get-tuple-element.111), channel_id=1, source_target_pairs={{0,16},{2,18},{4,20},{6,22},{8,24},{10,26},{12,28},{14,30},{16,0},... | collective-permute-start | bytes 393224 | tf_op jit(solution)/shard_map/ppermute | solution.py:377
  124.5 15.8 %collective-permute-start.38 = (bf16[64,1024]{1,0:T(8,128)(2,1)S(1)}, bf16[64,1024]{1,0:T(8,128)(2,1)S(1)}, u32[]{:S(2)}, u32[]{:S(2)}) collective-permute-start(bf16[64,1024]{1,0:T(8,128)(2,1)S(1)} %get-tuple-element.112), channel_id=1, source_target_pairs={{0,24},{2,26},{4,28},{6,30},{8,0},{10,2},{12,4},{14,6},{16,8},{18,... | collective-permute-start | bytes 393224 | tf_op jit(solution)/shard_map/ppermute | solution.py:377
  125.2 16.5 %collective-permute-start.18 = (bf16[2,4,64,128]{3,2,1,0:T(8,128)(2,1)S(1)}, bf16[2,4,64,128]{3,2,1,0:T(8,128)(2,1)S(1)}, u32[]{:S(2)}, u32[]{:S(2)}) collective-permute-start(bf16[2,4,64,128]{3,2,1,0:T(8,128)(2,1)S(1)} %shard_map.123), channel_id=1, source_target_pairs={{0,4},{2,6},{4,0},{6,2},{8,12},{10,14},{12,8},{14,10},{16,20},{18,... | collective-permute-start | bytes 393224 | tf_op jit(solution)/shard_map/ppermute | solution.py:374
  134.8 10.3 %collective-permute-start.30 = (f32[64,1024]{1,0:T(8,128)S(1)}, f32[64,1024]{1,0:T(8,128)S(1)}, u32[]{:S(2)}, u32[]{:S(2)}) collective-permute-start(f32[64,1024]{1,0:T(8,128)S(1)} %shard_map.130.refs_2_), channel_id=1, source_target_pairs={{2,0},{6,4},{10,8},{14,12},{18,16},{22,20},{26,24},{30,28},{3,1},{... | collective-permute-start | bytes 786440 | tf_op jit(solution)/shard_map/ppermute | solution.py:387
  140.4 4.7 %collective-permute-start.39 = (f32[64,1024]{1,0:T(8,128)S(1)}, f32[64,1024]{1,0:T(8,128)S(1)}, u32[]{:S(2)}, u32[]{:S(2)}) collective-permute-start(f32[64,1024]{1,0:T(8,128)S(1)} %shard_map.136.refs_4_), channel_id=1, source_target_pairs={{0,2},{4,6},{8,10},{12,14},{16,18},{20,22},{24,26},{28,30},{1,3},{... | collective-permute-start | bytes 786440 | tf_op jit(solution)/shard_map/ppermute | solution.py:387
  142.3 2.8 %collective-permute-start.19 = (bf16[8,64,128]{2,1,0:T(8,128)(2,1)S(1)}, bf16[8,64,128]{2,1,0:T(8,128)(2,1)S(1)}, u32[]{:S(2)}, u32[]{:S(2)}) collective-permute-start(bf16[8,64,128]{2,1,0:T(8,128)(2,1)S(1)} %get-tuple-element.86), channel_id=1, source_target_pairs={{0,2},{2,0},{4,6},{6,4},{8,10},{10,8},{12,14},{14,12},{16,18},{18,... | collective-permute-start | bytes 393224 | tf_op jit(solution)/shard_map/ppermute | solution.py:374

commit v7 on v6

--- a/solution.py
+++ b/solution.py
@@ -16,7 +16,7 @@
 LANES = 128
 MIB = 1 << 20
 PARTS = 4
-GROUPS = (((0, 1, 2, 3, 4, 5),), ((0, 2, 4), (1, 3, 5)))
+GROUPS = (((0, 1, 2, 3, 4, 5, 6),), ((0, 2, 4), (1, 3, 5, 6)))
 
 
 def silu(v):
@@ -412,7 +412,7 @@
             hand, columns[0][1] = lax.optimization_barrier((hand, columns[0][1]))
         columns.append([hand] + [along_z(hand, k) for k in range(1, levels)])
     near = call(near_kernel, [shape(2, 2 * slots, HD)] * 2, (*hands[2:4], *hands[:2]))
-    near = [over_tp(near[0]), across(near[1])]
+    near = [over_tp(near[0]), across(near[1]), over_ctx(near[1], 2)]
     pieces, places, blocks, compacted = [], [], [], near
     for core, (pick, column) in enumerate(zip(hands[2:4], columns)):
         mine, theirs, *own_rows = call(
@@ -423,12 +423,12 @@
         )
         blocks.append(own_rows)
         far = [over_tp(mine[1:]), across(theirs[1:])]
-        pieces.append([mine, over_ctx(theirs, 2), *far, *near])
+        pieces.append([mine, over_ctx(theirs[1:], 2), *far, *near])
         compacted = pieces[0][1:4]
         places.append(
-            [[(k, 0, f, k) for k in range(levels)] for f in (0, 2)]
-            + [[(k - 1, 1, f, k) for k in range(1, levels)] for f in (0, 2)]
-            + [[(core, 1, f, 0)] for f in (0, 2)]
+            [[(k, 0, 0, k) for k in range(levels)]]
+            + [[(k - 1, t, f, k) for k in range(1, levels)] for t, f in ((0, 2), (1, 0), (1, 2))]
+            + [[(core, t, f, 0)] for t, f in ((1, 0), (1, 2), (0, 2))]
         )
     fronts, after = [], pieces[1][0]
     for groups, got, where in zip(GROUPS, pieces, places):

time: 147 us -> 145 us (0.986)
  waiting for transfers between devices: 66.1 us -> 60.3 us
  starting transfers between devices: 45 us -> 47.7 us
    ppermute x12, waiting for transfers between devices: 28.6 us -> 21.4 us  [along_z(): lax.ppermute(x, 'ctx', [(c, (c + 4 * steps) % ctx) for c in range(ctx)])]
    ppermute x17 -> x18, starting transfers between devices: 18.6 us -> 12.3 us  [over_ctx(): lax.ppermute(x, 'ctx', [(c, c ^ mask) for c in range(ctx) if core is None...]
    ppermute x12, starting transfers between devices: 5.5 us -> 11.3 us  [along_z(): lax.ppermute(x, 'ctx', [(c, (c + 4 * steps) % ctx) for c in range(ctx)])]
    ppermute x17 -> x18, waiting for transfers between devices: 4.68 us -> 9.58 us  [over_ctx(): lax.ppermute(x, 'ctx', [(c, c ^ mask) for c in range(ctx) if core is None...]
    ppermute x3, waiting for transfers between devices: 3.27 us -> 0.01 us  [across(): return lax.ppermute(x, ('ctx', 'tp'), pairs)]
    ppermute x3, starting transfers between devices: 1.21 us -> 3.84 us  [across(): return lax.ppermute(x, ('ctx', 'tp'), pairs)]
    ppermute x2, starting transfers between devices: 6.21 us -> 8.04 us  [to_core(): lax.ppermute(x, 'ctx', [(c, c ^ 1) for c in range(ctx) if c % 2 != core])]
  transfers between devices with their start and end apart: 41 -> 42, of which waited for: 16 -> 14; matrix products, arithmetic and copies ran while one was open for 0% -> 0% of each run, Pallas kernels for 16% -> 16%
where the time goes in v7:
time: 145 us; the launch traced here: 143 us
  waiting for transfers between devices  60.3 us (42%)
  starting transfers between devices  47.7 us (33%)
  Pallas kernels  32.5 us (22%)
  local copies, waits for them, and re-layouts  2.3 us (2%)
    pallas_call x29, Pallas kernels, call(): pl.pallas_call(kernel, out_shape=out_shape, in_specs=[pl.BlockSpec(memory...  32.5 us
    all_to_all x1, waiting for transfers between devices, heads_over_ctx(): lax.all_to_all(packed, 'ctx', split_axis=0, concat_axis=0, tiled=True)  23.5 us
    ppermute x12, waiting for transfers between devices, along_z(): lax.ppermute(x, 'ctx', [(c, (c + 4 * steps) % ctx) for c in range(ctx)])  21.4 us
    ppermute x18, starting transfers between devices, over_ctx(): lax.ppermute(x, 'ctx', [(c, c ^ mask) for c in range(ctx) if core is None...  12.3 us
    ppermute x12, starting transfers between devices, along_z(): lax.ppermute(x, 'ctx', [(c, (c + 4 * steps) % ctx) for c in range(ctx)])  11.3 us
    ppermute x18, waiting for transfers between devices, over_ctx(): lax.ppermute(x, 'ctx', [(c, c ^ mask) for c in range(ctx) if core is None...  9.58 us
    ppermute x2, starting transfers between devices, to_core(): lax.ppermute(x, 'ctx', [(c, c ^ 1) for c in range(ctx) if c % 2 != core])  8.04 us
    all_to_all x1, starting transfers between devices, heads_over_ctx(): lax.all_to_all(packed, 'ctx', split_axis=0, concat_axis=0, tiled=True)  6.57 us
  transfers between devices with their start and end apart: 42, of which 14 were waited for; matrix products, arithmetic and copies ran while one was open for 0% of the time, Pallas kernels for 16%

profile of v7, /device:TPU:13, one launch (start us, length us, event | category | flops | bytes accessed | tf_op | source)
XLA Modules:
  0.0 143.4 jit_solution(14691799975278199051)
XLA Ops:
  0.0 3.0 %shard_map.109 = bf16[16,272,128]{2,1,0:T(8,128)(2,1)} custom-call(s32[1,64]{1,0:T(1,128)} %bitcast.26, s32[4,64]{1,0:T(4,128)} %bitcast.24, f32[4,64]{1,0:T(4,128)} %bitcast.25, bf16[64,2048]{1,0:T(8,128)(2,1)} %q_ref.1, bf16[64,2048]{1,0:T(8,128)(2,1)} %k_ref.1, bf16[64,2048]{1,0:T(8,128)(2,1)} %v_ref.1, bf16[64,2048]{1,0:T(8,128)(2,1)} %r_ref.1), custom_call_target="tpu_custom_call" | custom-call | tf_op jit(solution)/shard_map/pallas_call | solution.py:30
  3.0 6.6 %all-to-all-start = ((bf16[16,272,128]{2,1,0:T(8,128)(2,1)}), bf16[16,272,128]{2,1,0:T(8,128)(2,1)S(1)}, u32[]{:S(2)}, u32[]{:S(2)}) async-start(bf16[16,272,128]{2,1,0:T(8,128)(2,1)} %shard_map.109), calls=%async_computation | async-start | bytes 2228224 | tf_op jit(solution)/shard_map/all_to_all | solution.py:398
  9.6 1.3 collective-permute-start
  10.9 1.5 %collective-permute-done = bf16[2048]{0:T(1024)(128)(2,1)S(1)} collective-permute-done((bf16[2048]{0:T(1024)(128)(2,1)S(1)}, bf16[2048]{0:T(1024)(128)(2,1)S(1)}, u32[]{:S(2)}, u32[]{:S(2)}) %collective-permute-start) | collective-permute-done | bytes 4128 | tf_op jit(solution)/shard_map/ppermute | solution.py:380
  12.4 23.5 %all-to-all-done.x_ref = bf16[16,272,128]{2,1,0:T(8,128)(2,1)S(1)} async-done(((bf16[16,272,128]{2,1,0:T(8,128)(2,1)}), bf16[16,272,128]{2,1,0:T(8,128)(2,1)S(1)}, u32[]{:S(2)}, u32[]{:S(2)}) %all-to-all-start) | async-done | bytes 1114144 | tf_op jit(solution)/shard_map/all_to_all | solution.py:398
  36.0 2.0 %shard_map.110 = (bf16[512,128]{1,0:T(8,128)(2,1)S(1)}, bf16[512,128]{1,0:T(8,128)(2,1)S(1)}, bf16[2,320,256]{2,1,0:T(8,128)(2,1)S(1)}, bf16[2,320,256]{2,1,0:T(...) custom-call(bf16[16,272,128]{2,1,0:T(8,128)(2,1)S(1)} %all-to-all-done.x_ref), custom_call_target="tpu_custom_call" | custom-call | tf_op jit(solution)/shard_map/pallas_call | solution.py:30
  38.0 1.1 collective-permute-start.2
  40.5 1.4 %collective-permute-start.6 = (bf16[2,320,128]{2,1,0:T(8,128)(2,1)S(1)}, bf16[2,320,128]{2,1,0:T(8,128)(2,1)S(1)}, u32[]{:S(2)}, u32[]{:S(2)}) collective-permute-start(bf16[2,320,128]{2,1,0:T(8,128)(2,1)S(1)} %get-tuple-element.66), channel_id=1, source_target_pairs={{0,4},{2,6},{4,0},{6,2},{8,12},{10,14},{12,8},{14,10},{16,20},{18,... | collective-permute-start | bytes 491528 | tf_op jit(solution)/shard_map/ppermute | solution.py:374
  42.9 1.1 collective-permute-start.3
  44.0 3.8 %collective-permute-done.2.refs_2_ = bf16[512,128]{1,0:T(8,128)(2,1)S(1)} collective-permute-done((bf16[512,128]{1,0:T(8,128)(2,1)S(1)}, bf16[512,128]{1,0:T(8,128)(2,1)S(1)}, u32[]{:S(2)}, u32[]{:S(2)}) %collective-permute-start.2) | collective-permute-done | bytes 131104 | tf_op jit(solution)/shard_map/ppermute | solution.py:377
  48.0 3.5 %collective-permute-done.3.refs_3_ = bf16[512,128]{1,0:T(8,128)(2,1)S(1)} collective-permute-done((bf16[512,128]{1,0:T(8,128)(2,1)S(1)}, bf16[512,128]{1,0:T(8,128)(2,1)S(1)}, u32[]{:S(2)}, u32[]{:S(2)}) %collective-permute-start.3) | collective-permute-done | bytes 131104 | tf_op jit(solution)/shard_map/ppermute | solution.py:377
  52.5 1.3 collective-permute-start.11
  53.8 1.4 collective-permute-start.12
  55.3 1.0 collective-permute-start.8
  56.3 1.5 %collective-permute-start.9 = (bf16[512,128]{1,0:T(8,128)(2,1)S(1)}, bf16[512,128]{1,0:T(8,128)(2,1)S(1)}, u32[]{:S(2)}, u32[]{:S(2)}) collective-permute-start(bf16[512,128]{1,0:T(8,128)(2,1)S(1)} %get-tuple-element.68.odd_ref.refs_0_), channel_id=1, source_target_pairs={{0,24},{2,26},{4,28},{6,30},{8,0},{10,2},{12,4},{14,6},{16,8},{18,... | collective-permute-start | bytes 393224 | tf_op jit(solution)/shard_map/ppermute | solution.py:377
  57.8 2.4 %collective-permute-done.8.refs_2_ = bf16[512,128]{1,0:T(8,128)(2,1)S(1)} collective-permute-done((bf16[512,128]{1,0:T(8,128)(2,1)S(1)}, bf16[512,128]{1,0:T(8,128)(2,1)S(1)}, u32[]{:S(2)}, u32[]{:S(2)}) %collective-permute-start.8) | collective-permute-done | bytes 131104 | tf_op jit(solution)/shard_map/ppermute | solution.py:377
  60.1 4.8 %collective-permute-done.9.refs_3_ = bf16[512,128]{1,0:T(8,128)(2,1)S(1)} collective-permute-done((bf16[512,128]{1,0:T(8,128)(2,1)S(1)}, bf16[512,128]{1,0:T(8,128)(2,1)S(1)}, u32[]{:S(2)}, u32[]{:S(2)}) %collective-permute-start.9) | collective-permute-done | bytes 131104 | tf_op jit(solution)/shard_map/ppermute | solution.py:377
  66.9 2.5 %collective-permute-start.15 = (bf16[320,2176]{1,0:T(8,128)(2,1)S(1)}, bf16[320,2176]{1,0:T(8,128)(2,1)S(1)}, u32[]{:S(2)}, u32[]{:S(2)}) collective-permute-start(bf16[320,2176]{1,0:T(8,128)(2,1)S(1)} %shard_map.114.lhs_ref.refs_0_), channel_id=1, source_target_pairs={{0,2},{2,0},{4,6},{6,4},{8,10},{10,8},{12,14},{14,12},{16,18},{18,... | collective-permute-start | bytes 4177928 | tf_op jit(solution)/shard_map/ppermute | solution.py:374
  69.4 1.3 collective-permute-start.16
  70.8 1.4 collective-permute-start.14
  72.2 2.2 %copy-done.1 = bf16[1,4096,512]{2,1,0:T(8,128)(2,1)S(1)} copy-done((bf16[1,4096,512]{2,1,0:T(8,128)(2,1)S(1)}, bf16[1,4096,512]{2,1,0:T(8,128)(2,1)}, u32[]{:S(2)}) %copy-start.1) | copy-done | bytes 4194328
  74.4 2.1 %shard_map.115 = (f32[320,512]{1,0:T(8,128)S(1)}, f32[320,512]{1,0:T(8,128)S(1)}) custom-call(s32[2]{0:T(128)S(1)} %pad_add_fusion.idx_ref, bf16[4096,512]{1,0:T(8,128)(2,1)S(1)} %bitcast.8, bf16[4096,512]{1,0:T(8,128)(2,1)S(1)} %bitcast.14, bf16[320,2176]{1,0:T(8,128)(2,1)S(1)} %shard_map.114.lhs_ref.refs_0_), custom_call_target="tpu_custom_call" | custom-call | tf_op jit(solution)/shard_map/pallas_call | solution.py:30
  76.5 2.1 %shard_map.116.refs_4_.refs_3_.own_ref = bf16[320,512]{1,0:T(8,128)(2,1)S(1)} custom-call(s32[2]{0:T(128)S(1)} %pad_add_fusion.idx_ref, bf16[4096,512]{1,0:T(8,128)(2,1)S(1)} %bitcast.9, bf16[4096,512]{1,0:T(8,128)(2,1)S(1)} %bitcast.15, f32[320,512]{1,0:T(8,128)S(1)} %get-tuple-element.77.gate_ref, f32[320,512]{1,0:T(8,128)S(1)} %get-tuple-element.78.up_ref, ...), custom_call_target="tpu_custom_call" | custom-call | tf_op jit(solution)/shard_map/pallas_call | solution.py:30
  80.4 2.9 %collective-permute-done.13.refs_0_ = bf16[3,320,128]{2,1,0:T(8,128)(2,1)S(1)} collective-permute-done((bf16[3,320,128]{2,1,0:T(8,128)(2,1)S(1)}, bf16[3,320,128]{2,1,0:T(8,128)(2,1)S(1)}, u32[]{:S(2)}, u32[]{:S(2)}) %collective-permute-start.13) | collective-permute-done | bytes 245792 | tf_op jit(solution)/shard_map/ppermute | solution.py:374
  84.1 1.2 collective-permute-start.18
  85.6 1.4 shard_map.119
  87.0 1.4 shard_map.120
  88.4 1.4 shard_map.121
  89.8 1.5 %shard_map.122.refs_2_.refs_0_.own_ref = bf16[320,512]{1,0:T(8,128)(2,1)S(1)} custom-call(s32[2]{0:T(128)S(1)} %pad_add_fusion.idx_ref, bf16[4096,512]{1,0:T(8,128)(2,1)S(1)} %bitcast.13, bf16[4096,512]{1,0:T(8,128)(2,1)S(1)} %bitcast.19, f32[320,512]{1,0:T(8,128)S(1)} %get-tuple-element.83.gate_ref, f32[320,512]{1,0:T(8,128)S(1)} %get-tuple-element.84.up_ref, ...), custom_call_target="tpu_custom_call" | custom-call | tf_op jit(solution)/shard_map/pallas_call | solution.py:30
  91.3 1.3 collective-permute-start.26
  92.6 2.0 %collective-permute-done.21.peer_ref = bf16[320,512]{1,0:T(8,128)(2,1)S(1)} collective-permute-done((bf16[320,512]{1,0:T(8,128)(2,1)S(1)}, bf16[320,512]{1,0:T(8,128)(2,1)S(1)}, u32[]{:S(2)}, u32[]{:S(2)}) %collective-permute-start.21) | collective-permute-done | bytes 327712 | tf_op jit(solution)/shard_map/ppermute | solution.py:380
  94.6 1.4 shard_map.126
  96.0 1.4 collective-permute-start.22
  98.0 1.4 shard_map.125
  99.4 2.2 %collective-permute-done.26.refs_8_.peer_ref = bf16[320,512]{1,0:T(8,128)(2,1)S(1)} collective-permute-done((bf16[320,512]{1,0:T(8,128)(2,1)S(1)}, bf16[320,512]{1,0:T(8,128)(2,1)S(1)}, u32[]{:S(2)}, u32[]{:S(2)}) %collective-permute-start.26) | collective-permute-done | bytes 327712 | tf_op jit(solution)/shard_map/ppermute | solution.py:380
  102.3 1.4 shard_map.132
  103.8 1.2 collective-permute-start.32
  106.6 1.4 shard_map.131
  108.0 2.7 %collective-permute-done.27.got_ref = bf16[160,1024]{1,0:T(8,128)(2,1)S(1)} collective-permute-done((bf16[160,1024]{1,0:T(8,128)(2,1)S(1)}, bf16[160,1024]{1,0:T(8,128)(2,1)S(1)}, u32[]{:S(2)}, u32[]{:S(2)}) %collective-permute-start.27) | collective-permute-done | bytes 327712 | tf_op jit(solution)/shard_map/ppermute | solution.py:374
  112.4 1.3 collective-permute-start.28
  115.7 1.2 collective-permute-start.30
  116.9 2.9 %collective-permute-done.36.got_ref = bf16[160,1024]{1,0:T(8,128)(2,1)S(1)} collective-permute-done((bf16[160,1024]{1,0:T(8,128)(2,1)S(1)}, bf16[160,1024]{1,0:T(8,128)(2,1)S(1)}, u32[]{:S(2)}, u32[]{:S(2)}) %collective-permute-start.36) | collective-permute-done | bytes 327712 | tf_op jit(solution)/shard_map/ppermute | solution.py:374
  120.9 1.3 collective-permute-start.37
  124.4 6.3 %collective-permute-done.30.refs_2_ = bf16[64,1024]{1,0:T(8,128)(2,1)S(1)} collective-permute-done((bf16[64,1024]{1,0:T(8,128)(2,1)S(1)}, bf16[64,1024]{1,0:T(8,128)(2,1)S(1)}, u32[]{:S(2)}, u32[]{:S(2)}) %collective-permute-start.30) | collective-permute-done | bytes 131104 | tf_op jit(solution)/shard_map/ppermute | solution.py:377
  130.8 6.8 %collective-permute-start.31 = (f32[64,1024]{1,0:T(8,128)S(1)}, f32[64,1024]{1,0:T(8,128)S(1)}, u32[]{:S(2)}, u32[]{:S(2)}) collective-permute-start(f32[64,1024]{1,0:T(8,128)S(1)} %shard_map.130.refs_2_), channel_id=1, source_target_pairs={{2,0},{6,4},{10,8},{14,12},{18,16},{22,20},{26,24},{30,28},{3,1},{... | collective-permute-start | bytes 786440 | tf_op jit(solution)/shard_map/ppermute | solution.py:387
  137.7 1.3 collective-permute-start.40
  139.6 1.4 collective-permute-start.20
  142.0 1.4 shard_map.137
  (83 shorter events, 20.0 us)
Async XLA Ops:
  3.0 6.6 %copy-start.4 = (bf16[2048]{0:T(1024)(128)(2,1)S(1)}, bf16[2048]{0:T(1024)(128)(2,1)}, u32[]{:S(2)}) copy-start(bf16[2048]{0:T(1024)(128)(2,1)} %param.15) | copy-start | bytes 12292
  3.0 32.9 %all-to-all-start = ((bf16[16,272,128]{2,1,0:T(8,128)(2,1)}), bf16[16,272,128]{2,1,0:T(8,128)(2,1)S(1)}, u32[]{:S(2)}, u32[]{:S(2)}) async-start(bf16[16,272,128]{2,1,0:T(8,128)(2,1)} %shard_map.109), calls=%async_computation | async-start | bytes 2228224 | tf_op jit(solution)/shard_map/all_to_all | solution.py:398
  9.6 2.8 %collective-permute-start = (bf16[2048]{0:T(1024)(128)(2,1)S(1)}, bf16[2048]{0:T(1024)(128)(2,1)S(1)}, u32[]{:S(2)}, u32[]{:S(2)}) collective-permute-start(bf16[2048]{0:T(1024)(128)(2,1)S(1)} %copy-done.4), channel_id=1, source_target_pairs={{0,1},{1,0},{2,3},{3,2},{4,5},{5,4},{6,7},{7,6},{8,9},{9,8},{10,11... | collective-permute-start | bytes 12296 | tf_op jit(solution)/shard_map/ppermute | solution.py:380
  37.9 4.9 %collective-permute-start.1 = (bf16[512,128]{1,0:T(8,128)(2,1)S(1)}, bf16[512,128]{1,0:T(8,128)(2,1)S(1)}, u32[]{:S(2)}, u32[]{:S(2)}) collective-permute-start(bf16[512,128]{1,0:T(8,128)(2,1)S(1)} %get-tuple-element.61.even_ref.refs_0_), channel_id=1, source_target_pairs={{0,8},{2,10},{4,12},{6,14},{8,16},{10,18},{12,20},{14,22},{16,24},... | collective-permute-start | bytes 393224 | tf_op jit(solution)/shard_map/ppermute | solution.py:377
  38.0 9.8 %collective-permute-start.2 = (bf16[512,128]{1,0:T(8,128)(2,1)S(1)}, bf16[512,128]{1,0:T(8,128)(2,1)S(1)}, u32[]{:S(2)}, u32[]{:S(2)}) collective-permute-start(bf16[512,128]{1,0:T(8,128)(2,1)S(1)} %get-tuple-element.61.even_ref.refs_0_), channel_id=1, source_target_pairs={{0,16},{2,18},{4,20},{6,22},{8,24},{10,26},{12,28},{14,30},{16,0},... | collective-permute-start | bytes 393224 | tf_op jit(solution)/shard_map/ppermute | solution.py:377
  39.5 12.0 %collective-permute-start.5 = (bf16[2,320,128]{2,1,0:T(8,128)(2,1)S(1)}, bf16[2,320,128]{2,1,0:T(8,128)(2,1)S(1)}, u32[]{:S(2)}, u32[]{:S(2)}) collective-permute-start(bf16[2,320,128]{2,1,0:T(8,128)(2,1)S(1)} %get-tuple-element.66), channel_id=1, source_target_pairs={{0,5},{1,4},{2,7},{3,6},{4,1},{5,0},{6,3},{7,2},{8,13},{9,12},{10,... | collective-permute-start | bytes 491528 | tf_op jit(solution)/shard_map/ppermute | solution.py:384
  40.5 11.0 %collective-permute-start.6 = (bf16[2,320,128]{2,1,0:T(8,128)(2,1)S(1)}, bf16[2,320,128]{2,1,0:T(8,128)(2,1)S(1)}, u32[]{:S(2)}, u32[]{:S(2)}) collective-permute-start(bf16[2,320,128]{2,1,0:T(8,128)(2,1)S(1)} %get-tuple-element.66), channel_id=1, source_target_pairs={{0,4},{2,6},{4,0},{6,2},{8,12},{10,14},{12,8},{14,10},{16,20},{18,... | collective-permute-start | bytes 491528 | tf_op jit(solution)/shard_map/ppermute | solution.py:374
  41.9 9.6 %collective-permute-start.4 = (bf16[2,320,128]{2,1,0:T(8,128)(2,1)S(1)}, bf16[2,320,128]{2,1,0:T(8,128)(2,1)S(1)}, u32[]{:S(2)}, u32[]{:S(2)}) collective-permute-start(bf16[2,320,128]{2,1,0:T(8,128)(2,1)S(1)} %get-tuple-element.65), channel_id=1, source_target_pairs={{0,1},{1,0},{2,3},{3,2},{4,5},{5,4},{6,7},{7,6},{8,9},{9,8},{10,11... | collective-permute-start | bytes 491528 | tf_op jit(solution)/shard_map/ppermute | solution.py:380
  42.9 8.6 %collective-permute-start.3 = (bf16[512,128]{1,0:T(8,128)(2,1)S(1)}, bf16[512,128]{1,0:T(8,128)(2,1)S(1)}, u32[]{:S(2)}, u32[]{:S(2)}) collective-permute-start(bf16[512,128]{1,0:T(8,128)(2,1)S(1)} %get-tuple-element.61.even_ref.refs_0_), channel_id=1, source_target_pairs={{0,24},{2,26},{4,28},{6,30},{8,0},{10,2},{12,4},{14,6},{16,8},{18,... | collective-permute-start | bytes 393224 | tf_op jit(solution)/shard_map/ppermute | solution.py:377
  47.8 8.5 %collective-permute-start.7 = (bf16[512,128]{1,0:T(8,128)(2,1)S(1)}, bf16[512,128]{1,0:T(8,128)(2,1)S(1)}, u32[]{:S(2)}, u32[]{:S(2)}) collective-permute-start(bf16[512,128]{1,0:T(8,128)(2,1)S(1)} %get-tuple-element.68.odd_ref.refs_0_), channel_id=1, source_target_pairs={{0,8},{2,10},{4,12},{6,14},{8,16},{10,18},{12,20},{14,22},{16,24},... | collective-permute-start | bytes 393224 | tf_op jit(solution)/shard_map/ppermute | solution.py:377
  52.4 12.5 %collective-permute-start.10 = (bf16[3,320,128]{2,1,0:T(8,128)(2,1)S(1)}, bf16[3,320,128]{2,1,0:T(8,128)(2,1)S(1)}, u32[]{:S(2)}, u32[]{:S(2)}) collective-permute-start(bf16[3,320,128]{2,1,0:T(8,128)(2,1)S(1)} %slice.14), channel_id=1, source_target_pairs={{0,4},{2,6},{4,0},{6,2},{8,12},{10,14},{12,8},{14,10},{16,20},{18,... | collective-permute-start | bytes 737288 | tf_op jit(solution)/shard_map/ppermute | solution.py:374
  52.5 12.4 %collective-permute-start.11 = (bf16[3,320,128]{2,1,0:T(8,128)(2,1)S(1)}, bf16[3,320,128]{2,1,0:T(8,128)(2,1)S(1)}, u32[]{:S(2)}, u32[]{:S(2)}) collective-permute-start(bf16[3,320,128]{2,1,0:T(8,128)(2,1)S(1)} %slice.15), channel_id=1, source_target_pairs={{0,1},{1,0},{2,3},{3,2},{4,5},{5,4},{6,7},{7,6},{8,9},{9,8},{10,11... | collective-permute-start | bytes 737288 | tf_op jit(solution)/shard_map/ppermute | solution.py:380
  53.8 11.1 %collective-permute-start.12 = (bf16[3,320,128]{2,1,0:T(8,128)(2,1)S(1)}, bf16[3,320,128]{2,1,0:T(8,128)(2,1)S(1)}, u32[]{:S(2)}, u32[]{:S(2)}) collective-permute-start(bf16[3,320,128]{2,1,0:T(8,128)(2,1)S(1)} %slice.14), channel_id=1, source_target_pairs={{0,5},{1,4},{2,7},{3,6},{4,1},{5,0},{6,3},{7,2},{8,13},{9,12},{10,... | collective-permute-start | bytes 737288 | tf_op jit(solution)/shard_map/ppermute | solution.py:384
  55.3 4.9 %collective-permute-start.8 = (bf16[512,128]{1,0:T(8,128)(2,1)S(1)}, bf16[512,128]{1,0:T(8,128)(2,1)S(1)}, u32[]{:S(2)}, u32[]{:S(2)}) collective-permute-start(bf16[512,128]{1,0:T(8,128)(2,1)S(1)} %get-tuple-element.68.odd_ref.refs_0_), channel_id=1, source_target_pairs={{0,16},{2,18},{4,20},{6,22},{8,24},{10,26},{12,28},{14,30},{16,0},... | collective-permute-start | bytes 393224 | tf_op jit(solution)/shard_map/ppermute | solution.py:377
  56.3 8.6 %collective-permute-start.9 = (bf16[512,128]{1,0:T(8,128)(2,1)S(1)}, bf16[512,128]{1,0:T(8,128)(2,1)S(1)}, u32[]{:S(2)}, u32[]{:S(2)}) collective-permute-start(bf16[512,128]{1,0:T(8,128)(2,1)S(1)} %get-tuple-element.68.odd_ref.refs_0_), channel_id=1, source_target_pairs={{0,24},{2,26},{4,28},{6,30},{8,0},{10,2},{12,4},{14,6},{16,8},{18,... | collective-permute-start | bytes 393224 | tf_op jit(solution)/shard_map/ppermute | solution.py:377
  65.8 6.4 %copy-start = (bf16[1,4096,512]{2,1,0:T(8,128)(2,1)S(1)}, bf16[1,4096,512]{2,1,0:T(8,128)(2,1)}, u32[]{:S(2)}) copy-start(bf16[1,4096,512]{2,1,0:T(8,128)(2,1)} %param.19) | copy-start | bytes 12582916
  66.9 9.6 %collective-permute-start.15 = (bf16[320,2176]{1,0:T(8,128)(2,1)S(1)}, bf16[320,2176]{1,0:T(8,128)(2,1)S(1)}, u32[]{:S(2)}, u32[]{:S(2)}) collective-permute-start(bf16[320,2176]{1,0:T(8,128)(2,1)S(1)} %shard_map.114.lhs_ref.refs_0_), channel_id=1, source_target_pairs={{0,2},{2,0},{4,6},{6,4},{8,10},{10,8},{12,14},{14,12},{16,18},{18,... | collective-permute-start | bytes 4177928 | tf_op jit(solution)/shard_map/ppermute | solution.py:374
  69.4 9.2 %collective-permute-start.16 = (bf16[3,320,128]{2,1,0:T(8,128)(2,1)S(1)}, bf16[3,320,128]{2,1,0:T(8,128)(2,1)S(1)}, u32[]{:S(2)}, u32[]{:S(2)}) collective-permute-start(bf16[3,320,128]{2,1,0:T(8,128)(2,1)S(1)} %slice.17), channel_id=1, source_target_pairs={{0,1},{1,0},{2,3},{3,2},{4,5},{5,4},{6,7},{7,6},{8,9},{9,8},{10,11... | collective-permute-start | bytes 737288 | tf_op jit(solution)/shard_map/ppermute | solution.py:380
  70.7 12.6 %collective-permute-start.13 = (bf16[3,320,128]{2,1,0:T(8,128)(2,1)S(1)}, bf16[3,320,128]{2,1,0:T(8,128)(2,1)S(1)}, u32[]{:S(2)}, u32[]{:S(2)}) collective-permute-start(bf16[3,320,128]{2,1,0:T(8,128)(2,1)S(1)} %slice.16), channel_id=1, source_target_pairs={{0,4},{2,6},{4,0},{6,2},{8,12},{10,14},{12,8},{14,10},{16,20},{18,... | collective-permute-start | bytes 737288 | tf_op jit(solution)/shard_map/ppermute | solution.py:374
  70.8 12.5 %collective-permute-start.14 = (bf16[3,320,128]{2,1,0:T(8,128)(2,1)S(1)}, bf16[3,320,128]{2,1,0:T(8,128)(2,1)S(1)}, u32[]{:S(2)}, u32[]{:S(2)}) collective-permute-start(bf16[3,320,128]{2,1,0:T(8,128)(2,1)S(1)} %slice.16), channel_id=1, source_target_pairs={{0,5},{1,4},{2,7},{3,6},{4,1},{5,0},{6,3},{7,2},{8,13},{9,12},{10,... | collective-permute-start | bytes 737288 | tf_op jit(solution)/shard_map/ppermute | solution.py:384
  72.2 2.2 %copy-start.1 = (bf16[1,4096,512]{2,1,0:T(8,128)(2,1)S(1)}, bf16[1,4096,512]{2,1,0:T(8,128)(2,1)}, u32[]{:S(2)}) copy-start(bf16[1,4096,512]{2,1,0:T(8,128)(2,1)} %param.20) | copy-start | bytes 12582916
  76.5 9.1 %copy-start.2 = (bf16[1,4096,512]{2,1,0:T(8,128)(2,1)S(1)}, bf16[1,4096,512]{2,1,0:T(8,128)(2,1)}, u32[]{:S(2)}) copy-start(bf16[1,4096,512]{2,1,0:T(8,128)(2,1)} %param.20) | copy-start | bytes 12582916
  79.5 7.5 %collective-permute-start.17 = (bf16[320,1152]{1,0:T(8,128)(2,1)S(1)}, bf16[320,1152]{1,0:T(8,128)(2,1)S(1)}, u32[]{:S(2)}, u32[]{:S(2)}) collective-permute-start(bf16[320,1152]{1,0:T(8,128)(2,1)S(1)} %shard_map.118.lhs_ref.refs_0_), channel_id=1, source_target_pairs={{0,2},{2,0},{4,6},{6,4},{8,10},{10,8},{12,14},{14,12},{16,18},{18,... | collective-permute-start | bytes 2211848 | tf_op jit(solution)/shard_map/ppermute | solution.py:374
  84.1 5.7 %collective-permute-start.18 = (bf16[320,1152]{1,0:T(8,128)(2,1)S(1)}, bf16[320,1152]{1,0:T(8,128)(2,1)S(1)}, u32[]{:S(2)}, u32[]{:S(2)}) collective-permute-start(bf16[320,1152]{1,0:T(8,128)(2,1)S(1)} %shard_map.117.lhs_ref.refs_2_), channel_id=1, source_target_pairs={{0,2},{2,0},{4,6},{6,4},{8,10},{10,8},{12,14},{14,12},{16,18},{18,... | collective-permute-start | bytes 2211848 | tf_op jit(solution)/shard_map/ppermute | solution.py:374
  85.3 9.3 %collective-permute-start.21 = (bf16[320,512]{1,0:T(8,128)(2,1)S(1)}, bf16[320,512]{1,0:T(8,128)(2,1)S(1)}, u32[]{:S(2)}, u32[]{:S(2)}) collective-permute-start(bf16[320,512]{1,0:T(8,128)(2,1)S(1)} %shard_map.116.refs_4_.refs_3_.own_ref), channel_id=1, source_target_pairs={{0,1},{1,0},{2,3},{3,2},{4,5},{5,4},{6,7},{7,6},{8,9},{9,8},{10,11... | collective-permute-start | bytes 983048 | tf_op jit(solution)/shard_map/ppermute | solution.py:380
  89.8 4.8 %copy-start.3 = (bf16[1,1024,2048]{2,1,0:T(8,128)(2,1)S(1)}, bf16[1,1024,2048]{2,1,0:T(8,128)(2,1)}, u32[]{:S(2)}) copy-start(bf16[1,1024,2048]{2,1,0:T(8,128)(2,1)} %param.21) | copy-start | bytes 12582916
  91.3 10.3 %collective-permute-start.26 = (bf16[320,512]{1,0:T(8,128)(2,1)S(1)}, bf16[320,512]{1,0:T(8,128)(2,1)S(1)}, u32[]{:S(2)}, u32[]{:S(2)}) collective-permute-start(bf16[320,512]{1,0:T(8,128)(2,1)S(1)} %shard_map.122.refs_2_.refs_0_.own_ref), channel_id=1, source_target_pairs={{0,1},{1,0},{2,3},{3,2},{4,5},{5,4},{6,7},{7,6},{8,9},{9,8},{10,11... | collective-permute-start | bytes 983048 | tf_op jit(solution)/shard_map/ppermute | solution.py:380
  96.0 3.4 %collective-permute-start.22 = (bf16[320,256]{1,0:T(8,128)(2,1)S(1)}, bf16[320,256]{1,0:T(8,128)(2,1)S(1)}, u32[]{:S(2)}, u32[]{:S(2)}) collective-permute-start(bf16[320,256]{1,0:T(8,128)(2,1)S(1)} %get-tuple-element.92), channel_id=1, source_target_pairs={{0,2},{2,0},{4,6},{6,4},{8,10},{10,8},{12,14},{14,12},{16,18},{18,... | collective-permute-start | bytes 491528 | tf_op jit(solution)/shard_map/ppermute | solution.py:374
  97.4 2.0 %collective-permute-start.23 = (bf16[320,256]{1,0:T(8,128)(2,1)S(1)}, bf16[320,256]{1,0:T(8,128)(2,1)S(1)}, u32[]{:S(2)}, u32[]{:S(2)}) collective-permute-start(bf16[320,256]{1,0:T(8,128)(2,1)S(1)} %get-tuple-element.93), channel_id=1, source_target_pairs={{0,2},{2,0},{4,6},{6,4},{8,10},{10,8},{12,14},{14,12},{16,18},{18,... | collective-permute-start | bytes 491528 | tf_op jit(solution)/shard_map/ppermute | solution.py:374
  97.5 1.9 %collective-permute-start.24 = (bf16[320,256]{1,0:T(8,128)(2,1)S(1)}, bf16[320,256]{1,0:T(8,128)(2,1)S(1)}, u32[]{:S(2)}, u32[]{:S(2)}) collective-permute-start(bf16[320,256]{1,0:T(8,128)(2,1)S(1)} %get-tuple-element.94), channel_id=1, source_target_pairs={{0,2},{2,0},{4,6},{6,4},{8,10},{10,8},{12,14},{14,12},{16,18},{18,... | collective-permute-start | bytes 491528 | tf_op jit(solution)/shard_map/ppermute | solution.py:374
  97.9 1.5 %collective-permute-start.25 = (bf16[320,256]{1,0:T(8,128)(2,1)S(1)}, bf16[320,256]{1,0:T(8,128)(2,1)S(1)}, u32[]{:S(2)}, u32[]{:S(2)}) collective-permute-start(bf16[320,256]{1,0:T(8,128)(2,1)S(1)} %get-tuple-element.95), channel_id=1, source_target_pairs={{0,2},{2,0},{4,6},{6,4},{8,10},{10,8},{12,14},{14,12},{16,18},{18,... | collective-permute-start | bytes 491528 | tf_op jit(solution)/shard_map/ppermute | solution.py:374
  102.3 8.4 %collective-permute-start.27 = (bf16[160,1024]{1,0:T(8,128)(2,1)S(1)}, bf16[160,1024]{1,0:T(8,128)(2,1)S(1)}, u32[]{:S(2)}, u32[]{:S(2)}) collective-permute-start(bf16[160,1024]{1,0:T(8,128)(2,1)S(1)} %shard_map.128.refs_0_), channel_id=1, source_target_pairs={{0,4},{2,6},{4,0},{6,2},{8,12},{10,14},{12,8},{14,10},{16,20},{18,... | collective-permute-start | bytes 983048 | tf_op jit(solution)/shard_map/ppermute | solution.py:374
  103.8 7.9 %collective-permute-start.32 = (bf16[320,256]{1,0:T(8,128)(2,1)S(1)}, bf16[320,256]{1,0:T(8,128)(2,1)S(1)}, u32[]{:S(2)}, u32[]{:S(2)}) collective-permute-start(bf16[320,256]{1,0:T(8,128)(2,1)S(1)} %get-tuple-element.105), channel_id=1, source_target_pairs={{0,2},{2,0},{4,6},{6,4},{8,10},{10,8},{12,14},{14,12},{16,18},{18,... | collective-permute-start | bytes 491528 | tf_op jit(solution)/shard_map/ppermute | solution.py:374
  105.0 6.7 %collective-permute-start.33 = (bf16[320,256]{1,0:T(8,128)(2,1)S(1)}, bf16[320,256]{1,0:T(8,128)(2,1)S(1)}, u32[]{:S(2)}, u32[]{:S(2)}) collective-permute-start(bf16[320,256]{1,0:T(8,128)(2,1)S(1)} %get-tuple-element.106), channel_id=1, source_target_pairs={{0,2},{2,0},{4,6},{6,4},{8,10},{10,8},{12,14},{14,12},{16,18},{18,... | collective-permute-start | bytes 491528 | tf_op jit(solution)/shard_map/ppermute | solution.py:374
  105.1 6.7 %collective-permute-start.34 = (bf16[320,256]{1,0:T(8,128)(2,1)S(1)}, bf16[320,256]{1,0:T(8,128)(2,1)S(1)}, u32[]{:S(2)}, u32[]{:S(2)}) collective-permute-start(bf16[320,256]{1,0:T(8,128)(2,1)S(1)} %get-tuple-element.107), channel_id=1, source_target_pairs={{0,2},{2,0},{4,6},{6,4},{8,10},{10,8},{12,14},{14,12},{16,18},{18,... | collective-permute-start | bytes 491528 | tf_op jit(solution)/shard_map/ppermute | solution.py:374
  105.5 6.2 %collective-permute-start.35 = (bf16[320,256]{1,0:T(8,128)(2,1)S(1)}, bf16[320,256]{1,0:T(8,128)(2,1)S(1)}, u32[]{:S(2)}, u32[]{:S(2)}) collective-permute-start(bf16[320,256]{1,0:T(8,128)(2,1)S(1)} %get-tuple-element.108), channel_id=1, source_target_pairs={{0,2},{2,0},{4,6},{6,4},{8,10},{10,8},{12,14},{14,12},{16,18},{18,... | collective-permute-start | bytes 491528 | tf_op jit(solution)/shard_map/ppermute | solution.py:374
  112.4 7.5 %collective-permute-start.36 = (bf16[160,1024]{1,0:T(8,128)(2,1)S(1)}, bf16[160,1024]{1,0:T(8,128)(2,1)S(1)}, u32[]{:S(2)}, u32[]{:S(2)}) collective-permute-start(bf16[160,1024]{1,0:T(8,128)(2,1)S(1)} %shard_map.134), channel_id=1, source_target_pairs={{0,4},{2,6},{4,0},{6,2},{8,12},{10,14},{12,8},{14,10},{16,20},{18,... | collective-permute-start | bytes 983048 | tf_op jit(solution)/shard_map/ppermute | solution.py:374
  112.4 10.6 %collective-permute-start.28 = (bf16[64,1024]{1,0:T(8,128)(2,1)S(1)}, bf16[64,1024]{1,0:T(8,128)(2,1)S(1)}, u32[]{:S(2)}, u32[]{:S(2)}) collective-permute-start(bf16[64,1024]{1,0:T(8,128)(2,1)S(1)} %get-tuple-element.97), channel_id=1, source_target_pairs={{0,8},{2,10},{4,12},{6,14},{8,16},{10,18},{12,20},{14,22},{16,24},... | collective-permute-start | bytes 393224 | tf_op jit(solution)/shard_map/ppermute | solution.py:377
  114.8 9.0 %collective-permute-start.29 = (bf16[64,1024]{1,0:T(8,128)(2,1)S(1)}, bf16[64,1024]{1,0:T(8,128)(2,1)S(1)}, u32[]{:S(2)}, u32[]{:S(2)}) collective-permute-start(bf16[64,1024]{1,0:T(8,128)(2,1)S(1)} %get-tuple-element.98), channel_id=1, source_target_pairs={{0,16},{2,18},{4,20},{6,22},{8,24},{10,26},{12,28},{14,30},{16,0},... | collective-permute-start | bytes 393224 | tf_op jit(solution)/shard_map/ppermute | solution.py:377
  115.7 15.0 %collective-permute-start.30 = (bf16[64,1024]{1,0:T(8,128)(2,1)S(1)}, bf16[64,1024]{1,0:T(8,128)(2,1)S(1)}, u32[]{:S(2)}, u32[]{:S(2)}) collective-permute-start(bf16[64,1024]{1,0:T(8,128)(2,1)S(1)} %get-tuple-element.99), channel_id=1, source_target_pairs={{0,24},{2,26},{4,28},{6,30},{8,0},{10,2},{12,4},{14,6},{16,8},{18,... | collective-permute-start | bytes 393224 | tf_op jit(solution)/shard_map/ppermute | solution.py:377
  120.9 16.7 %collective-permute-start.37 = (bf16[64,1024]{1,0:T(8,128)(2,1)S(1)}, bf16[64,1024]{1,0:T(8,128)(2,1)S(1)}, u32[]{:S(2)}, u32[]{:S(2)}) collective-permute-start(bf16[64,1024]{1,0:T(8,128)(2,1)S(1)} %get-tuple-element.110), channel_id=1, source_target_pairs={{0,8},{2,10},{4,12},{6,14},{8,16},{10,18},{12,20},{14,22},{16,24},... | collective-permute-start | bytes 393224 | tf_op jit(solution)/shard_map/ppermute | solution.py:377
  122.2 15.4 %collective-permute-start.38 = (bf16[64,1024]{1,0:T(8,128)(2,1)S(1)}, bf16[64,1024]{1,0:T(8,128)(2,1)S(1)}, u32[]{:S(2)}, u32[]{:S(2)}) collective-permute-start(bf16[64,1024]{1,0:T(8,128)(2,1)S(1)} %get-tuple-element.111), channel_id=1, source_target_pairs={{0,16},{2,18},{4,20},{6,22},{8,24},{10,26},{12,28},{14,30},{16,0},... | collective-permute-start | bytes 393224 | tf_op jit(solution)/shard_map/ppermute | solution.py:377
  123.0 14.5 %collective-permute-start.39 = (bf16[64,1024]{1,0:T(8,128)(2,1)S(1)}, bf16[64,1024]{1,0:T(8,128)(2,1)S(1)}, u32[]{:S(2)}, u32[]{:S(2)}) collective-permute-start(bf16[64,1024]{1,0:T(8,128)(2,1)S(1)} %get-tuple-element.112), channel_id=1, source_target_pairs={{0,24},{2,26},{4,28},{6,30},{8,0},{10,2},{12,4},{14,6},{16,8},{18,... | collective-permute-start | bytes 393224 | tf_op jit(solution)/shard_map/ppermute | solution.py:377
  123.7 15.2 %collective-permute-start.19 = (bf16[2,4,64,128]{3,2,1,0:T(8,128)(2,1)S(1)}, bf16[2,4,64,128]{3,2,1,0:T(8,128)(2,1)S(1)}, u32[]{:S(2)}, u32[]{:S(2)}) collective-permute-start(bf16[2,4,64,128]{3,2,1,0:T(8,128)(2,1)S(1)} %shard_map.123), channel_id=1, source_target_pairs={{0,4},{2,6},{4,0},{6,2},{8,12},{10,14},{12,8},{14,10},{16,20},{18,... | collective-permute-start | bytes 393224 | tf_op jit(solution)/shard_map/ppermute | solution.py:374
  130.8 11.2 %collective-permute-start.31 = (f32[64,1024]{1,0:T(8,128)S(1)}, f32[64,1024]{1,0:T(8,128)S(1)}, u32[]{:S(2)}, u32[]{:S(2)}) collective-permute-start(f32[64,1024]{1,0:T(8,128)S(1)} %shard_map.130.refs_2_), channel_id=1, source_target_pairs={{2,0},{6,4},{10,8},{14,12},{18,16},{22,20},{26,24},{30,28},{3,1},{... | collective-permute-start | bytes 786440 | tf_op jit(solution)/shard_map/ppermute | solution.py:387
  137.7 4.3 %collective-permute-start.40 = (f32[64,1024]{1,0:T(8,128)S(1)}, f32[64,1024]{1,0:T(8,128)S(1)}, u32[]{:S(2)}, u32[]{:S(2)}) collective-permute-start(f32[64,1024]{1,0:T(8,128)S(1)} %shard_map.136.refs_4_), channel_id=1, source_target_pairs={{0,2},{4,6},{8,10},{12,14},{16,18},{20,22},{24,26},{28,30},{1,3},{... | collective-permute-start | bytes 786440 | tf_op jit(solution)/shard_map/ppermute | solution.py:387
  139.6 2.4 %collective-permute-start.20 = (bf16[8,64,128]{2,1,0:T(8,128)(2,1)S(1)}, bf16[8,64,128]{2,1,0:T(8,128)(2,1)S(1)}, u32[]{:S(2)}, u32[]{:S(2)}) collective-permute-start(bf16[8,64,128]{2,1,0:T(8,128)(2,1)S(1)} %get-tuple-element.86), channel_id=1, source_target_pairs={{0,2},{2,0},{4,6},{6,4},{8,10},{10,8},{12,14},{14,12},{16,18},{18,... | collective-permute-start | bytes 393224 | tf_op jit(solution)/shard_map/ppermute | solution.py:374

commit v8 on v7

--- a/solution.py
+++ b/solution.py
@@ -16,7 +16,7 @@
 LANES = 128
 MIB = 1 << 20
 PARTS = 4
-GROUPS = (((0, 1, 2, 3, 4, 5, 6),), ((0, 2, 4), (1, 3, 5, 6)))
+GROUPS = (((0, 1, 2, 3, 4, 5, 6),), ((0, 1, 2, 3, 4, 5, 6),))
 
 
 def silu(v):
@@ -424,7 +424,7 @@
         blocks.append(own_rows)
         far = [over_tp(mine[1:]), across(theirs[1:])]
         pieces.append([mine, over_ctx(theirs[1:], 2), *far, *near])
-        compacted = pieces[0][1:4]
+        compacted = [theirs]
         places.append(
             [[(k, 0, 0, k) for k in range(levels)]]
             + [[(k - 1, t, f, k) for k in range(1, levels)] for t, f in ((0, 2), (1, 0), (1, 2))]

time: 145 us -> 144 us (level)
  waiting for transfers between devices: 60.3 us -> 64 us
  Pallas kernels: 32.5 us -> 30.5 us
  starting transfers between devices: 47.7 us -> 45.9 us
    ppermute x3, waiting for transfers between devices: 0.01 us -> 4.63 us  [across(): return lax.ppermute(x, ('ctx', 'tp'), pairs)]
    ppermute x18 -> x17, waiting for transfers between devices: 9.58 us -> 5.58 us  [over_ctx(): lax.ppermute(x, 'ctx', [(c, c ^ mask) for c in range(ctx) if core is None...]
    pallas_call x29 -> x26, Pallas kernels: 32.5 us -> 30.5 us  [call(): pl.pallas_call(kernel, out_shape=out_shape, in_specs=[pl.BlockSpec(memory...]
    ppermute x12, waiting for transfers between devices: 21.4 us -> 23.4 us  [along_z(): lax.ppermute(x, 'ctx', [(c, (c + 4 * steps) % ctx) for c in range(ctx)])]
    ppermute x2, starting transfers between devices: 8.04 us -> 6.02 us  [to_core(): lax.ppermute(x, 'ctx', [(c, c ^ 1) for c in range(ctx) if c % 2 != core])]
    ppermute x18 -> x17, starting transfers between devices: 12.3 us -> 11.3 us  [over_ctx(): lax.ppermute(x, 'ctx', [(c, c ^ mask) for c in range(ctx) if core is None...]
  transfers between devices with their start and end apart: 42 -> 41, of which waited for: 14 -> 16; matrix products, arithmetic and copies ran while one was open for 0% -> 0% of each run, Pallas kernels for 16% -> 14%
where the time goes in v8:
time: 144 us; the launch traced here: 143 us
  waiting for transfers between devices  64 us (44%)
  starting transfers between devices  45.9 us (32%)
  Pallas kernels  30.5 us (21%)
  local copies, waits for them, and re-layouts  2.3 us (2%)
    pallas_call x26, Pallas kernels, call(): pl.pallas_call(kernel, out_shape=out_shape, in_specs=[pl.BlockSpec(memory...  30.5 us
    all_to_all x1, waiting for transfers between devices, heads_over_ctx(): lax.all_to_all(packed, 'ctx', split_axis=0, concat_axis=0, tiled=True)  23.5 us
    ppermute x12, waiting for transfers between devices, along_z(): lax.ppermute(x, 'ctx', [(c, (c + 4 * steps) % ctx) for c in range(ctx)])  23.4 us
    ppermute x12, starting transfers between devices, along_z(): lax.ppermute(x, 'ctx', [(c, (c + 4 * steps) % ctx) for c in range(ctx)])  12.5 us
    ppermute x17, starting transfers between devices, over_ctx(): lax.ppermute(x, 'ctx', [(c, c ^ mask) for c in range(ctx) if core is None...  11.3 us
    ppermute x6, waiting for transfers between devices, over_tp(): return lax.ppermute(x, 'tp', [(0, 1), (1, 0)])  6.84 us
    all_to_all x1, starting transfers between devices, heads_over_ctx(): lax.all_to_all(packed, 'ctx', split_axis=0, concat_axis=0, tiled=True)  6.57 us
    ppermute x2, starting transfers between devices, to_core(): lax.ppermute(x, 'ctx', [(c, c ^ 1) for c in range(ctx) if c % 2 != core])  6.02 us
  transfers between devices with their start and end apart: 41, of which 16 were waited for; matrix products, arithmetic and copies ran while one was open for 0% of the time, Pallas kernels for 14%

profile of v8, /device:TPU:13, one launch (start us, length us, event | category | flops | bytes accessed | tf_op | source)
XLA Modules:
  0.0 143.2 jit_solution(9686789285391926603)
XLA Ops:
  0.0 3.0 %shard_map.109 = bf16[16,272,128]{2,1,0:T(8,128)(2,1)} custom-call(s32[1,64]{1,0:T(1,128)} %bitcast.22, s32[4,64]{1,0:T(4,128)} %bitcast.20, f32[4,64]{1,0:T(4,128)} %bitcast.21, bf16[64,2048]{1,0:T(8,128)(2,1)} %q_ref.1, bf16[64,2048]{1,0:T(8,128)(2,1)} %k_ref.1, bf16[64,2048]{1,0:T(8,128)(2,1)} %v_ref.1, bf16[64,2048]{1,0:T(8,128)(2,1)} %r_ref.1), custom_call_target="tpu_custom_call" | custom-call | tf_op jit(solution)/shard_map/pallas_call | solution.py:30
  3.1 6.6 %all-to-all-start = ((bf16[16,272,128]{2,1,0:T(8,128)(2,1)}), bf16[16,272,128]{2,1,0:T(8,128)(2,1)S(1)}, u32[]{:S(2)}, u32[]{:S(2)}) async-start(bf16[16,272,128]{2,1,0:T(8,128)(2,1)} %shard_map.109), calls=%async_computation | async-start | bytes 2228224 | tf_op jit(solution)/shard_map/all_to_all | solution.py:398
  9.6 1.3 collective-permute-start
  10.9 1.5 %collective-permute-done = bf16[2048]{0:T(1024)(128)(2,1)S(1)} collective-permute-done((bf16[2048]{0:T(1024)(128)(2,1)S(1)}, bf16[2048]{0:T(1024)(128)(2,1)S(1)}, u32[]{:S(2)}, u32[]{:S(2)}) %collective-permute-start) | collective-permute-done | bytes 4128 | tf_op jit(solution)/shard_map/ppermute | solution.py:380
  12.4 23.5 %all-to-all-done.x_ref = bf16[16,272,128]{2,1,0:T(8,128)(2,1)S(1)} async-done(((bf16[16,272,128]{2,1,0:T(8,128)(2,1)}), bf16[16,272,128]{2,1,0:T(8,128)(2,1)S(1)}, u32[]{:S(2)}, u32[]{:S(2)}) %all-to-all-start) | async-done | bytes 1114144 | tf_op jit(solution)/shard_map/all_to_all | solution.py:398
  36.0 2.0 %shard_map.110 = (bf16[512,128]{1,0:T(8,128)(2,1)S(1)}, bf16[512,128]{1,0:T(8,128)(2,1)S(1)}, bf16[2,320,256]{2,1,0:T(8,128)(2,1)S(1)}, bf16[2,320,256]{2,1,0:T(...) custom-call(bf16[16,272,128]{2,1,0:T(8,128)(2,1)S(1)} %all-to-all-done.x_ref), custom_call_target="tpu_custom_call" | custom-call | tf_op jit(solution)/shard_map/pallas_call | solution.py:30
  38.0 1.1 collective-permute-start.2
  40.5 1.4 %collective-permute-start.6 = (bf16[2,320,128]{2,1,0:T(8,128)(2,1)S(1)}, bf16[2,320,128]{2,1,0:T(8,128)(2,1)S(1)}, u32[]{:S(2)}, u32[]{:S(2)}) collective-permute-start(bf16[2,320,128]{2,1,0:T(8,128)(2,1)S(1)} %get-tuple-element.62), channel_id=1, source_target_pairs={{0,4},{2,6},{4,0},{6,2},{8,12},{10,14},{12,8},{14,10},{16,20},{18,... | collective-permute-start | bytes 491528 | tf_op jit(solution)/shard_map/ppermute | solution.py:374
  42.9 1.1 collective-permute-start.3
  44.0 3.8 %collective-permute-done.2.refs_2_ = bf16[512,128]{1,0:T(8,128)(2,1)S(1)} collective-permute-done((bf16[512,128]{1,0:T(8,128)(2,1)S(1)}, bf16[512,128]{1,0:T(8,128)(2,1)S(1)}, u32[]{:S(2)}, u32[]{:S(2)}) %collective-permute-start.2) | collective-permute-done | bytes 131104 | tf_op jit(solution)/shard_map/ppermute | solution.py:377
  48.1 3.5 %collective-permute-done.3.refs_3_ = bf16[512,128]{1,0:T(8,128)(2,1)S(1)} collective-permute-done((bf16[512,128]{1,0:T(8,128)(2,1)S(1)}, bf16[512,128]{1,0:T(8,128)(2,1)S(1)}, u32[]{:S(2)}, u32[]{:S(2)}) %collective-permute-start.3) | collective-permute-done | bytes 131104 | tf_op jit(solution)/shard_map/ppermute | solution.py:377
  52.6 1.3 collective-permute-start.14
  53.8 1.4 collective-permute-start.15
  55.3 1.0 collective-permute-start.8
  56.3 1.5 %collective-permute-start.9 = (bf16[512,128]{1,0:T(8,128)(2,1)S(1)}, bf16[512,128]{1,0:T(8,128)(2,1)S(1)}, u32[]{:S(2)}, u32[]{:S(2)}) collective-permute-start(bf16[512,128]{1,0:T(8,128)(2,1)S(1)} %get-tuple-element.64.odd_ref.refs_0_), channel_id=1, source_target_pairs={{0,24},{2,26},{4,28},{6,30},{8,0},{10,2},{12,4},{14,6},{16,8},{18,... | collective-permute-start | bytes 393224 | tf_op jit(solution)/shard_map/ppermute | solution.py:377
  57.8 2.4 %collective-permute-done.8.refs_2_ = bf16[512,128]{1,0:T(8,128)(2,1)S(1)} collective-permute-done((bf16[512,128]{1,0:T(8,128)(2,1)S(1)}, bf16[512,128]{1,0:T(8,128)(2,1)S(1)}, u32[]{:S(2)}, u32[]{:S(2)}) %collective-permute-start.8) | collective-permute-done | bytes 131104 | tf_op jit(solution)/shard_map/ppermute | solution.py:377
  60.2 4.8 %collective-permute-done.9.refs_3_ = bf16[512,128]{1,0:T(8,128)(2,1)S(1)} collective-permute-done((bf16[512,128]{1,0:T(8,128)(2,1)S(1)}, bf16[512,128]{1,0:T(8,128)(2,1)S(1)}, u32[]{:S(2)}, u32[]{:S(2)}) %collective-permute-start.9) | collective-permute-done | bytes 131104 | tf_op jit(solution)/shard_map/ppermute | solution.py:377
  66.9 1.8 %collective-permute-start.16 = (bf16[320,2176]{1,0:T(8,128)(2,1)S(1)}, bf16[320,2176]{1,0:T(8,128)(2,1)S(1)}, u32[]{:S(2)}, u32[]{:S(2)}) collective-permute-start(bf16[320,2176]{1,0:T(8,128)(2,1)S(1)} %shard_map.114.lhs_ref.refs_0_), channel_id=1, source_target_pairs={{0,2},{2,0},{4,6},{6,4},{8,10},{10,8},{12,14},{14,12},{16,18},{18,... | collective-permute-start | bytes 4177928 | tf_op jit(solution)/shard_map/ppermute | solution.py:374
  69.2 1.2 collective-permute-start.11
  70.4 1.1 collective-permute-start.12
  71.5 2.2 %copy-done.1 = bf16[1,4096,512]{2,1,0:T(8,128)(2,1)S(1)} copy-done((bf16[1,4096,512]{2,1,0:T(8,128)(2,1)S(1)}, bf16[1,4096,512]{2,1,0:T(8,128)(2,1)}, u32[]{:S(2)}) %copy-start.1) | copy-done | bytes 4194328
  73.6 2.1 %shard_map.115 = (f32[320,512]{1,0:T(8,128)S(1)}, f32[320,512]{1,0:T(8,128)S(1)}) custom-call(s32[2]{0:T(128)S(1)} %pad_add_fusion.idx_ref, bf16[4096,512]{1,0:T(8,128)(2,1)S(1)} %bitcast.8, bf16[4096,512]{1,0:T(8,128)(2,1)S(1)} %bitcast.12, bf16[320,2176]{1,0:T(8,128)(2,1)S(1)} %shard_map.114.lhs_ref.refs_0_), custom_call_target="tpu_custom_call" | custom-call | tf_op jit(solution)/shard_map/pallas_call | solution.py:30
  75.7 2.1 %shard_map.116.refs_7_.own_ref = bf16[320,512]{1,0:T(8,128)(2,1)S(1)} custom-call(s32[2]{0:T(128)S(1)} %pad_add_fusion.idx_ref, bf16[4096,512]{1,0:T(8,128)(2,1)S(1)} %bitcast.9, bf16[4096,512]{1,0:T(8,128)(2,1)S(1)} %bitcast.13, f32[320,512]{1,0:T(8,128)S(1)} %get-tuple-element.73.gate_ref, f32[320,512]{1,0:T(8,128)S(1)} %get-tuple-element.74.up_ref, ...), custom_call_target="tpu_custom_call" | custom-call | tf_op jit(solution)/shard_map/pallas_call | solution.py:30
  77.9 4.6 %collective-permute-done.12.refs_3_ = bf16[3,320,128]{2,1,0:T(8,128)(2,1)S(1)} collective-permute-done((bf16[3,320,128]{2,1,0:T(8,128)(2,1)S(1)}, bf16[3,320,128]{2,1,0:T(8,128)(2,1)S(1)}, u32[]{:S(2)}, u32[]{:S(2)}) %collective-permute-start.12) | collective-permute-done | bytes 245792 | tf_op jit(solution)/shard_map/ppermute | solution.py:384
  83.5 1.2 collective-permute-start.17
  84.7 1.2 collective-permute-start.20
  85.9 2.1 %shard_map.118 = (f32[320,512]{1,0:T(8,128)S(1)}, f32[320,512]{1,0:T(8,128)S(1)}) custom-call(s32[2]{0:T(128)S(1)} %pad_add_fusion.idx_ref, bf16[4096,512]{1,0:T(8,128)(2,1)S(1)} %bitcast.10, bf16[4096,512]{1,0:T(8,128)(2,1)S(1)} %bitcast.14, bf16[320,2176]{1,0:T(8,128)(2,1)S(1)} %shard_map.117.lhs_ref.refs_0_), custom_call_target="tpu_custom_call" | custom-call | tf_op jit(solution)/shard_map/pallas_call | solution.py:30
  88.0 2.1 %shard_map.119.refs_2_.refs_0_.own_ref = bf16[320,512]{1,0:T(8,128)(2,1)S(1)} custom-call(s32[2]{0:T(128)S(1)} %pad_add_fusion.idx_ref, bf16[4096,512]{1,0:T(8,128)(2,1)S(1)} %bitcast.11, bf16[4096,512]{1,0:T(8,128)(2,1)S(1)} %bitcast.15, f32[320,512]{1,0:T(8,128)S(1)} %get-tuple-element.75.gate_ref, f32[320,512]{1,0:T(8,128)S(1)} %get-tuple-element.76.up_ref, ...), custom_call_target="tpu_custom_call" | custom-call | tf_op jit(solution)/shard_map/pallas_call | solution.py:30
  90.9 3.1 %collective-permute-done.20.peer_ref = bf16[320,512]{1,0:T(8,128)(2,1)S(1)} collective-permute-done((bf16[320,512]{1,0:T(8,128)(2,1)S(1)}, bf16[320,512]{1,0:T(8,128)(2,1)S(1)}, u32[]{:S(2)}, u32[]{:S(2)}) %collective-permute-start.20) | collective-permute-done | bytes 327712 | tf_op jit(solution)/shard_map/ppermute | solution.py:380
  94.0 1.4 shard_map.123
  95.4 1.4 collective-permute-start.21
  97.4 1.4 shard_map.122
  98.8 2.2 %collective-permute-done.25.refs_8_.peer_ref = bf16[320,512]{1,0:T(8,128)(2,1)S(1)} collective-permute-done((bf16[320,512]{1,0:T(8,128)(2,1)S(1)}, bf16[320,512]{1,0:T(8,128)(2,1)S(1)}, u32[]{:S(2)}, u32[]{:S(2)}) %collective-permute-start.25) | collective-permute-done | bytes 327712 | tf_op jit(solution)/shard_map/ppermute | solution.py:380
  102.1 1.4 shard_map.129
  103.5 1.2 collective-permute-start.31
  106.3 1.4 shard_map.128
  107.7 2.4 %collective-permute-done.26.got_ref = bf16[160,1024]{1,0:T(8,128)(2,1)S(1)} collective-permute-done((bf16[160,1024]{1,0:T(8,128)(2,1)S(1)}, bf16[160,1024]{1,0:T(8,128)(2,1)S(1)}, u32[]{:S(2)}, u32[]{:S(2)}) %collective-permute-start.26) | collective-permute-done | bytes 327712 | tf_op jit(solution)/shard_map/ppermute | solution.py:374
  114.0 1.6 %collective-permute-start.28 = (bf16[64,1024]{1,0:T(8,128)(2,1)S(1)}, bf16[64,1024]{1,0:T(8,128)(2,1)S(1)}, u32[]{:S(2)}, u32[]{:S(2)}) collective-permute-start(bf16[64,1024]{1,0:T(8,128)(2,1)S(1)} %get-tuple-element.90), channel_id=1, source_target_pairs={{0,16},{2,18},{4,20},{6,22},{8,24},{10,26},{12,28},{14,30},{16,0},... | collective-permute-start | bytes 393224 | tf_op jit(solution)/shard_map/ppermute | solution.py:377
  115.6 1.5 %collective-permute-start.29 = (bf16[64,1024]{1,0:T(8,128)(2,1)S(1)}, bf16[64,1024]{1,0:T(8,128)(2,1)S(1)}, u32[]{:S(2)}, u32[]{:S(2)}) collective-permute-start(bf16[64,1024]{1,0:T(8,128)(2,1)S(1)} %get-tuple-element.91), channel_id=1, source_target_pairs={{0,24},{2,26},{4,28},{6,30},{8,0},{10,2},{12,4},{14,6},{16,8},{18,... | collective-permute-start | bytes 393224 | tf_op jit(solution)/shard_map/ppermute | solution.py:377
  117.1 2.2 %collective-permute-done.35.got_ref = bf16[160,1024]{1,0:T(8,128)(2,1)S(1)} collective-permute-done((bf16[160,1024]{1,0:T(8,128)(2,1)S(1)}, bf16[160,1024]{1,0:T(8,128)(2,1)S(1)}, u32[]{:S(2)}, u32[]{:S(2)}) %collective-permute-start.35) | collective-permute-done | bytes 327712 | tf_op jit(solution)/shard_map/ppermute | solution.py:374
  120.2 1.1 collective-permute-start.36
  121.4 1.1 collective-permute-start.37
  122.5 1.4 collective-permute-start.38
  124.6 7.4 %collective-permute-done.29.refs_2_ = bf16[64,1024]{1,0:T(8,128)(2,1)S(1)} collective-permute-done((bf16[64,1024]{1,0:T(8,128)(2,1)S(1)}, bf16[64,1024]{1,0:T(8,128)(2,1)S(1)}, u32[]{:S(2)}, u32[]{:S(2)}) %collective-permute-start.29) | collective-permute-done | bytes 131104 | tf_op jit(solution)/shard_map/ppermute | solution.py:377
  132.1 4.7 %collective-permute-start.30 = (f32[64,1024]{1,0:T(8,128)S(1)}, f32[64,1024]{1,0:T(8,128)S(1)}, u32[]{:S(2)}, u32[]{:S(2)}) collective-permute-start(f32[64,1024]{1,0:T(8,128)S(1)} %shard_map.127.refs_2_), channel_id=1, source_target_pairs={{2,0},{6,4},{10,8},{14,12},{18,16},{22,20},{26,24},{30,28},{3,1},{... | collective-permute-start | bytes 786440 | tf_op jit(solution)/shard_map/ppermute | solution.py:387
  137.7 1.3 collective-permute-start.39
  139.6 1.2 collective-permute-start.19
  141.8 1.4 shard_map.134
  (78 shorter events, 19.1 us)
Async XLA Ops:
  3.0 6.6 %copy-start.4 = (bf16[2048]{0:T(1024)(128)(2,1)S(1)}, bf16[2048]{0:T(1024)(128)(2,1)}, u32[]{:S(2)}) copy-start(bf16[2048]{0:T(1024)(128)(2,1)} %param.15) | copy-start | bytes 12292
  3.1 32.9 %all-to-all-start = ((bf16[16,272,128]{2,1,0:T(8,128)(2,1)}), bf16[16,272,128]{2,1,0:T(8,128)(2,1)S(1)}, u32[]{:S(2)}, u32[]{:S(2)}) async-start(bf16[16,272,128]{2,1,0:T(8,128)(2,1)} %shard_map.109), calls=%async_computation | async-start | bytes 2228224 | tf_op jit(solution)/shard_map/all_to_all | solution.py:398
  9.6 2.8 %collective-permute-start = (bf16[2048]{0:T(1024)(128)(2,1)S(1)}, bf16[2048]{0:T(1024)(128)(2,1)S(1)}, u32[]{:S(2)}, u32[]{:S(2)}) collective-permute-start(bf16[2048]{0:T(1024)(128)(2,1)S(1)} %copy-done.4), channel_id=1, source_target_pairs={{0,1},{1,0},{2,3},{3,2},{4,5},{5,4},{6,7},{7,6},{8,9},{9,8},{10,11... | collective-permute-start | bytes 12296 | tf_op jit(solution)/shard_map/ppermute | solution.py:380
  38.0 4.9 %collective-permute-start.1 = (bf16[512,128]{1,0:T(8,128)(2,1)S(1)}, bf16[512,128]{1,0:T(8,128)(2,1)S(1)}, u32[]{:S(2)}, u32[]{:S(2)}) collective-permute-start(bf16[512,128]{1,0:T(8,128)(2,1)S(1)} %get-tuple-element.57.even_ref.refs_0_), channel_id=1, source_target_pairs={{0,8},{2,10},{4,12},{6,14},{8,16},{10,18},{12,20},{14,22},{16,24},... | collective-permute-start | bytes 393224 | tf_op jit(solution)/shard_map/ppermute | solution.py:377
  38.0 9.8 %collective-permute-start.2 = (bf16[512,128]{1,0:T(8,128)(2,1)S(1)}, bf16[512,128]{1,0:T(8,128)(2,1)S(1)}, u32[]{:S(2)}, u32[]{:S(2)}) collective-permute-start(bf16[512,128]{1,0:T(8,128)(2,1)S(1)} %get-tuple-element.57.even_ref.refs_0_), channel_id=1, source_target_pairs={{0,16},{2,18},{4,20},{6,22},{8,24},{10,26},{12,28},{14,30},{16,0},... | collective-permute-start | bytes 393224 | tf_op jit(solution)/shard_map/ppermute | solution.py:377
  39.5 12.0 %collective-permute-start.5 = (bf16[2,320,128]{2,1,0:T(8,128)(2,1)S(1)}, bf16[2,320,128]{2,1,0:T(8,128)(2,1)S(1)}, u32[]{:S(2)}, u32[]{:S(2)}) collective-permute-start(bf16[2,320,128]{2,1,0:T(8,128)(2,1)S(1)} %get-tuple-element.62), channel_id=1, source_target_pairs={{0,5},{1,4},{2,7},{3,6},{4,1},{5,0},{6,3},{7,2},{8,13},{9,12},{10,... | collective-permute-start | bytes 491528 | tf_op jit(solution)/shard_map/ppermute | solution.py:384
  40.5 11.0 %collective-permute-start.6 = (bf16[2,320,128]{2,1,0:T(8,128)(2,1)S(1)}, bf16[2,320,128]{2,1,0:T(8,128)(2,1)S(1)}, u32[]{:S(2)}, u32[]{:S(2)}) collective-permute-start(bf16[2,320,128]{2,1,0:T(8,128)(2,1)S(1)} %get-tuple-element.62), channel_id=1, source_target_pairs={{0,4},{2,6},{4,0},{6,2},{8,12},{10,14},{12,8},{14,10},{16,20},{18,... | collective-permute-start | bytes 491528 | tf_op jit(solution)/shard_map/ppermute | solution.py:374
  41.9 9.6 %collective-permute-start.4 = (bf16[2,320,128]{2,1,0:T(8,128)(2,1)S(1)}, bf16[2,320,128]{2,1,0:T(8,128)(2,1)S(1)}, u32[]{:S(2)}, u32[]{:S(2)}) collective-permute-start(bf16[2,320,128]{2,1,0:T(8,128)(2,1)S(1)} %get-tuple-element.61), channel_id=1, source_target_pairs={{0,1},{1,0},{2,3},{3,2},{4,5},{5,4},{6,7},{7,6},{8,9},{9,8},{10,11... | collective-permute-start | bytes 491528 | tf_op jit(solution)/shard_map/ppermute | solution.py:380
  42.9 8.6 %collective-permute-start.3 = (bf16[512,128]{1,0:T(8,128)(2,1)S(1)}, bf16[512,128]{1,0:T(8,128)(2,1)S(1)}, u32[]{:S(2)}, u32[]{:S(2)}) collective-permute-start(bf16[512,128]{1,0:T(8,128)(2,1)S(1)} %get-tuple-element.57.even_ref.refs_0_), channel_id=1, source_target_pairs={{0,24},{2,26},{4,28},{6,30},{8,0},{10,2},{12,4},{14,6},{16,8},{18,... | collective-permute-start | bytes 393224 | tf_op jit(solution)/shard_map/ppermute | solution.py:377
  47.8 8.5 %collective-permute-start.7 = (bf16[512,128]{1,0:T(8,128)(2,1)S(1)}, bf16[512,128]{1,0:T(8,128)(2,1)S(1)}, u32[]{:S(2)}, u32[]{:S(2)}) collective-permute-start(bf16[512,128]{1,0:T(8,128)(2,1)S(1)} %get-tuple-element.64.odd_ref.refs_0_), channel_id=1, source_target_pairs={{0,8},{2,10},{4,12},{6,14},{8,16},{10,18},{12,20},{14,22},{16,24},... | collective-permute-start | bytes 393224 | tf_op jit(solution)/shard_map/ppermute | solution.py:377
  52.5 13.4 %collective-permute-start.13 = (bf16[3,320,128]{2,1,0:T(8,128)(2,1)S(1)}, bf16[3,320,128]{2,1,0:T(8,128)(2,1)S(1)}, u32[]{:S(2)}, u32[]{:S(2)}) collective-permute-start(bf16[3,320,128]{2,1,0:T(8,128)(2,1)S(1)} %slice.16), channel_id=1, source_target_pairs={{0,4},{2,6},{4,0},{6,2},{8,12},{10,14},{12,8},{14,10},{16,20},{18,... | collective-permute-start | bytes 737288 | tf_op jit(solution)/shard_map/ppermute | solution.py:374
  52.6 13.3 %collective-permute-start.14 = (bf16[3,320,128]{2,1,0:T(8,128)(2,1)S(1)}, bf16[3,320,128]{2,1,0:T(8,128)(2,1)S(1)}, u32[]{:S(2)}, u32[]{:S(2)}) collective-permute-start(bf16[3,320,128]{2,1,0:T(8,128)(2,1)S(1)} %slice.17), channel_id=1, source_target_pairs={{0,1},{1,0},{2,3},{3,2},{4,5},{5,4},{6,7},{7,6},{8,9},{9,8},{10,11... | collective-permute-start | bytes 737288 | tf_op jit(solution)/shard_map/ppermute | solution.py:380
  53.8 12.0 %collective-permute-start.15 = (bf16[3,320,128]{2,1,0:T(8,128)(2,1)S(1)}, bf16[3,320,128]{2,1,0:T(8,128)(2,1)S(1)}, u32[]{:S(2)}, u32[]{:S(2)}) collective-permute-start(bf16[3,320,128]{2,1,0:T(8,128)(2,1)S(1)} %slice.16), channel_id=1, source_target_pairs={{0,5},{1,4},{2,7},{3,6},{4,1},{5,0},{6,3},{7,2},{8,13},{9,12},{10,... | collective-permute-start | bytes 737288 | tf_op jit(solution)/shard_map/ppermute | solution.py:384
  55.3 4.9 %collective-permute-start.8 = (bf16[512,128]{1,0:T(8,128)(2,1)S(1)}, bf16[512,128]{1,0:T(8,128)(2,1)S(1)}, u32[]{:S(2)}, u32[]{:S(2)}) collective-permute-start(bf16[512,128]{1,0:T(8,128)(2,1)S(1)} %get-tuple-element.64.odd_ref.refs_0_), channel_id=1, source_target_pairs={{0,16},{2,18},{4,20},{6,22},{8,24},{10,26},{12,28},{14,30},{16,0},... | collective-permute-start | bytes 393224 | tf_op jit(solution)/shard_map/ppermute | solution.py:377
  56.3 8.6 %collective-permute-start.9 = (bf16[512,128]{1,0:T(8,128)(2,1)S(1)}, bf16[512,128]{1,0:T(8,128)(2,1)S(1)}, u32[]{:S(2)}, u32[]{:S(2)}) collective-permute-start(bf16[512,128]{1,0:T(8,128)(2,1)S(1)} %get-tuple-element.64.odd_ref.refs_0_), channel_id=1, source_target_pairs={{0,24},{2,26},{4,28},{6,30},{8,0},{10,2},{12,4},{14,6},{16,8},{18,... | collective-permute-start | bytes 393224 | tf_op jit(solution)/shard_map/ppermute | solution.py:377
  65.9 5.6 %copy-start = (bf16[1,4096,512]{2,1,0:T(8,128)(2,1)S(1)}, bf16[1,4096,512]{2,1,0:T(8,128)(2,1)}, u32[]{:S(2)}) copy-start(bf16[1,4096,512]{2,1,0:T(8,128)(2,1)} %param.19) | copy-start | bytes 12582916
  66.9 8.8 %collective-permute-start.16 = (bf16[320,2176]{1,0:T(8,128)(2,1)S(1)}, bf16[320,2176]{1,0:T(8,128)(2,1)S(1)}, u32[]{:S(2)}, u32[]{:S(2)}) collective-permute-start(bf16[320,2176]{1,0:T(8,128)(2,1)S(1)} %shard_map.114.lhs_ref.refs_0_), channel_id=1, source_target_pairs={{0,2},{2,0},{4,6},{6,4},{8,10},{10,8},{12,14},{14,12},{16,18},{18,... | collective-permute-start | bytes 4177928 | tf_op jit(solution)/shard_map/ppermute | solution.py:374
  68.7 9.1 %collective-permute-start.10 = (bf16[3,320,128]{2,1,0:T(8,128)(2,1)S(1)}, bf16[3,320,128]{2,1,0:T(8,128)(2,1)S(1)}, u32[]{:S(2)}, u32[]{:S(2)}) collective-permute-start(bf16[3,320,128]{2,1,0:T(8,128)(2,1)S(1)} %slice.14), channel_id=1, source_target_pairs={{0,4},{2,6},{4,0},{6,2},{8,12},{10,14},{12,8},{14,10},{16,20},{18,... | collective-permute-start | bytes 737288 | tf_op jit(solution)/shard_map/ppermute | solution.py:374
  69.2 8.7 %collective-permute-start.11 = (bf16[3,320,128]{2,1,0:T(8,128)(2,1)S(1)}, bf16[3,320,128]{2,1,0:T(8,128)(2,1)S(1)}, u32[]{:S(2)}, u32[]{:S(2)}) collective-permute-start(bf16[3,320,128]{2,1,0:T(8,128)(2,1)S(1)} %slice.15), channel_id=1, source_target_pairs={{0,1},{1,0},{2,3},{3,2},{4,5},{5,4},{6,7},{7,6},{8,9},{9,8},{10,11... | collective-permute-start | bytes 737288 | tf_op jit(solution)/shard_map/ppermute | solution.py:380
  70.4 12.1 %collective-permute-start.12 = (bf16[3,320,128]{2,1,0:T(8,128)(2,1)S(1)}, bf16[3,320,128]{2,1,0:T(8,128)(2,1)S(1)}, u32[]{:S(2)}, u32[]{:S(2)}) collective-permute-start(bf16[3,320,128]{2,1,0:T(8,128)(2,1)S(1)} %slice.14), channel_id=1, source_target_pairs={{0,5},{1,4},{2,7},{3,6},{4,1},{5,0},{6,3},{7,2},{8,13},{9,12},{10,... | collective-permute-start | bytes 737288 | tf_op jit(solution)/shard_map/ppermute | solution.py:384
  71.5 2.2 %copy-start.1 = (bf16[1,4096,512]{2,1,0:T(8,128)(2,1)S(1)}, bf16[1,4096,512]{2,1,0:T(8,128)(2,1)}, u32[]{:S(2)}) copy-start(bf16[1,4096,512]{2,1,0:T(8,128)(2,1)} %param.20) | copy-start | bytes 12582916
  75.7 10.2 %copy-start.2 = (bf16[1,4096,512]{2,1,0:T(8,128)(2,1)S(1)}, bf16[1,4096,512]{2,1,0:T(8,128)(2,1)}, u32[]{:S(2)}) copy-start(bf16[1,4096,512]{2,1,0:T(8,128)(2,1)} %param.20) | copy-start | bytes 12582916
  83.5 4.5 %collective-permute-start.17 = (bf16[320,2176]{1,0:T(8,128)(2,1)S(1)}, bf16[320,2176]{1,0:T(8,128)(2,1)S(1)}, u32[]{:S(2)}, u32[]{:S(2)}) collective-permute-start(bf16[320,2176]{1,0:T(8,128)(2,1)S(1)} %shard_map.117.lhs_ref.refs_0_), channel_id=1, source_target_pairs={{0,2},{2,0},{4,6},{6,4},{8,10},{10,8},{12,14},{14,12},{16,18},{18,... | collective-permute-start | bytes 4177928 | tf_op jit(solution)/shard_map/ppermute | solution.py:374
  84.7 9.3 %collective-permute-start.20 = (bf16[320,512]{1,0:T(8,128)(2,1)S(1)}, bf16[320,512]{1,0:T(8,128)(2,1)S(1)}, u32[]{:S(2)}, u32[]{:S(2)}) collective-permute-start(bf16[320,512]{1,0:T(8,128)(2,1)S(1)} %shard_map.116.refs_7_.own_ref), channel_id=1, source_target_pairs={{0,1},{1,0},{2,3},{3,2},{4,5},{5,4},{6,7},{7,6},{8,9},{9,8},{10,11... | collective-permute-start | bytes 983048 | tf_op jit(solution)/shard_map/ppermute | solution.py:380
  88.0 6.0 %copy-start.3 = (bf16[1,1024,2048]{2,1,0:T(8,128)(2,1)S(1)}, bf16[1,1024,2048]{2,1,0:T(8,128)(2,1)}, u32[]{:S(2)}) copy-start(bf16[1,1024,2048]{2,1,0:T(8,128)(2,1)} %param.21) | copy-start | bytes 12582916
  90.2 10.9 %collective-permute-start.25 = (bf16[320,512]{1,0:T(8,128)(2,1)S(1)}, bf16[320,512]{1,0:T(8,128)(2,1)S(1)}, u32[]{:S(2)}, u32[]{:S(2)}) collective-permute-start(bf16[320,512]{1,0:T(8,128)(2,1)S(1)} %shard_map.119.refs_2_.refs_0_.own_ref), channel_id=1, source_target_pairs={{0,1},{1,0},{2,3},{3,2},{4,5},{5,4},{6,7},{7,6},{8,9},{9,8},{10,11... | collective-permute-start | bytes 983048 | tf_op jit(solution)/shard_map/ppermute | solution.py:380
  95.4 3.4 %collective-permute-start.21 = (bf16[320,256]{1,0:T(8,128)(2,1)S(1)}, bf16[320,256]{1,0:T(8,128)(2,1)S(1)}, u32[]{:S(2)}, u32[]{:S(2)}) collective-permute-start(bf16[320,256]{1,0:T(8,128)(2,1)S(1)} %get-tuple-element.84), channel_id=1, source_target_pairs={{0,2},{2,0},{4,6},{6,4},{8,10},{10,8},{12,14},{14,12},{16,18},{18,... | collective-permute-start | bytes 491528 | tf_op jit(solution)/shard_map/ppermute | solution.py:374
  96.8 2.0 %collective-permute-start.22 = (bf16[320,256]{1,0:T(8,128)(2,1)S(1)}, bf16[320,256]{1,0:T(8,128)(2,1)S(1)}, u32[]{:S(2)}, u32[]{:S(2)}) collective-permute-start(bf16[320,256]{1,0:T(8,128)(2,1)S(1)} %get-tuple-element.85), channel_id=1, source_target_pairs={{0,2},{2,0},{4,6},{6,4},{8,10},{10,8},{12,14},{14,12},{16,18},{18,... | collective-permute-start | bytes 491528 | tf_op jit(solution)/shard_map/ppermute | solution.py:374
  96.9 2.0 %collective-permute-start.23 = (bf16[320,256]{1,0:T(8,128)(2,1)S(1)}, bf16[320,256]{1,0:T(8,128)(2,1)S(1)}, u32[]{:S(2)}, u32[]{:S(2)}) collective-permute-start(bf16[320,256]{1,0:T(8,128)(2,1)S(1)} %get-tuple-element.86), channel_id=1, source_target_pairs={{0,2},{2,0},{4,6},{6,4},{8,10},{10,8},{12,14},{14,12},{16,18},{18,... | collective-permute-start | bytes 491528 | tf_op jit(solution)/shard_map/ppermute | solution.py:374
  97.3 1.5 %collective-permute-start.24 = (bf16[320,256]{1,0:T(8,128)(2,1)S(1)}, bf16[320,256]{1,0:T(8,128)(2,1)S(1)}, u32[]{:S(2)}, u32[]{:S(2)}) collective-permute-start(bf16[320,256]{1,0:T(8,128)(2,1)S(1)} %get-tuple-element.87), channel_id=1, source_target_pairs={{0,2},{2,0},{4,6},{6,4},{8,10},{10,8},{12,14},{14,12},{16,18},{18,... | collective-permute-start | bytes 491528 | tf_op jit(solution)/shard_map/ppermute | solution.py:374
  101.7 8.4 %collective-permute-start.26 = (bf16[160,1024]{1,0:T(8,128)(2,1)S(1)}, bf16[160,1024]{1,0:T(8,128)(2,1)S(1)}, u32[]{:S(2)}, u32[]{:S(2)}) collective-permute-start(bf16[160,1024]{1,0:T(8,128)(2,1)S(1)} %shard_map.125.refs_0_), channel_id=1, source_target_pairs={{0,4},{2,6},{4,0},{6,2},{8,12},{10,14},{12,8},{14,10},{16,20},{18,... | collective-permute-start | bytes 983048 | tf_op jit(solution)/shard_map/ppermute | solution.py:374
  103.5 7.6 %collective-permute-start.31 = (bf16[320,256]{1,0:T(8,128)(2,1)S(1)}, bf16[320,256]{1,0:T(8,128)(2,1)S(1)}, u32[]{:S(2)}, u32[]{:S(2)}) collective-permute-start(bf16[320,256]{1,0:T(8,128)(2,1)S(1)} %get-tuple-element.97), channel_id=1, source_target_pairs={{0,2},{2,0},{4,6},{6,4},{8,10},{10,8},{12,14},{14,12},{16,18},{18,... | collective-permute-start | bytes 491528 | tf_op jit(solution)/shard_map/ppermute | solution.py:374
  104.7 6.4 %collective-permute-start.32 = (bf16[320,256]{1,0:T(8,128)(2,1)S(1)}, bf16[320,256]{1,0:T(8,128)(2,1)S(1)}, u32[]{:S(2)}, u32[]{:S(2)}) collective-permute-start(bf16[320,256]{1,0:T(8,128)(2,1)S(1)} %get-tuple-element.98), channel_id=1, source_target_pairs={{0,2},{2,0},{4,6},{6,4},{8,10},{10,8},{12,14},{14,12},{16,18},{18,... | collective-permute-start | bytes 491528 | tf_op jit(solution)/shard_map/ppermute | solution.py:374
  104.8 6.3 %collective-permute-start.33 = (bf16[320,256]{1,0:T(8,128)(2,1)S(1)}, bf16[320,256]{1,0:T(8,128)(2,1)S(1)}, u32[]{:S(2)}, u32[]{:S(2)}) collective-permute-start(bf16[320,256]{1,0:T(8,128)(2,1)S(1)} %get-tuple-element.99), channel_id=1, source_target_pairs={{0,2},{2,0},{4,6},{6,4},{8,10},{10,8},{12,14},{14,12},{16,18},{18,... | collective-permute-start | bytes 491528 | tf_op jit(solution)/shard_map/ppermute | solution.py:374
  105.2 5.9 %collective-permute-start.34 = (bf16[320,256]{1,0:T(8,128)(2,1)S(1)}, bf16[320,256]{1,0:T(8,128)(2,1)S(1)}, u32[]{:S(2)}, u32[]{:S(2)}) collective-permute-start(bf16[320,256]{1,0:T(8,128)(2,1)S(1)} %get-tuple-element.100), channel_id=1, source_target_pairs={{0,2},{2,0},{4,6},{6,4},{8,10},{10,8},{12,14},{14,12},{16,18},{18,... | collective-permute-start | bytes 491528 | tf_op jit(solution)/shard_map/ppermute | solution.py:374
  111.8 7.5 %collective-permute-start.35 = (bf16[160,1024]{1,0:T(8,128)(2,1)S(1)}, bf16[160,1024]{1,0:T(8,128)(2,1)S(1)}, u32[]{:S(2)}, u32[]{:S(2)}) collective-permute-start(bf16[160,1024]{1,0:T(8,128)(2,1)S(1)} %shard_map.131), channel_id=1, source_target_pairs={{0,4},{2,6},{4,0},{6,2},{8,12},{10,14},{12,8},{14,10},{16,20},{18,... | collective-permute-start | bytes 983048 | tf_op jit(solution)/shard_map/ppermute | solution.py:374
  112.2 10.3 %collective-permute-start.27 = (bf16[64,1024]{1,0:T(8,128)(2,1)S(1)}, bf16[64,1024]{1,0:T(8,128)(2,1)S(1)}, u32[]{:S(2)}, u32[]{:S(2)}) collective-permute-start(bf16[64,1024]{1,0:T(8,128)(2,1)S(1)} %get-tuple-element.89), channel_id=1, source_target_pairs={{0,8},{2,10},{4,12},{6,14},{8,16},{10,18},{12,20},{14,22},{16,24},... | collective-permute-start | bytes 393224 | tf_op jit(solution)/shard_map/ppermute | solution.py:377
  114.0 10.0 %collective-permute-start.28 = (bf16[64,1024]{1,0:T(8,128)(2,1)S(1)}, bf16[64,1024]{1,0:T(8,128)(2,1)S(1)}, u32[]{:S(2)}, u32[]{:S(2)}) collective-permute-start(bf16[64,1024]{1,0:T(8,128)(2,1)S(1)} %get-tuple-element.90), channel_id=1, source_target_pairs={{0,16},{2,18},{4,20},{6,22},{8,24},{10,26},{12,28},{14,30},{16,0},... | collective-permute-start | bytes 393224 | tf_op jit(solution)/shard_map/ppermute | solution.py:377
  115.6 16.4 %collective-permute-start.29 = (bf16[64,1024]{1,0:T(8,128)(2,1)S(1)}, bf16[64,1024]{1,0:T(8,128)(2,1)S(1)}, u32[]{:S(2)}, u32[]{:S(2)}) collective-permute-start(bf16[64,1024]{1,0:T(8,128)(2,1)S(1)} %get-tuple-element.91), channel_id=1, source_target_pairs={{0,24},{2,26},{4,28},{6,30},{8,0},{10,2},{12,4},{14,6},{16,8},{18,... | collective-permute-start | bytes 393224 | tf_op jit(solution)/shard_map/ppermute | solution.py:377
  120.2 16.6 %collective-permute-start.36 = (bf16[64,1024]{1,0:T(8,128)(2,1)S(1)}, bf16[64,1024]{1,0:T(8,128)(2,1)S(1)}, u32[]{:S(2)}, u32[]{:S(2)}) collective-permute-start(bf16[64,1024]{1,0:T(8,128)(2,1)S(1)} %get-tuple-element.102), channel_id=1, source_target_pairs={{0,8},{2,10},{4,12},{6,14},{8,16},{10,18},{12,20},{14,22},{16,24},... | collective-permute-start | bytes 393224 | tf_op jit(solution)/shard_map/ppermute | solution.py:377
  121.4 15.4 %collective-permute-start.37 = (bf16[64,1024]{1,0:T(8,128)(2,1)S(1)}, bf16[64,1024]{1,0:T(8,128)(2,1)S(1)}, u32[]{:S(2)}, u32[]{:S(2)}) collective-permute-start(bf16[64,1024]{1,0:T(8,128)(2,1)S(1)} %get-tuple-element.103), channel_id=1, source_target_pairs={{0,16},{2,18},{4,20},{6,22},{8,24},{10,26},{12,28},{14,30},{16,0},... | collective-permute-start | bytes 393224 | tf_op jit(solution)/shard_map/ppermute | solution.py:377
  122.5 15.2 %collective-permute-start.38 = (bf16[64,1024]{1,0:T(8,128)(2,1)S(1)}, bf16[64,1024]{1,0:T(8,128)(2,1)S(1)}, u32[]{:S(2)}, u32[]{:S(2)}) collective-permute-start(bf16[64,1024]{1,0:T(8,128)(2,1)S(1)} %get-tuple-element.104), channel_id=1, source_target_pairs={{0,24},{2,26},{4,28},{6,30},{8,0},{10,2},{12,4},{14,6},{16,8},{18,... | collective-permute-start | bytes 393224 | tf_op jit(solution)/shard_map/ppermute | solution.py:377
  124.0 15.0 %collective-permute-start.18 = (bf16[2,4,64,128]{3,2,1,0:T(8,128)(2,1)S(1)}, bf16[2,4,64,128]{3,2,1,0:T(8,128)(2,1)S(1)}, u32[]{:S(2)}, u32[]{:S(2)}) collective-permute-start(bf16[2,4,64,128]{3,2,1,0:T(8,128)(2,1)S(1)} %shard_map.120), channel_id=1, source_target_pairs={{0,4},{2,6},{4,0},{6,2},{8,12},{10,14},{12,8},{14,10},{16,20},{18,... | collective-permute-start | bytes 393224 | tf_op jit(solution)/shard_map/ppermute | solution.py:374
  132.1 9.7 %collective-permute-start.30 = (f32[64,1024]{1,0:T(8,128)S(1)}, f32[64,1024]{1,0:T(8,128)S(1)}, u32[]{:S(2)}, u32[]{:S(2)}) collective-permute-start(f32[64,1024]{1,0:T(8,128)S(1)} %shard_map.127.refs_2_), channel_id=1, source_target_pairs={{2,0},{6,4},{10,8},{14,12},{18,16},{22,20},{26,24},{30,28},{3,1},{... | collective-permute-start | bytes 786440 | tf_op jit(solution)/shard_map/ppermute | solution.py:387
  137.7 4.1 %collective-permute-start.39 = (f32[64,1024]{1,0:T(8,128)S(1)}, f32[64,1024]{1,0:T(8,128)S(1)}, u32[]{:S(2)}, u32[]{:S(2)}) collective-permute-start(f32[64,1024]{1,0:T(8,128)S(1)} %shard_map.133.refs_4_), channel_id=1, source_target_pairs={{0,2},{4,6},{8,10},{12,14},{16,18},{20,22},{24,26},{28,30},{1,3},{... | collective-permute-start | bytes 786440 | tf_op jit(solution)/shard_map/ppermute | solution.py:387
  139.6 2.2 %collective-permute-start.19 = (bf16[8,64,128]{2,1,0:T(8,128)(2,1)S(1)}, bf16[8,64,128]{2,1,0:T(8,128)(2,1)S(1)}, u32[]{:S(2)}, u32[]{:S(2)}) collective-permute-start(bf16[8,64,128]{2,1,0:T(8,128)(2,1)S(1)} %get-tuple-element.78), channel_id=1, source_target_pairs={{0,2},{2,0},{4,6},{6,4},{8,10},{10,8},{12,14},{14,12},{16,18},{18,... | collective-permute-start | bytes 393224 | tf_op jit(solution)/shard_map/ppermute | solution.py:374

commit v9 on v8

--- a/solution.py
+++ b/solution.py
@@ -23,10 +23,10 @@
     return v * (0.5 * jnp.tanh(0.5 * v) + 0.5)
 
 
-def call(kernel, out_shape, args, smem=0, hbm=(), scratch=(), vmem=8, flops=0, moved=0):
+def call(kernel, out_shape, args, smem=0, hbm=(), scratch=(), vmem=8, out_space=pltpu.VMEM):
     spaces = [pltpu.SMEM if n < smem else pltpu.HBM if n in hbm else pltpu.VMEM for n in range(len(args))]
     several = isinstance(out_shape, (tuple, list))
-    out = pl.BlockSpec(memory_space=pltpu.VMEM)
+    out = pl.BlockSpec(memory_space=out_space)
     return pl.pallas_call(
         kernel,
         out_shape=out_shape,
@@ -37,9 +37,10 @@
     )(*args)
 
 
-def pack_kernel(seg_ref, route_ref, gate_ref, q_ref, k_ref, v_ref, r_ref, out_ref, held_ref, sems):
+def pack_kernel(seg_ref, route_ref, gate_ref, q_ref, k_ref, v_ref, r_ref, out_ref, held_ref, meta_ref, staged_ref, sems):
     heads, tok = out_ref.shape[0], q_ref.shape[0]
-    copies = [pltpu.make_async_copy(ref, held_ref.at[n], sems.at[n]) for n, ref in enumerate((q_ref, k_ref, v_ref, r_ref))]
+    arrays = (q_ref, k_ref, v_ref, r_ref)
+    copies = [pltpu.make_async_copy(ref, held_ref.at[n], sems.at[0, n]) for n, ref in enumerate(arrays)]
     for copy in copies:
         copy.start()
     row = lax.broadcasted_iota(jnp.int32, (META, tok), 0)
@@ -51,16 +52,22 @@
         high = gate.astype(jnp.bfloat16).astype(jnp.float32)
         middle = (gate - high).astype(jnp.bfloat16).astype(jnp.float32)
         parts.append((high, middle, gate - high - middle))
-    out_ref[:, 4 * tok :, :] = jnp.zeros((heads, META, HD), jnp.bfloat16)
+    meta_ref[...] = jnp.zeros(meta_ref.shape, jnp.bfloat16)
     for h in range(heads):
         meta = jnp.where(row == 0, seg, 0.0)
         for n, piece in enumerate(parts[h // 2] + parts[h // 2 ^ 1], 1):
             meta = jnp.where(row == n, piece, meta)
-        out_ref[h, 4 * tok :, 0:tok] = meta.astype(jnp.bfloat16)
+        meta_ref[h, :, 0:tok] = meta.astype(jnp.bfloat16)
+    sent = [pltpu.make_async_copy(meta_ref, out_ref.at[:, 4 * tok :, :], sems.at[1, 4])]
+    sent[0].start()
     for n, copy in enumerate(copies):
         copy.wait()
         for h in range(heads):
-            out_ref[h, n * tok : (n + 1) * tok, :] = held_ref[n, :, h * HD : (h + 1) * HD]
+            staged_ref[n, h, :, :] = held_ref[n, :, h * HD : (h + 1) * HD]
+        sent.append(pltpu.make_async_copy(staged_ref.at[n], out_ref.at[:, n * tok : (n + 1) * tok, :], sems.at[1, n]))
+        sent[-1].start()
+    for copy in sent:
+        copy.wait()
 
 
 def attend_kernel(capacity, x_ref, even_ref, odd_ref, pick_even_ref, pick_odd_ref, gate_even_ref, gate_odd_ref):
@@ -338,21 +345,16 @@
     heads = out_ref.shape[1] // HD
     for n in range(2):
         own_ref, other_ref = sum_refs[2 * n : 2 * n + 2]
-        half = own_ref.shape[1]
 
         @pl.when(core == n)
-        def _(halves=(own_ref, other_ref) if n == 0 else (other_ref, own_ref)):
-            for flip, hand_ref in enumerate(hand_refs):
-                for low in range(2):
-                    for back in range(levels):
-                        head = lax.rem((me ^ (2 * low) ^ flip) + heads - 4 * back, heads)
-                        hand = hand_ref[low * levels + back].astype(jnp.float32)
-                        at = pl.multiple_of(head * HD, HD)
-                        inside = pl.multiple_of(lax.rem(head, heads // 2) * HD, HD)
-                        first = halves[0][:, pl.ds(inside, HD)].astype(jnp.float32)
-                        second = halves[1][:, pl.ds(inside, HD)].astype(jnp.float32)
-                        total = hand + jnp.where(head < heads // 2, first, second)
-                        out_ref[:, pl.ds(at, HD)] = total.astype(jnp.bfloat16)
+        def _(halves=(own_ref, other_ref) if n == 0 else (other_ref, own_ref), n=n):
+            for head in range(heads):
+                low = lax.rem(lax.div(me ^ head, 2), 2)
+                back = lax.rem(lax.div(me, 4) + levels - head // 4, levels)
+                hand = hand_refs[(head % 2) ^ n][low * levels + back].astype(jnp.float32)
+                first = head % (heads // 2) * HD
+                total = halves[head // (heads // 2)][:, first : first + HD].astype(jnp.float32)
+                out_ref[:, head * HD : (head + 1) * HD] = (hand + total).astype(jnp.bfloat16)
 
 
 def heads_over_ctx(
@@ -391,8 +393,10 @@
         shape(ctx, 4 * tok + META, HD),
         (segment_ids[None, :], routes.T, route_gates.T, query, key, value, resid),
         hbm=(3, 4, 5, 6),
-        scratch=[pltpu.VMEM((4, tok, width), bf16), pltpu.SemaphoreType.DMA((4,))],
+        scratch=[pltpu.VMEM((4, tok, width), bf16), pltpu.VMEM((ctx, META, HD), bf16)]
+        + [pltpu.VMEM((4, ctx, tok, HD), bf16), pltpu.SemaphoreType.DMA((2, 5))],
         vmem=60,
+        out_space=pltpu.HBM,
     )
     gain = over_tp(norm_gain)
     arrived = lax.all_to_all(packed, "ctx", split_axis=0, concat_axis=0, tiled=True)

time: 144 us -> 144 us (level)
  transfers between devices with their start and end apart: 41 -> 41, of which waited for: 16 -> 16; matrix products, arithmetic and copies ran while one was open for 0% -> 0% of each run, Pallas kernels for 14% -> 15%
where the time goes in v9:
time: 144 us; the launch traced here: 143 us
  waiting for transfers between devices  64 us (44%)
  starting transfers between devices  45.9 us (32%)
  Pallas kernels  30.2 us (21%)
  local copies, waits for them, and re-layouts  2.3 us (2%)
    pallas_call x26, Pallas kernels, call(): pl.pallas_call(kernel, out_shape=out_shape, in_specs=[pl.BlockSpec(memory...  30.2 us
    all_to_all x1, waiting for transfers between devices, heads_over_ctx(): lax.all_to_all(packed, 'ctx', split_axis=0, concat_axis=0, tiled=True)  23.5 us
    ppermute x12, waiting for transfers between devices, along_z(): lax.ppermute(x, 'ctx', [(c, (c + 4 * steps) % ctx) for c in range(ctx)])  23.4 us
    ppermute x12, starting transfers between devices, along_z(): lax.ppermute(x, 'ctx', [(c, (c + 4 * steps) % ctx) for c in range(ctx)])  12.5 us
    ppermute x17, starting transfers between devices, over_ctx(): lax.ppermute(x, 'ctx', [(c, c ^ mask) for c in range(ctx) if core is None...  11.3 us
    ppermute x6, waiting for transfers between devices, over_tp(): return lax.ppermute(x, 'tp', [(0, 1), (1, 0)])  6.84 us
    all_to_all x1, starting transfers between devices, heads_over_ctx(): lax.all_to_all(packed, 'ctx', split_axis=0, concat_axis=0, tiled=True)  6.57 us
    ppermute x2, starting transfers between devices, to_core(): lax.ppermute(x, 'ctx', [(c, c ^ 1) for c in range(ctx) if c % 2 != core])  6.03 us
  transfers between devices with their start and end apart: 41, of which 16 were waited for; matrix products, arithmetic and copies ran while one was open for 0% of the time, Pallas kernels for 15%

profile of v9, /device:TPU:13, one launch (start us, length us, event | category | flops | bytes accessed | tf_op | source)
XLA Modules:
  0.0 143.0 jit_solution(5422086075819891864)
XLA Ops:
  0.0 2.9 %shard_map.109 = bf16[16,272,128]{2,1,0:T(8,128)(2,1)} custom-call(s32[1,64]{1,0:T(1,128)} %bitcast.22, s32[4,64]{1,0:T(4,128)} %bitcast.20, f32[4,64]{1,0:T(4,128)} %bitcast.21, bf16[64,2048]{1,0:T(8,128)(2,1)} %q_ref.1, bf16[64,2048]{1,0:T(8,128)(2,1)} %k_ref.1, bf16[64,2048]{1,0:T(8,128)(2,1)} %v_ref.1, bf16[64,2048]{1,0:T(8,128)(2,1)} %r_ref.1), custom_call_target="tpu_custom_call" | custom-call | tf_op jit(solution)/shard_map/pallas_call | solution.py:30
  2.9 6.6 %all-to-all-start = ((bf16[16,272,128]{2,1,0:T(8,128)(2,1)}), bf16[16,272,128]{2,1,0:T(8,128)(2,1)S(1)}, u32[]{:S(2)}, u32[]{:S(2)}) async-start(bf16[16,272,128]{2,1,0:T(8,128)(2,1)} %shard_map.109), calls=%async_computation | async-start | bytes 2228224 | tf_op jit(solution)/shard_map/all_to_all | solution.py:402
  9.5 1.3 collective-permute-start
  10.7 1.5 %collective-permute-done = bf16[2048]{0:T(1024)(128)(2,1)S(1)} collective-permute-done((bf16[2048]{0:T(1024)(128)(2,1)S(1)}, bf16[2048]{0:T(1024)(128)(2,1)S(1)}, u32[]{:S(2)}, u32[]{:S(2)}) %collective-permute-start) | collective-permute-done | bytes 4128 | tf_op jit(solution)/shard_map/ppermute | solution.py:382
  12.3 23.5 %all-to-all-done.x_ref = bf16[16,272,128]{2,1,0:T(8,128)(2,1)S(1)} async-done(((bf16[16,272,128]{2,1,0:T(8,128)(2,1)}), bf16[16,272,128]{2,1,0:T(8,128)(2,1)S(1)}, u32[]{:S(2)}, u32[]{:S(2)}) %all-to-all-start) | async-done | bytes 1114144 | tf_op jit(solution)/shard_map/all_to_all | solution.py:402
  35.8 2.0 %shard_map.110 = (bf16[512,128]{1,0:T(8,128)(2,1)S(1)}, bf16[512,128]{1,0:T(8,128)(2,1)S(1)}, bf16[2,320,256]{2,1,0:T(8,128)(2,1)S(1)}, bf16[2,320,256]{2,1,0:T(...) custom-call(bf16[16,272,128]{2,1,0:T(8,128)(2,1)S(1)} %all-to-all-done.x_ref), custom_call_target="tpu_custom_call" | custom-call | tf_op jit(solution)/shard_map/pallas_call | solution.py:30
  37.9 1.1 collective-permute-start.2
  40.3 1.4 %collective-permute-start.6 = (bf16[2,320,128]{2,1,0:T(8,128)(2,1)S(1)}, bf16[2,320,128]{2,1,0:T(8,128)(2,1)S(1)}, u32[]{:S(2)}, u32[]{:S(2)}) collective-permute-start(bf16[2,320,128]{2,1,0:T(8,128)(2,1)S(1)} %get-tuple-element.62), channel_id=1, source_target_pairs={{0,4},{2,6},{4,0},{6,2},{8,12},{10,14},{12,8},{14,10},{16,20},{18,... | collective-permute-start | bytes 491528 | tf_op jit(solution)/shard_map/ppermute | solution.py:376
  42.7 1.1 collective-permute-start.3
  43.9 3.8 %collective-permute-done.2.refs_2_ = bf16[512,128]{1,0:T(8,128)(2,1)S(1)} collective-permute-done((bf16[512,128]{1,0:T(8,128)(2,1)S(1)}, bf16[512,128]{1,0:T(8,128)(2,1)S(1)}, u32[]{:S(2)}, u32[]{:S(2)}) %collective-permute-start.2) | collective-permute-done | bytes 131104 | tf_op jit(solution)/shard_map/ppermute | solution.py:379
  47.9 3.5 %collective-permute-done.3.refs_3_ = bf16[512,128]{1,0:T(8,128)(2,1)S(1)} collective-permute-done((bf16[512,128]{1,0:T(8,128)(2,1)S(1)}, bf16[512,128]{1,0:T(8,128)(2,1)S(1)}, u32[]{:S(2)}, u32[]{:S(2)}) %collective-permute-start.3) | collective-permute-done | bytes 131104 | tf_op jit(solution)/shard_map/ppermute | solution.py:379
  52.4 1.3 collective-permute-start.14
  53.7 1.4 collective-permute-start.15
  55.1 1.0 collective-permute-start.8
  56.2 1.5 %collective-permute-start.9 = (bf16[512,128]{1,0:T(8,128)(2,1)S(1)}, bf16[512,128]{1,0:T(8,128)(2,1)S(1)}, u32[]{:S(2)}, u32[]{:S(2)}) collective-permute-start(bf16[512,128]{1,0:T(8,128)(2,1)S(1)} %get-tuple-element.64.odd_ref.refs_0_), channel_id=1, source_target_pairs={{0,24},{2,26},{4,28},{6,30},{8,0},{10,2},{12,4},{14,6},{16,8},{18,... | collective-permute-start | bytes 393224 | tf_op jit(solution)/shard_map/ppermute | solution.py:379
  57.6 2.4 %collective-permute-done.8.refs_2_ = bf16[512,128]{1,0:T(8,128)(2,1)S(1)} collective-permute-done((bf16[512,128]{1,0:T(8,128)(2,1)S(1)}, bf16[512,128]{1,0:T(8,128)(2,1)S(1)}, u32[]{:S(2)}, u32[]{:S(2)}) %collective-permute-start.8) | collective-permute-done | bytes 131104 | tf_op jit(solution)/shard_map/ppermute | solution.py:379
  60.0 4.8 %collective-permute-done.9.refs_3_ = bf16[512,128]{1,0:T(8,128)(2,1)S(1)} collective-permute-done((bf16[512,128]{1,0:T(8,128)(2,1)S(1)}, bf16[512,128]{1,0:T(8,128)(2,1)S(1)}, u32[]{:S(2)}, u32[]{:S(2)}) %collective-permute-start.9) | collective-permute-done | bytes 131104 | tf_op jit(solution)/shard_map/ppermute | solution.py:379
  66.7 1.8 %collective-permute-start.16 = (bf16[320,2176]{1,0:T(8,128)(2,1)S(1)}, bf16[320,2176]{1,0:T(8,128)(2,1)S(1)}, u32[]{:S(2)}, u32[]{:S(2)}) collective-permute-start(bf16[320,2176]{1,0:T(8,128)(2,1)S(1)} %shard_map.114.lhs_ref.refs_0_), channel_id=1, source_target_pairs={{0,2},{2,0},{4,6},{6,4},{8,10},{10,8},{12,14},{14,12},{16,18},{18,... | collective-permute-start | bytes 4177928 | tf_op jit(solution)/shard_map/ppermute | solution.py:376
  69.0 1.2 collective-permute-start.11
  70.2 1.1 collective-permute-start.12
  71.3 2.2 %copy-done.1 = bf16[1,4096,512]{2,1,0:T(8,128)(2,1)S(1)} copy-done((bf16[1,4096,512]{2,1,0:T(8,128)(2,1)S(1)}, bf16[1,4096,512]{2,1,0:T(8,128)(2,1)}, u32[]{:S(2)}) %copy-start.1) | copy-done | bytes 4194328
  73.5 2.1 %shard_map.115 = (f32[320,512]{1,0:T(8,128)S(1)}, f32[320,512]{1,0:T(8,128)S(1)}) custom-call(s32[2]{0:T(128)S(1)} %pad_add_fusion.idx_ref, bf16[4096,512]{1,0:T(8,128)(2,1)S(1)} %bitcast.8, bf16[4096,512]{1,0:T(8,128)(2,1)S(1)} %bitcast.12, bf16[320,2176]{1,0:T(8,128)(2,1)S(1)} %shard_map.114.lhs_ref.refs_0_), custom_call_target="tpu_custom_call" | custom-call | tf_op jit(solution)/shard_map/pallas_call | solution.py:30
  75.6 2.1 %shard_map.116.refs_7_.own_ref = bf16[320,512]{1,0:T(8,128)(2,1)S(1)} custom-call(s32[2]{0:T(128)S(1)} %pad_add_fusion.idx_ref, bf16[4096,512]{1,0:T(8,128)(2,1)S(1)} %bitcast.9, bf16[4096,512]{1,0:T(8,128)(2,1)S(1)} %bitcast.13, f32[320,512]{1,0:T(8,128)S(1)} %get-tuple-element.73.gate_ref, f32[320,512]{1,0:T(8,128)S(1)} %get-tuple-element.74.up_ref, ...), custom_call_target="tpu_custom_call" | custom-call | tf_op jit(solution)/shard_map/pallas_call | solution.py:30
  77.7 4.6 %collective-permute-done.12.refs_3_ = bf16[3,320,128]{2,1,0:T(8,128)(2,1)S(1)} collective-permute-done((bf16[3,320,128]{2,1,0:T(8,128)(2,1)S(1)}, bf16[3,320,128]{2,1,0:T(8,128)(2,1)S(1)}, u32[]{:S(2)}, u32[]{:S(2)}) %collective-permute-start.12) | collective-permute-done | bytes 245792 | tf_op jit(solution)/shard_map/ppermute | solution.py:386
  83.4 1.2 collective-permute-start.17
  84.6 1.2 collective-permute-start.20
  85.8 2.1 %shard_map.118 = (f32[320,512]{1,0:T(8,128)S(1)}, f32[320,512]{1,0:T(8,128)S(1)}) custom-call(s32[2]{0:T(128)S(1)} %pad_add_fusion.idx_ref, bf16[4096,512]{1,0:T(8,128)(2,1)S(1)} %bitcast.10, bf16[4096,512]{1,0:T(8,128)(2,1)S(1)} %bitcast.14, bf16[320,2176]{1,0:T(8,128)(2,1)S(1)} %shard_map.117.lhs_ref.refs_0_), custom_call_target="tpu_custom_call" | custom-call | tf_op jit(solution)/shard_map/pallas_call | solution.py:30
  87.9 2.1 %shard_map.119.refs_2_.refs_0_.own_ref = bf16[320,512]{1,0:T(8,128)(2,1)S(1)} custom-call(s32[2]{0:T(128)S(1)} %pad_add_fusion.idx_ref, bf16[4096,512]{1,0:T(8,128)(2,1)S(1)} %bitcast.11, bf16[4096,512]{1,0:T(8,128)(2,1)S(1)} %bitcast.15, f32[320,512]{1,0:T(8,128)S(1)} %get-tuple-element.75.gate_ref, f32[320,512]{1,0:T(8,128)S(1)} %get-tuple-element.76.up_ref, ...), custom_call_target="tpu_custom_call" | custom-call | tf_op jit(solution)/shard_map/pallas_call | solution.py:30
  90.7 3.1 %collective-permute-done.20.peer_ref = bf16[320,512]{1,0:T(8,128)(2,1)S(1)} collective-permute-done((bf16[320,512]{1,0:T(8,128)(2,1)S(1)}, bf16[320,512]{1,0:T(8,128)(2,1)S(1)}, u32[]{:S(2)}, u32[]{:S(2)}) %collective-permute-start.20) | collective-permute-done | bytes 327712 | tf_op jit(solution)/shard_map/ppermute | solution.py:382
  93.8 1.4 shard_map.123
  95.3 1.4 collective-permute-start.21
  97.2 1.4 shard_map.122
  98.7 2.2 %collective-permute-done.25.refs_8_.peer_ref = bf16[320,512]{1,0:T(8,128)(2,1)S(1)} collective-permute-done((bf16[320,512]{1,0:T(8,128)(2,1)S(1)}, bf16[320,512]{1,0:T(8,128)(2,1)S(1)}, u32[]{:S(2)}, u32[]{:S(2)}) %collective-permute-start.25) | collective-permute-done | bytes 327712 | tf_op jit(solution)/shard_map/ppermute | solution.py:382
  101.9 1.4 shard_map.129
  103.3 1.2 collective-permute-start.31
  106.1 1.4 shard_map.128
  107.6 2.4 %collective-permute-done.26.got_ref = bf16[160,1024]{1,0:T(8,128)(2,1)S(1)} collective-permute-done((bf16[160,1024]{1,0:T(8,128)(2,1)S(1)}, bf16[160,1024]{1,0:T(8,128)(2,1)S(1)}, u32[]{:S(2)}, u32[]{:S(2)}) %collective-permute-start.26) | collective-permute-done | bytes 327712 | tf_op jit(solution)/shard_map/ppermute | solution.py:376
  113.8 1.6 %collective-permute-start.28 = (bf16[64,1024]{1,0:T(8,128)(2,1)S(1)}, bf16[64,1024]{1,0:T(8,128)(2,1)S(1)}, u32[]{:S(2)}, u32[]{:S(2)}) collective-permute-start(bf16[64,1024]{1,0:T(8,128)(2,1)S(1)} %get-tuple-element.90), channel_id=1, source_target_pairs={{0,16},{2,18},{4,20},{6,22},{8,24},{10,26},{12,28},{14,30},{16,0},... | collective-permute-start | bytes 393224 | tf_op jit(solution)/shard_map/ppermute | solution.py:379
  115.5 1.5 %collective-permute-start.29 = (bf16[64,1024]{1,0:T(8,128)(2,1)S(1)}, bf16[64,1024]{1,0:T(8,128)(2,1)S(1)}, u32[]{:S(2)}, u32[]{:S(2)}) collective-permute-start(bf16[64,1024]{1,0:T(8,128)(2,1)S(1)} %get-tuple-element.91), channel_id=1, source_target_pairs={{0,24},{2,26},{4,28},{6,30},{8,0},{10,2},{12,4},{14,6},{16,8},{18,... | collective-permute-start | bytes 393224 | tf_op jit(solution)/shard_map/ppermute | solution.py:379
  116.9 2.2 %collective-permute-done.35.got_ref = bf16[160,1024]{1,0:T(8,128)(2,1)S(1)} collective-permute-done((bf16[160,1024]{1,0:T(8,128)(2,1)S(1)}, bf16[160,1024]{1,0:T(8,128)(2,1)S(1)}, u32[]{:S(2)}, u32[]{:S(2)}) %collective-permute-start.35) | collective-permute-done | bytes 327712 | tf_op jit(solution)/shard_map/ppermute | solution.py:376
  120.1 1.1 collective-permute-start.36
  121.2 1.1 collective-permute-start.37
  122.3 1.4 collective-permute-start.38
  124.4 7.4 %collective-permute-done.29.refs_2_ = bf16[64,1024]{1,0:T(8,128)(2,1)S(1)} collective-permute-done((bf16[64,1024]{1,0:T(8,128)(2,1)S(1)}, bf16[64,1024]{1,0:T(8,128)(2,1)S(1)}, u32[]{:S(2)}, u32[]{:S(2)}) %collective-permute-start.29) | collective-permute-done | bytes 131104 | tf_op jit(solution)/shard_map/ppermute | solution.py:379
  131.9 4.7 %collective-permute-start.30 = (f32[64,1024]{1,0:T(8,128)S(1)}, f32[64,1024]{1,0:T(8,128)S(1)}, u32[]{:S(2)}, u32[]{:S(2)}) collective-permute-start(f32[64,1024]{1,0:T(8,128)S(1)} %shard_map.127.refs_2_), channel_id=1, source_target_pairs={{2,0},{6,4},{10,8},{14,12},{18,16},{22,20},{26,24},{30,28},{3,1},{... | collective-permute-start | bytes 786440 | tf_op jit(solution)/shard_map/ppermute | solution.py:389
  137.5 1.3 collective-permute-start.39
  139.4 1.2 collective-permute-start.19
  141.6 1.4 shard_map.134
  (78 shorter events, 19.0 us)
Async XLA Ops:
  2.9 6.6 %copy-start.4 = (bf16[2048]{0:T(1024)(128)(2,1)S(1)}, bf16[2048]{0:T(1024)(128)(2,1)}, u32[]{:S(2)}) copy-start(bf16[2048]{0:T(1024)(128)(2,1)} %param.15) | copy-start | bytes 12292
  2.9 32.9 %all-to-all-start = ((bf16[16,272,128]{2,1,0:T(8,128)(2,1)}), bf16[16,272,128]{2,1,0:T(8,128)(2,1)S(1)}, u32[]{:S(2)}, u32[]{:S(2)}) async-start(bf16[16,272,128]{2,1,0:T(8,128)(2,1)} %shard_map.109), calls=%async_computation | async-start | bytes 2228224 | tf_op jit(solution)/shard_map/all_to_all | solution.py:402
  9.5 2.8 %collective-permute-start = (bf16[2048]{0:T(1024)(128)(2,1)S(1)}, bf16[2048]{0:T(1024)(128)(2,1)S(1)}, u32[]{:S(2)}, u32[]{:S(2)}) collective-permute-start(bf16[2048]{0:T(1024)(128)(2,1)S(1)} %copy-done.4), channel_id=1, source_target_pairs={{0,1},{1,0},{2,3},{3,2},{4,5},{5,4},{6,7},{7,6},{8,9},{9,8},{10,11... | collective-permute-start | bytes 12296 | tf_op jit(solution)/shard_map/ppermute | solution.py:382
  37.8 4.9 %collective-permute-start.1 = (bf16[512,128]{1,0:T(8,128)(2,1)S(1)}, bf16[512,128]{1,0:T(8,128)(2,1)S(1)}, u32[]{:S(2)}, u32[]{:S(2)}) collective-permute-start(bf16[512,128]{1,0:T(8,128)(2,1)S(1)} %get-tuple-element.57.even_ref.refs_0_), channel_id=1, source_target_pairs={{0,8},{2,10},{4,12},{6,14},{8,16},{10,18},{12,20},{14,22},{16,24},... | collective-permute-start | bytes 393224 | tf_op jit(solution)/shard_map/ppermute | solution.py:379
  37.9 9.8 %collective-permute-start.2 = (bf16[512,128]{1,0:T(8,128)(2,1)S(1)}, bf16[512,128]{1,0:T(8,128)(2,1)S(1)}, u32[]{:S(2)}, u32[]{:S(2)}) collective-permute-start(bf16[512,128]{1,0:T(8,128)(2,1)S(1)} %get-tuple-element.57.even_ref.refs_0_), channel_id=1, source_target_pairs={{0,16},{2,18},{4,20},{6,22},{8,24},{10,26},{12,28},{14,30},{16,0},... | collective-permute-start | bytes 393224 | tf_op jit(solution)/shard_map/ppermute | solution.py:379
  39.3 12.0 %collective-permute-start.5 = (bf16[2,320,128]{2,1,0:T(8,128)(2,1)S(1)}, bf16[2,320,128]{2,1,0:T(8,128)(2,1)S(1)}, u32[]{:S(2)}, u32[]{:S(2)}) collective-permute-start(bf16[2,320,128]{2,1,0:T(8,128)(2,1)S(1)} %get-tuple-element.62), channel_id=1, source_target_pairs={{0,5},{1,4},{2,7},{3,6},{4,1},{5,0},{6,3},{7,2},{8,13},{9,12},{10,... | collective-permute-start | bytes 491528 | tf_op jit(solution)/shard_map/ppermute | solution.py:386
  40.3 11.0 %collective-permute-start.6 = (bf16[2,320,128]{2,1,0:T(8,128)(2,1)S(1)}, bf16[2,320,128]{2,1,0:T(8,128)(2,1)S(1)}, u32[]{:S(2)}, u32[]{:S(2)}) collective-permute-start(bf16[2,320,128]{2,1,0:T(8,128)(2,1)S(1)} %get-tuple-element.62), channel_id=1, source_target_pairs={{0,4},{2,6},{4,0},{6,2},{8,12},{10,14},{12,8},{14,10},{16,20},{18,... | collective-permute-start | bytes 491528 | tf_op jit(solution)/shard_map/ppermute | solution.py:376
  41.8 9.6 %collective-permute-start.4 = (bf16[2,320,128]{2,1,0:T(8,128)(2,1)S(1)}, bf16[2,320,128]{2,1,0:T(8,128)(2,1)S(1)}, u32[]{:S(2)}, u32[]{:S(2)}) collective-permute-start(bf16[2,320,128]{2,1,0:T(8,128)(2,1)S(1)} %get-tuple-element.61), channel_id=1, source_target_pairs={{0,1},{1,0},{2,3},{3,2},{4,5},{5,4},{6,7},{7,6},{8,9},{9,8},{10,11... | collective-permute-start | bytes 491528 | tf_op jit(solution)/shard_map/ppermute | solution.py:382
  42.7 8.6 %collective-permute-start.3 = (bf16[512,128]{1,0:T(8,128)(2,1)S(1)}, bf16[512,128]{1,0:T(8,128)(2,1)S(1)}, u32[]{:S(2)}, u32[]{:S(2)}) collective-permute-start(bf16[512,128]{1,0:T(8,128)(2,1)S(1)} %get-tuple-element.57.even_ref.refs_0_), channel_id=1, source_target_pairs={{0,24},{2,26},{4,28},{6,30},{8,0},{10,2},{12,4},{14,6},{16,8},{18,... | collective-permute-start | bytes 393224 | tf_op jit(solution)/shard_map/ppermute | solution.py:379
  47.7 8.5 %collective-permute-start.7 = (bf16[512,128]{1,0:T(8,128)(2,1)S(1)}, bf16[512,128]{1,0:T(8,128)(2,1)S(1)}, u32[]{:S(2)}, u32[]{:S(2)}) collective-permute-start(bf16[512,128]{1,0:T(8,128)(2,1)S(1)} %get-tuple-element.64.odd_ref.refs_0_), channel_id=1, source_target_pairs={{0,8},{2,10},{4,12},{6,14},{8,16},{10,18},{12,20},{14,22},{16,24},... | collective-permute-start | bytes 393224 | tf_op jit(solution)/shard_map/ppermute | solution.py:379
  52.3 13.4 %collective-permute-start.13 = (bf16[3,320,128]{2,1,0:T(8,128)(2,1)S(1)}, bf16[3,320,128]{2,1,0:T(8,128)(2,1)S(1)}, u32[]{:S(2)}, u32[]{:S(2)}) collective-permute-start(bf16[3,320,128]{2,1,0:T(8,128)(2,1)S(1)} %slice.16), channel_id=1, source_target_pairs={{0,4},{2,6},{4,0},{6,2},{8,12},{10,14},{12,8},{14,10},{16,20},{18,... | collective-permute-start | bytes 737288 | tf_op jit(solution)/shard_map/ppermute | solution.py:376
  52.4 13.3 %collective-permute-start.14 = (bf16[3,320,128]{2,1,0:T(8,128)(2,1)S(1)}, bf16[3,320,128]{2,1,0:T(8,128)(2,1)S(1)}, u32[]{:S(2)}, u32[]{:S(2)}) collective-permute-start(bf16[3,320,128]{2,1,0:T(8,128)(2,1)S(1)} %slice.17), channel_id=1, source_target_pairs={{0,1},{1,0},{2,3},{3,2},{4,5},{5,4},{6,7},{7,6},{8,9},{9,8},{10,11... | collective-permute-start | bytes 737288 | tf_op jit(solution)/shard_map/ppermute | solution.py:382
  53.7 12.0 %collective-permute-start.15 = (bf16[3,320,128]{2,1,0:T(8,128)(2,1)S(1)}, bf16[3,320,128]{2,1,0:T(8,128)(2,1)S(1)}, u32[]{:S(2)}, u32[]{:S(2)}) collective-permute-start(bf16[3,320,128]{2,1,0:T(8,128)(2,1)S(1)} %slice.16), channel_id=1, source_target_pairs={{0,5},{1,4},{2,7},{3,6},{4,1},{5,0},{6,3},{7,2},{8,13},{9,12},{10,... | collective-permute-start | bytes 737288 | tf_op jit(solution)/shard_map/ppermute | solution.py:386
  55.1 4.9 %collective-permute-start.8 = (bf16[512,128]{1,0:T(8,128)(2,1)S(1)}, bf16[512,128]{1,0:T(8,128)(2,1)S(1)}, u32[]{:S(2)}, u32[]{:S(2)}) collective-permute-start(bf16[512,128]{1,0:T(8,128)(2,1)S(1)} %get-tuple-element.64.odd_ref.refs_0_), channel_id=1, source_target_pairs={{0,16},{2,18},{4,20},{6,22},{8,24},{10,26},{12,28},{14,30},{16,0},... | collective-permute-start | bytes 393224 | tf_op jit(solution)/shard_map/ppermute | solution.py:379
  56.2 8.6 %collective-permute-start.9 = (bf16[512,128]{1,0:T(8,128)(2,1)S(1)}, bf16[512,128]{1,0:T(8,128)(2,1)S(1)}, u32[]{:S(2)}, u32[]{:S(2)}) collective-permute-start(bf16[512,128]{1,0:T(8,128)(2,1)S(1)} %get-tuple-element.64.odd_ref.refs_0_), channel_id=1, source_target_pairs={{0,24},{2,26},{4,28},{6,30},{8,0},{10,2},{12,4},{14,6},{16,8},{18,... | collective-permute-start | bytes 393224 | tf_op jit(solution)/shard_map/ppermute | solution.py:379
  65.7 5.6 %copy-start = (bf16[1,4096,512]{2,1,0:T(8,128)(2,1)S(1)}, bf16[1,4096,512]{2,1,0:T(8,128)(2,1)}, u32[]{:S(2)}) copy-start(bf16[1,4096,512]{2,1,0:T(8,128)(2,1)} %param.19) | copy-start | bytes 12582916
  66.7 8.8 %collective-permute-start.16 = (bf16[320,2176]{1,0:T(8,128)(2,1)S(1)}, bf16[320,2176]{1,0:T(8,128)(2,1)S(1)}, u32[]{:S(2)}, u32[]{:S(2)}) collective-permute-start(bf16[320,2176]{1,0:T(8,128)(2,1)S(1)} %shard_map.114.lhs_ref.refs_0_), channel_id=1, source_target_pairs={{0,2},{2,0},{4,6},{6,4},{8,10},{10,8},{12,14},{14,12},{16,18},{18,... | collective-permute-start | bytes 4177928 | tf_op jit(solution)/shard_map/ppermute | solution.py:376
  68.6 9.1 %collective-permute-start.10 = (bf16[3,320,128]{2,1,0:T(8,128)(2,1)S(1)}, bf16[3,320,128]{2,1,0:T(8,128)(2,1)S(1)}, u32[]{:S(2)}, u32[]{:S(2)}) collective-permute-start(bf16[3,320,128]{2,1,0:T(8,128)(2,1)S(1)} %slice.14), channel_id=1, source_target_pairs={{0,4},{2,6},{4,0},{6,2},{8,12},{10,14},{12,8},{14,10},{16,20},{18,... | collective-permute-start | bytes 737288 | tf_op jit(solution)/shard_map/ppermute | solution.py:376
  69.0 8.7 %collective-permute-start.11 = (bf16[3,320,128]{2,1,0:T(8,128)(2,1)S(1)}, bf16[3,320,128]{2,1,0:T(8,128)(2,1)S(1)}, u32[]{:S(2)}, u32[]{:S(2)}) collective-permute-start(bf16[3,320,128]{2,1,0:T(8,128)(2,1)S(1)} %slice.15), channel_id=1, source_target_pairs={{0,1},{1,0},{2,3},{3,2},{4,5},{5,4},{6,7},{7,6},{8,9},{9,8},{10,11... | collective-permute-start | bytes 737288 | tf_op jit(solution)/shard_map/ppermute | solution.py:382
  70.2 12.1 %collective-permute-start.12 = (bf16[3,320,128]{2,1,0:T(8,128)(2,1)S(1)}, bf16[3,320,128]{2,1,0:T(8,128)(2,1)S(1)}, u32[]{:S(2)}, u32[]{:S(2)}) collective-permute-start(bf16[3,320,128]{2,1,0:T(8,128)(2,1)S(1)} %slice.14), channel_id=1, source_target_pairs={{0,5},{1,4},{2,7},{3,6},{4,1},{5,0},{6,3},{7,2},{8,13},{9,12},{10,... | collective-permute-start | bytes 737288 | tf_op jit(solution)/shard_map/ppermute | solution.py:386
  71.3 2.2 %copy-start.1 = (bf16[1,4096,512]{2,1,0:T(8,128)(2,1)S(1)}, bf16[1,4096,512]{2,1,0:T(8,128)(2,1)}, u32[]{:S(2)}) copy-start(bf16[1,4096,512]{2,1,0:T(8,128)(2,1)} %param.20) | copy-start | bytes 12582916
  75.6 10.2 %copy-start.2 = (bf16[1,4096,512]{2,1,0:T(8,128)(2,1)S(1)}, bf16[1,4096,512]{2,1,0:T(8,128)(2,1)}, u32[]{:S(2)}) copy-start(bf16[1,4096,512]{2,1,0:T(8,128)(2,1)} %param.20) | copy-start | bytes 12582916
  83.4 4.5 %collective-permute-start.17 = (bf16[320,2176]{1,0:T(8,128)(2,1)S(1)}, bf16[320,2176]{1,0:T(8,128)(2,1)S(1)}, u32[]{:S(2)}, u32[]{:S(2)}) collective-permute-start(bf16[320,2176]{1,0:T(8,128)(2,1)S(1)} %shard_map.117.lhs_ref.refs_0_), channel_id=1, source_target_pairs={{0,2},{2,0},{4,6},{6,4},{8,10},{10,8},{12,14},{14,12},{16,18},{18,... | collective-permute-start | bytes 4177928 | tf_op jit(solution)/shard_map/ppermute | solution.py:376
  84.6 9.3 %collective-permute-start.20 = (bf16[320,512]{1,0:T(8,128)(2,1)S(1)}, bf16[320,512]{1,0:T(8,128)(2,1)S(1)}, u32[]{:S(2)}, u32[]{:S(2)}) collective-permute-start(bf16[320,512]{1,0:T(8,128)(2,1)S(1)} %shard_map.116.refs_7_.own_ref), channel_id=1, source_target_pairs={{0,1},{1,0},{2,3},{3,2},{4,5},{5,4},{6,7},{7,6},{8,9},{9,8},{10,11... | collective-permute-start | bytes 983048 | tf_op jit(solution)/shard_map/ppermute | solution.py:382
  87.9 6.0 %copy-start.3 = (bf16[1,1024,2048]{2,1,0:T(8,128)(2,1)S(1)}, bf16[1,1024,2048]{2,1,0:T(8,128)(2,1)}, u32[]{:S(2)}) copy-start(bf16[1,1024,2048]{2,1,0:T(8,128)(2,1)} %param.21) | copy-start | bytes 12582916
  90.0 10.9 %collective-permute-start.25 = (bf16[320,512]{1,0:T(8,128)(2,1)S(1)}, bf16[320,512]{1,0:T(8,128)(2,1)S(1)}, u32[]{:S(2)}, u32[]{:S(2)}) collective-permute-start(bf16[320,512]{1,0:T(8,128)(2,1)S(1)} %shard_map.119.refs_2_.refs_0_.own_ref), channel_id=1, source_target_pairs={{0,1},{1,0},{2,3},{3,2},{4,5},{5,4},{6,7},{7,6},{8,9},{9,8},{10,11... | collective-permute-start | bytes 983048 | tf_op jit(solution)/shard_map/ppermute | solution.py:382
  95.3 3.4 %collective-permute-start.21 = (bf16[320,256]{1,0:T(8,128)(2,1)S(1)}, bf16[320,256]{1,0:T(8,128)(2,1)S(1)}, u32[]{:S(2)}, u32[]{:S(2)}) collective-permute-start(bf16[320,256]{1,0:T(8,128)(2,1)S(1)} %get-tuple-element.84), channel_id=1, source_target_pairs={{0,2},{2,0},{4,6},{6,4},{8,10},{10,8},{12,14},{14,12},{16,18},{18,... | collective-permute-start | bytes 491528 | tf_op jit(solution)/shard_map/ppermute | solution.py:376
  96.6 2.0 %collective-permute-start.22 = (bf16[320,256]{1,0:T(8,128)(2,1)S(1)}, bf16[320,256]{1,0:T(8,128)(2,1)S(1)}, u32[]{:S(2)}, u32[]{:S(2)}) collective-permute-start(bf16[320,256]{1,0:T(8,128)(2,1)S(1)} %get-tuple-element.85), channel_id=1, source_target_pairs={{0,2},{2,0},{4,6},{6,4},{8,10},{10,8},{12,14},{14,12},{16,18},{18,... | collective-permute-start | bytes 491528 | tf_op jit(solution)/shard_map/ppermute | solution.py:376
  96.7 2.0 %collective-permute-start.23 = (bf16[320,256]{1,0:T(8,128)(2,1)S(1)}, bf16[320,256]{1,0:T(8,128)(2,1)S(1)}, u32[]{:S(2)}, u32[]{:S(2)}) collective-permute-start(bf16[320,256]{1,0:T(8,128)(2,1)S(1)} %get-tuple-element.86), channel_id=1, source_target_pairs={{0,2},{2,0},{4,6},{6,4},{8,10},{10,8},{12,14},{14,12},{16,18},{18,... | collective-permute-start | bytes 491528 | tf_op jit(solution)/shard_map/ppermute | solution.py:376
  97.1 1.5 %collective-permute-start.24 = (bf16[320,256]{1,0:T(8,128)(2,1)S(1)}, bf16[320,256]{1,0:T(8,128)(2,1)S(1)}, u32[]{:S(2)}, u32[]{:S(2)}) collective-permute-start(bf16[320,256]{1,0:T(8,128)(2,1)S(1)} %get-tuple-element.87), channel_id=1, source_target_pairs={{0,2},{2,0},{4,6},{6,4},{8,10},{10,8},{12,14},{14,12},{16,18},{18,... | collective-permute-start | bytes 491528 | tf_op jit(solution)/shard_map/ppermute | solution.py:376
  101.5 8.4 %collective-permute-start.26 = (bf16[160,1024]{1,0:T(8,128)(2,1)S(1)}, bf16[160,1024]{1,0:T(8,128)(2,1)S(1)}, u32[]{:S(2)}, u32[]{:S(2)}) collective-permute-start(bf16[160,1024]{1,0:T(8,128)(2,1)S(1)} %shard_map.125.refs_0_), channel_id=1, source_target_pairs={{0,4},{2,6},{4,0},{6,2},{8,12},{10,14},{12,8},{14,10},{16,20},{18,... | collective-permute-start | bytes 983048 | tf_op jit(solution)/shard_map/ppermute | solution.py:376
  103.3 7.6 %collective-permute-start.31 = (bf16[320,256]{1,0:T(8,128)(2,1)S(1)}, bf16[320,256]{1,0:T(8,128)(2,1)S(1)}, u32[]{:S(2)}, u32[]{:S(2)}) collective-permute-start(bf16[320,256]{1,0:T(8,128)(2,1)S(1)} %get-tuple-element.97), channel_id=1, source_target_pairs={{0,2},{2,0},{4,6},{6,4},{8,10},{10,8},{12,14},{14,12},{16,18},{18,... | collective-permute-start | bytes 491528 | tf_op jit(solution)/shard_map/ppermute | solution.py:376
  104.5 6.4 %collective-permute-start.32 = (bf16[320,256]{1,0:T(8,128)(2,1)S(1)}, bf16[320,256]{1,0:T(8,128)(2,1)S(1)}, u32[]{:S(2)}, u32[]{:S(2)}) collective-permute-start(bf16[320,256]{1,0:T(8,128)(2,1)S(1)} %get-tuple-element.98), channel_id=1, source_target_pairs={{0,2},{2,0},{4,6},{6,4},{8,10},{10,8},{12,14},{14,12},{16,18},{18,... | collective-permute-start | bytes 491528 | tf_op jit(solution)/shard_map/ppermute | solution.py:376
  104.6 6.3 %collective-permute-start.33 = (bf16[320,256]{1,0:T(8,128)(2,1)S(1)}, bf16[320,256]{1,0:T(8,128)(2,1)S(1)}, u32[]{:S(2)}, u32[]{:S(2)}) collective-permute-start(bf16[320,256]{1,0:T(8,128)(2,1)S(1)} %get-tuple-element.99), channel_id=1, source_target_pairs={{0,2},{2,0},{4,6},{6,4},{8,10},{10,8},{12,14},{14,12},{16,18},{18,... | collective-permute-start | bytes 491528 | tf_op jit(solution)/shard_map/ppermute | solution.py:376
  105.0 5.9 %collective-permute-start.34 = (bf16[320,256]{1,0:T(8,128)(2,1)S(1)}, bf16[320,256]{1,0:T(8,128)(2,1)S(1)}, u32[]{:S(2)}, u32[]{:S(2)}) collective-permute-start(bf16[320,256]{1,0:T(8,128)(2,1)S(1)} %get-tuple-element.100), channel_id=1, source_target_pairs={{0,2},{2,0},{4,6},{6,4},{8,10},{10,8},{12,14},{14,12},{16,18},{18,... | collective-permute-start | bytes 491528 | tf_op jit(solution)/shard_map/ppermute | solution.py:376
  111.6 7.5 %collective-permute-start.35 = (bf16[160,1024]{1,0:T(8,128)(2,1)S(1)}, bf16[160,1024]{1,0:T(8,128)(2,1)S(1)}, u32[]{:S(2)}, u32[]{:S(2)}) collective-permute-start(bf16[160,1024]{1,0:T(8,128)(2,1)S(1)} %shard_map.131), channel_id=1, source_target_pairs={{0,4},{2,6},{4,0},{6,2},{8,12},{10,14},{12,8},{14,10},{16,20},{18,... | collective-permute-start | bytes 983048 | tf_op jit(solution)/shard_map/ppermute | solution.py:376
  112.0 10.3 %collective-permute-start.27 = (bf16[64,1024]{1,0:T(8,128)(2,1)S(1)}, bf16[64,1024]{1,0:T(8,128)(2,1)S(1)}, u32[]{:S(2)}, u32[]{:S(2)}) collective-permute-start(bf16[64,1024]{1,0:T(8,128)(2,1)S(1)} %get-tuple-element.89), channel_id=1, source_target_pairs={{0,8},{2,10},{4,12},{6,14},{8,16},{10,18},{12,20},{14,22},{16,24},... | collective-permute-start | bytes 393224 | tf_op jit(solution)/shard_map/ppermute | solution.py:379
  113.8 9.9 %collective-permute-start.28 = (bf16[64,1024]{1,0:T(8,128)(2,1)S(1)}, bf16[64,1024]{1,0:T(8,128)(2,1)S(1)}, u32[]{:S(2)}, u32[]{:S(2)}) collective-permute-start(bf16[64,1024]{1,0:T(8,128)(2,1)S(1)} %get-tuple-element.90), channel_id=1, source_target_pairs={{0,16},{2,18},{4,20},{6,22},{8,24},{10,26},{12,28},{14,30},{16,0},... | collective-permute-start | bytes 393224 | tf_op jit(solution)/shard_map/ppermute | solution.py:379
  115.5 16.4 %collective-permute-start.29 = (bf16[64,1024]{1,0:T(8,128)(2,1)S(1)}, bf16[64,1024]{1,0:T(8,128)(2,1)S(1)}, u32[]{:S(2)}, u32[]{:S(2)}) collective-permute-start(bf16[64,1024]{1,0:T(8,128)(2,1)S(1)} %get-tuple-element.91), channel_id=1, source_target_pairs={{0,24},{2,26},{4,28},{6,30},{8,0},{10,2},{12,4},{14,6},{16,8},{18,... | collective-permute-start | bytes 393224 | tf_op jit(solution)/shard_map/ppermute | solution.py:379
  120.1 16.6 %collective-permute-start.36 = (bf16[64,1024]{1,0:T(8,128)(2,1)S(1)}, bf16[64,1024]{1,0:T(8,128)(2,1)S(1)}, u32[]{:S(2)}, u32[]{:S(2)}) collective-permute-start(bf16[64,1024]{1,0:T(8,128)(2,1)S(1)} %get-tuple-element.102), channel_id=1, source_target_pairs={{0,8},{2,10},{4,12},{6,14},{8,16},{10,18},{12,20},{14,22},{16,24},... | collective-permute-start | bytes 393224 | tf_op jit(solution)/shard_map/ppermute | solution.py:379
  121.2 15.4 %collective-permute-start.37 = (bf16[64,1024]{1,0:T(8,128)(2,1)S(1)}, bf16[64,1024]{1,0:T(8,128)(2,1)S(1)}, u32[]{:S(2)}, u32[]{:S(2)}) collective-permute-start(bf16[64,1024]{1,0:T(8,128)(2,1)S(1)} %get-tuple-element.103), channel_id=1, source_target_pairs={{0,16},{2,18},{4,20},{6,22},{8,24},{10,26},{12,28},{14,30},{16,0},... | collective-permute-start | bytes 393224 | tf_op jit(solution)/shard_map/ppermute | solution.py:379
  122.3 15.2 %collective-permute-start.38 = (bf16[64,1024]{1,0:T(8,128)(2,1)S(1)}, bf16[64,1024]{1,0:T(8,128)(2,1)S(1)}, u32[]{:S(2)}, u32[]{:S(2)}) collective-permute-start(bf16[64,1024]{1,0:T(8,128)(2,1)S(1)} %get-tuple-element.104), channel_id=1, source_target_pairs={{0,24},{2,26},{4,28},{6,30},{8,0},{10,2},{12,4},{14,6},{16,8},{18,... | collective-permute-start | bytes 393224 | tf_op jit(solution)/shard_map/ppermute | solution.py:379
  123.8 15.1 %collective-permute-start.18 = (bf16[2,4,64,128]{3,2,1,0:T(8,128)(2,1)S(1)}, bf16[2,4,64,128]{3,2,1,0:T(8,128)(2,1)S(1)}, u32[]{:S(2)}, u32[]{:S(2)}) collective-permute-start(bf16[2,4,64,128]{3,2,1,0:T(8,128)(2,1)S(1)} %shard_map.120), channel_id=1, source_target_pairs={{0,4},{2,6},{4,0},{6,2},{8,12},{10,14},{12,8},{14,10},{16,20},{18,... | collective-permute-start | bytes 393224 | tf_op jit(solution)/shard_map/ppermute | solution.py:376
  131.9 9.7 %collective-permute-start.30 = (f32[64,1024]{1,0:T(8,128)S(1)}, f32[64,1024]{1,0:T(8,128)S(1)}, u32[]{:S(2)}, u32[]{:S(2)}) collective-permute-start(f32[64,1024]{1,0:T(8,128)S(1)} %shard_map.127.refs_2_), channel_id=1, source_target_pairs={{2,0},{6,4},{10,8},{14,12},{18,16},{22,20},{26,24},{30,28},{3,1},{... | collective-permute-start | bytes 786440 | tf_op jit(solution)/shard_map/ppermute | solution.py:389
  137.5 4.1 %collective-permute-start.39 = (f32[64,1024]{1,0:T(8,128)S(1)}, f32[64,1024]{1,0:T(8,128)S(1)}, u32[]{:S(2)}, u32[]{:S(2)}) collective-permute-start(f32[64,1024]{1,0:T(8,128)S(1)} %shard_map.133.refs_4_), channel_id=1, source_target_pairs={{0,2},{4,6},{8,10},{12,14},{16,18},{20,22},{24,26},{28,30},{1,3},{... | collective-permute-start | bytes 786440 | tf_op jit(solution)/shard_map/ppermute | solution.py:389
  139.4 2.2 %collective-permute-start.19 = (bf16[8,64,128]{2,1,0:T(8,128)(2,1)S(1)}, bf16[8,64,128]{2,1,0:T(8,128)(2,1)S(1)}, u32[]{:S(2)}, u32[]{:S(2)}) collective-permute-start(bf16[8,64,128]{2,1,0:T(8,128)(2,1)S(1)} %get-tuple-element.78), channel_id=1, source_target_pairs={{0,2},{2,0},{4,6},{6,4},{8,10},{10,8},{12,14},{14,12},{16,18},{18,... | collective-permute-start | bytes 393224 | tf_op jit(solution)/shard_map/ppermute | solution.py:376
